TPU v7x, 128 devices: a whole 4x4x4 slice. The times are simulated.
128 devices in a mesh: grp: 4 (over z), dev: 32 (over x, y, core).
Axes of the slice: x: 4, y: 4, z: 4, core: 2. Of those that a mesh axis runs over, the one named last changes fastest.
Arguments:
- queries: float32 [16384, 4096], P(('grp', 'dev'))
- passages: float32 [16384, 4096], P(('grp', 'dev'))
- pairs: int32 [128, 8], P('grp'), may hold values from 0 to 127, as said below
- counts: int32 [4, 32], P('grp'), may hold values from 1 to 8, 128 in all within a row
- positives: int32 [16384], P(('grp', 'dev')), may hold values from 0 to 127
Outputs:
- loss: float32 [16384], P(('grp', 'dev'))
- grad_queries: float32 [16384, 4096], P(('grp', 'dev'))
- grad_passages: float32 [16384, 4096], P(('grp', 'dev'))
Inputs may be any that keep to these rules, and one draw needn't show every extreme that they name: `pairs`: entries k < c_b of row b name passage blocks anywhere in the whole set; later entries are ignored. A list may name a block twice. The counts of one group sum to exactly 128.
All inputs are finite; a program needn't handle non-finite values.
Results may differ from a plain program's by a relative error of at most 0.0059.
Values may be sent and summed in bfloat16 or wider, within the bound.
No kernel may reach another device: no remote copies, remote signals or barrier semaphores. Data moves between devices by JAX's collectives and lax.ppermute only.
A program may use at most 128 MiB of HBM per device.

v0:
```python
import jax
import jax.numpy as jnp
from jax import lax
from jax.sharding import PartitionSpec as P


def select_blocks(table, ids):
    number = table.shape[0]
    onehot = (ids[:, None] == jnp.arange(number, dtype=jnp.int32)[None, :]).astype(table.dtype)
    picked = jnp.dot(onehot, table.reshape(number, -1), preferred_element_type=jnp.float32)
    return picked.astype(table.dtype).reshape((ids.shape[0],) + table.shape[1:])


def add_blocks(total, ids, terms):
    number = total.shape[0]
    onehot = (jnp.arange(number, dtype=jnp.int32)[:, None] == ids[None, :]).astype(jnp.float32)
    summed = jnp.dot(
        onehot,
        terms.reshape(ids.shape[0], -1),
        precision=lax.Precision.HIGHEST,
        preferred_element_type=jnp.float32,
    )
    return summed.reshape(total.shape)


def per_device(queries, passages, pairs, counts, positives):
    ndev = lax.axis_size("dev")
    ngrp = lax.axis_size("grp")
    blk = queries.shape[0]
    width = queries.shape[1]
    part = width // ndev
    maxp = pairs.shape[1]
    scale = width ** (-0.5)
    q_half = queries.astype(jnp.bfloat16)
    p_half = passages.astype(jnp.bfloat16)
    q_cols, p_cols = (
        lax.all_to_all(q_half, "dev", split_axis=1, concat_axis=0, tiled=True),
        lax.all_to_all(p_half, "dev", split_axis=1, concat_axis=0, tiled=True),
    )
    p_every = lax.all_gather(p_cols, "grp", axis=0, tiled=True)
    p_blocks = p_every.reshape(ngrp * ndev, blk, part)
    q_blocks = q_cols.reshape(ndev, blk, part)
    group_counts = counts[0]
    own = lax.axis_index("dev")
    places = jnp.arange(ndev, dtype=jnp.int32)
    columns = jnp.arange(blk, dtype=jnp.int32)
    grad_p_zero = jnp.zeros((ngrp * ndev, blk, part), jnp.float32)
    q_sel = q_blocks
    ids = pairs
    p_sel = select_blocks(p_blocks, ids.reshape(-1)).reshape(
        lax.axis_size("dev") * 1, maxp, blk, part
    )
    scores = (
        lax.psum_scatter(
            jnp.einsum("bif,bkjf->bkij", q_sel, p_sel, preferred_element_type=jnp.float32),
            "dev",
            scatter_dimension=0,
            tiled=True,
        )[0]
        * scale
    )
    own_count = jnp.sum(jnp.where(places == own, group_counts, 0))
    valid = (jnp.arange(maxp, dtype=jnp.int32) < own_count)[:, None, None]
    masked = jnp.where(valid, scores, -1e30)
    top = jnp.max(masked, axis=(0, 2))
    total = jnp.sum(jnp.where(valid, jnp.exp(masked - top[None, :, None]), 0.0), axis=(0, 2))
    lse = top + jnp.log(total)
    hit = columns[None, :] == positives[:, None]
    positive = jnp.sum(jnp.where(hit, scores[0], 0.0), axis=1)
    loss = lse - positive
    first = (jnp.arange(maxp, dtype=jnp.int32) == 0)[:, None, None] & hit[None]
    prob = jnp.where(valid, jnp.exp(masked - lse[None, :, None]), 0.0)
    weights = (prob - first.astype(jnp.float32)).astype(jnp.bfloat16)
    piece = lax.all_gather(weights[None], "dev", axis=0, tiled=True)
    grad_p = grad_p_zero
    count = piece.shape[0]
    q_sel = q_blocks
    ids = pairs.reshape(-1)
    p_sel = select_blocks(p_blocks, ids).reshape(count, maxp, blk, part)
    q_terms = jnp.einsum("bkij,bkjf->bif", piece, p_sel, preferred_element_type=jnp.float32)
    grad_q = q_terms
    p_terms = jnp.einsum("bkij,bif->bkjf", piece, q_sel, preferred_element_type=jnp.float32)
    grad_p = add_blocks(grad_p, ids, p_terms.reshape(count * maxp, blk, part))
    grad_q, grad_p = (grad_q, grad_p)
    group_grad = lax.psum_scatter(
        grad_p.reshape(ngrp * ndev * blk, part), "grp", scatter_dimension=0, tiled=True
    )
    q_rows, p_rows = (
        lax.all_to_all(
            grad_q.reshape(ndev * blk, part), "dev", split_axis=0, concat_axis=1, tiled=True
        ),
        lax.all_to_all(group_grad, "dev", split_axis=0, concat_axis=1, tiled=True),
    )
    return (loss, q_rows, p_rows)


def solution(mesh):
    placed = (
        P(("grp", "dev"), None),
        P(("grp", "dev"), None),
        P("grp", None),
        P("grp", None),
        P(("grp", "dev")),
    )
    return jax.shard_map(
        per_device,
        mesh=mesh,
        in_specs=placed,
        out_specs=(P(("grp", "dev")), P(("grp", "dev"), None), P(("grp", "dev"), None)),
        check_vma=False,
    )
```

profile of v0, /device:TPU:1, one launch (start us, length us, event | category | flops | bytes accessed | tf_op | source)
XLA Modules:
  0.0 453.3 jit_solution(7194434560551107886)
XLA Ops:
  7.2 0.0 copy-start
  7.2 0.0 all-gather.3.cloned.1.call-start
  7.2 1.8 copy.44
  9.1 25.3 %all_to_all.70 = bf16[128,32,128]{0,2,1:T(8,128)(2,1)S(1)} all-to-all(bf16[128,32,128]{0,2,1:T(8,128)(2,1)S(1)} %bitcast.52), channel_id=1, replica_groups=mesh['grp'=4,'dev'=32] {'dev'}, dimensions={1} | all-to-all | bytes 2097152 | tf_op jit(solution)/shard_map/all_to_all | solution.py:38
  34.4 1.3 copy.45
  35.7 0.0 all-gather.3.cloned.1.call-update
  35.7 1.8 copy.46
  37.5 1.3 copy.47
  38.9 4.0 all-to-all-start.1
  42.8 0.0 reduce-scatter.3.cloned.1.call-start
  42.9 0.0 copy-done
  42.9 0.1 copy.43
  43.0 0.1 eq.67
  43.0 39.9 %all-gather.3.cloned.1.call-done = bf16[16384,128]{1,0:T(8,128)(2,1)} async-done(((bf16[4096,128]{1,0:T(8,128)(2,1)}), bf16[16384,128]{1,0:T(8,128)(2,1)}) %all-gather.3.cloned.1.call-update) | async-done | bytes 4194320 | tf_op jit(solution)/shard_map/all_gather | solution.py:40
  82.9 7.3 %reshape_reshape.14 = bf16[128,16384]{1,0:T(8,128)(2,1)} reshape(bf16[16384,128]{1,0:T(8,128)(2,1)} %all-gather.3.cloned.1.call-done) | data formatting | bytes 8388608 | tf_op jit(solution)/shard_map/reshape;reshape | solution.py:10
  90.2 7.8 %fusion.6 = bf16[32,8,128,128]{3,1,2,0:T(8,128)(2,1)} fusion(bf16[128,16384]{1,0:T(8,128)(2,1)} %reshape_reshape.14, s32[256]{0:T(256)S(1)} %eq.67), kind=kOutput, calls=%fused_computation.9 | convolution fusion | flops 1077968896 | bytes 12583936 | tf_op jit(solution)/shard_map/dot_general | solution.py:10
  98.0 0.0 all-to-all-done.1
  98.0 11.5 %convolution_bitcast_fusion.1 = f32[32,8,128,128]{2,3,1,0:T(8,128)} fusion(bf16[32,8,128,128]{3,1,2,0:T(8,128)(2,1)} %fusion.6, bf16[128,32,128]{2,0,1:T(8,128)(2,1)S(1)} %all-to-all-done.1), kind=kOutput, calls=%fused_computation.5 | convolution fusion | flops 1073741824 | bytes 26214400 | tf_op jit(solution)/shard_map/bif,bkjf->bkij/dot_general | solution.py:55
  109.4 0.0 copy-start.2
  109.4 0.0 reduce-scatter.3.cloned.1.call-update
  109.5 0.0 all-gather.5.cloned.1.call-start
  109.5 0.6 copy-done.2
  110.1 0.6 fusion.17
  110.7 0.6 iota_compare_fusion.5
  111.4 0.0 copy-done.1
  111.4 112.3 %reduce-scatter.3.cloned.1.call-done = f32[1,8,128,128]{2,3,1,0:T(8,128)} async-done(((f32[32,8,128,128]{2,3,1,0:T(8,128)}), f32[1,8,128,128]{2,3,1,0:T(8,128)}) %reduce-scatter.3.cloned.1.call-update) | async-done | bytes 524304 | tf_op jit(solution)/shard_map/reduce_scatter | solution.py:54
  223.7 1.1 broadcast_multiply_fusion
  224.9 1.3 fusion.12
  226.1 1.3 select_reduce_fusion
  227.4 0.5 fusion.18
  227.9 1.3 subtract_convert_fusion
  229.2 0.9 copy.49
  230.0 0.0 all-gather.5.cloned.1.call-update
  230.1 0.2 reduce-scatter.5.cloned.1.call-start
  230.3 53.7 %all-gather.5.cloned.1.call-done = bf16[32,8,128,128]{3,2,1,0:T(8,128)(2,1)} async-done(((bf16[1,8,128,128]{3,2,1,0:T(8,128)(2,1)}), bf16[32,8,128,128]{3,2,1,0:T(8,128)(2,1)}) %all-gather.5.cloned.1.call-update) | async-done | bytes 8388624 | tf_op jit(solution)/shard_map/all_gather | solution.py:74
  284.0 11.5 %convolution_bitcast_fusion = f32[32,8,128,128]{3,2,1,0:T(8,128)} fusion(bf16[32,8,128,128]{3,2,1,0:T(8,128)(2,1)} %all-gather.5.cloned.1.call-done, bf16[128,32,128]{2,0,1:T(8,128)(2,1)S(1)} %all-to-all-done.1), kind=kOutput, calls=%fused_computation.4 | convolution fusion | flops 1073741824 | bytes 26214400 | tf_op jit(solution)/shard_map/bkij,bif->bkjf/dot_general | solution.py:82
  295.5 21.3 %fusion = f32[128,16384]{1,0:T(8,128)} fusion(f32[32,8,128,128]{3,2,1,0:T(8,128)} %convolution_bitcast_fusion, s32[256]{0:T(256)S(1)} %eq.67), kind=kOutput, calls=%fused_computation.1 | convolution fusion | flops 6442483712 | bytes 25166848 | tf_op jit(solution)/shard_map/dot_general | solution.py:17
  316.8 9.3 %reshape_reshape.17 = f32[16384,128]{1,0:T(8,128)} reshape(f32[128,16384]{1,0:T(8,128)} %fusion) | data formatting | bytes 16777216 | tf_op jit(solution)/shard_map/reshape;reshape | solution.py:86
  326.1 0.0 reduce-scatter.5.cloned.1.call-update
  326.1 8.1 %fusion.7 = f32[32,128,128]{2,1,0:T(8,128)S(1)} fusion(bf16[32,8,128,128]{3,2,1,0:T(8,128)(2,1)} %all-gather.5.cloned.1.call-done, bf16[32,8,128,128]{3,1,2,0:T(8,128)(2,1)} %fusion.6), kind=kOutput, calls=%fused_computation.10 | convolution fusion | flops 1073741824 | bytes 18874368 | tf_op jit(solution)/shard_map/bkij,bkjf->bif/dot_general | solution.py:80
  334.3 33.5 %all_to_all.71 = f32[32,128,128]{2,1,0:T(8,128)} all-to-all(f32[32,128,128]{2,1,0:T(8,128)S(1)} %fusion.7), channel_id=1, replica_groups=mesh['grp'=4,'dev'=32] {'dev'}, dimensions={0} | all-to-all | bytes 4194304 | tf_op jit(solution)/shard_map/all_to_all | solution.py:89
  367.8 38.5 %reduce-scatter.5.cloned.1.call-done = f32[4096,128]{1,0:T(8,128)} async-done(((f32[16384,128]{1,0:T(8,128)}), f32[4096,128]{1,0:T(8,128)}) %reduce-scatter.5.cloned.1.call-update) | async-done | bytes 2097168 | tf_op jit(solution)/shard_map/reduce_scatter | solution.py:85
  406.3 7.5 %all-to-all-start.3 = ((f32[32,128,128]{2,1,0:T(8,128)}), f32[32,128,128]{2,1,0:T(8,128)S(1)}, u32[]{:S(2)}, u32[]{:S(2)}) async-start(f32[32,128,128]{2,1,0:T(8,128)} %bitcast.56), calls=%async_computation.5 | async-start | bytes 4194304 | tf_op jit(solution)/shard_map/all_to_all | solution.py:92
  413.7 2.9 copy.51
  416.6 2.9 copy.54
  419.5 22.5 %all-to-all-done.3 = f32[32,128,128]{2,1,0:T(8,128)S(1)} async-done(((f32[32,128,128]{2,1,0:T(8,128)}), f32[32,128,128]{2,1,0:T(8,128)S(1)}, u32[]{:S(2)}, u32[]{:S(2)}) %all-to-all-start.3) | async-done | bytes 2097184 | tf_op jit(solution)/shard_map/all_to_all | solution.py:92
  442.0 1.9 copy.53
  443.9 2.9 copy.55
  (3 shorter events, 0.1 us)
Async XLA Ops:
  7.2 35.7 %copy-start = (s32[32,8]{0,1:T(8,128)S(1)}, s32[32,8]{0,1:T(8,128)}, u32[]{:S(2)}) copy-start(s32[32,8]{0,1:T(8,128)} %param.7) | copy-start | bytes 3076
  7.2 75.7 %all-gather.3.cloned.1.call-start = ((), (), s32[]{:S(2)}) async-start(), calls=%async_computation.6 | async-start | bytes 5242880 | tf_op jit(solution)/shard_map/all_gather | solution.py:40
  38.9 59.1 %all-to-all-start.1 = ((bf16[128,32,128]{2,0,1:T(8,128)(2,1)}), bf16[128,32,128]{2,0,1:T(8,128)(2,1)S(1)}, u32[]{:S(2)}, u32[]{:S(2)}) async-start(bf16[128,32,128]{2,0,1:T(8,128)(2,1)} %copy.47), calls=%async_computation.1 | async-start | bytes 2097152 | tf_op jit(solution)/shard_map/all_to_all | solution.py:37
  42.8 180.9 %reduce-scatter.3.cloned.1.call-start = ((), (), s32[]{:S(2)}) async-start(), calls=%async_computation.7 | async-start | bytes 17301504 | tf_op jit(solution)/shard_map/reduce_scatter | solution.py:54
  109.4 0.7 copy-start.2
  109.4 1.9 copy-start.1
  109.5 174.5 %all-gather.5.cloned.1.call-start = ((), (), s32[]{:S(2)}) async-start(), calls=%async_computation.8 | async-start | bytes 8650752 | tf_op jit(solution)/shard_map/all_gather | solution.py:74
  230.1 176.2 %reduce-scatter.5.cloned.1.call-start = ((), (), s32[]{:S(2)}) async-start(), calls=%async_computation.9 | async-start | bytes 10485760 | tf_op jit(solution)/shard_map/reduce_scatter | solution.py:85
  406.3 35.8 %all-to-all-start.3 = ((f32[32,128,128]{2,1,0:T(8,128)}), f32[32,128,128]{2,1,0:T(8,128)S(1)}, u32[]{:S(2)}, u32[]{:S(2)}) async-start(f32[32,128,128]{2,1,0:T(8,128)} %bitcast.56), calls=%async_computation.5 | async-start | bytes 4194304 | tf_op jit(solution)/shard_map/all_to_all | solution.py:92
Sparse Core Ops, SparseCore 0:
  35.8 47.0 all-gather.2
  109.6 114.0 reduce-scatter.2
  230.2 53.7 all-gather.4
  326.3 79.9 reduce-scatter.4
where the time goes:
time: 454 us; the launch traced here: 453 us
  waiting for transfers between devices  267 us (59%)
  matrix products  60.2 us (13%)
  blocking collectives  58.8 us (13%)
  local copies, waits for them, and re-layouts  34.9 us (8%)
  between operations  13.9 us (3%)
  starting transfers between devices  11.8 us (3%)
  other arithmetic  6.74 us (1%)
    reduce_scatter x1, waiting for transfers between devices, per_device(): lax.psum_scatter(jnp.einsum('bif,bkjf->bkij', q_sel, p_sel, preferred_ele...  112 us
    all_gather x1, waiting for transfers between devices, per_device(): piece = lax.all_gather(weights[None], 'dev', axis=0, tiled=True)  53.7 us
    all_gather x1, waiting for transfers between devices, per_device(): p_every = lax.all_gather(p_cols, 'grp', axis=0, tiled=True)  39.9 us
    reduce_scatter x1, waiting for transfers between devices, per_device(): lax.psum_scatter(grad_p.reshape(ngrp * ndev * blk, part), 'grp', scatter_...  38.5 us
    all_to_all x1, blocking collectives, per_device(): lax.all_to_all(grad_q.reshape(ndev * blk, part), 'dev', split_axis=0, con...  33.5 us
    all_to_all x1, blocking collectives, per_device(): lax.all_to_all(p_half, 'dev', split_axis=1, concat_axis=0, tiled=True)  25.3 us
    all_to_all x1, waiting for transfers between devices, per_device(): lax.all_to_all(group_grad, 'dev', split_axis=0, concat_axis=1, tiled=True)  22.5 us
    dot_general x1, matrix products, add_blocks(): jnp.dot(onehot, terms.reshape(ids.shape[0], -1), precision=lax.Precision....  21.3 us
  transfers between devices with their start and end apart: 6, of which 5 were waited for; matrix products, arithmetic and copies ran while one was open for 7% of the time, Pallas kernels for 0%

commit v1 on v0

v1 whole, which is shorter than its diff:
```python
import functools

import jax
import jax.numpy as jnp
from jax import lax
from jax.experimental import pallas as pl
from jax.experimental.pallas import tpu as pltpu
from jax.sharding import PartitionSpec as P

BLK = 128
PAIRS = 128
PART = PAIRS // 2
ROWS = 8 * PART
TAIL = 16
STEP = 8
PARTS = 8
MIB = 1024 * 1024
SMEM = pl.BlockSpec(memory_space=pltpu.SMEM)
ANY = pl.BlockSpec(memory_space=pl.ANY)
VMEM = pl.BlockSpec(memory_space=pltpu.VMEM)


def params(limit, moved, flops=0):
    cost = pl.CostEstimate(flops=flops, bytes_accessed=moved, transcendentals=0)
    limit = pltpu.CompilerParams(vmem_limit_bytes=limit * MIB)
    return dict(compiler_params=limit, cost_estimate=cost)


def run_copies(copies):
    for copy in copies:
        copy.start()
    for copy in copies:
        copy.wait()


def pack_kernel(x, *refs):
    *given, out, xv, outv, marks, sems = refs
    width = x.shape[1]
    number = outv.shape[0] // PARTS
    loads, stores = [], []
    for n in range(PARTS):
        cols = slice(n * width // PARTS, (n + 1) * width // PARTS)
        loads.append(pltpu.make_async_copy(x.at[:, cols], xv.at[:, cols], sems.at[n]))
        part = slice(n * number, (n + 1) * number)
        stores.append(pltpu.make_async_copy(outv.at[part], out.at[part], sems.at[PARTS + n]))
    for copy in loads:
        copy.start()
    if given:
        run_copies([pltpu.make_async_copy(given[0], marks, sems.at[2 * PARTS])])
        tile = jnp.broadcast_to(marks[...].astype(jnp.float32), (16, 128)).astype(jnp.bfloat16)
    for n in range(PARTS):
        loads[n].wait()
        for m in range(n * number, (n + 1) * number):
            outv[m, 0:BLK, :] = xv[:, 128 * m : 128 * m + 128].astype(jnp.bfloat16)
            if given:
                outv[m, BLK:, :] = tile
        stores[n].start()
    for copy in stores:
        copy.wait()


def by_features(x, pos=None):
    width = x.shape[1]
    shape = (width // 128, BLK + (0 if pos is None else 16), 128)
    given = (x,) if pos is None else (x, pos)
    return pl.pallas_call(
        pack_kernel,
        in_specs=[ANY] * len(given),
        out_specs=ANY,
        out_shape=jax.ShapeDtypeStruct(shape, jnp.bfloat16),
        scratch_shapes=[
            pltpu.VMEM(x.shape, x.dtype),
            pltpu.VMEM(shape, jnp.bfloat16),
            pltpu.VMEM((1, BLK), jnp.int32),
            pltpu.SemaphoreType.DMA((2 * PARTS + 1,)),
        ],
        **params(56 if pos is None else 5, 5 * MIB),
        name="pack",
    )(*given)


def unpack_kernel(x, out, xv, outv, sems):
    number = x.shape[0] // PARTS
    loads, stores = [], []
    for n in range(PARTS):
        part = slice(n * number, (n + 1) * number)
        loads.append(pltpu.make_async_copy(x.at[part], xv.at[part], sems.at[n]))
        cols = slice(n * number * 128, (n + 1) * number * 128)
        stores.append(pltpu.make_async_copy(outv.at[:, cols], out.at[:, cols], sems.at[PARTS + n]))
    for copy in loads:
        copy.start()
    for n in range(PARTS):
        loads[n].wait()
        for m in range(n * number, (n + 1) * number):
            outv[:, 128 * m : 128 * m + 128] = xv[m].astype(jnp.float32)
        stores[n].start()
    for copy in stores:
        copy.wait()


def by_rows(x):
    number = x.shape[0]
    return pl.pallas_call(
        unpack_kernel,
        in_specs=[ANY],
        out_specs=ANY,
        out_shape=jax.ShapeDtypeStruct((BLK, number * 128), jnp.float32),
        scratch_shapes=[
            pltpu.VMEM(x.shape, x.dtype),
            pltpu.VMEM((BLK, number * 128), jnp.float32),
            pltpu.SemaphoreType.DMA((2 * PARTS,)),
        ],
        **params(5, 8 * MIB),
        name="unpack",
    )(x)


PIECES = ((0, 32), (32, 16), (48, 16), (64, 16), (80, 16), (96, 16), (112, 16))
GIVEN = ((0, 0, 0, 32), (1, 0, 32, 16), (1, 16, 112, 16), (1, 32, 64, 32), (2, 0, 48, 16), (3, 0, 96, 16))


def chip_at(at, core, lead, other):
    rx = jnp.where(core == 0, lead, other)
    ry = jnp.where(core == 0, other, lead)
    return ((at[1] + rx) % 4) * 4 + (at[2] + ry) % 4


def score_kernel(ids, own, at, *refs):
    q, pieces, given, outs = refs[:2], refs[2:9], refs[9:13], refs[13:20]
    qv, pv, sv, sems = refs[20:]
    core = at[0]
    moves = [(q[n].at[:, 0:BLK, :], qv.at[n]) for n in range(2)]
    moves += [(pieces[n], pv.at[0, first : first + size]) for n, (first, size) in enumerate(PIECES)]
    for n, begin, first, size in GIVEN:
        moves.append((given[n].at[begin : begin + size], pv.at[1, first : first + size]))
    run_copies([pltpu.make_async_copy(*move, sems.at[n]) for n, move in enumerate(moves)])

    stores = []
    for half in range(2):

        @pl.loop(0, PART // 2 // STEP)
        def _(step):
            for u in range(STEP):
                n = half * PART // 2 + step * STEP + u
                t = PART * core + n
                left = jnp.concatenate([qv[0, own[t]], qv[1, own[t]]], axis=1)
                right = jnp.concatenate([pv[0, ids[t]], pv[1, ids[t]]], axis=1)
                tile = lax.dot_general(
                    left, right, (((1,), (1,)), ((), ())), preferred_element_type=jnp.float32
                )
                where = pl.ds(pl.multiple_of(8 * n, 8), 8)
                sv[:, where, :] = tile.reshape(BLK // 8, 8, 128)

        rows = slice(half * ROWS // 2, (half + 1) * ROWS // 2)
        for lead in (2, 1, 3, 0):
            for other in range(4):
                if lead == 0:
                    target = outs[6].at[other, rows, :]
                else:
                    target = outs[2 * lead - 2 + other // 2].at[other % 2, rows, :]
                source = sv.at[chip_at(at, core, lead, other), rows, :]
                sem = sems.at[15 + 16 * half + 4 * lead + other]
                stores.append(pltpu.make_async_copy(source, target, sem))
                stores[-1].start()
    for copy in stores:
        copy.wait()


def partial_scores(ids, own, at, q, pieces, given):
    nblk = q[0].shape[0]
    shapes = [(2, ROWS, 128)] * 6 + [(4, ROWS, 128)]
    return pl.pallas_call(
        score_kernel,
        in_specs=[SMEM] * 3 + [ANY] * 13,
        out_specs=[ANY] * 7,
        out_shape=[jax.ShapeDtypeStruct(s, jnp.float32) for s in shapes],
        scratch_shapes=[
            pltpu.VMEM((2, nblk, BLK, 128), jnp.bfloat16),
            pltpu.VMEM((2, 4 * nblk, BLK, 128), jnp.bfloat16),
            pltpu.VMEM((BLK // 8, ROWS, 128), jnp.float32),
            pltpu.SemaphoreType.DMA((47,)),
        ],
        **params(17, 32 * MIB),
        name="partial_scores",
    )(ids, own, at, *q, *pieces, *given)


def softmax_kernel(at, *refs, scale):
    terms, lists, q, out, xv, listv, markv, sems = refs[:2], *refs[2:]
    loads = [
        pltpu.make_async_copy(terms[n], xv.at[ROWS * n : ROWS * n + ROWS, :], sems.at[n])
        for n in range(2)
    ]
    loads.append(pltpu.make_async_copy(lists, listv, sems.at[2]))
    loads.append(pltpu.make_async_copy(q.at[:, BLK:, :], markv, sems.at[3]))
    run_copies(loads)

    core = at[0]
    row = lax.broadcasted_iota(jnp.int32, (2 * ROWS, 1), 0)
    side = row // ROWS
    t = PART * (core + side - 2 * core * side) + (row & (ROWS - 1)) // 8
    r = row & 7
    lane = lax.broadcasted_iota(jnp.int32, (2 * ROWS, 128), 1)
    own = jnp.sum((listv[0:1, :] <= t).astype(jnp.int32), axis=1, keepdims=True)
    key = own * 8 + r

    x = xv[...] * scale
    high = jnp.max(x, axis=1, keepdims=True)
    part = jnp.sum(jnp.exp(x - high), axis=1, keepdims=True)
    lines = jnp.where(lane == 0, high, jnp.where(lane == 1, part, key.astype(jnp.float32))).T
    high, part, keys = lines[0:1], lines[1:2], lines[2:3]

    x, t, r, lane, own, key = [v[:ROWS] for v in (x, t, r, lane, own, key)]
    same = key.astype(jnp.float32) == keys
    top = jnp.max(jnp.where(same, high, -jnp.inf), axis=1, keepdims=True)
    total = jnp.where(same, part * jnp.exp(high - top), 0.0)
    lse = top + jnp.log(jnp.sum(total, axis=1, keepdims=True))

    block = lane == own
    first = t == jnp.sum(jnp.where(block, listv[1:2, :], 0), axis=1, keepdims=True)
    marks = jnp.max(markv[...].astype(jnp.float32), axis=1)
    marks = jnp.concatenate([marks, jnp.zeros((128 - marks.shape[0], 128), jnp.float32)], axis=0)
    listed = jnp.dot(
        block.astype(jnp.bfloat16), marks.astype(jnp.bfloat16), preferred_element_type=jnp.float32
    )
    target = jnp.sum(jnp.where(lane == at[4] * 8 + r, listed, 0.0), axis=1, keepdims=True)
    hit = first & (lane == target.astype(jnp.int32))
    weights = jnp.exp(x - lse) - hit.astype(jnp.float32)
    out[0:ROWS, :] = weights.astype(jnp.bfloat16)

    loss = lse - jnp.sum(jnp.where(hit, x, 0.0), axis=1, keepdims=True)
    line = lax.broadcasted_iota(jnp.int32, (TAIL, 128), 0)
    tail = jnp.zeros((TAIL, 128), jnp.float32)
    for h in range(2):
        here = first & (lane + 128 * h == key)
        rest = jnp.sum(jnp.where(here, loss, 0.0), axis=0, keepdims=True)
        for n in range(3):
            term = rest.astype(jnp.bfloat16).astype(jnp.float32)
            tail = jnp.where(line == 3 * h + n, term, tail)
            rest = rest - term
    out[ROWS:, :] = tail.astype(jnp.bfloat16)


def softmax_weights(at, terms, lists, q, scale):
    return pl.pallas_call(
        functools.partial(softmax_kernel, scale=scale),
        in_specs=[SMEM] + [ANY] * 4,
        out_specs=VMEM,
        out_shape=jax.ShapeDtypeStruct((ROWS + TAIL, 128), jnp.bfloat16),
        scratch_shapes=[
            pltpu.VMEM((2 * ROWS, 128), jnp.float32),
            pltpu.VMEM(lists.shape, jnp.int32),
            pltpu.VMEM((q.shape[0], TAIL, 128), jnp.bfloat16),
            pltpu.SemaphoreType.DMA((4,)),
        ],
        **params(16, 8 * MIB),
        name="softmax_weights",
    )(at, *terms, lists, q)


def grad_kernel(ids, own, at, q, *refs):
    pieces, parts, outs, gq, loss = refs[:7], refs[7:15], refs[15:22], *refs[22:24]
    wv, qv, pv, gq_sum, gp_sum, sems = refs[24:]
    core = at[0]
    moves = [(q.at[:, 0:BLK, :], qv)]
    moves += [(pieces[n], pv.at[first : first + size]) for n, (first, size) in enumerate(PIECES)]
    for n, piece in enumerate(parts):
        side = jnp.where(core == n // 4, 0, 1)
        for lead in range(4):
            chip = chip_at(at, side, lead, (0, 3, 1, 2)[n % 4])
            moves.append((piece.at[lead], wv.at[side, chip]))
    loads = [pltpu.make_async_copy(*move, sems.at[n]) for n, move in enumerate(moves)]
    for copy in loads:
        copy.start()

    @pl.loop(0, gq_sum.shape[0])
    def _(n):
        gq_sum[n] = jnp.zeros((BLK, 128), jnp.float32)
        for m in range(4):
            gp_sum[4 * n + m] = jnp.zeros((BLK, 128), jnp.float32)

    for copy in loads:
        copy.wait()

    for side in range(2):

        @pl.loop(0, PART // STEP)
        def _(step):
            for v in range(STEP // 2):
                where = pl.ds(pl.multiple_of(8 * STEP * step + 16 * v, 16), 16)
                two = wv[side, :, where, :].astype(jnp.float32)
                for o in range(2):
                    t = side * PART + step * STEP + 2 * v + o
                    here, there = own[t], ids[t]
                    tile = two[:, 8 * o : 8 * o + 8, :].reshape(BLK, 128).astype(jnp.bfloat16)
                    gq_sum[here] += jnp.dot(tile, pv[there], preferred_element_type=jnp.float32)
                    gp_sum[there] += lax.dot_general(
                        tile, qv[here], (((0,), (0,)), ((), ())), preferred_element_type=jnp.float32
                    )

    stores = []

    def send(source, target):
        stores.append(pltpu.make_async_copy(source, target, sems.at[len(stores)]))
        stores[-1].start()

    for m in (3, 4, 1, 2, 5, 6, 0):
        first, size = PIECES[m]

        @pl.loop(0, size // 4)
        def _(n):
            for e in range(4):
                pv[first + 4 * n + e] = gp_sum[first + 4 * n + e].astype(jnp.bfloat16)

        send(pv.at[first : first + size], outs[m])

    @pl.loop(0, gq_sum.shape[0] // 4)
    def _(n):
        for e in range(4):
            qv[4 * n + e] = gq_sum[4 * n + e].astype(jnp.bfloat16)

    send(qv, gq)
    tails = wv[0, :, ROWS:, :].astype(jnp.float32) + wv[1, :, ROWS:, :].astype(jnp.float32)
    line = lax.broadcasted_iota(jnp.int32, tails.shape, 1) // 3
    mine = jnp.sum(jnp.where(line == at[3] // 16, tails, 0.0), axis=1)
    loss[...] = pltpu.roll(mine, (128 - 8 * (at[3] % 16)) % 128, 1)
    for copy in stores:
        copy.wait()


def gradients(ids, own, at, q, pieces, parts):
    nblk = q.shape[0]
    shapes = [(size, BLK, 128) for _, size in PIECES] + [(nblk, BLK, 128)]
    return pl.pallas_call(
        grad_kernel,
        in_specs=[SMEM] * 3 + [ANY] * 16,
        out_specs=[ANY] * 8 + [VMEM],
        out_shape=[jax.ShapeDtypeStruct(s, jnp.bfloat16) for s in shapes]
        + [jax.ShapeDtypeStruct((BLK // 8, 128), jnp.float32)],
        scratch_shapes=[
            pltpu.VMEM((2, BLK // 8, ROWS + TAIL, 128), jnp.bfloat16),
            pltpu.VMEM((nblk, BLK, 128), jnp.bfloat16),
            pltpu.VMEM((4 * nblk, BLK, 128), jnp.bfloat16),
            pltpu.VMEM((nblk, BLK, 128), jnp.float32),
            pltpu.VMEM((4 * nblk, BLK, 128), jnp.float32),
            pltpu.SemaphoreType.DMA((40,)),
        ],
        **params(23, 32 * MIB),
        name="gradients",
    )(ids, own, at, q, *pieces, *parts)


def join_kernel(*refs):
    kept, terms, out, keptv, termv, outv, sems = refs[0], refs[1:5], refs[5], *refs[6:]
    half = kept.shape[0] // 2
    loads = [pltpu.make_async_copy(terms[n], termv.at[n], sems.at[n]) for n in range(4)]
    stores = []
    for h in range(2):
        part = slice(half * h, half * h + half)
        loads.append(pltpu.make_async_copy(kept.at[part], keptv.at[part], sems.at[4 + h]))
        stores.append(pltpu.make_async_copy(outv.at[part], out.at[part], sems.at[6 + h]))
    for copy in loads:
        copy.start()
    for h in range(2):
        for n in (4 + h, 2 * h, 2 * h + 1):
            loads[n].wait()

        @pl.loop(0, half)
        def _(n):
            value = keptv[half * h + n].astype(jnp.float32)
            for m in (2 * h, 2 * h + 1):
                value = value + termv[m, n].astype(jnp.float32)
            outv[half * h + n] = value.astype(out.dtype)

        stores[h].start()
    for copy in stores:
        copy.wait()


def join(kept, low, high):
    term = low[0].shape
    return pl.pallas_call(
        join_kernel,
        in_specs=[ANY] * 5,
        out_specs=ANY,
        out_shape=jax.ShapeDtypeStruct(kept.shape, kept.dtype),
        scratch_shapes=[
            pltpu.VMEM(kept.shape, kept.dtype),
            pltpu.VMEM((4,) + term, kept.dtype),
            pltpu.VMEM(kept.shape, kept.dtype),
            pltpu.SemaphoreType.DMA((8,)),
        ],
        **params(5, 8 * MIB),
        name="join",
    )(kept, *low, *high)


def along(axis, delta):
    if axis == "z":
        number = lax.axis_size("grp")
        perm = [(i, (i + delta) % number) for i in range(number)]
        return lambda v: lax.ppermute(v, "grp", perm)

    def target(d):
        x, y, core = d // 8, d // 2 % 4, d % 2
        if axis == "core":
            core = 1 - core
        elif (axis == "first") == (core == 0):
            x = (x + delta) % 4
        else:
            y = (y + delta) % 4
        return x * 8 + y * 2 + core

    perm = [(d, target(d)) for d in range(32)]
    return lambda v: lax.ppermute(v, "dev", perm)


def add(*terms):
    total = terms[0].astype(jnp.float32)
    for term in terms[1:]:
        total = total + term.astype(jnp.float32)
    return total.astype(terms[0].dtype)


def ring_terms(axis, rel1, rel2, rel3):
    up, down = along(axis, 1), along(axis, -1)
    from_below = up(rel2[0])
    from_above = down(rel2[1])
    below1 = up(rel1[1])
    above0 = down(rel3[0])
    below0 = up(add(rel1[0], from_below))
    above1 = down(add(rel3[1], from_above))
    return (below0, above0), (below1, above1)


def scatter_scores(outs):
    halves = ring_terms("first", outs[0:2], outs[2:4], outs[4:6])
    sums = [outs[6][n] + halves[n // 2][0][n % 2] + halves[n // 2][1][n % 2] for n in range(4)]
    got = [along("second", n)(sums[n]) for n in (1, 2, 3)]
    return sums[0] + got[0] + got[1] + got[2]


def gather_weights(v):
    got = {3: along("first", 1)(v), 1: along("first", -1)(v), 2: along("first", 2)(v)}
    near = jnp.stack([v, got[1], got[2], got[3]])
    up, down, flip = along("second", 1), along("second", -1), along("core", 1)
    below, above = up(near), down(near)
    side = [near, below, above, down(above)]
    return side + [flip(w) for w in side]


def per_device(queries, passages, pairs, counts, positives):
    ndev = lax.axis_size("dev")
    ngrp = lax.axis_size("grp")
    width = queries.shape[1]
    maxp = pairs.shape[1]
    me = lax.axis_index("dev")
    z = lax.axis_index("grp")
    chip, core = me // 2, me % 2
    at = jnp.stack([core, chip // 4, chip % 4, me, chip]).astype(jnp.int32)

    def exchange(v):
        return lax.all_to_all(v, "dev", 0, 0, tiled=True)

    up, down, flip = along("z", 1), along("z", -1), along("core", 1)
    p_own = exchange(by_features(passages))
    low, high = p_own[: ndev // 2], p_own[ndev // 2 :]
    above0, below1 = down(low), up(high)
    low, _ = lax.optimization_barrier((low, below1))
    high, _ = lax.optimization_barrier((high, above0))
    far0, far1 = down(above0), up(below1)
    above1, below0 = down(high), up(low)
    pieces = [p_own, above0, above1, far0, far1, below0, below1]
    q_own = exchange(by_features(queries, positives.reshape(1, BLK)))
    early = jnp.concatenate([above0, below1, far0, far1])
    given = [flip(v) for v in (p_own, early, above1, below0)]
    q = [q_own, flip(q_own)]

    group = counts[0]
    block = jnp.arange(ndev, dtype=jnp.int32)
    ends = jnp.sum(jnp.where(block[None, :] <= block[:, None], group[None, :], 0), axis=1)
    starts = ends - group
    t = jnp.arange(PAIRS, dtype=jnp.int32)
    own = jnp.sum((ends[None, :] <= t[:, None]).astype(jnp.int32), axis=1)
    start = jnp.sum(jnp.where(block[None, :] == own[:, None], starts[None, :], 0), axis=1)
    entry = own * maxp + t - start
    slot = jnp.arange(ndev * maxp, dtype=jnp.int32)
    ids = jnp.sum(jnp.where(slot[None, :] == entry[:, None], pairs.reshape(1, -1), 0), axis=1)
    ids = (ids + (ngrp - z) * ndev) % (ngrp * ndev)
    spare = jnp.full((128 - ndev,), 2 * PAIRS, jnp.int32)
    lists = jnp.stack([jnp.concatenate([v, spare]) for v in (ends, starts)] * 4)

    scores = scatter_scores(partial_scores(ids, own, at, q, pieces, given))
    weights = softmax_weights(at, (scores, flip(scores)), lists, q_own, width ** (-0.5))
    *g, gq, lines = gradients(ids, own, at, q_own, pieces, gather_weights(weights))

    low, high = ring_terms("z", g[1:3], g[3:5], g[5:7])
    q_rows = by_rows(exchange(gq))
    p_rows = by_rows(exchange(join(g[0], low, high)))
    return lines[:, 0:8].reshape(BLK), q_rows, p_rows


def solution(mesh):
    placed = (
        P(("grp", "dev"), None),
        P(("grp", "dev"), None),
        P("grp", None),
        P("grp", None),
        P(("grp", "dev")),
    )
    return jax.shard_map(
        per_device,
        mesh=mesh,
        in_specs=placed,
        out_specs=(P(("grp", "dev")), P(("grp", "dev"), None), P(("grp", "dev"), None)),
        check_vma=False,
    )
```

time: 454 us -> 260 us (0.57)
  waiting for transfers between devices: 267 us -> 111 us
  matrix products: 60.2 us -> 0 us
  starting transfers between devices: 11.8 us -> 64.7 us
  Pallas kernels: 0 us -> 42.3 us
  blocking collectives: 58.8 us -> 25.6 us
  local copies, waits for them, and re-layouts: 34.9 us -> 8.03 us
  between operations: 13.9 us -> 1.21 us
    reduce_scatter x2 -> x0, waiting for transfers between devices: 151 us -> none  [the longest x1 112 us: per_device(): lax.psum_scatter(jnp.einsum('bif,bkjf->bkij', q_sel, p_sel, preferred_ele...]
    all_gather x2 -> x0, waiting for transfers between devices: 93.6 us -> none  [the longest x1 53.7 us: per_device(): piece = lax.all_gather(weights[None], 'dev', axis=0, tiled=True)]
    ppermute x0 -> x37, waiting for transfers between devices: none -> 89 us  [the longest x12 49.4 us: along(): return lambda v: lax.ppermute(v, 'grp', perm)]
    dot_general x5 -> x0, matrix products: 60.2 us -> none  [the longest x1 21.3 us: add_blocks(): jnp.dot(onehot, terms.reshape(ids.shape[0], -1), precision=lax.Precision....]
    ppermute x0 -> x37, starting transfers between devices: none -> 45.3 us  [the longest x25 29.1 us: along(): return lambda v: lax.ppermute(v, 'dev', perm)]
    pallas_call x0 -> x8, Pallas kernels: none -> 42.3 us  [the longest x1 15.2 us: gradients(): pl.pallas_call(grad_kernel, in_specs=[SMEM] * 3 + [ANY] * 16, out_specs=[...]
    all_to_all x2 -> x1, blocking collectives: 58.8 us -> 25.6 us  [exchange(): return lax.all_to_all(v, 'dev', 0, 0, tiled=True)]
    another operation x2 -> x4, local copies, waits for them, and re-layouts: 16.6 us -> 1.97 us  [the longest x3 1.88 us: per_device(): lists = jnp.stack([jnp.concatenate([v, spare]) for v in (ends, starts)] * 4)]
  transfers between devices with their start and end apart: 6 -> 40, of which waited for: 5 -> 23; matrix products, arithmetic and copies ran while one was open for 7% -> 3% of each run, Pallas kernels for 0% -> 2%
where the time goes in v1:
time: 260 us; the launch traced here: 259 us
  waiting for transfers between devices  111 us (43%)
  starting transfers between devices  64.7 us (25%)
  Pallas kernels  42.3 us (16%)
  blocking collectives  25.6 us (10%)
  local copies, waits for them, and re-layouts  8.03 us (3%)
  other arithmetic  6.02 us (2%)
    ppermute x12, waiting for transfers between devices, along(): return lambda v: lax.ppermute(v, 'grp', perm)  49.4 us
    ppermute x25, waiting for transfers between devices, along(): return lambda v: lax.ppermute(v, 'dev', perm)  39.6 us
    ppermute x25, starting transfers between devices, along(): return lambda v: lax.ppermute(v, 'dev', perm)  29.1 us
    all_to_all x1, blocking collectives, exchange(): return lax.all_to_all(v, 'dev', 0, 0, tiled=True)  25.6 us
    all_to_all x3, waiting for transfers between devices, exchange(): return lax.all_to_all(v, 'dev', 0, 0, tiled=True)  22.4 us
    all_to_all x3, starting transfers between devices, exchange(): return lax.all_to_all(v, 'dev', 0, 0, tiled=True)  19.3 us
    ppermute x12, starting transfers between devices, along(): return lambda v: lax.ppermute(v, 'grp', perm)  16.3 us
    pallas_call x1, Pallas kernels, gradients(): pl.pallas_call(grad_kernel, in_specs=[SMEM] * 3 + [ANY] * 16, out_specs=[...  15.2 us
  transfers between devices with their start and end apart: 40, of which 23 were waited for; matrix products, arithmetic and copies ran while one was open for 3% of the time, Pallas kernels for 2%

profile of v1, /device:TPU:1, one launch (start us, length us, event | category | flops | bytes accessed | tf_op | source)
XLA Modules:
  0.0 259.3 jit_solution(4018893335289286020)
XLA Ops:
  0.6 2.3 pack.3
  3.0 25.6 %all_to_all.20.refs_2_.refs_0_ = bf16[32,128,128]{2,1,0:T(8,128)(2,1)S(1)} all-to-all(bf16[32,128,128]{2,1,0:T(8,128)(2,1)} %pack.3), channel_id=1, replica_groups=mesh['grp'=4,'dev'=32] {'dev'}, dimensions={0} | all-to-all | bytes 2097152 | tf_op jit(solution)/shard_map/all_to_all | solution.py:463
  28.8 1.7 collective-permute-start.3
  30.5 2.2 collective-permute-start
  32.7 12.1 %collective-permute-done.3.refs_8_.refs_6_ = bf16[16,128,128]{2,1,0:T(8,128)(2,1)S(1)} collective-permute-done((bf16[16,128,128]{2,1,0:T(8,128)(2,1)S(1)}, bf16[16,128,128]{2,1,0:T(8,128)(2,1)S(1)}, u32[]{:S(2)}, u32[]{:S(2)}) %collective-permute-start.3) | collective-permute-done | bytes 524320 | tf_op jit(solution)/shard_map/ppermute | solution.py:402
  44.8 2.7 %collective-permute-start.2 = (bf16[16,128,128]{2,1,0:T(8,128)(2,1)S(1)}, bf16[16,128,128]{2,1,0:T(8,128)(2,1)}, u32[]{:S(2)}, u32[]{:S(2)}) collective-permute-start(bf16[16,128,128]{2,1,0:T(8,128)(2,1)S(1)} %collective-permute-done.refs_3_.refs_1_), channel_id=1, source_target_pairs={{0,96},{32,0},{64,32},{96,64},{1,97},{33,1},{65,33},{97,65},{2,98}... | collective-permute-start | bytes 1572872 | tf_op jit(solution)/shard_map/ppermute | solution.py:402
  47.5 1.3 pack.2
  48.8 4.9 %all-to-all-start = ((bf16[32,144,128]{2,1,0:T(8,128)(2,1)}), bf16[32,144,128]{2,1,0:T(8,128)(2,1)S(1)}, u32[]{:S(2)}, u32[]{:S(2)}) async-start(bf16[32,144,128]{2,1,0:T(8,128)(2,1)} %pack.2), calls=%async_computation | async-start | bytes 2359296 | tf_op jit(solution)/shard_map/all_to_all | solution.py:463
  53.7 5.1 %collective-permute-done.4.refs_6_.refs_4_ = bf16[16,128,128]{2,1,0:T(8,128)(2,1)} collective-permute-done((bf16[16,128,128]{2,1,0:T(8,128)(2,1)S(1)}, bf16[16,128,128]{2,1,0:T(8,128)(2,1)}, u32[]{:S(2)}, u32[]{:S(2)}) %collective-permute-start.4) | collective-permute-done | bytes 524320 | tf_op jit(solution)/shard_map/ppermute | solution.py:402
  58.8 2.8 %pad_maximum_fusion = bf16[64,128,128]{2,1,0:T(8,128)(2,1)} fusion(bf16[16,128,128]{2,1,0:T(8,128)(2,1)} %collective-permute-done.4.refs_6_.refs_4_, bf16[16,128,128]{2,1,0:T(8,128)(2,1)} %collective-permute-done.2.refs_5_.refs_3_, bf16[16,128,128]{2,1,0:T(8,128)(2,1)S(1)} %collective-permute-done.3.refs_8_.refs_6_, ...), kind=kLoop, calls=%fused_computation | loop fusion | flops 3145728 | bytes 4194304 | tf_op jit(solution)/shard_map/concatenate | solution.py:475
  61.6 1.6 collective-permute-start.8
  63.2 8.9 %all-to-all-done.refs_0_.refs_3_.q = bf16[32,144,128]{2,1,0:T(8,128)(2,1)S(1)} async-done(((bf16[32,144,128]{2,1,0:T(8,128)(2,1)}), bf16[32,144,128]{2,1,0:T(8,128)(2,1)S(1)}, u32[]{:S(2)}, u32[]{:S(2)}) %all-to-all-start) | async-done | bytes 1179680 | tf_op jit(solution)/shard_map/all_to_all | solution.py:463
  72.6 2.7 %collective-permute-start.1 = (bf16[16,128,128]{2,1,0:T(8,128)(2,1)}, bf16[16,128,128]{2,1,0:T(8,128)(2,1)}, u32[]{:S(2)}, u32[]{:S(2)}) collective-permute-start(bf16[16,128,128]{2,1,0:T(8,128)(2,1)} %copy-done.11), channel_id=1, source_target_pairs={{0,96},{32,0},{64,32},{96,64},{1,97},{33,1},{65,33},{97,65},{2,98}... | collective-permute-start | bytes 1572872 | tf_op jit(solution)/shard_map/ppermute | solution.py:402
  75.9 11.5 %collective-permute-done.5.refs_7_.refs_5_ = bf16[16,128,128]{2,1,0:T(8,128)(2,1)} collective-permute-done((bf16[16,128,128]{2,1,0:T(8,128)(2,1)}, bf16[16,128,128]{2,1,0:T(8,128)(2,1)}, u32[]{:S(2)}, u32[]{:S(2)}) %collective-permute-start.5) | collective-permute-done | bytes 524320 | tf_op jit(solution)/shard_map/ppermute | solution.py:402
  88.7 1.5 collective-permute-done.10.refs_12_
  91.0 12.7 %partial_scores.1 = (f32[2,512,128]{2,1,0:T(8,128)S(1)}, f32[2,512,128]{2,1,0:T(8,128)S(1)}, f32[2,512,128]{2,1,0:T(8,128)S(1)}, f32[2,512,128]{2,1,0:T(8,128)S(...) custom-call(s32[128]{0:T(128)S(1)} %and_select_fusion.ids, ...), custom_call_target="tpu_custom_call" | custom-call | bytes 33554432 | tf_op jit(solution)/shard_map/partial_scores/pallas_call | solution.py:172
  103.8 2.7 %collective-permute-start.16 = (f32[2,512,128]{2,1,0:T(8,128)S(1)}, f32[2,512,128]{2,1,0:T(8,128)S(1)}, u32[]{:S(2)}, u32[]{:S(2)}) collective-permute-start(f32[2,512,128]{2,1,0:T(8,128)S(1)} %get-tuple-element.29), channel_id=1, source_target_pairs={{0,24},{1,7},{2,26},{3,1},{4,28},{5,3},{6,30},{7,5},{8,0},{9,15},{... | collective-permute-start | bytes 1572872 | tf_op jit(solution)/shard_map/ppermute | solution.py:415
  106.5 1.4 collective-permute-start.15
  107.9 5.4 %collective-permute-done.11 = f32[2,512,128]{2,1,0:T(8,128)S(1)} collective-permute-done((f32[2,512,128]{2,1,0:T(8,128)S(1)}, f32[2,512,128]{2,1,0:T(8,128)S(1)}, u32[]{:S(2)}, u32[]{:S(2)}) %collective-permute-start.11) | collective-permute-done | bytes 524320 | tf_op jit(solution)/shard_map/ppermute | solution.py:415
  113.6 2.7 %collective-permute-start.17 = (f32[2,512,128]{2,1,0:T(8,128)S(1)}, f32[2,512,128]{2,1,0:T(8,128)S(1)}, u32[]{:S(2)}, u32[]{:S(2)}) collective-permute-start(f32[2,512,128]{2,1,0:T(8,128)S(1)} %add.108), channel_id=1, source_target_pairs={{0,24},{1,7},{2,26},{3,1},{4,28},{5,3},{6,30},{7,5},{8,0},{9,15},{... | collective-permute-start | bytes 1572872 | tf_op jit(solution)/shard_map/ppermute | solution.py:415
  116.3 1.9 collective-permute-done.13
  118.9 5.6 %collective-permute-done.12 = f32[2,512,128]{2,1,0:T(8,128)S(1)} collective-permute-done((f32[2,512,128]{2,1,0:T(8,128)S(1)}, f32[2,512,128]{2,1,0:T(8,128)S(1)}, u32[]{:S(2)}, u32[]{:S(2)}) %collective-permute-start.12) | collective-permute-done | bytes 524320 | tf_op jit(solution)/shard_map/ppermute | solution.py:415
  127.1 4.6 %collective-permute-done.18 = f32[512,128]{1,0:T(8,128)S(1)} collective-permute-done((f32[512,128]{1,0:T(8,128)S(1)}, f32[512,128]{1,0:T(8,128)S(1)}, u32[]{:S(2)}, u32[]{:S(2)}) %collective-permute-start.18) | collective-permute-done | bytes 262176 | tf_op jit(solution)/shard_map/ppermute | solution.py:415
  131.8 1.3 collective-permute-done.19
  133.1 1.5 collective-permute-done.14
  134.7 2.3 collective-permute-start.20
  138.9 3.5 %softmax_weights.1 = bf16[528,128]{1,0:T(8,128)(2,1)S(1)} custom-call(s32[5]{0:T(128)S(1)} %stack.53.at, f32[512,128]{1,0:T(8,128)S(1)} %fusion.6.refs_0_, f32[512,128]{1,0:T(8,128)} %collective-permute-done.20.refs_1_, s32[8,128]{1,0:T(8,128)S(1)} %stack.56.refs_2_, bf16[32,144,128]{2,1,0:T(8,128)(2,1)S(1)} %all-to-all-done.refs_0_.refs_3_.q), custom_call_target="tpu_custom_call" | custom-call | bytes 8388608 | tf_op jit(solution)/shard_map/softmax_weights/pallas_call | solution.py:245
  142.5 2.3 collective-permute-start.22
  145.7 3.3 %collective-permute-done.23 = bf16[528,128]{1,0:T(8,128)(2,1)S(1)} collective-permute-done((bf16[528,128]{1,0:T(8,128)(2,1)S(1)}, bf16[528,128]{1,0:T(8,128)(2,1)S(1)}, u32[]{:S(2)}, u32[]{:S(2)}) %collective-permute-start.23) | collective-permute-done | bytes 135200 | tf_op jit(solution)/shard_map/ppermute | solution.py:415
  150.0 3.0 %collective-permute-start.25 = (bf16[4,528,128]{2,1,0:T(8,128)(2,1)S(1)}, bf16[4,528,128]{2,1,0:T(8,128)(2,1)S(1)}, u32[]{:S(2)}, u32[]{:S(2)}) collective-permute-start(bf16[4,528,128]{2,1,0:T(8,128)(2,1)S(1)} %pad_maximum_fusion.1.refs_7_), channel_id=1, source_target_pairs={{0,6},{1,25},{2,0},{3,27},{4,2},{5,29},{6,4},{7,31},{8,14},{9,1},{... | collective-permute-start | bytes 1622024 | tf_op jit(solution)/shard_map/ppermute | solution.py:415
  153.0 6.3 %collective-permute-done.25.refs_9_ = bf16[4,528,128]{2,1,0:T(8,128)(2,1)S(1)} collective-permute-done((bf16[4,528,128]{2,1,0:T(8,128)(2,1)S(1)}, bf16[4,528,128]{2,1,0:T(8,128)(2,1)S(1)}, u32[]{:S(2)}, u32[]{:S(2)}) %collective-permute-start.25) | collective-permute-done | bytes 540704 | tf_op jit(solution)/shard_map/ppermute | solution.py:415
  159.3 3.4 %collective-permute-start.26 = (bf16[4,528,128]{2,1,0:T(8,128)(2,1)S(1)}, bf16[4,528,128]{2,1,0:T(8,128)(2,1)S(1)}, u32[]{:S(2)}, u32[]{:S(2)}) collective-permute-start(bf16[4,528,128]{2,1,0:T(8,128)(2,1)S(1)} %collective-permute-done.25.refs_9_), channel_id=1, source_target_pairs={{0,6},{1,25},{2,0},{3,27},{4,2},{5,29},{6,4},{7,31},{8,14},{9,1},{... | collective-permute-start | bytes 1622024 | tf_op jit(solution)/shard_map/ppermute | solution.py:415
  162.7 1.7 collective-permute-start.27
  164.9 4.1 %collective-permute-done.26.refs_10_ = bf16[4,528,128]{2,1,0:T(8,128)(2,1)S(1)} collective-permute-done((bf16[4,528,128]{2,1,0:T(8,128)(2,1)S(1)}, bf16[4,528,128]{2,1,0:T(8,128)(2,1)S(1)}, u32[]{:S(2)}, u32[]{:S(2)}) %collective-permute-start.26) | collective-permute-done | bytes 540704 | tf_op jit(solution)/shard_map/ppermute | solution.py:415
  169.0 2.2 collective-permute-start.30
  171.3 1.5 collective-permute-done.30.refs_14_
  172.8 15.2 %gradients.1 = (bf16[32,128,128]{2,1,0:T(8,128)(2,1)S(1)}, bf16[16,128,128]{2,1,0:T(8,128)(2,1)S(1)}, bf16[16,128,128]{2,1,0:T(8,128)(2,1)S(1)}, bf16[16,128,128...) custom-call(s32[128]{0:T(128)S(1)} %and_select_fusion.ids, ...), custom_call_target="tpu_custom_call" | custom-call | bytes 33554432 | tf_op jit(solution)/shard_map/gradients/pallas_call | solution.py:334
  193.2 2.7 %collective-permute-start.35 = (bf16[16,128,128]{2,1,0:T(8,128)(2,1)}, bf16[16,128,128]{2,1,0:T(8,128)(2,1)}, u32[]{:S(2)}, u32[]{:S(2)}) collective-permute-start(bf16[16,128,128]{2,1,0:T(8,128)(2,1)} %get-tuple-element.38), channel_id=1, source_target_pairs={{0,96},{32,0},{64,32},{96,64},{1,97},{33,1},{65,33},{97,65},{2,98}... | collective-permute-start | bytes 1572872 | tf_op jit(solution)/shard_map/ppermute | solution.py:402
  195.9 7.1 %all-to-all-start.2 = ((bf16[32,128,128]{2,1,0:T(8,128)(2,1)}), bf16[32,128,128]{2,1,0:T(8,128)(2,1)S(1)}, u32[]{:S(2)}, u32[]{:S(2)}) async-start(bf16[32,128,128]{2,1,0:T(8,128)(2,1)} %copy-done.1), calls=%async_computation.2 | async-start | bytes 2097152 | tf_op jit(solution)/shard_map/all_to_all | solution.py:463
  204.5 3.4 %collective-permute-done.31 = bf16[16,128,128]{2,1,0:T(8,128)(2,1)} collective-permute-done((bf16[16,128,128]{2,1,0:T(8,128)(2,1)}, bf16[16,128,128]{2,1,0:T(8,128)(2,1)}, u32[]{:S(2)}, u32[]{:S(2)}) %collective-permute-start.31) | collective-permute-done | bytes 524320 | tf_op jit(solution)/shard_map/ppermute | solution.py:402
  210.3 2.7 %collective-permute-start.36 = (bf16[16,128,128]{2,1,0:T(8,128)(2,1)S(1)}, bf16[16,128,128]{2,1,0:T(8,128)(2,1)S(1)}, u32[]{:S(2)}, u32[]{:S(2)}) collective-permute-start(bf16[16,128,128]{2,1,0:T(8,128)(2,1)S(1)} %add_convert_fusion), channel_id=1, source_target_pairs={{0,96},{32,0},{64,32},{96,64},{1,97},{33,1},{65,33},{97,65},{2,98}... | collective-permute-start | bytes 1572872 | tf_op jit(solution)/shard_map/ppermute | solution.py:402
  213.1 5.0 %collective-permute-done.33.refs_2_ = bf16[16,128,128]{2,1,0:T(8,128)(2,1)S(1)} collective-permute-done((bf16[16,128,128]{2,1,0:T(8,128)(2,1)}, bf16[16,128,128]{2,1,0:T(8,128)(2,1)S(1)}, u32[]{:S(2)}, u32[]{:S(2)}) %collective-permute-start.33) | collective-permute-done | bytes 524320 | tf_op jit(solution)/shard_map/ppermute | solution.py:402
  219.2 11.2 %collective-permute-done.32.refs_1_ = bf16[16,128,128]{2,1,0:T(8,128)(2,1)S(1)} collective-permute-done((bf16[16,128,128]{2,1,0:T(8,128)(2,1)S(1)}, bf16[16,128,128]{2,1,0:T(8,128)(2,1)S(1)}, u32[]{:S(2)}, u32[]{:S(2)}) %collective-permute-start.32) | collective-permute-done | bytes 524320 | tf_op jit(solution)/shard_map/ppermute | solution.py:402
  230.4 1.6 join.1
  232.1 7.4 %all-to-all-start.3 = ((bf16[32,128,128]{2,1,0:T(8,128)(2,1)}), bf16[32,128,128]{2,1,0:T(8,128)(2,1)S(1)}, u32[]{:S(2)}, u32[]{:S(2)}) async-start(bf16[32,128,128]{2,1,0:T(8,128)(2,1)} %join.1), calls=%async_computation.3 | async-start | bytes 2097152 | tf_op jit(solution)/shard_map/all_to_all | solution.py:463
  240.1 2.8 %unpack.2 = f32[128,4096]{1,0:T(8,128)} custom-call(bf16[32,128,128]{2,1,0:T(8,128)(2,1)S(1)} %all-to-all-done.2.x), custom_call_target="tpu_custom_call" | custom-call | bytes 8388608 | tf_op jit(solution)/shard_map/unpack/pallas_call | solution.py:103
  242.8 13.5 %all-to-all-done.3.x = bf16[32,128,128]{2,1,0:T(8,128)(2,1)S(1)} async-done(((bf16[32,128,128]{2,1,0:T(8,128)(2,1)}), bf16[32,128,128]{2,1,0:T(8,128)(2,1)S(1)}, u32[]{:S(2)}, u32[]{:S(2)}) %all-to-all-start.3) | async-done | bytes 1048608 | tf_op jit(solution)/shard_map/all_to_all | solution.py:463
  256.4 2.8 %unpack.3 = f32[128,4096]{1,0:T(8,128)} custom-call(bf16[32,128,128]{2,1,0:T(8,128)(2,1)S(1)} %all-to-all-done.3.x), custom_call_target="tpu_custom_call" | custom-call | bytes 8388608 | tf_op jit(solution)/shard_map/unpack/pallas_call | solution.py:103
  (99 shorter events, 22.1 us)
Async XLA Ops:
  3.0 44.5 %copy-start = (f32[128,4096]{1,0:T(8,128)S(1)}, f32[128,4096]{1,0:T(8,128)}, u32[]{:S(2)}) copy-start(f32[128,4096]{1,0:T(8,128)} %x.6) | copy-start | bytes 6291460
  3.0 44.5 %copy-start.8 = (s32[128]{0:T(128)S(1)}, s32[128]{0:T(128)}, u32[]{:S(2)}) copy-start(s32[128]{0:T(128)} %param.9) | copy-start | bytes 1540
  28.7 16.0 %copy-start.11 = (bf16[16,128,128]{2,1,0:T(8,128)(2,1)}, bf16[16,128,128]{2,1,0:T(8,128)(2,1)S(1)}, u32[]{:S(2)}) copy-start(bf16[16,128,128]{2,1,0:T(8,128)(2,1)S(1)} %get-tuple-element.21) | copy-start | bytes 1572868
  28.8 18.7 %copy-start.12 = (bf16[16,128,128]{2,1,0:T(8,128)(2,1)}, bf16[16,128,128]{2,1,0:T(8,128)(2,1)S(1)}, u32[]{:S(2)}) copy-start(bf16[16,128,128]{2,1,0:T(8,128)(2,1)S(1)} %get-tuple-element.22) | copy-start | bytes 1572868
  28.8 16.0 %collective-permute-start.3 = (bf16[16,128,128]{2,1,0:T(8,128)(2,1)S(1)}, bf16[16,128,128]{2,1,0:T(8,128)(2,1)S(1)}, u32[]{:S(2)}, u32[]{:S(2)}) collective-permute-start(bf16[16,128,128]{2,1,0:T(8,128)(2,1)S(1)} %get-tuple-element.21), channel_id=1, source_target_pairs={{0,32},{32,64},{64,96},{96,0},{1,33},{33,65},{65,97},{97,1},{2,34}... | collective-permute-start | bytes 1572872 | tf_op jit(solution)/shard_map/ppermute | solution.py:402
  30.5 14.3 %collective-permute-start = (bf16[16,128,128]{2,1,0:T(8,128)(2,1)S(1)}, bf16[16,128,128]{2,1,0:T(8,128)(2,1)S(1)}, u32[]{:S(2)}, u32[]{:S(2)}) collective-permute-start(bf16[16,128,128]{2,1,0:T(8,128)(2,1)S(1)} %get-tuple-element.22), channel_id=1, source_target_pairs={{0,96},{32,0},{64,32},{96,64},{1,97},{33,1},{65,33},{97,65},{2,98}... | collective-permute-start | bytes 1572872 | tf_op jit(solution)/shard_map/ppermute | solution.py:402
  44.8 14.1 %collective-permute-start.4 = (bf16[16,128,128]{2,1,0:T(8,128)(2,1)S(1)}, bf16[16,128,128]{2,1,0:T(8,128)(2,1)}, u32[]{:S(2)}, u32[]{:S(2)}) collective-permute-start(bf16[16,128,128]{2,1,0:T(8,128)(2,1)S(1)} %collective-permute-done.3.refs_8_.refs_6_), channel_id=1, source_target_pairs={{0,32},{32,64},{64,96},{96,0},{1,33},{33,65},{65,97},{97,1},{2,34}... | collective-permute-start | bytes 1572872 | tf_op jit(solution)/shard_map/ppermute | solution.py:402
  44.8 14.1 %collective-permute-start.2 = (bf16[16,128,128]{2,1,0:T(8,128)(2,1)S(1)}, bf16[16,128,128]{2,1,0:T(8,128)(2,1)}, u32[]{:S(2)}, u32[]{:S(2)}) collective-permute-start(bf16[16,128,128]{2,1,0:T(8,128)(2,1)S(1)} %collective-permute-done.refs_3_.refs_1_), channel_id=1, source_target_pairs={{0,96},{32,0},{64,32},{96,64},{1,97},{33,1},{65,33},{97,65},{2,98}... | collective-permute-start | bytes 1572872 | tf_op jit(solution)/shard_map/ppermute | solution.py:402
  48.8 23.3 %all-to-all-start = ((bf16[32,144,128]{2,1,0:T(8,128)(2,1)}), bf16[32,144,128]{2,1,0:T(8,128)(2,1)S(1)}, u32[]{:S(2)}, u32[]{:S(2)}) async-start(bf16[32,144,128]{2,1,0:T(8,128)(2,1)} %pack.2), calls=%async_computation | async-start | bytes 2359296 | tf_op jit(solution)/shard_map/all_to_all | solution.py:463
  53.7 21.6 %copy-start.14 = (s32[1,32]{1,0:T(1,128)S(1)}, s32[1,32]{1,0:T(1,128)}, u32[]{:S(2)}) copy-start(s32[1,32]{1,0:T(1,128)} %param.8) | copy-start | bytes 388
  53.7 21.8 %copy-start.13 = (s32[32,8]{0,1:T(8,128)S(1)}, s32[32,8]{0,1:T(8,128)}, u32[]{:S(2)}) copy-start(s32[32,8]{0,1:T(8,128)} %param.7) | copy-start | bytes 3076
  61.6 29.4 %collective-permute-start.8 = (bf16[64,128,128]{2,1,0:T(8,128)(2,1)}, bf16[64,128,128]{2,1,0:T(8,128)(2,1)}, u32[]{:S(2)}, u32[]{:S(2)}) collective-permute-start(bf16[64,128,128]{2,1,0:T(8,128)(2,1)} %pad_maximum_fusion), channel_id=1, source_target_pairs={{0,1},{1,0},{2,3},{3,2},{4,5},{5,4},{6,7},{7,6},{8,9},{9,8},{10,11... | collective-permute-start | bytes 6291464 | tf_op jit(solution)/shard_map/ppermute | solution.py:415
  72.1 16.6 %collective-permute-start.6 = (bf16[32,144,128]{2,1,0:T(8,128)(2,1)S(1)}, bf16[32,144,128]{2,1,0:T(8,128)(2,1)}, u32[]{:S(2)}, u32[]{:S(2)}) collective-permute-start(bf16[32,144,128]{2,1,0:T(8,128)(2,1)S(1)} %all-to-all-done.refs_0_.refs_3_.q), channel_id=1, source_target_pairs={{0,1},{1,0},{2,3},{3,2},{4,5},{5,4},{6,7},{7,6},{8,9},{9,8},{10,11... | collective-permute-start | bytes 3538952 | tf_op jit(solution)/shard_map/ppermute | solution.py:415
  72.4 16.3 %collective-permute-start.7 = (bf16[32,128,128]{2,1,0:T(8,128)(2,1)S(1)}, bf16[32,128,128]{2,1,0:T(8,128)(2,1)}, u32[]{:S(2)}, u32[]{:S(2)}) collective-permute-start(bf16[32,128,128]{2,1,0:T(8,128)(2,1)S(1)} %all_to_all.20.refs_2_.refs_0_), channel_id=1, source_target_pairs={{0,1},{1,0},{2,3},{3,2},{4,5},{5,4},{6,7},{7,6},{8,9},{9,8},{10,11... | collective-permute-start | bytes 3145736 | tf_op jit(solution)/shard_map/ppermute | solution.py:415
  72.6 14.8 %collective-permute-start.5 = (bf16[16,128,128]{2,1,0:T(8,128)(2,1)}, bf16[16,128,128]{2,1,0:T(8,128)(2,1)}, u32[]{:S(2)}, u32[]{:S(2)}) collective-permute-start(bf16[16,128,128]{2,1,0:T(8,128)(2,1)} %copy-done.12), channel_id=1, source_target_pairs={{0,32},{32,64},{64,96},{96,0},{1,33},{33,65},{65,97},{97,1},{2,34}... | collective-permute-start | bytes 1572872 | tf_op jit(solution)/shard_map/ppermute | solution.py:402
  72.6 15.9 %collective-permute-start.1 = (bf16[16,128,128]{2,1,0:T(8,128)(2,1)}, bf16[16,128,128]{2,1,0:T(8,128)(2,1)}, u32[]{:S(2)}, u32[]{:S(2)}) collective-permute-start(bf16[16,128,128]{2,1,0:T(8,128)(2,1)} %copy-done.11), channel_id=1, source_target_pairs={{0,96},{32,0},{64,32},{96,64},{1,97},{33,1},{65,33},{97,65},{2,98}... | collective-permute-start | bytes 1572872 | tf_op jit(solution)/shard_map/ppermute | solution.py:402
  75.4 28.3 %copy-start.15 = (s32[32]{0:T(128)}, s32[32]{0:T(128)S(1)}, u32[]{:S(2)}) copy-start(s32[32]{0:T(128)S(1)} %select_reduce_fusion.2) | copy-start | bytes 388
  87.4 2.8 %collective-permute-start.10 = (bf16[16,128,128]{2,1,0:T(8,128)(2,1)}, bf16[16,128,128]{2,1,0:T(8,128)(2,1)S(1)}, u32[]{:S(2)}, u32[]{:S(2)}) collective-permute-start(bf16[16,128,128]{2,1,0:T(8,128)(2,1)} %collective-permute-done.5.refs_7_.refs_5_), channel_id=1, source_target_pairs={{0,1},{1,0},{2,3},{3,2},{4,5},{5,4},{6,7},{7,6},{8,9},{9,8},{10,11... | collective-permute-start | bytes 1572872 | tf_op jit(solution)/shard_map/ppermute | solution.py:415
  88.5 2.5 collective-permute-start.9
  103.7 9.6 %collective-permute-start.11 = (f32[2,512,128]{2,1,0:T(8,128)S(1)}, f32[2,512,128]{2,1,0:T(8,128)S(1)}, u32[]{:S(2)}, u32[]{:S(2)}) collective-permute-start(f32[2,512,128]{2,1,0:T(8,128)S(1)} %get-tuple-element.25), channel_id=1, source_target_pairs={{0,8},{1,3},{2,10},{3,5},{4,12},{5,7},{6,14},{7,1},{8,16},{9,11},{... | collective-permute-start | bytes 1572872 | tf_op jit(solution)/shard_map/ppermute | solution.py:415
  103.8 9.7 %collective-permute-start.16 = (f32[2,512,128]{2,1,0:T(8,128)S(1)}, f32[2,512,128]{2,1,0:T(8,128)S(1)}, u32[]{:S(2)}, u32[]{:S(2)}) collective-permute-start(f32[2,512,128]{2,1,0:T(8,128)S(1)} %get-tuple-element.29), channel_id=1, source_target_pairs={{0,24},{1,7},{2,26},{3,1},{4,28},{5,3},{6,30},{7,5},{8,0},{9,15},{... | collective-permute-start | bytes 1572872 | tf_op jit(solution)/shard_map/ppermute | solution.py:415
  106.5 11.7 %collective-permute-start.13 = (f32[2,512,128]{2,1,0:T(8,128)S(1)}, f32[2,512,128]{2,1,0:T(8,128)S(1)}, u32[]{:S(2)}, u32[]{:S(2)}) collective-permute-start(f32[2,512,128]{2,1,0:T(8,128)S(1)} %get-tuple-element.26), channel_id=1, source_target_pairs={{0,24},{1,7},{2,26},{3,1},{4,28},{5,3},{6,30},{7,5},{8,0},{9,15},{... | collective-permute-start | bytes 1572872 | tf_op jit(solution)/shard_map/ppermute | solution.py:415
  106.5 12.4 %collective-permute-start.15 = (f32[2,512,128]{2,1,0:T(8,128)S(1)}, f32[2,512,128]{2,1,0:T(8,128)S(1)}, u32[]{:S(2)}, u32[]{:S(2)}) collective-permute-start(f32[2,512,128]{2,1,0:T(8,128)S(1)} %get-tuple-element.27), channel_id=1, source_target_pairs={{0,8},{1,3},{2,10},{3,5},{4,12},{5,7},{6,14},{7,1},{8,16},{9,11},{... | collective-permute-start | bytes 1572872 | tf_op jit(solution)/shard_map/ppermute | solution.py:415
  113.4 11.2 %collective-permute-start.12 = (f32[2,512,128]{2,1,0:T(8,128)S(1)}, f32[2,512,128]{2,1,0:T(8,128)S(1)}, u32[]{:S(2)}, u32[]{:S(2)}) collective-permute-start(f32[2,512,128]{2,1,0:T(8,128)S(1)} %add.99), channel_id=1, source_target_pairs={{0,8},{1,3},{2,10},{3,5},{4,12},{5,7},{6,14},{7,1},{8,16},{9,11},{... | collective-permute-start | bytes 1572872 | tf_op jit(solution)/shard_map/ppermute | solution.py:415
  113.6 11.0 %collective-permute-start.17 = (f32[2,512,128]{2,1,0:T(8,128)S(1)}, f32[2,512,128]{2,1,0:T(8,128)S(1)}, u32[]{:S(2)}, u32[]{:S(2)}) collective-permute-start(f32[2,512,128]{2,1,0:T(8,128)S(1)} %add.108), channel_id=1, source_target_pairs={{0,24},{1,7},{2,26},{3,1},{4,28},{5,3},{6,30},{7,5},{8,0},{9,15},{... | collective-permute-start | bytes 1572872 | tf_op jit(solution)/shard_map/ppermute | solution.py:415
  124.7 7.1 %collective-permute-start.18 = (f32[512,128]{1,0:T(8,128)S(1)}, f32[512,128]{1,0:T(8,128)S(1)}, u32[]{:S(2)}, u32[]{:S(2)}) collective-permute-start(f32[512,128]{1,0:T(8,128)S(1)} %get-tuple-element.39), channel_id=1, source_target_pairs={{0,4},{1,17},{2,6},{3,19},{4,0},{5,21},{6,2},{7,23},{8,12},{9,25},... | collective-permute-start | bytes 786440 | tf_op jit(solution)/shard_map/ppermute | solution.py:415
  125.7 7.4 %collective-permute-start.19 = (f32[512,128]{1,0:T(8,128)S(1)}, f32[512,128]{1,0:T(8,128)S(1)}, u32[]{:S(2)}, u32[]{:S(2)}) collective-permute-start(f32[512,128]{1,0:T(8,128)S(1)} %get-tuple-element.40), channel_id=1, source_target_pairs={{0,6},{1,25},{2,0},{3,27},{4,2},{5,29},{6,4},{7,31},{8,14},{9,1},{... | collective-permute-start | bytes 786440 | tf_op jit(solution)/shard_map/ppermute | solution.py:415
  126.4 8.2 %collective-permute-start.14 = (f32[512,128]{1,0:T(8,128)S(1)}, f32[512,128]{1,0:T(8,128)S(1)}, u32[]{:S(2)}, u32[]{:S(2)}) collective-permute-start(f32[512,128]{1,0:T(8,128)S(1)} %get-tuple-element.41), channel_id=1, source_target_pairs={{0,2},{1,9},{2,4},{3,11},{4,6},{5,13},{6,0},{7,15},{8,10},{9,17},{... | collective-permute-start | bytes 786440 | tf_op jit(solution)/shard_map/ppermute | solution.py:415
  134.7 4.2 %collective-permute-start.20 = (f32[512,128]{1,0:T(8,128)S(1)}, f32[512,128]{1,0:T(8,128)}, u32[]{:S(2)}, u32[]{:S(2)}) collective-permute-start(f32[512,128]{1,0:T(8,128)S(1)} %fusion.6.refs_0_), channel_id=1, source_target_pairs={{0,1},{1,0},{2,3},{3,2},{4,5},{5,4},{6,7},{7,6},{8,9},{9,8},{10,11... | collective-permute-start | bytes 786440 | tf_op jit(solution)/shard_map/ppermute | solution.py:415
  142.4 6.6 %collective-permute-start.23 = (bf16[528,128]{1,0:T(8,128)(2,1)S(1)}, bf16[528,128]{1,0:T(8,128)(2,1)S(1)}, u32[]{:S(2)}, u32[]{:S(2)}) collective-permute-start(bf16[528,128]{1,0:T(8,128)(2,1)S(1)} %softmax_weights.1), channel_id=1, source_target_pairs={{0,8},{1,3},{2,10},{3,5},{4,12},{5,7},{6,14},{7,1},{8,16},{9,11},{... | collective-permute-start | bytes 405512 | tf_op jit(solution)/shard_map/ppermute | solution.py:415
  142.5 6.5 %collective-permute-start.22 = (bf16[528,128]{1,0:T(8,128)(2,1)S(1)}, bf16[528,128]{1,0:T(8,128)(2,1)S(1)}, u32[]{:S(2)}, u32[]{:S(2)}) collective-permute-start(bf16[528,128]{1,0:T(8,128)(2,1)S(1)} %softmax_weights.1), channel_id=1, source_target_pairs={{0,16},{1,5},{2,18},{3,7},{4,20},{5,1},{6,22},{7,3},{8,24},{9,13},... | collective-permute-start | bytes 405512 | tf_op jit(solution)/shard_map/ppermute | solution.py:415
  144.8 5.1 %collective-permute-start.21 = (bf16[528,128]{1,0:T(8,128)(2,1)S(1)}, bf16[528,128]{1,0:T(8,128)(2,1)S(1)}, u32[]{:S(2)}, u32[]{:S(2)}) collective-permute-start(bf16[528,128]{1,0:T(8,128)(2,1)S(1)} %softmax_weights.1), channel_id=1, source_target_pairs={{0,24},{1,7},{2,26},{3,1},{4,28},{5,3},{6,30},{7,5},{8,0},{9,15},{... | collective-permute-start | bytes 405512 | tf_op jit(solution)/shard_map/ppermute | solution.py:415
  150.0 9.3 %collective-permute-start.25 = (bf16[4,528,128]{2,1,0:T(8,128)(2,1)S(1)}, bf16[4,528,128]{2,1,0:T(8,128)(2,1)S(1)}, u32[]{:S(2)}, u32[]{:S(2)}) collective-permute-start(bf16[4,528,128]{2,1,0:T(8,128)(2,1)S(1)} %pad_maximum_fusion.1.refs_7_), channel_id=1, source_target_pairs={{0,6},{1,25},{2,0},{3,27},{4,2},{5,29},{6,4},{7,31},{8,14},{9,1},{... | collective-permute-start | bytes 1622024 | tf_op jit(solution)/shard_map/ppermute | solution.py:415
  153.0 11.4 %collective-permute-start.24 = (bf16[4,528,128]{2,1,0:T(8,128)(2,1)S(1)}, bf16[4,528,128]{2,1,0:T(8,128)(2,1)S(1)}, u32[]{:S(2)}, u32[]{:S(2)}) collective-permute-start(bf16[4,528,128]{2,1,0:T(8,128)(2,1)S(1)} %pad_maximum_fusion.1.refs_7_), channel_id=1, source_target_pairs={{0,2},{1,9},{2,4},{3,11},{4,6},{5,13},{6,0},{7,15},{8,10},{9,17},{... | collective-permute-start | bytes 1622024 | tf_op jit(solution)/shard_map/ppermute | solution.py:415
  159.3 9.7 %collective-permute-start.26 = (bf16[4,528,128]{2,1,0:T(8,128)(2,1)S(1)}, bf16[4,528,128]{2,1,0:T(8,128)(2,1)S(1)}, u32[]{:S(2)}, u32[]{:S(2)}) collective-permute-start(bf16[4,528,128]{2,1,0:T(8,128)(2,1)S(1)} %collective-permute-done.25.refs_9_), channel_id=1, source_target_pairs={{0,6},{1,25},{2,0},{3,27},{4,2},{5,29},{6,4},{7,31},{8,14},{9,1},{... | collective-permute-start | bytes 1622024 | tf_op jit(solution)/shard_map/ppermute | solution.py:415
  162.7 8.5 %collective-permute-start.27 = (bf16[4,528,128]{2,1,0:T(8,128)(2,1)S(1)}, bf16[4,528,128]{2,1,0:T(8,128)(2,1)S(1)}, u32[]{:S(2)}, u32[]{:S(2)}) collective-permute-start(bf16[4,528,128]{2,1,0:T(8,128)(2,1)S(1)} %pad_maximum_fusion.1.refs_7_), channel_id=1, source_target_pairs={{0,1},{1,0},{2,3},{3,2},{4,5},{5,4},{6,7},{7,6},{8,9},{9,8},{10,11... | collective-permute-start | bytes 1622024 | tf_op jit(solution)/shard_map/ppermute | solution.py:415
  164.4 6.9 %collective-permute-start.29 = (bf16[4,528,128]{2,1,0:T(8,128)(2,1)S(1)}, bf16[4,528,128]{2,1,0:T(8,128)(2,1)S(1)}, u32[]{:S(2)}, u32[]{:S(2)}) collective-permute-start(bf16[4,528,128]{2,1,0:T(8,128)(2,1)S(1)} %collective-permute-done.25.refs_9_), channel_id=1, source_target_pairs={{0,1},{1,0},{2,3},{3,2},{4,5},{5,4},{6,7},{7,6},{8,9},{9,8},{10,11... | collective-permute-start | bytes 1622024 | tf_op jit(solution)/shard_map/ppermute | solution.py:415
  164.4 6.9 %collective-permute-start.28 = (bf16[4,528,128]{2,1,0:T(8,128)(2,1)S(1)}, bf16[4,528,128]{2,1,0:T(8,128)(2,1)S(1)}, u32[]{:S(2)}, u32[]{:S(2)}) collective-permute-start(bf16[4,528,128]{2,1,0:T(8,128)(2,1)S(1)} %collective-permute-done.24.refs_8_), channel_id=1, source_target_pairs={{0,1},{1,0},{2,3},{3,2},{4,5},{5,4},{6,7},{7,6},{8,9},{9,8},{10,11... | collective-permute-start | bytes 1622024 | tf_op jit(solution)/shard_map/ppermute | solution.py:415
  169.0 3.8 %collective-permute-start.30 = (bf16[4,528,128]{2,1,0:T(8,128)(2,1)S(1)}, bf16[4,528,128]{2,1,0:T(8,128)(2,1)S(1)}, u32[]{:S(2)}, u32[]{:S(2)}) collective-permute-start(bf16[4,528,128]{2,1,0:T(8,128)(2,1)S(1)} %collective-permute-done.26.refs_10_), channel_id=1, source_target_pairs={{0,1},{1,0},{2,3},{3,2},{4,5},{5,4},{6,7},{7,6},{8,9},{9,8},{10,11... | collective-permute-start | bytes 1622024 | tf_op jit(solution)/shard_map/ppermute | solution.py:415
  193.2 14.7 %collective-permute-start.31 = (bf16[16,128,128]{2,1,0:T(8,128)(2,1)}, bf16[16,128,128]{2,1,0:T(8,128)(2,1)}, u32[]{:S(2)}, u32[]{:S(2)}) collective-permute-start(bf16[16,128,128]{2,1,0:T(8,128)(2,1)} %get-tuple-element.34), channel_id=1, source_target_pairs={{0,32},{32,64},{64,96},{96,0},{1,33},{33,65},{65,97},{97,1},{2,34}... | collective-permute-start | bytes 1572872 | tf_op jit(solution)/shard_map/ppermute | solution.py:402
  193.2 15.9 %collective-permute-start.35 = (bf16[16,128,128]{2,1,0:T(8,128)(2,1)}, bf16[16,128,128]{2,1,0:T(8,128)(2,1)}, u32[]{:S(2)}, u32[]{:S(2)}) collective-permute-start(bf16[16,128,128]{2,1,0:T(8,128)(2,1)} %get-tuple-element.38), channel_id=1, source_target_pairs={{0,96},{32,0},{64,32},{96,64},{1,97},{33,1},{65,33},{97,65},{2,98}... | collective-permute-start | bytes 1572872 | tf_op jit(solution)/shard_map/ppermute | solution.py:402
  195.9 36.2 %all-to-all-start.2 = ((bf16[32,128,128]{2,1,0:T(8,128)(2,1)}), bf16[32,128,128]{2,1,0:T(8,128)(2,1)S(1)}, u32[]{:S(2)}, u32[]{:S(2)}) async-start(bf16[32,128,128]{2,1,0:T(8,128)(2,1)} %copy-done.1), calls=%async_computation.2 | async-start | bytes 2097152 | tf_op jit(solution)/shard_map/all_to_all | solution.py:463
  203.0 27.5 %copy-start.3 = (bf16[32,128,128]{2,1,0:T(8,128)(2,1)S(1)}, bf16[32,128,128]{2,1,0:T(8,128)(2,1)}, u32[]{:S(2)}) copy-start(bf16[32,128,128]{2,1,0:T(8,128)(2,1)} %copy-done.2) | copy-start | bytes 3145732
  203.0 15.1 %collective-permute-start.33 = (bf16[16,128,128]{2,1,0:T(8,128)(2,1)}, bf16[16,128,128]{2,1,0:T(8,128)(2,1)S(1)}, u32[]{:S(2)}, u32[]{:S(2)}) collective-permute-start(bf16[16,128,128]{2,1,0:T(8,128)(2,1)} %copy-done.10), channel_id=1, source_target_pairs={{0,96},{32,0},{64,32},{96,64},{1,97},{33,1},{65,33},{97,65},{2,98}... | collective-permute-start | bytes 1572872 | tf_op jit(solution)/shard_map/ppermute | solution.py:402
  203.8 15.4 %collective-permute-start.34 = (bf16[16,128,128]{2,1,0:T(8,128)(2,1)}, bf16[16,128,128]{2,1,0:T(8,128)(2,1)S(1)}, u32[]{:S(2)}, u32[]{:S(2)}) collective-permute-start(bf16[16,128,128]{2,1,0:T(8,128)(2,1)} %copy-done.9), channel_id=1, source_target_pairs={{0,32},{32,64},{64,96},{96,0},{1,33},{33,65},{65,97},{97,1},{2,34}... | collective-permute-start | bytes 1572872 | tf_op jit(solution)/shard_map/ppermute | solution.py:402
  209.0 21.4 %collective-permute-start.32 = (bf16[16,128,128]{2,1,0:T(8,128)(2,1)S(1)}, bf16[16,128,128]{2,1,0:T(8,128)(2,1)S(1)}, u32[]{:S(2)}, u32[]{:S(2)}) collective-permute-start(bf16[16,128,128]{2,1,0:T(8,128)(2,1)S(1)} %add_convert_fusion.1), channel_id=1, source_target_pairs={{0,32},{32,64},{64,96},{96,0},{1,33},{33,65},{65,97},{97,1},{2,34}... | collective-permute-start | bytes 1572872 | tf_op jit(solution)/shard_map/ppermute | solution.py:402
  210.3 20.1 %collective-permute-start.36 = (bf16[16,128,128]{2,1,0:T(8,128)(2,1)S(1)}, bf16[16,128,128]{2,1,0:T(8,128)(2,1)S(1)}, u32[]{:S(2)}, u32[]{:S(2)}) collective-permute-start(bf16[16,128,128]{2,1,0:T(8,128)(2,1)S(1)} %add_convert_fusion), channel_id=1, source_target_pairs={{0,96},{32,0},{64,32},{96,64},{1,97},{33,1},{65,33},{97,65},{2,98}... | collective-permute-start | bytes 1572872 | tf_op jit(solution)/shard_map/ppermute | solution.py:402
  232.1 24.3 %all-to-all-start.3 = ((bf16[32,128,128]{2,1,0:T(8,128)(2,1)}), bf16[32,128,128]{2,1,0:T(8,128)(2,1)S(1)}, u32[]{:S(2)}, u32[]{:S(2)}) async-start(bf16[32,128,128]{2,1,0:T(8,128)(2,1)} %join.1), calls=%async_computation.3 | async-start | bytes 2097152 | tf_op jit(solution)/shard_map/all_to_all | solution.py:463
  (9 other events, 48.2 us)

commit v2 on v1

--- a/solution.py
+++ b/solution.py
@@ -116,7 +116,6 @@
 
 
 PIECES = ((0, 32), (32, 16), (48, 16), (64, 16), (80, 16), (96, 16), (112, 16))
-GIVEN = ((0, 0, 0, 32), (1, 0, 32, 16), (1, 16, 112, 16), (1, 32, 64, 32), (2, 0, 48, 16), (3, 0, 96, 16))
 
 
 def chip_at(at, core, lead, other):
@@ -126,13 +125,13 @@
 
 
 def score_kernel(ids, own, at, *refs):
-    q, pieces, given, outs = refs[:2], refs[2:9], refs[9:13], refs[13:20]
-    qv, pv, sv, sems = refs[20:]
+    q, pieces, outs = refs[:2], refs[2:16], refs[16:23]
+    qv, pv, sv, sems = refs[23:]
     core = at[0]
     moves = [(q[n].at[:, 0:BLK, :], qv.at[n]) for n in range(2)]
-    moves += [(pieces[n], pv.at[0, first : first + size]) for n, (first, size) in enumerate(PIECES)]
-    for n, begin, first, size in GIVEN:
-        moves.append((given[n].at[begin : begin + size], pv.at[1, first : first + size]))
+    for n, piece in enumerate(pieces):
+        first, size = PIECES[n % 7]
+        moves.append((piece, pv.at[n // 7, first : first + size]))
     run_copies([pltpu.make_async_copy(*move, sems.at[n]) for n, move in enumerate(moves)])
 
     stores = []
@@ -159,7 +158,7 @@
                 else:
                     target = outs[2 * lead - 2 + other // 2].at[other % 2, rows, :]
                 source = sv.at[chip_at(at, core, lead, other), rows, :]
-                sem = sems.at[15 + 16 * half + 4 * lead + other]
+                sem = sems.at[16 + 16 * half + 4 * lead + other]
                 stores.append(pltpu.make_async_copy(source, target, sem))
                 stores[-1].start()
     for copy in stores:
@@ -171,14 +170,14 @@
     shapes = [(2, ROWS, 128)] * 6 + [(4, ROWS, 128)]
     return pl.pallas_call(
         score_kernel,
-        in_specs=[SMEM] * 3 + [ANY] * 13,
+        in_specs=[SMEM] * 3 + [ANY] * 16,
         out_specs=[ANY] * 7,
         out_shape=[jax.ShapeDtypeStruct(s, jnp.float32) for s in shapes],
         scratch_shapes=[
             pltpu.VMEM((2, nblk, BLK, 128), jnp.bfloat16),
             pltpu.VMEM((2, 4 * nblk, BLK, 128), jnp.bfloat16),
             pltpu.VMEM((BLK // 8, ROWS, 128), jnp.float32),
-            pltpu.SemaphoreType.DMA((47,)),
+            pltpu.SemaphoreType.DMA((48,)),
         ],
         **params(17, 32 * MIB),
         name="partial_scores",
@@ -279,10 +278,10 @@
         for m in range(4):
             gp_sum[4 * n + m] = jnp.zeros((BLK, 128), jnp.float32)
 
-    for copy in loads:
-        copy.wait()
-
-    for side in range(2):
+    for n in range(2):
+        for copy in loads[24 * n : 24 + 16 * n]:
+            copy.wait()
+        side = jnp.where(core == n, 0, 1)
 
         @pl.loop(0, PART // STEP)
         def _(step):
@@ -465,15 +464,14 @@
     up, down, flip = along("z", 1), along("z", -1), along("core", 1)
     p_own = exchange(by_features(passages))
     low, high = p_own[: ndev // 2], p_own[ndev // 2 :]
-    above0, below1 = down(low), up(high)
-    low, _ = lax.optimization_barrier((low, below1))
-    high, _ = lax.optimization_barrier((high, above0))
-    far0, far1 = down(above0), up(below1)
-    above1, below0 = down(high), up(low)
+    above0, below1, given0 = down(low), up(high), flip(p_own)
+    low, high, *_ = lax.optimization_barrier((low, high, above0, below1, given0))
+    above1, below0, given1, given2 = down(high), up(low), flip(above0), flip(below1)
+    last0, last1, *_ = lax.optimization_barrier((above0, below1, above1, below0, given1, given2))
+    far0, far1 = down(last0), up(last1)
     pieces = [p_own, above0, above1, far0, far1, below0, below1]
+    given = [given0, given1, flip(above1), flip(far0), flip(far1), flip(below0), given2]
     q_own = exchange(by_features(queries, positives.reshape(1, BLK)))
-    early = jnp.concatenate([above0, below1, far0, far1])
-    given = [flip(v) for v in (p_own, early, above1, below0)]
     q = [q_own, flip(q_own)]
 
     group = counts[0]

time: 260 us -> 257 us (0.988)
  waiting for transfers between devices: 111 us -> 105 us
  starting transfers between devices: 64.7 us -> 70.5 us
  other arithmetic: 6.02 us -> 3.24 us
    all_to_all x3, waiting for transfers between devices: 22.4 us -> 13.5 us  [exchange(): return lax.all_to_all(v, 'dev', 0, 0, tiled=True)]
    ppermute x25 -> x28, starting transfers between devices: 29.1 us -> 36.1 us  [along(): return lambda v: lax.ppermute(v, 'dev', perm)]
    ppermute x12, waiting for transfers between devices: 49.4 us -> 55.2 us  [along(): return lambda v: lax.ppermute(v, 'grp', perm)]
    ppermute x25 -> x28, waiting for transfers between devices: 39.6 us -> 36.6 us  [along(): return lambda v: lax.ppermute(v, 'dev', perm)]
    concatenate x1 -> x0, other arithmetic: 2.78 us -> none  [per_device(): early = jnp.concatenate([above0, below1, far0, far1])]
  transfers between devices with their start and end apart: 40 -> 43, of which waited for: 23 -> 23; matrix products, arithmetic and copies ran while one was open for 3% -> 3% of each run, Pallas kernels for 2% -> 2%
where the time goes in v2:
time: 257 us
  waiting for transfers between devices  105 us (41%)
  starting transfers between devices  70.5 us (27%)
  Pallas kernels  41.9 us (16%)
  blocking collectives  25.5 us (10%)
  local copies, waits for them, and re-layouts  8.99 us (3%)
  other arithmetic  3.24 us (1%)
    ppermute x12, waiting for transfers between devices, along(): return lambda v: lax.ppermute(v, 'grp', perm)  55.2 us
    ppermute x28, waiting for transfers between devices, along(): return lambda v: lax.ppermute(v, 'dev', perm)  36.6 us
    ppermute x28, starting transfers between devices, along(): return lambda v: lax.ppermute(v, 'dev', perm)  36.1 us
    all_to_all x1, blocking collectives, exchange(): return lax.all_to_all(v, 'dev', 0, 0, tiled=True)  25.5 us
    all_to_all x3, starting transfers between devices, exchange(): return lax.all_to_all(v, 'dev', 0, 0, tiled=True)  19.5 us
    pallas_call x1, Pallas kernels, gradients(): pl.pallas_call(grad_kernel, in_specs=[SMEM] * 3 + [ANY] * 16, out_specs=[...  15.3 us
    ppermute x12, starting transfers between devices, along(): return lambda v: lax.ppermute(v, 'grp', perm)  14.9 us
    all_to_all x3, waiting for transfers between devices, exchange(): return lax.all_to_all(v, 'dev', 0, 0, tiled=True)  13.5 us
  transfers between devices with their start and end apart: 43, of which 23 were waited for; matrix products, arithmetic and copies ran while one was open for 3% of the time, Pallas kernels for 2%

profile of v2, /device:TPU:1, one launch (start us, length us, event | category | flops | bytes accessed | tf_op | source)
XLA Modules:
  0.0 256.6 jit_solution(3314506615710214058)
XLA Ops:
  0.7 2.5 pack.3
  3.1 25.5 %all_to_all.20.refs_2_.refs_0_ = bf16[32,128,128]{2,1,0:T(8,128)(2,1)S(1)} all-to-all(bf16[32,128,128]{2,1,0:T(8,128)(2,1)} %pack.3), channel_id=1, replica_groups=mesh['grp'=4,'dev'=32] {'dev'}, dimensions={0} | all-to-all | bytes 2097152 | tf_op jit(solution)/shard_map/all_to_all | solution.py:462
  30.1 4.0 %all-to-all-start = ((bf16[32,144,128]{2,1,0:T(8,128)(2,1)}), bf16[32,144,128]{2,1,0:T(8,128)(2,1)S(1)}, u32[]{:S(2)}, u32[]{:S(2)}) async-start(bf16[32,144,128]{2,1,0:T(8,128)(2,1)} %pack.2), calls=%async_computation | async-start | bytes 2359296 | tf_op jit(solution)/shard_map/all_to_all | solution.py:462
  35.2 1.6 collective-permute-start.1
  36.9 2.1 collective-permute-start
  39.0 12.2 %collective-permute-done.1.refs_8_.refs_6_ = bf16[16,128,128]{2,1,0:T(8,128)(2,1)S(1)} collective-permute-done((bf16[16,128,128]{2,1,0:T(8,128)(2,1)}, bf16[16,128,128]{2,1,0:T(8,128)(2,1)S(1)}, u32[]{:S(2)}, u32[]{:S(2)}) %collective-permute-start.1) | collective-permute-done | bytes 524320 | tf_op jit(solution)/shard_map/ppermute | solution.py:401
  52.1 2.7 %collective-permute-start.3 = (bf16[16,128,128]{2,1,0:T(8,128)(2,1)}, bf16[16,128,128]{2,1,0:T(8,128)(2,1)}, u32[]{:S(2)}, u32[]{:S(2)}) collective-permute-start(bf16[16,128,128]{2,1,0:T(8,128)(2,1)} %get-tuple-element.23), channel_id=1, source_target_pairs={{0,96},{32,0},{64,32},{96,64},{1,97},{33,1},{65,33},{97,65},{2,98}... | collective-permute-start | bytes 1572872 | tf_op jit(solution)/shard_map/ppermute | solution.py:401
  55.3 11.1 %collective-permute-done.3.refs_4_.refs_2_ = bf16[16,128,128]{2,1,0:T(8,128)(2,1)} collective-permute-done((bf16[16,128,128]{2,1,0:T(8,128)(2,1)}, bf16[16,128,128]{2,1,0:T(8,128)(2,1)}, u32[]{:S(2)}, u32[]{:S(2)}) %collective-permute-start.3) | collective-permute-done | bytes 524320 | tf_op jit(solution)/shard_map/ppermute | solution.py:401
  66.4 3.1 %collective-permute-done.4.refs_7_.refs_5_ = bf16[16,128,128]{2,1,0:T(8,128)(2,1)} collective-permute-done((bf16[16,128,128]{2,1,0:T(8,128)(2,1)}, bf16[16,128,128]{2,1,0:T(8,128)(2,1)}, u32[]{:S(2)}, u32[]{:S(2)}) %collective-permute-start.4) | collective-permute-done | bytes 524320 | tf_op jit(solution)/shard_map/ppermute | solution.py:401
  71.3 1.7 collective-permute-start.10
  73.1 8.7 %collective-permute-done.7.refs_5_.refs_3_ = bf16[16,128,128]{2,1,0:T(8,128)(2,1)S(1)} collective-permute-done((bf16[16,128,128]{2,1,0:T(8,128)(2,1)S(1)}, bf16[16,128,128]{2,1,0:T(8,128)(2,1)S(1)}, u32[]{:S(2)}, u32[]{:S(2)}) %collective-permute-start.7) | collective-permute-done | bytes 524320 | tf_op jit(solution)/shard_map/ppermute | solution.py:401
  81.8 2.0 collective-permute-start.11
  83.9 1.5 collective-permute-start.12
  86.9 12.1 %partial_scores.1 = (f32[2,512,128]{2,1,0:T(8,128)S(1)}, f32[2,512,128]{2,1,0:T(8,128)S(1)}, f32[2,512,128]{2,1,0:T(8,128)S(1)}, f32[2,512,128]{2,1,0:T(8,128)S(...) custom-call(s32[128]{0:T(128)S(1)} %and_select_fusion.ids, ...), custom_call_target="tpu_custom_call" | custom-call | bytes 33554432 | tf_op jit(solution)/shard_map/partial_scores/pallas_call | solution.py:171
  99.1 1.5 collective-permute-start.14
  100.5 1.3 collective-permute-start.19
  101.8 1.4 collective-permute-start.16
  103.3 5.4 %collective-permute-done.14 = f32[2,512,128]{2,1,0:T(8,128)S(1)} collective-permute-done((f32[2,512,128]{2,1,0:T(8,128)S(1)}, f32[2,512,128]{2,1,0:T(8,128)S(1)}, u32[]{:S(2)}, u32[]{:S(2)}) %collective-permute-start.14) | collective-permute-done | bytes 524320 | tf_op jit(solution)/shard_map/ppermute | solution.py:414
  109.1 2.6 %collective-permute-start.20 = (f32[2,512,128]{2,1,0:T(8,128)S(1)}, f32[2,512,128]{2,1,0:T(8,128)S(1)}, u32[]{:S(2)}, u32[]{:S(2)}) collective-permute-start(f32[2,512,128]{2,1,0:T(8,128)S(1)} %add.108), channel_id=1, source_target_pairs={{0,24},{1,7},{2,26},{3,1},{4,28},{5,3},{6,30},{7,5},{8,0},{9,15},{... | collective-permute-start | bytes 1572872 | tf_op jit(solution)/shard_map/ppermute | solution.py:414
  111.6 2.8 %collective-permute-done.16 = f32[2,512,128]{2,1,0:T(8,128)S(1)} collective-permute-done((f32[2,512,128]{2,1,0:T(8,128)S(1)}, f32[2,512,128]{2,1,0:T(8,128)S(1)}, u32[]{:S(2)}, u32[]{:S(2)}) %collective-permute-start.16) | collective-permute-done | bytes 524320 | tf_op jit(solution)/shard_map/ppermute | solution.py:414
  114.5 5.4 %collective-permute-done.15 = f32[2,512,128]{2,1,0:T(8,128)S(1)} collective-permute-done((f32[2,512,128]{2,1,0:T(8,128)S(1)}, f32[2,512,128]{2,1,0:T(8,128)S(1)}, u32[]{:S(2)}, u32[]{:S(2)}) %collective-permute-start.15) | collective-permute-done | bytes 524320 | tf_op jit(solution)/shard_map/ppermute | solution.py:414
  120.2 2.9 %collective-permute-start.21 = (f32[512,128]{1,0:T(8,128)S(1)}, f32[512,128]{1,0:T(8,128)S(1)}, u32[]{:S(2)}, u32[]{:S(2)}) collective-permute-start(f32[512,128]{1,0:T(8,128)S(1)} %get-tuple-element.43), channel_id=1, source_target_pairs={{0,4},{1,17},{2,6},{3,19},{4,0},{5,21},{6,2},{7,23},{8,12},{9,25},... | collective-permute-start | bytes 786440 | tf_op jit(solution)/shard_map/ppermute | solution.py:414
  124.5 2.8 %collective-permute-done.21 = f32[512,128]{1,0:T(8,128)S(1)} collective-permute-done((f32[512,128]{1,0:T(8,128)S(1)}, f32[512,128]{1,0:T(8,128)S(1)}, u32[]{:S(2)}, u32[]{:S(2)}) %collective-permute-start.21) | collective-permute-done | bytes 262176 | tf_op jit(solution)/shard_map/ppermute | solution.py:414
  127.3 3.0 %collective-permute-done.22 = f32[512,128]{1,0:T(8,128)S(1)} collective-permute-done((f32[512,128]{1,0:T(8,128)S(1)}, f32[512,128]{1,0:T(8,128)S(1)}, u32[]{:S(2)}, u32[]{:S(2)}) %collective-permute-start.22) | collective-permute-done | bytes 262176 | tf_op jit(solution)/shard_map/ppermute | solution.py:414
  130.7 3.2 %collective-permute-start.23 = (f32[512,128]{1,0:T(8,128)S(1)}, f32[512,128]{1,0:T(8,128)}, u32[]{:S(2)}, u32[]{:S(2)}) collective-permute-start(f32[512,128]{1,0:T(8,128)S(1)} %fusion.6.refs_0_), channel_id=1, source_target_pairs={{0,1},{1,0},{2,3},{3,2},{4,5},{5,4},{6,7},{7,6},{8,9},{9,8},{10,11... | collective-permute-start | bytes 786440 | tf_op jit(solution)/shard_map/ppermute | solution.py:414
  135.8 3.5 %softmax_weights.1 = bf16[528,128]{1,0:T(8,128)(2,1)S(1)} custom-call(s32[5]{0:T(128)S(1)} %stack.53.at, f32[512,128]{1,0:T(8,128)S(1)} %fusion.6.refs_0_, f32[512,128]{1,0:T(8,128)} %collective-permute-done.23.refs_1_, s32[8,128]{1,0:T(8,128)S(1)} %stack.56.refs_2_, bf16[32,144,128]{2,1,0:T(8,128)(2,1)S(1)} %all-to-all-done.refs_0_.refs_3_.q), custom_call_target="tpu_custom_call" | custom-call | bytes 8388608 | tf_op jit(solution)/shard_map/softmax_weights/pallas_call | solution.py:244
  139.6 2.4 collective-permute-start.25
  143.2 1.6 collective-permute-done.26
  146.9 2.7 %collective-permute-start.28 = (bf16[4,528,128]{2,1,0:T(8,128)(2,1)S(1)}, bf16[4,528,128]{2,1,0:T(8,128)(2,1)S(1)}, u32[]{:S(2)}, u32[]{:S(2)}) collective-permute-start(bf16[4,528,128]{2,1,0:T(8,128)(2,1)S(1)} %pad_maximum_fusion.refs_7_), channel_id=1, source_target_pairs={{0,6},{1,25},{2,0},{3,27},{4,2},{5,29},{6,4},{7,31},{8,14},{9,1},{... | collective-permute-start | bytes 1622024 | tf_op jit(solution)/shard_map/ppermute | solution.py:414
  149.6 6.3 %collective-permute-done.28.refs_9_ = bf16[4,528,128]{2,1,0:T(8,128)(2,1)S(1)} collective-permute-done((bf16[4,528,128]{2,1,0:T(8,128)(2,1)S(1)}, bf16[4,528,128]{2,1,0:T(8,128)(2,1)S(1)}, u32[]{:S(2)}, u32[]{:S(2)}) %collective-permute-start.28) | collective-permute-done | bytes 540704 | tf_op jit(solution)/shard_map/ppermute | solution.py:414
  155.9 3.4 %collective-permute-start.29 = (bf16[4,528,128]{2,1,0:T(8,128)(2,1)S(1)}, bf16[4,528,128]{2,1,0:T(8,128)(2,1)S(1)}, u32[]{:S(2)}, u32[]{:S(2)}) collective-permute-start(bf16[4,528,128]{2,1,0:T(8,128)(2,1)S(1)} %collective-permute-done.28.refs_9_), channel_id=1, source_target_pairs={{0,6},{1,25},{2,0},{3,27},{4,2},{5,29},{6,4},{7,31},{8,14},{9,1},{... | collective-permute-start | bytes 1622024 | tf_op jit(solution)/shard_map/ppermute | solution.py:414
  159.3 1.9 collective-permute-start.30
  161.8 3.9 %collective-permute-done.29.refs_10_ = bf16[4,528,128]{2,1,0:T(8,128)(2,1)S(1)} collective-permute-done((bf16[4,528,128]{2,1,0:T(8,128)(2,1)S(1)}, bf16[4,528,128]{2,1,0:T(8,128)(2,1)S(1)}, u32[]{:S(2)}, u32[]{:S(2)}) %collective-permute-start.29) | collective-permute-done | bytes 540704 | tf_op jit(solution)/shard_map/ppermute | solution.py:414
  165.7 2.5 collective-permute-start.33
  168.1 1.5 collective-permute-done.33.refs_14_
  169.7 15.3 %gradients.1 = (bf16[32,128,128]{2,1,0:T(8,128)(2,1)S(1)}, bf16[16,128,128]{2,1,0:T(8,128)(2,1)S(1)}, bf16[16,128,128]{2,1,0:T(8,128)(2,1)S(1)}, bf16[16,128,128...) custom-call(s32[128]{0:T(128)S(1)} %and_select_fusion.ids, ...), custom_call_target="tpu_custom_call" | custom-call | bytes 33554432 | tf_op jit(solution)/shard_map/gradients/pallas_call | solution.py:333
  190.1 2.7 %collective-permute-start.38 = (bf16[16,128,128]{2,1,0:T(8,128)(2,1)}, bf16[16,128,128]{2,1,0:T(8,128)(2,1)}, u32[]{:S(2)}, u32[]{:S(2)}) collective-permute-start(bf16[16,128,128]{2,1,0:T(8,128)(2,1)} %get-tuple-element.42), channel_id=1, source_target_pairs={{0,96},{32,0},{64,32},{96,64},{1,97},{33,1},{65,33},{97,65},{2,98}... | collective-permute-start | bytes 1572872 | tf_op jit(solution)/shard_map/ppermute | solution.py:401
  192.8 7.7 %all-to-all-start.2 = ((bf16[32,128,128]{2,1,0:T(8,128)(2,1)}), bf16[32,128,128]{2,1,0:T(8,128)(2,1)S(1)}, u32[]{:S(2)}, u32[]{:S(2)}) async-start(bf16[32,128,128]{2,1,0:T(8,128)(2,1)} %copy-done.5), calls=%async_computation.2 | async-start | bytes 2097152 | tf_op jit(solution)/shard_map/all_to_all | solution.py:462
  200.6 1.5 collective-permute-start.37
  202.1 2.7 %collective-permute-done.34 = bf16[16,128,128]{2,1,0:T(8,128)(2,1)} collective-permute-done((bf16[16,128,128]{2,1,0:T(8,128)(2,1)}, bf16[16,128,128]{2,1,0:T(8,128)(2,1)}, u32[]{:S(2)}, u32[]{:S(2)}) %collective-permute-start.34) | collective-permute-done | bytes 524320 | tf_op jit(solution)/shard_map/ppermute | solution.py:401
  207.2 2.7 %collective-permute-start.39 = (bf16[16,128,128]{2,1,0:T(8,128)(2,1)S(1)}, bf16[16,128,128]{2,1,0:T(8,128)(2,1)S(1)}, u32[]{:S(2)}, u32[]{:S(2)}) collective-permute-start(bf16[16,128,128]{2,1,0:T(8,128)(2,1)S(1)} %add_convert_fusion), channel_id=1, source_target_pairs={{0,96},{32,0},{64,32},{96,64},{1,97},{33,1},{65,33},{97,65},{2,98}... | collective-permute-start | bytes 1572872 | tf_op jit(solution)/shard_map/ppermute | solution.py:401
  210.0 5.0 %collective-permute-done.36.refs_2_ = bf16[16,128,128]{2,1,0:T(8,128)(2,1)S(1)} collective-permute-done((bf16[16,128,128]{2,1,0:T(8,128)(2,1)}, bf16[16,128,128]{2,1,0:T(8,128)(2,1)S(1)}, u32[]{:S(2)}, u32[]{:S(2)}) %collective-permute-start.36) | collective-permute-done | bytes 524320 | tf_op jit(solution)/shard_map/ppermute | solution.py:401
  216.1 11.2 %collective-permute-done.35.refs_1_ = bf16[16,128,128]{2,1,0:T(8,128)(2,1)S(1)} collective-permute-done((bf16[16,128,128]{2,1,0:T(8,128)(2,1)S(1)}, bf16[16,128,128]{2,1,0:T(8,128)(2,1)S(1)}, u32[]{:S(2)}, u32[]{:S(2)}) %collective-permute-start.35) | collective-permute-done | bytes 524320 | tf_op jit(solution)/shard_map/ppermute | solution.py:401
  227.3 1.6 join.1
  229.0 7.8 %all-to-all-start.3 = ((bf16[32,128,128]{2,1,0:T(8,128)(2,1)}), bf16[32,128,128]{2,1,0:T(8,128)(2,1)S(1)}, u32[]{:S(2)}, u32[]{:S(2)}) async-start(bf16[32,128,128]{2,1,0:T(8,128)(2,1)} %join.1), calls=%async_computation.3 | async-start | bytes 2097152 | tf_op jit(solution)/shard_map/all_to_all | solution.py:462
  237.4 2.8 %unpack.2 = f32[128,4096]{1,0:T(8,128)} custom-call(bf16[32,128,128]{2,1,0:T(8,128)(2,1)S(1)} %all-to-all-done.2.x), custom_call_target="tpu_custom_call" | custom-call | bytes 8388608 | tf_op jit(solution)/shard_map/unpack/pallas_call | solution.py:103
  240.2 13.5 %all-to-all-done.3.x = bf16[32,128,128]{2,1,0:T(8,128)(2,1)S(1)} async-done(((bf16[32,128,128]{2,1,0:T(8,128)(2,1)}), bf16[32,128,128]{2,1,0:T(8,128)(2,1)S(1)}, u32[]{:S(2)}, u32[]{:S(2)}) %all-to-all-start.3) | async-done | bytes 1048608 | tf_op jit(solution)/shard_map/all_to_all | solution.py:462
  253.7 2.8 %unpack.3 = f32[128,4096]{1,0:T(8,128)} custom-call(bf16[32,128,128]{2,1,0:T(8,128)(2,1)S(1)} %all-to-all-done.3.x), custom_call_target="tpu_custom_call" | custom-call | bytes 8388608 | tf_op jit(solution)/shard_map/unpack/pallas_call | solution.py:103
  (104 shorter events, 25.3 us)
Async XLA Ops:
  0.6 28.2 %copy-start.12 = (s32[128]{0:T(128)S(1)}, s32[128]{0:T(128)}, u32[]{:S(2)}) copy-start(s32[128]{0:T(128)} %param.9) | copy-start | bytes 1540
  0.6 28.2 %copy-start.4 = (f32[128,4096]{1,0:T(8,128)S(1)}, f32[128,4096]{1,0:T(8,128)}, u32[]{:S(2)}) copy-start(f32[128,4096]{1,0:T(8,128)} %x.6) | copy-start | bytes 6291460
  28.7 23.4 %collective-permute-start.2 = (bf16[32,128,128]{2,1,0:T(8,128)(2,1)S(1)}, bf16[32,128,128]{2,1,0:T(8,128)(2,1)}, u32[]{:S(2)}, u32[]{:S(2)}) collective-permute-start(bf16[32,128,128]{2,1,0:T(8,128)(2,1)S(1)} %all_to_all.20.refs_2_.refs_0_), channel_id=1, source_target_pairs={{0,1},{1,0},{2,3},{3,2},{4,5},{5,4},{6,7},{7,6},{8,9},{9,8},{10,11... | collective-permute-start | bytes 3145736 | tf_op jit(solution)/shard_map/ppermute | solution.py:414
  30.1 40.9 %copy-start.16 = (s32[1,32]{1,0:T(1,128)S(1)}, s32[1,32]{1,0:T(1,128)}, u32[]{:S(2)}) copy-start(s32[1,32]{1,0:T(1,128)} %param.8) | copy-start | bytes 388
  30.1 24.6 %all-to-all-start = ((bf16[32,144,128]{2,1,0:T(8,128)(2,1)}), bf16[32,144,128]{2,1,0:T(8,128)(2,1)S(1)}, u32[]{:S(2)}, u32[]{:S(2)}) async-start(bf16[32,144,128]{2,1,0:T(8,128)(2,1)} %pack.2), calls=%async_computation | async-start | bytes 2359296 | tf_op jit(solution)/shard_map/all_to_all | solution.py:462
  35.2 16.0 %collective-permute-start.1 = (bf16[16,128,128]{2,1,0:T(8,128)(2,1)}, bf16[16,128,128]{2,1,0:T(8,128)(2,1)S(1)}, u32[]{:S(2)}, u32[]{:S(2)}) collective-permute-start(bf16[16,128,128]{2,1,0:T(8,128)(2,1)} %get-tuple-element.23), channel_id=1, source_target_pairs={{0,32},{32,64},{64,96},{96,0},{1,33},{33,65},{65,97},{97,1},{2,34}... | collective-permute-start | bytes 1572872 | tf_op jit(solution)/shard_map/ppermute | solution.py:401
  36.9 15.2 %collective-permute-start = (bf16[16,128,128]{2,1,0:T(8,128)(2,1)}, bf16[16,128,128]{2,1,0:T(8,128)(2,1)S(1)}, u32[]{:S(2)}, u32[]{:S(2)}) collective-permute-start(bf16[16,128,128]{2,1,0:T(8,128)(2,1)} %get-tuple-element.24), channel_id=1, source_target_pairs={{0,96},{32,0},{64,32},{96,64},{1,97},{33,1},{65,33},{97,65},{2,98}... | collective-permute-start | bytes 1572872 | tf_op jit(solution)/shard_map/ppermute | solution.py:401
  51.2 4.1 %collective-permute-start.6 = (bf16[16,128,128]{2,1,0:T(8,128)(2,1)S(1)}, bf16[16,128,128]{2,1,0:T(8,128)(2,1)}, u32[]{:S(2)}, u32[]{:S(2)}) collective-permute-start(bf16[16,128,128]{2,1,0:T(8,128)(2,1)S(1)} %collective-permute-done.1.refs_8_.refs_6_), channel_id=1, source_target_pairs={{0,1},{1,0},{2,3},{3,2},{4,5},{5,4},{6,7},{7,6},{8,9},{9,8},{10,11... | collective-permute-start | bytes 1572872 | tf_op jit(solution)/shard_map/ppermute | solution.py:414
  52.1 3.2 %collective-permute-start.5 = (bf16[16,128,128]{2,1,0:T(8,128)(2,1)S(1)}, bf16[16,128,128]{2,1,0:T(8,128)(2,1)}, u32[]{:S(2)}, u32[]{:S(2)}) collective-permute-start(bf16[16,128,128]{2,1,0:T(8,128)(2,1)S(1)} %collective-permute-done.refs_3_.refs_1_), channel_id=1, source_target_pairs={{0,1},{1,0},{2,3},{3,2},{4,5},{5,4},{6,7},{7,6},{8,9},{9,8},{10,11... | collective-permute-start | bytes 1572872 | tf_op jit(solution)/shard_map/ppermute | solution.py:414
  52.1 14.3 %collective-permute-start.3 = (bf16[16,128,128]{2,1,0:T(8,128)(2,1)}, bf16[16,128,128]{2,1,0:T(8,128)(2,1)}, u32[]{:S(2)}, u32[]{:S(2)}) collective-permute-start(bf16[16,128,128]{2,1,0:T(8,128)(2,1)} %get-tuple-element.23), channel_id=1, source_target_pairs={{0,96},{32,0},{64,32},{96,64},{1,97},{33,1},{65,33},{97,65},{2,98}... | collective-permute-start | bytes 1572872 | tf_op jit(solution)/shard_map/ppermute | solution.py:401
  54.8 14.8 %collective-permute-start.4 = (bf16[16,128,128]{2,1,0:T(8,128)(2,1)}, bf16[16,128,128]{2,1,0:T(8,128)(2,1)}, u32[]{:S(2)}, u32[]{:S(2)}) collective-permute-start(bf16[16,128,128]{2,1,0:T(8,128)(2,1)} %get-tuple-element.24), channel_id=1, source_target_pairs={{0,32},{32,64},{64,96},{96,0},{1,33},{33,65},{65,97},{97,1},{2,34}... | collective-permute-start | bytes 1572872 | tf_op jit(solution)/shard_map/ppermute | solution.py:401
  54.8 30.8 %collective-permute-start.9 = (bf16[32,144,128]{2,1,0:T(8,128)(2,1)S(1)}, bf16[32,144,128]{2,1,0:T(8,128)(2,1)}, u32[]{:S(2)}, u32[]{:S(2)}) collective-permute-start(bf16[32,144,128]{2,1,0:T(8,128)(2,1)S(1)} %all-to-all-done.refs_0_.refs_3_.q), channel_id=1, source_target_pairs={{0,1},{1,0},{2,3},{3,2},{4,5},{5,4},{6,7},{7,6},{8,9},{9,8},{10,11... | collective-permute-start | bytes 3538952 | tf_op jit(solution)/shard_map/ppermute | solution.py:414
  69.5 12.3 %collective-permute-start.7 = (bf16[16,128,128]{2,1,0:T(8,128)(2,1)S(1)}, bf16[16,128,128]{2,1,0:T(8,128)(2,1)S(1)}, u32[]{:S(2)}, u32[]{:S(2)}) collective-permute-start(bf16[16,128,128]{2,1,0:T(8,128)(2,1)S(1)} %collective-permute-done.refs_3_.refs_1_), channel_id=1, source_target_pairs={{0,96},{32,0},{64,32},{96,64},{1,97},{33,1},{65,33},{97,65},{2,98}... | collective-permute-start | bytes 1572872 | tf_op jit(solution)/shard_map/ppermute | solution.py:401
  69.8 14.0 %collective-permute-start.8 = (bf16[16,128,128]{2,1,0:T(8,128)(2,1)S(1)}, bf16[16,128,128]{2,1,0:T(8,128)(2,1)S(1)}, u32[]{:S(2)}, u32[]{:S(2)}) collective-permute-start(bf16[16,128,128]{2,1,0:T(8,128)(2,1)S(1)} %collective-permute-done.1.refs_8_.refs_6_), channel_id=1, source_target_pairs={{0,32},{32,64},{64,96},{96,0},{1,33},{33,65},{65,97},{97,1},{2,34}... | collective-permute-start | bytes 1572872 | tf_op jit(solution)/shard_map/ppermute | solution.py:401
  71.3 14.3 %collective-permute-start.10 = (bf16[16,128,128]{2,1,0:T(8,128)(2,1)}, bf16[16,128,128]{2,1,0:T(8,128)(2,1)S(1)}, u32[]{:S(2)}, u32[]{:S(2)}) collective-permute-start(bf16[16,128,128]{2,1,0:T(8,128)(2,1)} %collective-permute-done.3.refs_4_.refs_2_), channel_id=1, source_target_pairs={{0,1},{1,0},{2,3},{3,2},{4,5},{5,4},{6,7},{7,6},{8,9},{9,8},{10,11... | collective-permute-start | bytes 1572872 | tf_op jit(solution)/shard_map/ppermute | solution.py:414
  73.0 12.6 %collective-permute-start.13 = (bf16[16,128,128]{2,1,0:T(8,128)(2,1)}, bf16[16,128,128]{2,1,0:T(8,128)(2,1)S(1)}, u32[]{:S(2)}, u32[]{:S(2)}) collective-permute-start(bf16[16,128,128]{2,1,0:T(8,128)(2,1)} %collective-permute-done.4.refs_7_.refs_5_), channel_id=1, source_target_pairs={{0,1},{1,0},{2,3},{3,2},{4,5},{5,4},{6,7},{7,6},{8,9},{9,8},{10,11... | collective-permute-start | bytes 1572872 | tf_op jit(solution)/shard_map/ppermute | solution.py:414
  81.8 3.8 %collective-permute-start.11 = (bf16[16,128,128]{2,1,0:T(8,128)(2,1)S(1)}, bf16[16,128,128]{2,1,0:T(8,128)(2,1)S(1)}, u32[]{:S(2)}, u32[]{:S(2)}) collective-permute-start(bf16[16,128,128]{2,1,0:T(8,128)(2,1)S(1)} %collective-permute-done.7.refs_5_.refs_3_), channel_id=1, source_target_pairs={{0,1},{1,0},{2,3},{3,2},{4,5},{5,4},{6,7},{7,6},{8,9},{9,8},{10,11... | collective-permute-start | bytes 1572872 | tf_op jit(solution)/shard_map/ppermute | solution.py:414
  83.9 3.1 %collective-permute-start.12 = (bf16[16,128,128]{2,1,0:T(8,128)(2,1)S(1)}, bf16[16,128,128]{2,1,0:T(8,128)(2,1)S(1)}, u32[]{:S(2)}, u32[]{:S(2)}) collective-permute-start(bf16[16,128,128]{2,1,0:T(8,128)(2,1)S(1)} %collective-permute-done.8.refs_6_.refs_4_), channel_id=1, source_target_pairs={{0,1},{1,0},{2,3},{3,2},{4,5},{5,4},{6,7},{7,6},{8,9},{9,8},{10,11... | collective-permute-start | bytes 1572872 | tf_op jit(solution)/shard_map/ppermute | solution.py:414
  99.1 9.6 %collective-permute-start.14 = (f32[2,512,128]{2,1,0:T(8,128)S(1)}, f32[2,512,128]{2,1,0:T(8,128)S(1)}, u32[]{:S(2)}, u32[]{:S(2)}) collective-permute-start(f32[2,512,128]{2,1,0:T(8,128)S(1)} %get-tuple-element.29), channel_id=1, source_target_pairs={{0,8},{1,3},{2,10},{3,5},{4,12},{5,7},{6,14},{7,1},{8,16},{9,11},{... | collective-permute-start | bytes 1572872 | tf_op jit(solution)/shard_map/ppermute | solution.py:414
  100.5 8.5 %collective-permute-start.19 = (f32[2,512,128]{2,1,0:T(8,128)S(1)}, f32[2,512,128]{2,1,0:T(8,128)S(1)}, u32[]{:S(2)}, u32[]{:S(2)}) collective-permute-start(f32[2,512,128]{2,1,0:T(8,128)S(1)} %get-tuple-element.33), channel_id=1, source_target_pairs={{0,24},{1,7},{2,26},{3,1},{4,28},{5,3},{6,30},{7,5},{8,0},{9,15},{... | collective-permute-start | bytes 1572872 | tf_op jit(solution)/shard_map/ppermute | solution.py:414
  101.8 12.6 %collective-permute-start.16 = (f32[2,512,128]{2,1,0:T(8,128)S(1)}, f32[2,512,128]{2,1,0:T(8,128)S(1)}, u32[]{:S(2)}, u32[]{:S(2)}) collective-permute-start(f32[2,512,128]{2,1,0:T(8,128)S(1)} %get-tuple-element.30), channel_id=1, source_target_pairs={{0,24},{1,7},{2,26},{3,1},{4,28},{5,3},{6,30},{7,5},{8,0},{9,15},{... | collective-permute-start | bytes 1572872 | tf_op jit(solution)/shard_map/ppermute | solution.py:414
  103.2 11.2 %collective-permute-start.18 = (f32[2,512,128]{2,1,0:T(8,128)S(1)}, f32[2,512,128]{2,1,0:T(8,128)S(1)}, u32[]{:S(2)}, u32[]{:S(2)}) collective-permute-start(f32[2,512,128]{2,1,0:T(8,128)S(1)} %get-tuple-element.31), channel_id=1, source_target_pairs={{0,8},{1,3},{2,10},{3,5},{4,12},{5,7},{6,14},{7,1},{8,16},{9,11},{... | collective-permute-start | bytes 1572872 | tf_op jit(solution)/shard_map/ppermute | solution.py:414
  108.7 11.2 %collective-permute-start.15 = (f32[2,512,128]{2,1,0:T(8,128)S(1)}, f32[2,512,128]{2,1,0:T(8,128)S(1)}, u32[]{:S(2)}, u32[]{:S(2)}) collective-permute-start(f32[2,512,128]{2,1,0:T(8,128)S(1)} %add.99), channel_id=1, source_target_pairs={{0,8},{1,3},{2,10},{3,5},{4,12},{5,7},{6,14},{7,1},{8,16},{9,11},{... | collective-permute-start | bytes 1572872 | tf_op jit(solution)/shard_map/ppermute | solution.py:414
  109.1 11.0 %collective-permute-start.20 = (f32[2,512,128]{2,1,0:T(8,128)S(1)}, f32[2,512,128]{2,1,0:T(8,128)S(1)}, u32[]{:S(2)}, u32[]{:S(2)}) collective-permute-start(f32[2,512,128]{2,1,0:T(8,128)S(1)} %add.108), channel_id=1, source_target_pairs={{0,24},{1,7},{2,26},{3,1},{4,28},{5,3},{6,30},{7,5},{8,0},{9,15},{... | collective-permute-start | bytes 1572872 | tf_op jit(solution)/shard_map/ppermute | solution.py:414
  120.2 7.1 %collective-permute-start.21 = (f32[512,128]{1,0:T(8,128)S(1)}, f32[512,128]{1,0:T(8,128)S(1)}, u32[]{:S(2)}, u32[]{:S(2)}) collective-permute-start(f32[512,128]{1,0:T(8,128)S(1)} %get-tuple-element.43), channel_id=1, source_target_pairs={{0,4},{1,17},{2,6},{3,19},{4,0},{5,21},{6,2},{7,23},{8,12},{9,25},... | collective-permute-start | bytes 786440 | tf_op jit(solution)/shard_map/ppermute | solution.py:414
  123.1 7.3 %collective-permute-start.22 = (f32[512,128]{1,0:T(8,128)S(1)}, f32[512,128]{1,0:T(8,128)S(1)}, u32[]{:S(2)}, u32[]{:S(2)}) collective-permute-start(f32[512,128]{1,0:T(8,128)S(1)} %get-tuple-element.44), channel_id=1, source_target_pairs={{0,6},{1,25},{2,0},{3,27},{4,2},{5,29},{6,4},{7,31},{8,14},{9,1},{... | collective-permute-start | bytes 786440 | tf_op jit(solution)/shard_map/ppermute | solution.py:414
  123.9 6.7 %collective-permute-start.17 = (f32[512,128]{1,0:T(8,128)S(1)}, f32[512,128]{1,0:T(8,128)S(1)}, u32[]{:S(2)}, u32[]{:S(2)}) collective-permute-start(f32[512,128]{1,0:T(8,128)S(1)} %get-tuple-element.45), channel_id=1, source_target_pairs={{0,2},{1,9},{2,4},{3,11},{4,6},{5,13},{6,0},{7,15},{8,10},{9,17},{... | collective-permute-start | bytes 786440 | tf_op jit(solution)/shard_map/ppermute | solution.py:414
  130.7 5.1 %collective-permute-start.23 = (f32[512,128]{1,0:T(8,128)S(1)}, f32[512,128]{1,0:T(8,128)}, u32[]{:S(2)}, u32[]{:S(2)}) collective-permute-start(f32[512,128]{1,0:T(8,128)S(1)} %fusion.6.refs_0_), channel_id=1, source_target_pairs={{0,1},{1,0},{2,3},{3,2},{4,5},{5,4},{6,7},{7,6},{8,9},{9,8},{10,11... | collective-permute-start | bytes 786440 | tf_op jit(solution)/shard_map/ppermute | solution.py:414
  135.8 33.9 %copy-start.1 = (bf16[16,128,128]{2,1,0:T(8,128)(2,1)S(1)}, bf16[16,128,128]{2,1,0:T(8,128)(2,1)}, u32[]{:S(2)}) copy-start(bf16[16,128,128]{2,1,0:T(8,128)(2,1)} %copy-done) | copy-start | bytes 1572868
  135.8 33.9 %copy-start.3 = (bf16[16,128,128]{2,1,0:T(8,128)(2,1)S(1)}, bf16[16,128,128]{2,1,0:T(8,128)(2,1)}, u32[]{:S(2)}) copy-start(bf16[16,128,128]{2,1,0:T(8,128)(2,1)} %copy-done.2) | copy-start | bytes 1572868
  139.4 5.4 %collective-permute-start.26 = (bf16[528,128]{1,0:T(8,128)(2,1)S(1)}, bf16[528,128]{1,0:T(8,128)(2,1)S(1)}, u32[]{:S(2)}, u32[]{:S(2)}) collective-permute-start(bf16[528,128]{1,0:T(8,128)(2,1)S(1)} %softmax_weights.1), channel_id=1, source_target_pairs={{0,8},{1,3},{2,10},{3,5},{4,12},{5,7},{6,14},{7,1},{8,16},{9,11},{... | collective-permute-start | bytes 405512 | tf_op jit(solution)/shard_map/ppermute | solution.py:414
  139.6 6.3 %collective-permute-start.25 = (bf16[528,128]{1,0:T(8,128)(2,1)S(1)}, bf16[528,128]{1,0:T(8,128)(2,1)S(1)}, u32[]{:S(2)}, u32[]{:S(2)}) collective-permute-start(bf16[528,128]{1,0:T(8,128)(2,1)S(1)} %softmax_weights.1), channel_id=1, source_target_pairs={{0,16},{1,5},{2,18},{3,7},{4,20},{5,1},{6,22},{7,3},{8,24},{9,13},... | collective-permute-start | bytes 405512 | tf_op jit(solution)/shard_map/ppermute | solution.py:414
  142.0 4.8 %collective-permute-start.24 = (bf16[528,128]{1,0:T(8,128)(2,1)S(1)}, bf16[528,128]{1,0:T(8,128)(2,1)S(1)}, u32[]{:S(2)}, u32[]{:S(2)}) collective-permute-start(bf16[528,128]{1,0:T(8,128)(2,1)S(1)} %softmax_weights.1), channel_id=1, source_target_pairs={{0,24},{1,7},{2,26},{3,1},{4,28},{5,3},{6,30},{7,5},{8,0},{9,15},{... | collective-permute-start | bytes 405512 | tf_op jit(solution)/shard_map/ppermute | solution.py:414
  146.9 9.0 %collective-permute-start.28 = (bf16[4,528,128]{2,1,0:T(8,128)(2,1)S(1)}, bf16[4,528,128]{2,1,0:T(8,128)(2,1)S(1)}, u32[]{:S(2)}, u32[]{:S(2)}) collective-permute-start(bf16[4,528,128]{2,1,0:T(8,128)(2,1)S(1)} %pad_maximum_fusion.refs_7_), channel_id=1, source_target_pairs={{0,6},{1,25},{2,0},{3,27},{4,2},{5,29},{6,4},{7,31},{8,14},{9,1},{... | collective-permute-start | bytes 1622024 | tf_op jit(solution)/shard_map/ppermute | solution.py:414
  149.6 11.6 %collective-permute-start.27 = (bf16[4,528,128]{2,1,0:T(8,128)(2,1)S(1)}, bf16[4,528,128]{2,1,0:T(8,128)(2,1)S(1)}, u32[]{:S(2)}, u32[]{:S(2)}) collective-permute-start(bf16[4,528,128]{2,1,0:T(8,128)(2,1)S(1)} %pad_maximum_fusion.refs_7_), channel_id=1, source_target_pairs={{0,2},{1,9},{2,4},{3,11},{4,6},{5,13},{6,0},{7,15},{8,10},{9,17},{... | collective-permute-start | bytes 1622024 | tf_op jit(solution)/shard_map/ppermute | solution.py:414
  155.9 9.7 %collective-permute-start.29 = (bf16[4,528,128]{2,1,0:T(8,128)(2,1)S(1)}, bf16[4,528,128]{2,1,0:T(8,128)(2,1)S(1)}, u32[]{:S(2)}, u32[]{:S(2)}) collective-permute-start(bf16[4,528,128]{2,1,0:T(8,128)(2,1)S(1)} %collective-permute-done.28.refs_9_), channel_id=1, source_target_pairs={{0,6},{1,25},{2,0},{3,27},{4,2},{5,29},{6,4},{7,31},{8,14},{9,1},{... | collective-permute-start | bytes 1622024 | tf_op jit(solution)/shard_map/ppermute | solution.py:414
  159.3 8.8 %collective-permute-start.30 = (bf16[4,528,128]{2,1,0:T(8,128)(2,1)S(1)}, bf16[4,528,128]{2,1,0:T(8,128)(2,1)S(1)}, u32[]{:S(2)}, u32[]{:S(2)}) collective-permute-start(bf16[4,528,128]{2,1,0:T(8,128)(2,1)S(1)} %pad_maximum_fusion.refs_7_), channel_id=1, source_target_pairs={{0,1},{1,0},{2,3},{3,2},{4,5},{5,4},{6,7},{7,6},{8,9},{9,8},{10,11... | collective-permute-start | bytes 1622024 | tf_op jit(solution)/shard_map/ppermute | solution.py:414
  161.3 6.9 %collective-permute-start.32 = (bf16[4,528,128]{2,1,0:T(8,128)(2,1)S(1)}, bf16[4,528,128]{2,1,0:T(8,128)(2,1)S(1)}, u32[]{:S(2)}, u32[]{:S(2)}) collective-permute-start(bf16[4,528,128]{2,1,0:T(8,128)(2,1)S(1)} %collective-permute-done.28.refs_9_), channel_id=1, source_target_pairs={{0,1},{1,0},{2,3},{3,2},{4,5},{5,4},{6,7},{7,6},{8,9},{9,8},{10,11... | collective-permute-start | bytes 1622024 | tf_op jit(solution)/shard_map/ppermute | solution.py:414
  161.3 6.9 %collective-permute-start.31 = (bf16[4,528,128]{2,1,0:T(8,128)(2,1)S(1)}, bf16[4,528,128]{2,1,0:T(8,128)(2,1)S(1)}, u32[]{:S(2)}, u32[]{:S(2)}) collective-permute-start(bf16[4,528,128]{2,1,0:T(8,128)(2,1)S(1)} %collective-permute-done.27.refs_8_), channel_id=1, source_target_pairs={{0,1},{1,0},{2,3},{3,2},{4,5},{5,4},{6,7},{7,6},{8,9},{9,8},{10,11... | collective-permute-start | bytes 1622024 | tf_op jit(solution)/shard_map/ppermute | solution.py:414
  165.7 4.0 %collective-permute-start.33 = (bf16[4,528,128]{2,1,0:T(8,128)(2,1)S(1)}, bf16[4,528,128]{2,1,0:T(8,128)(2,1)S(1)}, u32[]{:S(2)}, u32[]{:S(2)}) collective-permute-start(bf16[4,528,128]{2,1,0:T(8,128)(2,1)S(1)} %collective-permute-done.29.refs_10_), channel_id=1, source_target_pairs={{0,1},{1,0},{2,3},{3,2},{4,5},{5,4},{6,7},{7,6},{8,9},{9,8},{10,11... | collective-permute-start | bytes 1622024 | tf_op jit(solution)/shard_map/ppermute | solution.py:414
  190.1 14.7 %collective-permute-start.34 = (bf16[16,128,128]{2,1,0:T(8,128)(2,1)}, bf16[16,128,128]{2,1,0:T(8,128)(2,1)}, u32[]{:S(2)}, u32[]{:S(2)}) collective-permute-start(bf16[16,128,128]{2,1,0:T(8,128)(2,1)} %get-tuple-element.38), channel_id=1, source_target_pairs={{0,32},{32,64},{64,96},{96,0},{1,33},{33,65},{65,97},{97,1},{2,34}... | collective-permute-start | bytes 1572872 | tf_op jit(solution)/shard_map/ppermute | solution.py:401
  190.1 15.9 %collective-permute-start.38 = (bf16[16,128,128]{2,1,0:T(8,128)(2,1)}, bf16[16,128,128]{2,1,0:T(8,128)(2,1)}, u32[]{:S(2)}, u32[]{:S(2)}) collective-permute-start(bf16[16,128,128]{2,1,0:T(8,128)(2,1)} %get-tuple-element.42), channel_id=1, source_target_pairs={{0,96},{32,0},{64,32},{96,64},{1,97},{33,1},{65,33},{97,65},{2,98}... | collective-permute-start | bytes 1572872 | tf_op jit(solution)/shard_map/ppermute | solution.py:401
  192.8 36.2 %all-to-all-start.2 = ((bf16[32,128,128]{2,1,0:T(8,128)(2,1)}), bf16[32,128,128]{2,1,0:T(8,128)(2,1)S(1)}, u32[]{:S(2)}, u32[]{:S(2)}) async-start(bf16[32,128,128]{2,1,0:T(8,128)(2,1)} %copy-done.5), calls=%async_computation.2 | async-start | bytes 2097152 | tf_op jit(solution)/shard_map/all_to_all | solution.py:462
  200.5 14.4 %collective-permute-start.36 = (bf16[16,128,128]{2,1,0:T(8,128)(2,1)}, bf16[16,128,128]{2,1,0:T(8,128)(2,1)S(1)}, u32[]{:S(2)}, u32[]{:S(2)}) collective-permute-start(bf16[16,128,128]{2,1,0:T(8,128)(2,1)} %copy-done.14), channel_id=1, source_target_pairs={{0,96},{32,0},{64,32},{96,64},{1,97},{33,1},{65,33},{97,65},{2,98}... | collective-permute-start | bytes 1572872 | tf_op jit(solution)/shard_map/ppermute | solution.py:401
  200.6 15.5 %collective-permute-start.37 = (bf16[16,128,128]{2,1,0:T(8,128)(2,1)}, bf16[16,128,128]{2,1,0:T(8,128)(2,1)S(1)}, u32[]{:S(2)}, u32[]{:S(2)}) collective-permute-start(bf16[16,128,128]{2,1,0:T(8,128)(2,1)} %copy-done.13), channel_id=1, source_target_pairs={{0,32},{32,64},{64,96},{96,0},{1,33},{33,65},{65,97},{97,1},{2,34}... | collective-permute-start | bytes 1572872 | tf_op jit(solution)/shard_map/ppermute | solution.py:401
  205.9 21.4 %collective-permute-start.35 = (bf16[16,128,128]{2,1,0:T(8,128)(2,1)S(1)}, bf16[16,128,128]{2,1,0:T(8,128)(2,1)S(1)}, u32[]{:S(2)}, u32[]{:S(2)}) collective-permute-start(bf16[16,128,128]{2,1,0:T(8,128)(2,1)S(1)} %add_convert_fusion.1), channel_id=1, source_target_pairs={{0,32},{32,64},{64,96},{96,0},{1,33},{33,65},{65,97},{97,1},{2,34}... | collective-permute-start | bytes 1572872 | tf_op jit(solution)/shard_map/ppermute | solution.py:401
  207.2 20.1 %collective-permute-start.39 = (bf16[16,128,128]{2,1,0:T(8,128)(2,1)S(1)}, bf16[16,128,128]{2,1,0:T(8,128)(2,1)S(1)}, u32[]{:S(2)}, u32[]{:S(2)}) collective-permute-start(bf16[16,128,128]{2,1,0:T(8,128)(2,1)S(1)} %add_convert_fusion), channel_id=1, source_target_pairs={{0,96},{32,0},{64,32},{96,64},{1,97},{33,1},{65,33},{97,65},{2,98}... | collective-permute-start | bytes 1572872 | tf_op jit(solution)/shard_map/ppermute | solution.py:401
  229.0 24.7 %all-to-all-start.3 = ((bf16[32,128,128]{2,1,0:T(8,128)(2,1)}), bf16[32,128,128]{2,1,0:T(8,128)(2,1)S(1)}, u32[]{:S(2)}, u32[]{:S(2)}) async-start(bf16[32,128,128]{2,1,0:T(8,128)(2,1)} %join.1), calls=%async_computation.3 | async-start | bytes 2097152 | tf_op jit(solution)/shard_map/all_to_all | solution.py:462
  (12 other events, 119.9 us)

commit v3 on v2

--- a/solution.py
+++ b/solution.py
@@ -118,70 +118,76 @@
 PIECES = ((0, 32), (32, 16), (48, 16), (64, 16), (80, 16), (96, 16), (112, 16))
 
 
+def place_kernel(*refs, spots):
+    *pieces, out, sems = refs
+    pieces = pieces[len(pieces) - len(spots) :]
+    run_copies(
+        [
+            pltpu.make_async_copy(piece, out.at[first : first + piece.shape[0]], sems.at[n])
+            for n, (piece, first) in enumerate(zip(pieces, spots))
+        ]
+    )
+
+
+def place(whole, pieces, spots):
+    given = tuple(pieces) if whole is None else (whole, *pieces)
+    shape = (4 * 32,) + pieces[0].shape[1:]
+    return pl.pallas_call(
+        functools.partial(place_kernel, spots=spots),
+        in_specs=[ANY] * len(given),
+        out_specs=ANY,
+        out_shape=jax.ShapeDtypeStruct(shape, pieces[0].dtype),
+        scratch_shapes=[pltpu.SemaphoreType.DMA((len(pieces),))],
+        input_output_aliases={} if whole is None else {0: 0},
+        **params(1, 4 * MIB),
+        name="place",
+    )(*given)
+
+
 def chip_at(at, core, lead, other):
     rx = jnp.where(core == 0, lead, other)
     ry = jnp.where(core == 0, other, lead)
     return ((at[1] + rx) % 4) * 4 + (at[2] + ry) % 4
 
 
-def score_kernel(ids, own, at, *refs):
-    q, pieces, outs = refs[:2], refs[2:16], refs[16:23]
-    qv, pv, sv, sems = refs[23:]
+def score_kernel(ids, own, at, q_own, q_sib, p_own, p_sib, *refs):
+    outs, sv = refs[:7], refs[7]
     core = at[0]
-    moves = [(q[n].at[:, 0:BLK, :], qv.at[n]) for n in range(2)]
-    for n, piece in enumerate(pieces):
-        first, size = PIECES[n % 7]
-        moves.append((piece, pv.at[n // 7, first : first + size]))
-    run_copies([pltpu.make_async_copy(*move, sems.at[n]) for n, move in enumerate(moves)])
-
-    stores = []
-    for half in range(2):
-
-        @pl.loop(0, PART // 2 // STEP)
-        def _(step):
-            for u in range(STEP):
-                n = half * PART // 2 + step * STEP + u
-                t = PART * core + n
-                left = jnp.concatenate([qv[0, own[t]], qv[1, own[t]]], axis=1)
-                right = jnp.concatenate([pv[0, ids[t]], pv[1, ids[t]]], axis=1)
-                tile = lax.dot_general(
-                    left, right, (((1,), (1,)), ((), ())), preferred_element_type=jnp.float32
-                )
-                where = pl.ds(pl.multiple_of(8 * n, 8), 8)
-                sv[:, where, :] = tile.reshape(BLK // 8, 8, 128)
-
-        rows = slice(half * ROWS // 2, (half + 1) * ROWS // 2)
-        for lead in (2, 1, 3, 0):
-            for other in range(4):
+    spots = [
+        (lead, other, chip_at(at, core, lead, other)) for lead in range(4) for other in range(4)
+    ]
+
+    @pl.loop(0, PART // STEP)
+    def _(step):
+        for u in range(STEP):
+            n = step * STEP + u
+            here, there = own[PART * core + n], ids[PART * core + n]
+            left = jnp.concatenate([q_own[here, 0:BLK, :], q_sib[here, 0:BLK, :]], axis=1)
+            right = jnp.concatenate([p_own[there], p_sib[there]], axis=1)
+            tile = lax.dot_general(
+                left, right, (((1,), (1,)), ((), ())), preferred_element_type=jnp.float32
+            )
+            sv[u] = tile.reshape(BLK // 8, 8, 128)
+        for u in range(STEP):
+            where = pl.ds(pl.multiple_of(8 * (step * STEP + u), 8), 8)
+            for lead, other, chip in spots:
                 if lead == 0:
-                    target = outs[6].at[other, rows, :]
+                    outs[6][other, where, :] = sv[u, chip]
                 else:
-                    target = outs[2 * lead - 2 + other // 2].at[other % 2, rows, :]
-                source = sv.at[chip_at(at, core, lead, other), rows, :]
-                sem = sems.at[16 + 16 * half + 4 * lead + other]
-                stores.append(pltpu.make_async_copy(source, target, sem))
-                stores[-1].start()
-    for copy in stores:
-        copy.wait()
-
-
-def partial_scores(ids, own, at, q, pieces, given):
-    nblk = q[0].shape[0]
+                    outs[2 * lead - 2 + other // 2][other % 2, where, :] = sv[u, chip]
+
+
+def partial_scores(ids, own, at, q, p):
     shapes = [(2, ROWS, 128)] * 6 + [(4, ROWS, 128)]
     return pl.pallas_call(
         score_kernel,
-        in_specs=[SMEM] * 3 + [ANY] * 16,
-        out_specs=[ANY] * 7,
+        in_specs=[SMEM] * 3 + [VMEM] * 4,
+        out_specs=[VMEM] * 7,
         out_shape=[jax.ShapeDtypeStruct(s, jnp.float32) for s in shapes],
-        scratch_shapes=[
-            pltpu.VMEM((2, nblk, BLK, 128), jnp.bfloat16),
-            pltpu.VMEM((2, 4 * nblk, BLK, 128), jnp.bfloat16),
-            pltpu.VMEM((BLK // 8, ROWS, 128), jnp.float32),
-            pltpu.SemaphoreType.DMA((48,)),
-        ],
-        **params(17, 32 * MIB),
+        scratch_shapes=[pltpu.VMEM((STEP, BLK // 8, 8, 128), jnp.float32)],
+        **params(17, 20 * MIB),
         name="partial_scores",
-    )(ids, own, at, *q, *pieces, *given)
+    )(ids, own, at, *q, *p)
 
 
 def softmax_kernel(at, *refs, scale):
@@ -257,20 +263,10 @@
     )(at, *terms, lists, q)
 
 
-def grad_kernel(ids, own, at, q, *refs):
-    pieces, parts, outs, gq, loss = refs[:7], refs[7:15], refs[15:22], *refs[22:24]
-    wv, qv, pv, gq_sum, gp_sum, sems = refs[24:]
+def grad_kernel(ids, own, at, q, p, *refs):
+    parts, outs, gq, loss = refs[:8], refs[8:15], *refs[15:17]
+    wv, gq_sum, gp_sum = refs[17:]
     core = at[0]
-    moves = [(q.at[:, 0:BLK, :], qv)]
-    moves += [(pieces[n], pv.at[first : first + size]) for n, (first, size) in enumerate(PIECES)]
-    for n, piece in enumerate(parts):
-        side = jnp.where(core == n // 4, 0, 1)
-        for lead in range(4):
-            chip = chip_at(at, side, lead, (0, 3, 1, 2)[n % 4])
-            moves.append((piece.at[lead], wv.at[side, chip]))
-    loads = [pltpu.make_async_copy(*move, sems.at[n]) for n, move in enumerate(moves)]
-    for copy in loads:
-        copy.start()
 
     @pl.loop(0, gq_sum.shape[0])
     def _(n):
@@ -278,75 +274,68 @@
         for m in range(4):
             gp_sum[4 * n + m] = jnp.zeros((BLK, 128), jnp.float32)
 
+    loss[...] = jnp.zeros(loss.shape, jnp.float32)
+    line = lax.broadcasted_iota(jnp.int32, (TAIL, 128), 0) // 3
+    mine = line == at[3] // 16
     for n in range(2):
-        for copy in loads[24 * n : 24 + 16 * n]:
-            copy.wait()
         side = jnp.where(core == n, 0, 1)
+        spots = []
+        for m in range(4):
+            for lead in range(4):
+                chip = chip_at(at, side, lead, (0, 3, 1, 2)[m])
+                spots.append((4 * n + m, lead, chip))
+                tail = parts[4 * n + m][lead, ROWS:, :].astype(jnp.float32)
+                loss[pl.ds(chip, 1), :] += jnp.sum(
+                    jnp.where(mine, tail, 0.0), axis=0, keepdims=True
+                )
 
         @pl.loop(0, PART // STEP)
         def _(step):
             for v in range(STEP // 2):
                 where = pl.ds(pl.multiple_of(8 * STEP * step + 16 * v, 16), 16)
-                two = wv[side, :, where, :].astype(jnp.float32)
+                for m, lead, chip in spots:
+                    wv[v, chip] = parts[m][lead, where, :]
+                two = wv[v].astype(jnp.float32)
                 for o in range(2):
                     t = side * PART + step * STEP + 2 * v + o
                     here, there = own[t], ids[t]
                     tile = two[:, 8 * o : 8 * o + 8, :].reshape(BLK, 128).astype(jnp.bfloat16)
-                    gq_sum[here] += jnp.dot(tile, pv[there], preferred_element_type=jnp.float32)
+                    gq_sum[here] += jnp.dot(tile, p[there], preferred_element_type=jnp.float32)
                     gp_sum[there] += lax.dot_general(
-                        tile, qv[here], (((0,), (0,)), ((), ())), preferred_element_type=jnp.float32
+                        tile,
+                        q[here, 0:BLK, :],
+                        (((0,), (0,)), ((), ())),
+                        preferred_element_type=jnp.float32,
                     )
 
-    stores = []
-
-    def send(source, target):
-        stores.append(pltpu.make_async_copy(source, target, sems.at[len(stores)]))
-        stores[-1].start()
-
-    for m in (3, 4, 1, 2, 5, 6, 0):
-        first, size = PIECES[m]
-
-        @pl.loop(0, size // 4)
-        def _(n):
-            for e in range(4):
-                pv[first + 4 * n + e] = gp_sum[first + 4 * n + e].astype(jnp.bfloat16)
-
-        send(pv.at[first : first + size], outs[m])
-
-    @pl.loop(0, gq_sum.shape[0] // 4)
+    @pl.loop(0, 16)
     def _(n):
-        for e in range(4):
-            qv[4 * n + e] = gq_sum[4 * n + e].astype(jnp.bfloat16)
-
-    send(qv, gq)
-    tails = wv[0, :, ROWS:, :].astype(jnp.float32) + wv[1, :, ROWS:, :].astype(jnp.float32)
-    line = lax.broadcasted_iota(jnp.int32, tails.shape, 1) // 3
-    mine = jnp.sum(jnp.where(line == at[3] // 16, tails, 0.0), axis=1)
-    loss[...] = pltpu.roll(mine, (128 - 8 * (at[3] % 16)) % 128, 1)
-    for copy in stores:
-        copy.wait()
-
-
-def gradients(ids, own, at, q, pieces, parts):
+        for m, (first, size) in enumerate(PIECES):
+            for e in range(size // 16):
+                outs[m][16 * e + n] = gp_sum[first + 16 * e + n].astype(jnp.bfloat16)
+        for e in range(2):
+            gq[16 * e + n] = gq_sum[16 * e + n].astype(jnp.bfloat16)
+
+    loss[...] = pltpu.roll(loss[...], (128 - 8 * (at[3] % 16)) % 128, 1)
+
+
+def gradients(ids, own, at, q, p, parts):
     nblk = q.shape[0]
     shapes = [(size, BLK, 128) for _, size in PIECES] + [(nblk, BLK, 128)]
     return pl.pallas_call(
         grad_kernel,
-        in_specs=[SMEM] * 3 + [ANY] * 16,
-        out_specs=[ANY] * 8 + [VMEM],
+        in_specs=[SMEM] * 3 + [VMEM] * 10,
+        out_specs=[VMEM] * 9,
         out_shape=[jax.ShapeDtypeStruct(s, jnp.bfloat16) for s in shapes]
         + [jax.ShapeDtypeStruct((BLK // 8, 128), jnp.float32)],
         scratch_shapes=[
-            pltpu.VMEM((2, BLK // 8, ROWS + TAIL, 128), jnp.bfloat16),
-            pltpu.VMEM((nblk, BLK, 128), jnp.bfloat16),
-            pltpu.VMEM((4 * nblk, BLK, 128), jnp.bfloat16),
+            pltpu.VMEM((STEP // 2, BLK // 8, 16, 128), jnp.bfloat16),
             pltpu.VMEM((nblk, BLK, 128), jnp.float32),
             pltpu.VMEM((4 * nblk, BLK, 128), jnp.float32),
-            pltpu.SemaphoreType.DMA((40,)),
         ],
-        **params(23, 32 * MIB),
+        **params(27, 32 * MIB),
         name="gradients",
-    )(ids, own, at, q, *pieces, *parts)
+    )(ids, own, at, q, p, *parts)
 
 
 def join_kernel(*refs):
@@ -463,14 +452,16 @@
 
     up, down, flip = along("z", 1), along("z", -1), along("core", 1)
     p_own = exchange(by_features(passages))
-    low, high = p_own[: ndev // 2], p_own[ndev // 2 :]
-    above0, below1, given0 = down(low), up(high), flip(p_own)
-    low, high, *_ = lax.optimization_barrier((low, high, above0, below1, given0))
-    above1, below0, given1, given2 = down(high), up(low), flip(above0), flip(below1)
-    last0, last1, *_ = lax.optimization_barrier((above0, below1, above1, below0, given1, given2))
-    far0, far1 = down(last0), up(last1)
-    pieces = [p_own, above0, above1, far0, far1, below0, below1]
-    given = [given0, given1, flip(above1), flip(far0), flip(far1), flip(below0), given2]
+    above, below, given = down(p_own), up(p_own), flip(p_own)
+    mine, theirs = place(None, [p_own], [0]), place(None, [given], [0])
+    low, high = above[: ndev // 2], below[ndev // 2 :]
+    low, high, theirs = lax.optimization_barrier((low, high, theirs))
+    far = [down(low), up(high)]
+    near = [above, below]
+    mine = place(mine, near, [32, 96])
+    theirs = place(theirs, [flip(v) for v in near], [32, 96])
+    mine = place(mine, far, [64, 80])
+    theirs = place(theirs, [flip(v) for v in far], [64, 80])
     q_own = exchange(by_features(queries, positives.reshape(1, BLK)))
     q = [q_own, flip(q_own)]
 
@@ -488,9 +479,9 @@
     spare = jnp.full((128 - ndev,), 2 * PAIRS, jnp.int32)
     lists = jnp.stack([jnp.concatenate([v, spare]) for v in (ends, starts)] * 4)
 
-    scores = scatter_scores(partial_scores(ids, own, at, q, pieces, given))
+    scores = scatter_scores(partial_scores(ids, own, at, q, (mine, theirs)))
     weights = softmax_weights(at, (scores, flip(scores)), lists, q_own, width ** (-0.5))
-    *g, gq, lines = gradients(ids, own, at, q_own, pieces, gather_weights(weights))
+    *g, gq, lines = gradients(ids, own, at, q_own, mine, gather_weights(weights))
 
     low, high = ring_terms("z", g[1:3], g[3:5], g[5:7])
     q_rows = by_rows(exchange(gq))

time: 257 us -> 244 us (0.949)
  blocking collectives: 25.5 us -> 0 us
  waiting for transfers between devices: 105 us -> 120 us
  Pallas kernels: 41.9 us -> 33.6 us
  starting transfers between devices: 70.5 us -> 73.8 us
    all_to_all x3 -> x4, waiting for transfers between devices: 13.5 us -> 41.5 us  [exchange(): return lax.all_to_all(v, 'dev', 0, 0, tiled=True)]
    all_to_all x1 -> x0, blocking collectives: 25.5 us -> none  [exchange(): return lax.all_to_all(v, 'dev', 0, 0, tiled=True)]
    ppermute x12 -> x10, waiting for transfers between devices: 55.2 us -> 41.6 us  [along(): return lambda v: lax.ppermute(v, 'grp', perm)]
    pallas_call x2 -> x8, Pallas kernels: 27.4 us -> 19.3 us  [the longest x1 9.11 us: gradients(): pl.pallas_call(grad_kernel, in_specs=[SMEM] * 3 + [VMEM] * 10, out_specs=...]
    all_to_all x3 -> x4, starting transfers between devices: 19.5 us -> 25.7 us  [exchange(): return lax.all_to_all(v, 'dev', 0, 0, tiled=True)]
    ppermute x12 -> x10, starting transfers between devices: 14.9 us -> 10.4 us  [along(): return lambda v: lax.ppermute(v, 'grp', perm)]
    unnamed x35 -> x17, local copies, waits for them, and re-layouts: 5.21 us -> 7.35 us
    ppermute x28 -> x26, starting transfers between devices: 36.1 us -> 37.7 us  [along(): return lambda v: lax.ppermute(v, 'dev', perm)]
  transfers between devices with their start and end apart: 43 -> 40, of which waited for: 23 -> 23; matrix products, arithmetic and copies ran while one was open for 3% -> 3% of each run, Pallas kernels for 2% -> 5%
where the time goes in v3:
time: 244 us; the launch traced here: 243 us
  waiting for transfers between devices  120 us (49%)
  starting transfers between devices  73.8 us (30%)
  Pallas kernels  33.6 us (14%)
  local copies, waits for them, and re-layouts  10.9 us (4%)
  other arithmetic  3.36 us (1%)
    ppermute x10, waiting for transfers between devices, along(): return lambda v: lax.ppermute(v, 'grp', perm)  41.6 us
    all_to_all x4, waiting for transfers between devices, exchange(): return lax.all_to_all(v, 'dev', 0, 0, tiled=True)  41.5 us
    ppermute x26, starting transfers between devices, along(): return lambda v: lax.ppermute(v, 'dev', perm)  37.7 us
    ppermute x26, waiting for transfers between devices, along(): return lambda v: lax.ppermute(v, 'dev', perm)  37.2 us
    all_to_all x4, starting transfers between devices, exchange(): return lax.all_to_all(v, 'dev', 0, 0, tiled=True)  25.7 us
    ppermute x10, starting transfers between devices, along(): return lambda v: lax.ppermute(v, 'grp', perm)  10.4 us
    pallas_call x1, Pallas kernels, gradients(): pl.pallas_call(grad_kernel, in_specs=[SMEM] * 3 + [VMEM] * 10, out_specs=...  9.11 us
    unnamed x17, local copies, waits for them, and re-layouts  7.35 us
  transfers between devices with their start and end apart: 40, of which 23 were waited for; matrix products, arithmetic and copies ran while one was open for 3% of the time, Pallas kernels for 5%

profile of v3, /device:TPU:1, one launch (start us, length us, event | category | flops | bytes accessed | tf_op | source)
XLA Modules:
  0.0 243.1 jit_solution(13196011578903000435)
XLA Ops:
  0.6 2.3 pack.3
  3.0 8.6 %all-to-all-start.1 = ((bf16[32,128,128]{2,1,0:T(8,128)(2,1)}), bf16[32,128,128]{2,1,0:T(8,128)(2,1)S(1)}, u32[]{:S(2)}, u32[]{:S(2)}) async-start(bf16[32,128,128]{2,1,0:T(8,128)(2,1)} %pack.3), calls=%async_computation.1 | async-start | bytes 2097152 | tf_op jit(solution)/shard_map/all_to_all | solution.py:451
  14.5 14.0 %all-to-all-done.1.refs_0_ = bf16[32,128,128]{2,1,0:T(8,128)(2,1)S(1)} async-done(((bf16[32,128,128]{2,1,0:T(8,128)(2,1)}), bf16[32,128,128]{2,1,0:T(8,128)(2,1)S(1)}, u32[]{:S(2)}, u32[]{:S(2)}) %all-to-all-start.1) | async-done | bytes 1048608 | tf_op jit(solution)/shard_map/all_to_all | solution.py:451
  28.5 4.0 %all-to-all-start = ((bf16[32,144,128]{2,1,0:T(8,128)(2,1)}), bf16[32,144,128]{2,1,0:T(8,128)(2,1)S(1)}, u32[]{:S(2)}, u32[]{:S(2)}) async-start(bf16[32,144,128]{2,1,0:T(8,128)(2,1)} %pack.2), calls=%async_computation | async-start | bytes 2359296 | tf_op jit(solution)/shard_map/all_to_all | solution.py:451
  32.5 3.8 %collective-permute-start = (bf16[32,128,128]{2,1,0:T(8,128)(2,1)S(1)}, bf16[32,128,128]{2,1,0:T(8,128)(2,1)S(1)}, u32[]{:S(2)}, u32[]{:S(2)}) collective-permute-start(bf16[32,128,128]{2,1,0:T(8,128)(2,1)S(1)} %all-to-all-done.1.refs_0_), channel_id=1, source_target_pairs={{0,96},{32,0},{64,32},{96,64},{1,97},{33,1},{65,33},{97,65},{2,98}... | collective-permute-start | bytes 3145736 | tf_op jit(solution)/shard_map/ppermute | solution.py:390
  36.8 14.0 %all-to-all-done.q_own.refs_3_.q = bf16[32,144,128]{2,1,0:T(8,128)(2,1)S(1)} async-done(((bf16[32,144,128]{2,1,0:T(8,128)(2,1)}), bf16[32,144,128]{2,1,0:T(8,128)(2,1)S(1)}, u32[]{:S(2)}, u32[]{:S(2)}) %all-to-all-start) | async-done | bytes 1179680 | tf_op jit(solution)/shard_map/all_to_all | solution.py:451
  51.1 7.5 %collective-permute-done.refs_1_ = bf16[32,128,128]{2,1,0:T(8,128)(2,1)S(1)} collective-permute-done((bf16[32,128,128]{2,1,0:T(8,128)(2,1)S(1)}, bf16[32,128,128]{2,1,0:T(8,128)(2,1)S(1)}, u32[]{:S(2)}, u32[]{:S(2)}) %collective-permute-start) | collective-permute-done | bytes 1048608 | tf_op jit(solution)/shard_map/ppermute | solution.py:390
  59.4 2.4 collective-permute-done.1.refs_2_
  61.8 1.9 slice.61
  65.0 2.0 copy-done.2
  68.4 1.9 collective-permute-start.6
  71.0 8.3 %collective-permute-done.3.refs_1_ = bf16[16,128,128]{2,1,0:T(8,128)(2,1)} collective-permute-done((bf16[16,128,128]{2,1,0:T(8,128)(2,1)}, bf16[16,128,128]{2,1,0:T(8,128)(2,1)}, u32[]{:S(2)}, u32[]{:S(2)}) %collective-permute-start.3) | collective-permute-done | bytes 524320 | tf_op jit(solution)/shard_map/ppermute | solution.py:390
  79.3 2.3 collective-permute-start.8
  81.6 2.2 collective-permute-start.9
  88.4 1.6 place.10.refs_0_
  90.2 4.4 %partial_scores.1 = (f32[2,512,128]{2,1,0:T(8,128)S(1)}, f32[2,512,128]{2,1,0:T(8,128)S(1)}, f32[2,512,128]{2,1,0:T(8,128)S(1)}, f32[2,512,128]{2,1,0:T(8,128)S(...) custom-call(s32[128]{0:T(128)S(1)} %and_select_fusion.ids, ...), custom_call_target="tpu_custom_call" | custom-call | bytes 20971520 | tf_op jit(solution)/shard_map/partial_scores/pallas_call | solution.py:182
  98.8 5.4 %collective-permute-done.10 = f32[2,512,128]{2,1,0:T(8,128)S(1)} collective-permute-done((f32[2,512,128]{2,1,0:T(8,128)S(1)}, f32[2,512,128]{2,1,0:T(8,128)S(1)}, u32[]{:S(2)}, u32[]{:S(2)}) %collective-permute-start.10) | collective-permute-done | bytes 524320 | tf_op jit(solution)/shard_map/ppermute | solution.py:403
  104.5 2.7 %collective-permute-start.16 = (f32[2,512,128]{2,1,0:T(8,128)S(1)}, f32[2,512,128]{2,1,0:T(8,128)S(1)}, u32[]{:S(2)}, u32[]{:S(2)}) collective-permute-start(f32[2,512,128]{2,1,0:T(8,128)S(1)} %add.108), channel_id=1, source_target_pairs={{0,24},{1,7},{2,26},{3,1},{4,28},{5,3},{6,30},{7,5},{8,0},{9,15},{... | collective-permute-start | bytes 1572872 | tf_op jit(solution)/shard_map/ppermute | solution.py:403
  107.2 2.7 %collective-permute-done.12 = f32[2,512,128]{2,1,0:T(8,128)S(1)} collective-permute-done((f32[2,512,128]{2,1,0:T(8,128)S(1)}, f32[2,512,128]{2,1,0:T(8,128)S(1)}, u32[]{:S(2)}, u32[]{:S(2)}) %collective-permute-start.12) | collective-permute-done | bytes 524320 | tf_op jit(solution)/shard_map/ppermute | solution.py:403
  109.9 5.6 %collective-permute-done.11 = f32[2,512,128]{2,1,0:T(8,128)S(1)} collective-permute-done((f32[2,512,128]{2,1,0:T(8,128)S(1)}, f32[2,512,128]{2,1,0:T(8,128)S(1)}, u32[]{:S(2)}, u32[]{:S(2)}) %collective-permute-start.11) | collective-permute-done | bytes 524320 | tf_op jit(solution)/shard_map/ppermute | solution.py:403
  116.9 2.5 %collective-permute-start.17 = (f32[512,128]{1,0:T(8,128)S(1)}, f32[512,128]{1,0:T(8,128)S(1)}, u32[]{:S(2)}, u32[]{:S(2)}) collective-permute-start(f32[512,128]{1,0:T(8,128)S(1)} %get-tuple-element.41), channel_id=1, source_target_pairs={{0,4},{1,17},{2,6},{3,19},{4,0},{5,21},{6,2},{7,23},{8,12},{9,25},... | collective-permute-start | bytes 786440 | tf_op jit(solution)/shard_map/ppermute | solution.py:403
  120.5 2.0 collective-permute-done.13
  122.5 3.8 %collective-permute-done.17 = f32[512,128]{1,0:T(8,128)S(1)} collective-permute-done((f32[512,128]{1,0:T(8,128)S(1)}, f32[512,128]{1,0:T(8,128)S(1)}, u32[]{:S(2)}, u32[]{:S(2)}) %collective-permute-start.17) | collective-permute-done | bytes 262176 | tf_op jit(solution)/shard_map/ppermute | solution.py:403
  126.4 2.0 collective-permute-start.19
  129.6 2.6 %softmax_weights.1 = bf16[528,128]{1,0:T(8,128)(2,1)S(1)} custom-call(s32[5]{0:T(128)S(1)} %stack.53.at, f32[512,128]{1,0:T(8,128)S(1)} %fusion.6.refs_0_, f32[512,128]{1,0:T(8,128)S(1)} %collective-permute-done.19.refs_1_, s32[8,128]{1,0:T(8,128)S(1)} %stack.56.refs_2_, bf16[32,144,128]{2,1,0:T(8,128)(2,1)S(1)} %all-to-all-done.q_own.refs_3_.q), custom_call_target="tpu_custom_call" | custom-call | bytes 8388608 | tf_op jit(solution)/shard_map/softmax_weights/pallas_call | solution.py:250
  132.2 2.6 %collective-permute-start.20 = (bf16[528,128]{1,0:T(8,128)(2,1)S(1)}, bf16[528,128]{1,0:T(8,128)(2,1)S(1)}, u32[]{:S(2)}, u32[]{:S(2)}) collective-permute-start(bf16[528,128]{1,0:T(8,128)(2,1)S(1)} %softmax_weights.1), channel_id=1, source_target_pairs={{0,24},{1,7},{2,26},{3,1},{4,28},{5,3},{6,30},{7,5},{8,0},{9,15},{... | collective-permute-start | bytes 405512 | tf_op jit(solution)/shard_map/ppermute | solution.py:403
  136.0 2.2 collective-permute-done.20
  138.2 2.0 collective-permute-done.21
  140.2 1.7 collective-permute-done.22
  142.0 2.4 collective-permute-start.24
  144.4 6.3 %collective-permute-done.24.refs_2_ = bf16[4,528,128]{2,1,0:T(8,128)(2,1)S(1)} collective-permute-done((bf16[4,528,128]{2,1,0:T(8,128)(2,1)S(1)}, bf16[4,528,128]{2,1,0:T(8,128)(2,1)S(1)}, u32[]{:S(2)}, u32[]{:S(2)}) %collective-permute-start.24) | collective-permute-done | bytes 540704 | tf_op jit(solution)/shard_map/ppermute | solution.py:403
  150.7 3.4 %collective-permute-start.25 = (bf16[4,528,128]{2,1,0:T(8,128)(2,1)S(1)}, bf16[4,528,128]{2,1,0:T(8,128)(2,1)S(1)}, u32[]{:S(2)}, u32[]{:S(2)}) collective-permute-start(bf16[4,528,128]{2,1,0:T(8,128)(2,1)S(1)} %collective-permute-done.24.refs_2_), channel_id=1, source_target_pairs={{0,6},{1,25},{2,0},{3,27},{4,2},{5,29},{6,4},{7,31},{8,14},{9,1},{... | collective-permute-start | bytes 1622024 | tf_op jit(solution)/shard_map/ppermute | solution.py:403
  154.1 2.9 %collective-permute-start.26 = (bf16[4,528,128]{2,1,0:T(8,128)(2,1)S(1)}, bf16[4,528,128]{2,1,0:T(8,128)(2,1)S(1)}, u32[]{:S(2)}, u32[]{:S(2)}) collective-permute-start(bf16[4,528,128]{2,1,0:T(8,128)(2,1)S(1)} %pad_maximum_fusion.refs_0_), channel_id=1, source_target_pairs={{0,1},{1,0},{2,3},{3,2},{4,5},{5,4},{6,7},{7,6},{8,9},{9,8},{10,11... | collective-permute-start | bytes 1622024 | tf_op jit(solution)/shard_map/ppermute | solution.py:403
  157.5 2.8 %collective-permute-done.25.refs_3_ = bf16[4,528,128]{2,1,0:T(8,128)(2,1)S(1)} collective-permute-done((bf16[4,528,128]{2,1,0:T(8,128)(2,1)S(1)}, bf16[4,528,128]{2,1,0:T(8,128)(2,1)S(1)}, u32[]{:S(2)}, u32[]{:S(2)}) %collective-permute-start.25) | collective-permute-done | bytes 540704 | tf_op jit(solution)/shard_map/ppermute | solution.py:403
  160.4 3.5 %collective-permute-start.29 = (bf16[4,528,128]{2,1,0:T(8,128)(2,1)S(1)}, bf16[4,528,128]{2,1,0:T(8,128)(2,1)S(1)}, u32[]{:S(2)}, u32[]{:S(2)}) collective-permute-start(bf16[4,528,128]{2,1,0:T(8,128)(2,1)S(1)} %collective-permute-done.25.refs_3_), channel_id=1, source_target_pairs={{0,1},{1,0},{2,3},{3,2},{4,5},{5,4},{6,7},{7,6},{8,9},{9,8},{10,11... | collective-permute-start | bytes 1622024 | tf_op jit(solution)/shard_map/ppermute | solution.py:403
  165.5 2.2 copy-done.1
  167.6 9.1 %gradients.1 = (bf16[32,128,128]{2,1,0:T(8,128)(2,1)S(1)}, bf16[16,128,128]{2,1,0:T(8,128)(2,1)S(1)}, bf16[16,128,128]{2,1,0:T(8,128)(2,1)}, bf16[16,128,128]{2,...) custom-call(s32[128]{0:T(128)S(1)} %and_select_fusion.ids, ...), custom_call_target="tpu_custom_call" | custom-call | bytes 33554432 | tf_op jit(solution)/shard_map/gradients/pallas_call | solution.py:325
  178.2 1.7 collective-permute-start.32
  179.9 6.5 %all-to-all-start.2 = ((bf16[32,128,128]{2,1,0:T(8,128)(2,1)}), bf16[32,128,128]{2,1,0:T(8,128)(2,1)S(1)}, u32[]{:S(2)}, u32[]{:S(2)}) async-start(bf16[32,128,128]{2,1,0:T(8,128)(2,1)} %get-tuple-element.33), calls=%async_computation.2 | async-start | bytes 2097152 | tf_op jit(solution)/shard_map/all_to_all | solution.py:451
  186.4 3.8 %collective-permute-done.34 = bf16[16,128,128]{2,1,0:T(8,128)(2,1)} collective-permute-done((bf16[16,128,128]{2,1,0:T(8,128)(2,1)}, bf16[16,128,128]{2,1,0:T(8,128)(2,1)}, u32[]{:S(2)}, u32[]{:S(2)}) %collective-permute-start.34) | collective-permute-done | bytes 524320 | tf_op jit(solution)/shard_map/ppermute | solution.py:390
  191.4 1.8 collective-permute-start.35
  194.5 7.0 %collective-permute-done.32.refs_2_ = bf16[16,128,128]{2,1,0:T(8,128)(2,1)} collective-permute-done((bf16[16,128,128]{2,1,0:T(8,128)(2,1)}, bf16[16,128,128]{2,1,0:T(8,128)(2,1)}, u32[]{:S(2)}, u32[]{:S(2)}) %collective-permute-start.32) | collective-permute-done | bytes 524320 | tf_op jit(solution)/shard_map/ppermute | solution.py:390
  202.9 9.7 %collective-permute-done.35.refs_4_ = bf16[16,128,128]{2,1,0:T(8,128)(2,1)S(1)} collective-permute-done((bf16[16,128,128]{2,1,0:T(8,128)(2,1)S(1)}, bf16[16,128,128]{2,1,0:T(8,128)(2,1)S(1)}, u32[]{:S(2)}, u32[]{:S(2)}) %collective-permute-start.35) | collective-permute-done | bytes 524320 | tf_op jit(solution)/shard_map/ppermute | solution.py:390
  214.0 2.5 %join.1 = bf16[32,128,128]{2,1,0:T(8,128)(2,1)} custom-call(bf16[32,128,128]{2,1,0:T(8,128)(2,1)S(1)} %get-tuple-element.34.refs_0_, bf16[16,128,128]{2,1,0:T(8,128)(2,1)S(1)} %collective-permute-done.31.refs_1_, bf16[16,128,128]{2,1,0:T(8,128)(2,1)} %collective-permute-done.32.refs_2_, bf16[16,128,128]{2,1,0:T(8,128)(2,1)} %collective-permute-done.33.refs_3_, ...), custom_call_target="tpu_custom_call" | custom-call | bytes 8388608 | tf_op jit(solution)/shard_map/join/pallas_call | solution.py:370
  216.5 6.7 %all-to-all-start.3 = ((bf16[32,128,128]{2,1,0:T(8,128)(2,1)}), bf16[32,128,128]{2,1,0:T(8,128)(2,1)S(1)}, u32[]{:S(2)}, u32[]{:S(2)}) async-start(bf16[32,128,128]{2,1,0:T(8,128)(2,1)} %join.1), calls=%async_computation.3 | async-start | bytes 2097152 | tf_op jit(solution)/shard_map/all_to_all | solution.py:451
  223.9 2.8 %unpack.2 = f32[128,4096]{1,0:T(8,128)} custom-call(bf16[32,128,128]{2,1,0:T(8,128)(2,1)S(1)} %all-to-all-done.2.x), custom_call_target="tpu_custom_call" | custom-call | bytes 8388608 | tf_op jit(solution)/shard_map/unpack/pallas_call | solution.py:103
  226.7 13.5 %all-to-all-done.3.x = bf16[32,128,128]{2,1,0:T(8,128)(2,1)S(1)} async-done(((bf16[32,128,128]{2,1,0:T(8,128)(2,1)}), bf16[32,128,128]{2,1,0:T(8,128)(2,1)S(1)}, u32[]{:S(2)}, u32[]{:S(2)}) %all-to-all-start.3) | async-done | bytes 1048608 | tf_op jit(solution)/shard_map/all_to_all | solution.py:451
  240.2 2.8 %unpack.3 = f32[128,4096]{1,0:T(8,128)} custom-call(bf16[32,128,128]{2,1,0:T(8,128)(2,1)S(1)} %all-to-all-done.3.x), custom_call_target="tpu_custom_call" | custom-call | bytes 8388608 | tf_op jit(solution)/shard_map/unpack/pallas_call | solution.py:103
  (86 shorter events, 31.4 us)
Async XLA Ops:
  0.6 11.0 %copy-start.5 = (s32[128]{0:T(128)S(1)}, s32[128]{0:T(128)}, u32[]{:S(2)}) copy-start(s32[128]{0:T(128)} %param.9) | copy-start | bytes 1540
  3.0 25.5 %all-to-all-start.1 = ((bf16[32,128,128]{2,1,0:T(8,128)(2,1)}), bf16[32,128,128]{2,1,0:T(8,128)(2,1)S(1)}, u32[]{:S(2)}, u32[]{:S(2)}) async-start(bf16[32,128,128]{2,1,0:T(8,128)(2,1)} %pack.3), calls=%async_computation.1 | async-start | bytes 2097152 | tf_op jit(solution)/shard_map/all_to_all | solution.py:451
  11.6 1.6 copy-start.4
  28.5 22.3 %all-to-all-start = ((bf16[32,144,128]{2,1,0:T(8,128)(2,1)}), bf16[32,144,128]{2,1,0:T(8,128)(2,1)S(1)}, u32[]{:S(2)}, u32[]{:S(2)}) async-start(bf16[32,144,128]{2,1,0:T(8,128)(2,1)} %pack.2), calls=%async_computation | async-start | bytes 2359296 | tf_op jit(solution)/shard_map/all_to_all | solution.py:451
  32.5 26.2 %collective-permute-start = (bf16[32,128,128]{2,1,0:T(8,128)(2,1)S(1)}, bf16[32,128,128]{2,1,0:T(8,128)(2,1)S(1)}, u32[]{:S(2)}, u32[]{:S(2)}) collective-permute-start(bf16[32,128,128]{2,1,0:T(8,128)(2,1)S(1)} %all-to-all-done.1.refs_0_), channel_id=1, source_target_pairs={{0,96},{32,0},{64,32},{96,64},{1,97},{33,1},{65,33},{97,65},{2,98}... | collective-permute-start | bytes 3145736 | tf_op jit(solution)/shard_map/ppermute | solution.py:390
  36.3 25.5 %collective-permute-start.1 = (bf16[32,128,128]{2,1,0:T(8,128)(2,1)S(1)}, bf16[32,128,128]{2,1,0:T(8,128)(2,1)}, u32[]{:S(2)}, u32[]{:S(2)}) collective-permute-start(bf16[32,128,128]{2,1,0:T(8,128)(2,1)S(1)} %all-to-all-done.1.refs_0_), channel_id=1, source_target_pairs={{0,32},{32,64},{64,96},{96,0},{1,33},{33,65},{65,97},{97,1},{2,34}... | collective-permute-start | bytes 3145736 | tf_op jit(solution)/shard_map/ppermute | solution.py:390
  36.3 27.4 %collective-permute-start.2 = (bf16[32,128,128]{2,1,0:T(8,128)(2,1)S(1)}, bf16[32,128,128]{2,1,0:T(8,128)(2,1)}, u32[]{:S(2)}, u32[]{:S(2)}) collective-permute-start(bf16[32,128,128]{2,1,0:T(8,128)(2,1)S(1)} %all-to-all-done.1.refs_0_), channel_id=1, source_target_pairs={{0,1},{1,0},{2,3},{3,2},{4,5},{5,4},{6,7},{7,6},{8,9},{9,8},{10,11... | collective-permute-start | bytes 3145736 | tf_op jit(solution)/shard_map/ppermute | solution.py:403
  50.8 39.4 %collective-permute-start.5 = (bf16[32,144,128]{2,1,0:T(8,128)(2,1)S(1)}, bf16[32,144,128]{2,1,0:T(8,128)(2,1)}, u32[]{:S(2)}, u32[]{:S(2)}) collective-permute-start(bf16[32,144,128]{2,1,0:T(8,128)(2,1)S(1)} %all-to-all-done.q_own.refs_3_.q), channel_id=1, source_target_pairs={{0,1},{1,0},{2,3},{3,2},{4,5},{5,4},{6,7},{7,6},{8,9},{9,8},{10,11... | collective-permute-start | bytes 3538952 | tf_op jit(solution)/shard_map/ppermute | solution.py:403
  63.7 6.7 %copy-start.7 = (s32[1,32]{1,0:T(1,128)S(1)}, s32[1,32]{1,0:T(1,128)}, u32[]{:S(2)}) copy-start(s32[1,32]{1,0:T(1,128)} %param.8) | copy-start | bytes 388
  63.7 6.8 %copy-start.6 = (s32[32,8]{0,1:T(8,128)S(1)}, s32[32,8]{0,1:T(8,128)}, u32[]{:S(2)}) copy-start(s32[32,8]{0,1:T(8,128)} %param.7) | copy-start | bytes 3076
  65.0 2.0 copy-start.2
  67.0 12.4 %collective-permute-start.3 = (bf16[16,128,128]{2,1,0:T(8,128)(2,1)}, bf16[16,128,128]{2,1,0:T(8,128)(2,1)}, u32[]{:S(2)}, u32[]{:S(2)}) collective-permute-start(bf16[16,128,128]{2,1,0:T(8,128)(2,1)} %slice.60), channel_id=1, source_target_pairs={{0,96},{32,0},{64,32},{96,64},{1,97},{33,1},{65,33},{97,65},{2,98}... | collective-permute-start | bytes 1572872 | tf_op jit(solution)/shard_map/ppermute | solution.py:390
  68.0 13.6 %collective-permute-start.4 = (bf16[16,128,128]{2,1,0:T(8,128)(2,1)}, bf16[16,128,128]{2,1,0:T(8,128)(2,1)}, u32[]{:S(2)}, u32[]{:S(2)}) collective-permute-start(bf16[16,128,128]{2,1,0:T(8,128)(2,1)} %slice.61), channel_id=1, source_target_pairs={{0,32},{32,64},{64,96},{96,0},{1,33},{33,65},{65,97},{97,1},{2,34}... | collective-permute-start | bytes 1572872 | tf_op jit(solution)/shard_map/ppermute | solution.py:390
  68.4 18.5 %collective-permute-start.6 = (bf16[32,128,128]{2,1,0:T(8,128)(2,1)S(1)}, bf16[32,128,128]{2,1,0:T(8,128)(2,1)}, u32[]{:S(2)}, u32[]{:S(2)}) collective-permute-start(bf16[32,128,128]{2,1,0:T(8,128)(2,1)S(1)} %collective-permute-done.refs_1_), channel_id=1, source_target_pairs={{0,1},{1,0},{2,3},{3,2},{4,5},{5,4},{6,7},{7,6},{8,9},{9,8},{10,11... | collective-permute-start | bytes 3145736 | tf_op jit(solution)/shard_map/ppermute | solution.py:403
  70.3 16.5 %collective-permute-start.7 = (bf16[32,128,128]{2,1,0:T(8,128)(2,1)}, bf16[32,128,128]{2,1,0:T(8,128)(2,1)}, u32[]{:S(2)}, u32[]{:S(2)}) collective-permute-start(bf16[32,128,128]{2,1,0:T(8,128)(2,1)} %collective-permute-done.1.refs_2_), channel_id=1, source_target_pairs={{0,1},{1,0},{2,3},{3,2},{4,5},{5,4},{6,7},{7,6},{8,9},{9,8},{10,11... | collective-permute-start | bytes 3145736 | tf_op jit(solution)/shard_map/ppermute | solution.py:403
  79.3 10.7 %collective-permute-start.8 = (bf16[16,128,128]{2,1,0:T(8,128)(2,1)}, bf16[16,128,128]{2,1,0:T(8,128)(2,1)S(1)}, u32[]{:S(2)}, u32[]{:S(2)}) collective-permute-start(bf16[16,128,128]{2,1,0:T(8,128)(2,1)} %collective-permute-done.3.refs_1_), channel_id=1, source_target_pairs={{0,1},{1,0},{2,3},{3,2},{4,5},{5,4},{6,7},{7,6},{8,9},{9,8},{10,11... | collective-permute-start | bytes 1572872 | tf_op jit(solution)/shard_map/ppermute | solution.py:403
  81.6 8.4 %collective-permute-start.9 = (bf16[16,128,128]{2,1,0:T(8,128)(2,1)}, bf16[16,128,128]{2,1,0:T(8,128)(2,1)S(1)}, u32[]{:S(2)}, u32[]{:S(2)}) collective-permute-start(bf16[16,128,128]{2,1,0:T(8,128)(2,1)} %collective-permute-done.4.refs_2_), channel_id=1, source_target_pairs={{0,1},{1,0},{2,3},{3,2},{4,5},{5,4},{6,7},{7,6},{8,9},{9,8},{10,11... | collective-permute-start | bytes 1572872 | tf_op jit(solution)/shard_map/ppermute | solution.py:403
  85.5 2.9 %copy-start.3 = (bf16[128,128,128]{2,1,0:T(8,128)(2,1)S(1)}, bf16[128,128,128]{2,1,0:T(8,128)(2,1)}, u32[]{:S(2)}) copy-start(bf16[128,128,128]{2,1,0:T(8,128)(2,1)} %copy-done.2) | copy-start | bytes 12582916
  86.9 3.3 %copy-start = (bf16[128,128,128]{2,1,0:T(8,128)(2,1)}, bf16[128,128,128]{2,1,0:T(8,128)(2,1)S(1)}, u32[]{:S(2)}) copy-start(bf16[128,128,128]{2,1,0:T(8,128)(2,1)S(1)} %place.9.p_own.p) | copy-start | bytes 12582916
  94.6 9.6 %collective-permute-start.10 = (f32[2,512,128]{2,1,0:T(8,128)S(1)}, f32[2,512,128]{2,1,0:T(8,128)S(1)}, u32[]{:S(2)}, u32[]{:S(2)}) collective-permute-start(f32[2,512,128]{2,1,0:T(8,128)S(1)} %get-tuple-element.27), channel_id=1, source_target_pairs={{0,8},{1,3},{2,10},{3,5},{4,12},{5,7},{6,14},{7,1},{8,16},{9,11},{... | collective-permute-start | bytes 1572872 | tf_op jit(solution)/shard_map/ppermute | solution.py:403
  95.9 8.5 %collective-permute-start.15 = (f32[2,512,128]{2,1,0:T(8,128)S(1)}, f32[2,512,128]{2,1,0:T(8,128)S(1)}, u32[]{:S(2)}, u32[]{:S(2)}) collective-permute-start(f32[2,512,128]{2,1,0:T(8,128)S(1)} %get-tuple-element.31), channel_id=1, source_target_pairs={{0,24},{1,7},{2,26},{3,1},{4,28},{5,3},{6,30},{7,5},{8,0},{9,15},{... | collective-permute-start | bytes 1572872 | tf_op jit(solution)/shard_map/ppermute | solution.py:403
  97.4 12.5 %collective-permute-start.12 = (f32[2,512,128]{2,1,0:T(8,128)S(1)}, f32[2,512,128]{2,1,0:T(8,128)S(1)}, u32[]{:S(2)}, u32[]{:S(2)}) collective-permute-start(f32[2,512,128]{2,1,0:T(8,128)S(1)} %get-tuple-element.28), channel_id=1, source_target_pairs={{0,24},{1,7},{2,26},{3,1},{4,28},{5,3},{6,30},{7,5},{8,0},{9,15},{... | collective-permute-start | bytes 1572872 | tf_op jit(solution)/shard_map/ppermute | solution.py:403
  98.6 11.3 %collective-permute-start.14 = (f32[2,512,128]{2,1,0:T(8,128)S(1)}, f32[2,512,128]{2,1,0:T(8,128)S(1)}, u32[]{:S(2)}, u32[]{:S(2)}) collective-permute-start(f32[2,512,128]{2,1,0:T(8,128)S(1)} %get-tuple-element.29), channel_id=1, source_target_pairs={{0,8},{1,3},{2,10},{3,5},{4,12},{5,7},{6,14},{7,1},{8,16},{9,11},{... | collective-permute-start | bytes 1572872 | tf_op jit(solution)/shard_map/ppermute | solution.py:403
  104.3 11.2 %collective-permute-start.11 = (f32[2,512,128]{2,1,0:T(8,128)S(1)}, f32[2,512,128]{2,1,0:T(8,128)S(1)}, u32[]{:S(2)}, u32[]{:S(2)}) collective-permute-start(f32[2,512,128]{2,1,0:T(8,128)S(1)} %add.99), channel_id=1, source_target_pairs={{0,8},{1,3},{2,10},{3,5},{4,12},{5,7},{6,14},{7,1},{8,16},{9,11},{... | collective-permute-start | bytes 1572872 | tf_op jit(solution)/shard_map/ppermute | solution.py:403
  104.5 11.0 %collective-permute-start.16 = (f32[2,512,128]{2,1,0:T(8,128)S(1)}, f32[2,512,128]{2,1,0:T(8,128)S(1)}, u32[]{:S(2)}, u32[]{:S(2)}) collective-permute-start(f32[2,512,128]{2,1,0:T(8,128)S(1)} %add.108), channel_id=1, source_target_pairs={{0,24},{1,7},{2,26},{3,1},{4,28},{5,3},{6,30},{7,5},{8,0},{9,15},{... | collective-permute-start | bytes 1572872 | tf_op jit(solution)/shard_map/ppermute | solution.py:403
  115.7 6.8 %collective-permute-start.13 = (f32[512,128]{1,0:T(8,128)S(1)}, f32[512,128]{1,0:T(8,128)S(1)}, u32[]{:S(2)}, u32[]{:S(2)}) collective-permute-start(f32[512,128]{1,0:T(8,128)S(1)} %get-tuple-element.43), channel_id=1, source_target_pairs={{0,2},{1,9},{2,4},{3,11},{4,6},{5,13},{6,0},{7,15},{8,10},{9,17},{... | collective-permute-start | bytes 786440 | tf_op jit(solution)/shard_map/ppermute | solution.py:403
  116.9 9.3 %collective-permute-start.17 = (f32[512,128]{1,0:T(8,128)S(1)}, f32[512,128]{1,0:T(8,128)S(1)}, u32[]{:S(2)}, u32[]{:S(2)}) collective-permute-start(f32[512,128]{1,0:T(8,128)S(1)} %get-tuple-element.41), channel_id=1, source_target_pairs={{0,4},{1,17},{2,6},{3,19},{4,0},{5,21},{6,2},{7,23},{8,12},{9,25},... | collective-permute-start | bytes 786440 | tf_op jit(solution)/shard_map/ppermute | solution.py:403
  119.4 6.9 %collective-permute-start.18 = (f32[512,128]{1,0:T(8,128)S(1)}, f32[512,128]{1,0:T(8,128)S(1)}, u32[]{:S(2)}, u32[]{:S(2)}) collective-permute-start(f32[512,128]{1,0:T(8,128)S(1)} %get-tuple-element.42), channel_id=1, source_target_pairs={{0,6},{1,25},{2,0},{3,27},{4,2},{5,29},{6,4},{7,31},{8,14},{9,1},{... | collective-permute-start | bytes 786440 | tf_op jit(solution)/shard_map/ppermute | solution.py:403
  126.4 3.2 %collective-permute-start.19 = (f32[512,128]{1,0:T(8,128)S(1)}, f32[512,128]{1,0:T(8,128)S(1)}, u32[]{:S(2)}, u32[]{:S(2)}) collective-permute-start(f32[512,128]{1,0:T(8,128)S(1)} %fusion.6.refs_0_), channel_id=1, source_target_pairs={{0,1},{1,0},{2,3},{3,2},{4,5},{5,4},{6,7},{7,6},{8,9},{9,8},{10,11... | collective-permute-start | bytes 786440 | tf_op jit(solution)/shard_map/ppermute | solution.py:403
  132.2 6.0 %collective-permute-start.20 = (bf16[528,128]{1,0:T(8,128)(2,1)S(1)}, bf16[528,128]{1,0:T(8,128)(2,1)S(1)}, u32[]{:S(2)}, u32[]{:S(2)}) collective-permute-start(bf16[528,128]{1,0:T(8,128)(2,1)S(1)} %softmax_weights.1), channel_id=1, source_target_pairs={{0,24},{1,7},{2,26},{3,1},{4,28},{5,3},{6,30},{7,5},{8,0},{9,15},{... | collective-permute-start | bytes 405512 | tf_op jit(solution)/shard_map/ppermute | solution.py:403
  134.8 5.4 %collective-permute-start.21 = (bf16[528,128]{1,0:T(8,128)(2,1)S(1)}, bf16[528,128]{1,0:T(8,128)(2,1)S(1)}, u32[]{:S(2)}, u32[]{:S(2)}) collective-permute-start(bf16[528,128]{1,0:T(8,128)(2,1)S(1)} %softmax_weights.1), channel_id=1, source_target_pairs={{0,16},{1,5},{2,18},{3,7},{4,20},{5,1},{6,22},{7,3},{8,24},{9,13},... | collective-permute-start | bytes 405512 | tf_op jit(solution)/shard_map/ppermute | solution.py:403
  135.9 6.0 %collective-permute-start.22 = (bf16[528,128]{1,0:T(8,128)(2,1)S(1)}, bf16[528,128]{1,0:T(8,128)(2,1)S(1)}, u32[]{:S(2)}, u32[]{:S(2)}) collective-permute-start(bf16[528,128]{1,0:T(8,128)(2,1)S(1)} %softmax_weights.1), channel_id=1, source_target_pairs={{0,8},{1,3},{2,10},{3,5},{4,12},{5,7},{6,14},{7,1},{8,16},{9,11},{... | collective-permute-start | bytes 405512 | tf_op jit(solution)/shard_map/ppermute | solution.py:403
  142.0 8.7 %collective-permute-start.24 = (bf16[4,528,128]{2,1,0:T(8,128)(2,1)S(1)}, bf16[4,528,128]{2,1,0:T(8,128)(2,1)S(1)}, u32[]{:S(2)}, u32[]{:S(2)}) collective-permute-start(bf16[4,528,128]{2,1,0:T(8,128)(2,1)S(1)} %pad_maximum_fusion.refs_0_), channel_id=1, source_target_pairs={{0,6},{1,25},{2,0},{3,27},{4,2},{5,29},{6,4},{7,31},{8,14},{9,1},{... | collective-permute-start | bytes 1622024 | tf_op jit(solution)/shard_map/ppermute | solution.py:403
  144.4 12.7 %collective-permute-start.23 = (bf16[4,528,128]{2,1,0:T(8,128)(2,1)S(1)}, bf16[4,528,128]{2,1,0:T(8,128)(2,1)S(1)}, u32[]{:S(2)}, u32[]{:S(2)}) collective-permute-start(bf16[4,528,128]{2,1,0:T(8,128)(2,1)S(1)} %pad_maximum_fusion.refs_0_), channel_id=1, source_target_pairs={{0,2},{1,9},{2,4},{3,11},{4,6},{5,13},{6,0},{7,15},{8,10},{9,17},{... | collective-permute-start | bytes 1622024 | tf_op jit(solution)/shard_map/ppermute | solution.py:403
  150.7 9.7 %collective-permute-start.25 = (bf16[4,528,128]{2,1,0:T(8,128)(2,1)S(1)}, bf16[4,528,128]{2,1,0:T(8,128)(2,1)S(1)}, u32[]{:S(2)}, u32[]{:S(2)}) collective-permute-start(bf16[4,528,128]{2,1,0:T(8,128)(2,1)S(1)} %collective-permute-done.24.refs_2_), channel_id=1, source_target_pairs={{0,6},{1,25},{2,0},{3,27},{4,2},{5,29},{6,4},{7,31},{8,14},{9,1},{... | collective-permute-start | bytes 1622024 | tf_op jit(solution)/shard_map/ppermute | solution.py:403
  154.1 9.8 %collective-permute-start.26 = (bf16[4,528,128]{2,1,0:T(8,128)(2,1)S(1)}, bf16[4,528,128]{2,1,0:T(8,128)(2,1)S(1)}, u32[]{:S(2)}, u32[]{:S(2)}) collective-permute-start(bf16[4,528,128]{2,1,0:T(8,128)(2,1)S(1)} %pad_maximum_fusion.refs_0_), channel_id=1, source_target_pairs={{0,1},{1,0},{2,3},{3,2},{4,5},{5,4},{6,7},{7,6},{8,9},{9,8},{10,11... | collective-permute-start | bytes 1622024 | tf_op jit(solution)/shard_map/ppermute | solution.py:403
  157.0 6.9 %collective-permute-start.28 = (bf16[4,528,128]{2,1,0:T(8,128)(2,1)S(1)}, bf16[4,528,128]{2,1,0:T(8,128)(2,1)S(1)}, u32[]{:S(2)}, u32[]{:S(2)}) collective-permute-start(bf16[4,528,128]{2,1,0:T(8,128)(2,1)S(1)} %collective-permute-done.24.refs_2_), channel_id=1, source_target_pairs={{0,1},{1,0},{2,3},{3,2},{4,5},{5,4},{6,7},{7,6},{8,9},{9,8},{10,11... | collective-permute-start | bytes 1622024 | tf_op jit(solution)/shard_map/ppermute | solution.py:403
  157.0 6.9 %collective-permute-start.27 = (bf16[4,528,128]{2,1,0:T(8,128)(2,1)S(1)}, bf16[4,528,128]{2,1,0:T(8,128)(2,1)S(1)}, u32[]{:S(2)}, u32[]{:S(2)}) collective-permute-start(bf16[4,528,128]{2,1,0:T(8,128)(2,1)S(1)} %collective-permute-done.23.refs_1_), channel_id=1, source_target_pairs={{0,1},{1,0},{2,3},{3,2},{4,5},{5,4},{6,7},{7,6},{8,9},{9,8},{10,11... | collective-permute-start | bytes 1622024 | tf_op jit(solution)/shard_map/ppermute | solution.py:403
  160.4 5.1 %collective-permute-start.29 = (bf16[4,528,128]{2,1,0:T(8,128)(2,1)S(1)}, bf16[4,528,128]{2,1,0:T(8,128)(2,1)S(1)}, u32[]{:S(2)}, u32[]{:S(2)}) collective-permute-start(bf16[4,528,128]{2,1,0:T(8,128)(2,1)S(1)} %collective-permute-done.25.refs_3_), channel_id=1, source_target_pairs={{0,1},{1,0},{2,3},{3,2},{4,5},{5,4},{6,7},{7,6},{8,9},{9,8},{10,11... | collective-permute-start | bytes 1622024 | tf_op jit(solution)/shard_map/ppermute | solution.py:403
  165.5 2.2 copy-start.1
  176.8 13.5 %collective-permute-start.34 = (bf16[16,128,128]{2,1,0:T(8,128)(2,1)}, bf16[16,128,128]{2,1,0:T(8,128)(2,1)}, u32[]{:S(2)}, u32[]{:S(2)}) collective-permute-start(bf16[16,128,128]{2,1,0:T(8,128)(2,1)} %get-tuple-element.40), channel_id=1, source_target_pairs={{0,96},{32,0},{64,32},{96,64},{1,97},{33,1},{65,33},{97,65},{2,98}... | collective-permute-start | bytes 1572872 | tf_op jit(solution)/shard_map/ppermute | solution.py:390
  177.3 15.9 %collective-permute-start.30 = (bf16[16,128,128]{2,1,0:T(8,128)(2,1)}, bf16[16,128,128]{2,1,0:T(8,128)(2,1)}, u32[]{:S(2)}, u32[]{:S(2)}) collective-permute-start(bf16[16,128,128]{2,1,0:T(8,128)(2,1)} %get-tuple-element.36), channel_id=1, source_target_pairs={{0,32},{32,64},{64,96},{96,0},{1,33},{33,65},{65,97},{97,1},{2,34}... | collective-permute-start | bytes 1572872 | tf_op jit(solution)/shard_map/ppermute | solution.py:390
  178.2 23.2 %collective-permute-start.32 = (bf16[16,128,128]{2,1,0:T(8,128)(2,1)}, bf16[16,128,128]{2,1,0:T(8,128)(2,1)}, u32[]{:S(2)}, u32[]{:S(2)}) collective-permute-start(bf16[16,128,128]{2,1,0:T(8,128)(2,1)} %get-tuple-element.37), channel_id=1, source_target_pairs={{0,96},{32,0},{64,32},{96,64},{1,97},{33,1},{65,33},{97,65},{2,98}... | collective-permute-start | bytes 1572872 | tf_op jit(solution)/shard_map/ppermute | solution.py:390
  179.9 22.9 %collective-permute-start.33 = (bf16[16,128,128]{2,1,0:T(8,128)(2,1)}, bf16[16,128,128]{2,1,0:T(8,128)(2,1)}, u32[]{:S(2)}, u32[]{:S(2)}) collective-permute-start(bf16[16,128,128]{2,1,0:T(8,128)(2,1)} %get-tuple-element.38), channel_id=1, source_target_pairs={{0,32},{32,64},{64,96},{96,0},{1,33},{33,65},{65,97},{97,1},{2,34}... | collective-permute-start | bytes 1572872 | tf_op jit(solution)/shard_map/ppermute | solution.py:390
  179.9 36.6 %all-to-all-start.2 = ((bf16[32,128,128]{2,1,0:T(8,128)(2,1)}), bf16[32,128,128]{2,1,0:T(8,128)(2,1)S(1)}, u32[]{:S(2)}, u32[]{:S(2)}) async-start(bf16[32,128,128]{2,1,0:T(8,128)(2,1)} %get-tuple-element.33), calls=%async_computation.2 | async-start | bytes 2097152 | tf_op jit(solution)/shard_map/all_to_all | solution.py:451
  191.4 21.2 %collective-permute-start.35 = (bf16[16,128,128]{2,1,0:T(8,128)(2,1)S(1)}, bf16[16,128,128]{2,1,0:T(8,128)(2,1)S(1)}, u32[]{:S(2)}, u32[]{:S(2)}) collective-permute-start(bf16[16,128,128]{2,1,0:T(8,128)(2,1)S(1)} %add_convert_fusion), channel_id=1, source_target_pairs={{0,96},{32,0},{64,32},{96,64},{1,97},{33,1},{65,33},{97,65},{2,98}... | collective-permute-start | bytes 1572872 | tf_op jit(solution)/shard_map/ppermute | solution.py:390
  194.4 19.6 %collective-permute-start.31 = (bf16[16,128,128]{2,1,0:T(8,128)(2,1)S(1)}, bf16[16,128,128]{2,1,0:T(8,128)(2,1)S(1)}, u32[]{:S(2)}, u32[]{:S(2)}) collective-permute-start(bf16[16,128,128]{2,1,0:T(8,128)(2,1)S(1)} %add_convert_fusion.1), channel_id=1, source_target_pairs={{0,32},{32,64},{64,96},{96,0},{1,33},{33,65},{65,97},{97,1},{2,34}... | collective-permute-start | bytes 1572872 | tf_op jit(solution)/shard_map/ppermute | solution.py:390
  216.5 23.7 %all-to-all-start.3 = ((bf16[32,128,128]{2,1,0:T(8,128)(2,1)}), bf16[32,128,128]{2,1,0:T(8,128)(2,1)S(1)}, u32[]{:S(2)}, u32[]{:S(2)}) async-start(bf16[32,128,128]{2,1,0:T(8,128)(2,1)} %join.1), calls=%async_computation.3 | async-start | bytes 2097152 | tf_op jit(solution)/shard_map/all_to_all | solution.py:451

commit v4 on v3

--- a/solution.py
+++ b/solution.py
@@ -8,6 +8,7 @@
 from jax.sharding import PartitionSpec as P
 
 BLK = 128
+HALF = BLK // 2
 PAIRS = 128
 PART = PAIRS // 2
 ROWS = 8 * PART
@@ -34,45 +35,53 @@
 
 
 def pack_kernel(x, *refs):
-    *given, out, xv, outv, marks, sems = refs
+    *outs, xv, outv, marks, sems = refs
+    extra = outv.shape[1] - BLK
+    if extra:
+        run_copies([pltpu.make_async_copy(outs[0], marks, sems.at[0])])
+        outs = outs[1:]
+        tile = jnp.broadcast_to(marks[...].astype(jnp.float32), (extra, 128)).astype(jnp.bfloat16)
     width = x.shape[1]
     number = outv.shape[0] // PARTS
+    tall = outv.shape[1] // len(outs)
     loads, stores = [], []
     for n in range(PARTS):
         cols = slice(n * width // PARTS, (n + 1) * width // PARTS)
         loads.append(pltpu.make_async_copy(x.at[:, cols], xv.at[:, cols], sems.at[n]))
         part = slice(n * number, (n + 1) * number)
-        stores.append(pltpu.make_async_copy(outv.at[part], out.at[part], sems.at[PARTS + n]))
+        for m, out in enumerate(outs):
+            source = outv.at[part, m * tall : (m + 1) * tall, :]
+            sem = sems.at[PARTS * (1 + m) + n]
+            stores.append(pltpu.make_async_copy(source, out.at[part], sem))
     for copy in loads:
         copy.start()
-    if given:
-        run_copies([pltpu.make_async_copy(given[0], marks, sems.at[2 * PARTS])])
-        tile = jnp.broadcast_to(marks[...].astype(jnp.float32), (16, 128)).astype(jnp.bfloat16)
     for n in range(PARTS):
         loads[n].wait()
         for m in range(n * number, (n + 1) * number):
             outv[m, 0:BLK, :] = xv[:, 128 * m : 128 * m + 128].astype(jnp.bfloat16)
-            if given:
+            if extra:
                 outv[m, BLK:, :] = tile
-        stores[n].start()
+        for copy in stores[n * len(outs) : (n + 1) * len(outs)]:
+            copy.start()
     for copy in stores:
         copy.wait()
 
 
 def by_features(x, pos=None):
-    width = x.shape[1]
-    shape = (width // 128, BLK + (0 if pos is None else 16), 128)
+    number = x.shape[1] // 128
+    tall = BLK + (0 if pos is None else 16)
+    shapes = [(number, HALF, 128)] * 2 if pos is None else [(number, tall, 128)]
     given = (x,) if pos is None else (x, pos)
     return pl.pallas_call(
         pack_kernel,
         in_specs=[ANY] * len(given),
-        out_specs=ANY,
-        out_shape=jax.ShapeDtypeStruct(shape, jnp.bfloat16),
+        out_specs=[ANY] * len(shapes),
+        out_shape=[jax.ShapeDtypeStruct(s, jnp.bfloat16) for s in shapes],
         scratch_shapes=[
             pltpu.VMEM(x.shape, x.dtype),
-            pltpu.VMEM(shape, jnp.bfloat16),
+            pltpu.VMEM((number, tall, 128), jnp.bfloat16),
             pltpu.VMEM((1, BLK), jnp.int32),
-            pltpu.SemaphoreType.DMA((2 * PARTS + 1,)),
+            pltpu.SemaphoreType.DMA((3 * PARTS,)),
         ],
         **params(56 if pos is None else 5, 5 * MIB),
         name="pack",
@@ -118,30 +127,25 @@
 PIECES = ((0, 32), (32, 16), (48, 16), (64, 16), (80, 16), (96, 16), (112, 16))
 
 
-def place_kernel(*refs, spots):
+def place_kernel(*refs):
     *pieces, out, sems = refs
-    pieces = pieces[len(pieces) - len(spots) :]
-    run_copies(
-        [
-            pltpu.make_async_copy(piece, out.at[first : first + piece.shape[0]], sems.at[n])
-            for n, (piece, first) in enumerate(zip(pieces, spots))
-        ]
-    )
-
-
-def place(whole, pieces, spots):
-    given = tuple(pieces) if whole is None else (whole, *pieces)
-    shape = (4 * 32,) + pieces[0].shape[1:]
-    return pl.pallas_call(
-        functools.partial(place_kernel, spots=spots),
-        in_specs=[ANY] * len(given),
+    copies = []
+    for n, piece in enumerate(pieces):
+        target = out.at[32 * (n // 2) : 32 * (n // 2) + 32, HALF * (n % 2) : HALF * (n % 2) + HALF, :]
+        copies.append(pltpu.make_async_copy(piece, target, sems.at[n]))
+    run_copies(copies)
+
+
+def place(pieces):
+    return pl.pallas_call(
+        place_kernel,
+        in_specs=[ANY] * 8,
         out_specs=ANY,
-        out_shape=jax.ShapeDtypeStruct(shape, pieces[0].dtype),
-        scratch_shapes=[pltpu.SemaphoreType.DMA((len(pieces),))],
-        input_output_aliases={} if whole is None else {0: 0},
-        **params(1, 4 * MIB),
+        out_shape=jax.ShapeDtypeStruct((4 * 32, BLK, 128), pieces[0].dtype),
+        scratch_shapes=[pltpu.SemaphoreType.DMA((8,))],
+        **params(1, 12 * MIB),
         name="place",
-    )(*given)
+    )(*pieces)
 
 
 def chip_at(at, core, lead, other):
@@ -150,8 +154,8 @@
     return ((at[1] + rx) % 4) * 4 + (at[2] + ry) % 4
 
 
-def score_kernel(ids, own, at, q_own, q_sib, p_own, p_sib, *refs):
-    outs, sv = refs[:7], refs[7]
+def score_kernel(ids, own, at, q_own, q_sib, *refs):
+    pieces, outs, (pv, sv) = (refs[:8], refs[8:16]), refs[16:23], refs[23:]
     core = at[0]
     spots = [
         (lead, other, chip_at(at, core, lead, other)) for lead in range(4) for other in range(4)
@@ -160,12 +164,22 @@
     @pl.loop(0, PART // STEP)
     def _(step):
         for u in range(STEP):
-            n = step * STEP + u
-            here, there = own[PART * core + n], ids[PART * core + n]
+            there = ids[PART * core + step * STEP + u]
+            for rel in range(4):
+
+                @pl.when(there // 32 == rel)
+                def _():
+                    for side in range(2):
+                        for h in range(2):
+                            rows = slice(HALF * h, HALF * h + HALF)
+                            lanes = slice(128 * side, 128 * side + 128)
+                            pv[u, rows, lanes] = pieces[side][2 * rel + h][there % 32]
+
+        for u in range(STEP):
+            here = own[PART * core + step * STEP + u]
             left = jnp.concatenate([q_own[here, 0:BLK, :], q_sib[here, 0:BLK, :]], axis=1)
-            right = jnp.concatenate([p_own[there], p_sib[there]], axis=1)
             tile = lax.dot_general(
-                left, right, (((1,), (1,)), ((), ())), preferred_element_type=jnp.float32
+                left, pv[u], (((1,), (1,)), ((), ())), preferred_element_type=jnp.float32
             )
             sv[u] = tile.reshape(BLK // 8, 8, 128)
         for u in range(STEP):
@@ -177,17 +191,20 @@
                     outs[2 * lead - 2 + other // 2][other % 2, where, :] = sv[u, chip]
 
 
-def partial_scores(ids, own, at, q, p):
+def partial_scores(ids, own, at, q, pieces):
     shapes = [(2, ROWS, 128)] * 6 + [(4, ROWS, 128)]
     return pl.pallas_call(
         score_kernel,
-        in_specs=[SMEM] * 3 + [VMEM] * 4,
+        in_specs=[SMEM] * 3 + [VMEM] * 18,
         out_specs=[VMEM] * 7,
         out_shape=[jax.ShapeDtypeStruct(s, jnp.float32) for s in shapes],
-        scratch_shapes=[pltpu.VMEM((STEP, BLK // 8, 8, 128), jnp.float32)],
-        **params(17, 20 * MIB),
+        scratch_shapes=[
+            pltpu.VMEM((STEP, BLK, 2 * 128), jnp.bfloat16),
+            pltpu.VMEM((STEP, BLK // 8, 8, 128), jnp.float32),
+        ],
+        **params(18, 20 * MIB),
         name="partial_scores",
-    )(ids, own, at, *q, *p)
+    )(ids, own, at, *q, *pieces)
 
 
 def softmax_kernel(at, *refs, scale):
@@ -451,18 +468,16 @@
         return lax.all_to_all(v, "dev", 0, 0, tiled=True)
 
     up, down, flip = along("z", 1), along("z", -1), along("core", 1)
-    p_own = exchange(by_features(passages))
-    above, below, given = down(p_own), up(p_own), flip(p_own)
-    mine, theirs = place(None, [p_own], [0]), place(None, [given], [0])
-    low, high = above[: ndev // 2], below[ndev // 2 :]
-    low, high, theirs = lax.optimization_barrier((low, high, theirs))
-    far = [down(low), up(high)]
-    near = [above, below]
-    mine = place(mine, near, [32, 96])
-    theirs = place(theirs, [flip(v) for v in near], [32, 96])
-    mine = place(mine, far, [64, 80])
-    theirs = place(theirs, [flip(v) for v in far], [64, 80])
-    q_own = exchange(by_features(queries, positives.reshape(1, BLK)))
+    low, high = [exchange(v) for v in by_features(passages)]
+    above0, below0 = down(low), up(low)
+    q_tiles = by_features(queries, positives.reshape(1, BLK))[0]
+    q_tiles, late, *_ = lax.optimization_barrier((q_tiles, high, above0, below0))
+    above1, below1 = down(late), up(late)
+    last0, last1, *_ = lax.optimization_barrier((above0, below1, above1))
+    far0, far1 = down(last0), up(last1)
+    pieces = [low, high, above0, above1, far0, far1, below0, below1]
+    others = [flip(v) for v in pieces]
+    q_own = exchange(q_tiles)
     q = [q_own, flip(q_own)]
 
     group = counts[0]
@@ -479,9 +494,9 @@
     spare = jnp.full((128 - ndev,), 2 * PAIRS, jnp.int32)
     lists = jnp.stack([jnp.concatenate([v, spare]) for v in (ends, starts)] * 4)
 
-    scores = scatter_scores(partial_scores(ids, own, at, q, (mine, theirs)))
+    scores = scatter_scores(partial_scores(ids, own, at, q, pieces + others))
     weights = softmax_weights(at, (scores, flip(scores)), lists, q_own, width ** (-0.5))
-    *g, gq, lines = gradients(ids, own, at, q_own, mine, gather_weights(weights))
+    *g, gq, lines = gradients(ids, own, at, q_own, place(pieces), gather_weights(weights))
 
     low, high = ring_terms("z", g[1:3], g[3:5], g[5:7])
     q_rows = by_rows(exchange(gq))

time: 244 us -> 239 us (0.980)
  blocking collectives: 0 us -> 20.2 us
  waiting for transfers between devices: 120 us -> 107 us
  starting transfers between devices: 73.8 us -> 67.7 us
  local copies, waits for them, and re-layouts: 10.9 us -> 5.91 us
    all_to_all x0 -> x1, blocking collectives: none -> 20.2 us  [exchange(): return lax.all_to_all(v, 'dev', 0, 0, tiled=True)]
    ppermute x10 -> x12, waiting for transfers between devices: 41.6 us -> 32 us  [along(): return lambda v: lax.ppermute(v, 'grp', perm)]
    ppermute x26 -> x29, starting transfers between devices: 37.7 us -> 30.3 us  [along(): return lambda v: lax.ppermute(v, 'dev', perm)]
    ppermute x10 -> x12, starting transfers between devices: 10.4 us -> 15.2 us  [along(): return lambda v: lax.ppermute(v, 'grp', perm)]
    all_to_all x4, waiting for transfers between devices: 41.5 us -> 36.9 us  [exchange(): return lax.all_to_all(v, 'dev', 0, 0, tiled=True)]
    unnamed x17 -> x21, local copies, waits for them, and re-layouts: 7.35 us -> 3.31 us
    all_to_all x4, starting transfers between devices: 25.7 us -> 22.1 us  [exchange(): return lax.all_to_all(v, 'dev', 0, 0, tiled=True)]
    slice x2 -> x0, local copies, waits for them, and re-layouts: 2.71 us -> none  [per_device(): low, high = (above[:ndev // 2], below[ndev // 2:])]
  transfers between devices with their start and end apart: 40 -> 45, of which waited for: 23 -> 24; matrix products, arithmetic and copies ran while one was open for 3% -> 2% of each run, Pallas kernels for 5% -> 3%
where the time goes in v4:
time: 239 us; the launch traced here: 238 us
  waiting for transfers between devices  107 us (45%)
  starting transfers between devices  67.7 us (28%)
  Pallas kernels  32.5 us (14%)
  blocking collectives  20.2 us (8%)
  local copies, waits for them, and re-layouts  5.91 us (2%)
  other arithmetic  3.32 us (1%)
    ppermute x29, waiting for transfers between devices, along(): return lambda v: lax.ppermute(v, 'dev', perm)  38.1 us
    all_to_all x4, waiting for transfers between devices, exchange(): return lax.all_to_all(v, 'dev', 0, 0, tiled=True)  36.9 us
    ppermute x12, waiting for transfers between devices, along(): return lambda v: lax.ppermute(v, 'grp', perm)  32 us
    ppermute x29, starting transfers between devices, along(): return lambda v: lax.ppermute(v, 'dev', perm)  30.3 us
    all_to_all x4, starting transfers between devices, exchange(): return lax.all_to_all(v, 'dev', 0, 0, tiled=True)  22.1 us
    all_to_all x1, blocking collectives, exchange(): return lax.all_to_all(v, 'dev', 0, 0, tiled=True)  20.2 us
    ppermute x12, starting transfers between devices, along(): return lambda v: lax.ppermute(v, 'grp', perm)  15.2 us
    pallas_call x1, Pallas kernels, gradients(): pl.pallas_call(grad_kernel, in_specs=[SMEM] * 3 + [VMEM] * 10, out_specs=...  8.76 us
  transfers between devices with their start and end apart: 45, of which 24 were waited for; matrix products, arithmetic and copies ran while one was open for 2% of the time, Pallas kernels for 3%

profile of v4, /device:TPU:1, one launch (start us, length us, event | category | flops | bytes accessed | tf_op | source)
XLA Modules:
  0.0 237.8 jit_solution(7629709616688967106)
XLA Ops:
  0.6 2.4 %pack.3 = (bf16[32,64,128]{2,1,0:T(8,128)(2,1)}, bf16[32,64,128]{2,1,0:T(8,128)(2,1)}) custom-call(f32[128,4096]{1,0:T(8,128)} %x.7), custom_call_target="tpu_custom_call" | custom-call | bytes 5242880 | tf_op jit(solution)/shard_map/pack/pallas_call | solution.py:75
  3.0 20.2 %all_to_all.25.refs_0_ = bf16[32,64,128]{2,1,0:T(8,128)(2,1)S(1)} all-to-all(bf16[32,64,128]{2,1,0:T(8,128)(2,1)} %get-tuple-element.26), channel_id=1, replica_groups=mesh['grp'=4,'dev'=32] {'dev'}, dimensions={0} | all-to-all | bytes 1048576 | tf_op jit(solution)/shard_map/all_to_all | solution.py:468
  23.3 1.6 collective-permute-start.1
  24.9 2.1 collective-permute-start
  27.0 3.9 %all-to-all-start = ((bf16[32,64,128]{2,1,0:T(8,128)(2,1)}), bf16[32,64,128]{2,1,0:T(8,128)(2,1)S(1)}, u32[]{:S(2)}, u32[]{:S(2)}) async-start(bf16[32,64,128]{2,1,0:T(8,128)(2,1)} %get-tuple-element.25), calls=%async_computation | async-start | bytes 1048576 | tf_op jit(solution)/shard_map/all_to_all | solution.py:468
  31.0 1.6 copy-done.4
  32.5 1.4 pack.2
  33.9 8.6 %all-to-all-done.refs_1_ = bf16[32,64,128]{2,1,0:T(8,128)(2,1)S(1)} async-done(((bf16[32,64,128]{2,1,0:T(8,128)(2,1)}), bf16[32,64,128]{2,1,0:T(8,128)(2,1)S(1)}, u32[]{:S(2)}, u32[]{:S(2)}) %all-to-all-start) | async-done | bytes 524320 | tf_op jit(solution)/shard_map/all_to_all | solution.py:468
  42.6 3.7 %all-to-all-start.2 = ((bf16[32,144,128]{2,1,0:T(8,128)(2,1)}), bf16[32,144,128]{2,1,0:T(8,128)(2,1)S(1)}, u32[]{:S(2)}, u32[]{:S(2)}) async-start(bf16[32,144,128]{2,1,0:T(8,128)(2,1)} %pack.2), calls=%async_computation.2 | async-start | bytes 2359296 | tf_op jit(solution)/shard_map/all_to_all | solution.py:468
  46.4 2.7 %collective-permute-start.2 = (bf16[32,64,128]{2,1,0:T(8,128)(2,1)S(1)}, bf16[32,64,128]{2,1,0:T(8,128)(2,1)}, u32[]{:S(2)}, u32[]{:S(2)}) collective-permute-start(bf16[32,64,128]{2,1,0:T(8,128)(2,1)S(1)} %all-to-all-done.refs_1_), channel_id=1, source_target_pairs={{0,96},{32,0},{64,32},{96,64},{1,97},{33,1},{65,33},{97,65},{2,98}... | collective-permute-start | bytes 1572872 | tf_op jit(solution)/shard_map/ppermute | solution.py:407
  49.8 14.8 %all-to-all-done.2.q_own.refs_3_.q = bf16[32,144,128]{2,1,0:T(8,128)(2,1)S(1)} async-done(((bf16[32,144,128]{2,1,0:T(8,128)(2,1)}), bf16[32,144,128]{2,1,0:T(8,128)(2,1)S(1)}, u32[]{:S(2)}, u32[]{:S(2)}) %all-to-all-start.2) | async-done | bytes 1179680 | tf_op jit(solution)/shard_map/all_to_all | solution.py:468
  65.6 1.7 collective-permute-start.4
  69.2 9.7 %collective-permute-done.4.refs_4_ = bf16[32,64,128]{2,1,0:T(8,128)(2,1)S(1)} collective-permute-done((bf16[32,64,128]{2,1,0:T(8,128)(2,1)S(1)}, bf16[32,64,128]{2,1,0:T(8,128)(2,1)S(1)}, u32[]{:S(2)}, u32[]{:S(2)}) %collective-permute-start.4) | collective-permute-done | bytes 524320 | tf_op jit(solution)/shard_map/ppermute | solution.py:407
  80.0 1.8 collective-permute-done.5.refs_5_
  81.7 1.4 collective-permute-start.12
  84.7 7.8 %partial_scores.1 = (f32[2,512,128]{2,1,0:T(8,128)S(1)}, f32[2,512,128]{2,1,0:T(8,128)S(1)}, f32[2,512,128]{2,1,0:T(8,128)S(1)}, f32[2,512,128]{2,1,0:T(8,128)S(...) custom-call(s32[128]{0:T(128)S(1)} %and_select_fusion.ids, ...), custom_call_target="tpu_custom_call" | custom-call | bytes 20971520 | tf_op jit(solution)/shard_map/partial_scores/pallas_call | solution.py:196
  92.6 2.7 %collective-permute-start.20 = (f32[2,512,128]{2,1,0:T(8,128)S(1)}, f32[2,512,128]{2,1,0:T(8,128)S(1)}, u32[]{:S(2)}, u32[]{:S(2)}) collective-permute-start(f32[2,512,128]{2,1,0:T(8,128)S(1)} %get-tuple-element.37), channel_id=1, source_target_pairs={{0,24},{1,7},{2,26},{3,1},{4,28},{5,3},{6,30},{7,5},{8,0},{9,15},{... | collective-permute-start | bytes 1572872 | tf_op jit(solution)/shard_map/ppermute | solution.py:420
  95.2 1.4 collective-permute-start.19
  96.7 5.4 %collective-permute-done.15 = f32[2,512,128]{2,1,0:T(8,128)S(1)} collective-permute-done((f32[2,512,128]{2,1,0:T(8,128)S(1)}, f32[2,512,128]{2,1,0:T(8,128)S(1)}, u32[]{:S(2)}, u32[]{:S(2)}) %collective-permute-start.15) | collective-permute-done | bytes 524320 | tf_op jit(solution)/shard_map/ppermute | solution.py:420
  102.3 2.7 %collective-permute-start.21 = (f32[2,512,128]{2,1,0:T(8,128)S(1)}, f32[2,512,128]{2,1,0:T(8,128)S(1)}, u32[]{:S(2)}, u32[]{:S(2)}) collective-permute-start(f32[2,512,128]{2,1,0:T(8,128)S(1)} %add.108), channel_id=1, source_target_pairs={{0,24},{1,7},{2,26},{3,1},{4,28},{5,3},{6,30},{7,5},{8,0},{9,15},{... | collective-permute-start | bytes 1572872 | tf_op jit(solution)/shard_map/ppermute | solution.py:420
  105.0 1.9 collective-permute-done.17
  107.7 5.6 %collective-permute-done.16 = f32[2,512,128]{2,1,0:T(8,128)S(1)} collective-permute-done((f32[2,512,128]{2,1,0:T(8,128)S(1)}, f32[2,512,128]{2,1,0:T(8,128)S(1)}, u32[]{:S(2)}, u32[]{:S(2)}) %collective-permute-start.16) | collective-permute-done | bytes 524320 | tf_op jit(solution)/shard_map/ppermute | solution.py:420
  115.7 4.8 %collective-permute-done.22 = f32[512,128]{1,0:T(8,128)S(1)} collective-permute-done((f32[512,128]{1,0:T(8,128)S(1)}, f32[512,128]{1,0:T(8,128)S(1)}, u32[]{:S(2)}, u32[]{:S(2)}) %collective-permute-start.22) | collective-permute-done | bytes 262176 | tf_op jit(solution)/shard_map/ppermute | solution.py:420
  120.6 1.5 collective-permute-done.23
  123.5 2.3 collective-permute-start.24
  127.7 3.5 %softmax_weights.1 = bf16[528,128]{1,0:T(8,128)(2,1)S(1)} custom-call(s32[5]{0:T(128)S(1)} %stack.53.at, f32[512,128]{1,0:T(8,128)S(1)} %fusion.6.refs_0_, f32[512,128]{1,0:T(8,128)} %collective-permute-done.24.refs_1_, s32[8,128]{1,0:T(8,128)S(1)} %stack.56.refs_2_, bf16[32,144,128]{2,1,0:T(8,128)(2,1)S(1)} %all-to-all-done.2.q_own.refs_3_.q), custom_call_target="tpu_custom_call" | custom-call | bytes 8388608 | tf_op jit(solution)/shard_map/softmax_weights/pallas_call | solution.py:267
  131.3 2.2 collective-permute-start.26
  134.7 3.1 %collective-permute-done.27 = bf16[528,128]{1,0:T(8,128)(2,1)S(1)} collective-permute-done((bf16[528,128]{1,0:T(8,128)(2,1)S(1)}, bf16[528,128]{1,0:T(8,128)(2,1)S(1)}, u32[]{:S(2)}, u32[]{:S(2)}) %collective-permute-start.27) | collective-permute-done | bytes 135200 | tf_op jit(solution)/shard_map/ppermute | solution.py:420
  138.7 3.0 %collective-permute-start.29 = (bf16[4,528,128]{2,1,0:T(8,128)(2,1)S(1)}, bf16[4,528,128]{2,1,0:T(8,128)(2,1)S(1)}, u32[]{:S(2)}, u32[]{:S(2)}) collective-permute-start(bf16[4,528,128]{2,1,0:T(8,128)(2,1)S(1)} %pad_maximum_fusion.refs_0_), channel_id=1, source_target_pairs={{0,6},{1,25},{2,0},{3,27},{4,2},{5,29},{6,4},{7,31},{8,14},{9,1},{... | collective-permute-start | bytes 1622024 | tf_op jit(solution)/shard_map/ppermute | solution.py:420
  141.8 6.3 %collective-permute-done.29.refs_2_ = bf16[4,528,128]{2,1,0:T(8,128)(2,1)S(1)} collective-permute-done((bf16[4,528,128]{2,1,0:T(8,128)(2,1)S(1)}, bf16[4,528,128]{2,1,0:T(8,128)(2,1)S(1)}, u32[]{:S(2)}, u32[]{:S(2)}) %collective-permute-start.29) | collective-permute-done | bytes 540704 | tf_op jit(solution)/shard_map/ppermute | solution.py:420
  148.1 3.4 %collective-permute-start.30 = (bf16[4,528,128]{2,1,0:T(8,128)(2,1)S(1)}, bf16[4,528,128]{2,1,0:T(8,128)(2,1)S(1)}, u32[]{:S(2)}, u32[]{:S(2)}) collective-permute-start(bf16[4,528,128]{2,1,0:T(8,128)(2,1)S(1)} %collective-permute-done.29.refs_2_), channel_id=1, source_target_pairs={{0,6},{1,25},{2,0},{3,27},{4,2},{5,29},{6,4},{7,31},{8,14},{9,1},{... | collective-permute-start | bytes 1622024 | tf_op jit(solution)/shard_map/ppermute | solution.py:420
  151.5 1.6 collective-permute-start.31
  153.6 4.2 %collective-permute-done.30.refs_3_ = bf16[4,528,128]{2,1,0:T(8,128)(2,1)S(1)} collective-permute-done((bf16[4,528,128]{2,1,0:T(8,128)(2,1)S(1)}, bf16[4,528,128]{2,1,0:T(8,128)(2,1)S(1)}, u32[]{:S(2)}, u32[]{:S(2)}) %collective-permute-start.30) | collective-permute-done | bytes 540704 | tf_op jit(solution)/shard_map/ppermute | solution.py:420
  157.8 2.2 collective-permute-start.34
  160.0 1.4 place.1.p
  161.5 8.8 %gradients.1 = (bf16[32,128,128]{2,1,0:T(8,128)(2,1)S(1)}, bf16[16,128,128]{2,1,0:T(8,128)(2,1)S(1)}, bf16[16,128,128]{2,1,0:T(8,128)(2,1)S(1)}, bf16[16,128,128...) custom-call(s32[128]{0:T(128)S(1)} %and_select_fusion.ids, ...), custom_call_target="tpu_custom_call" | custom-call | bytes 33554432 | tf_op jit(solution)/shard_map/gradients/pallas_call | solution.py:342
  171.9 2.7 %collective-permute-start.39 = (bf16[16,128,128]{2,1,0:T(8,128)(2,1)}, bf16[16,128,128]{2,1,0:T(8,128)(2,1)}, u32[]{:S(2)}, u32[]{:S(2)}) collective-permute-start(bf16[16,128,128]{2,1,0:T(8,128)(2,1)} %get-tuple-element.46), channel_id=1, source_target_pairs={{0,96},{32,0},{64,32},{96,64},{1,97},{33,1},{65,33},{97,65},{2,98}... | collective-permute-start | bytes 1572872 | tf_op jit(solution)/shard_map/ppermute | solution.py:407
  174.6 7.1 %all-to-all-start.3 = ((bf16[32,128,128]{2,1,0:T(8,128)(2,1)}), bf16[32,128,128]{2,1,0:T(8,128)(2,1)S(1)}, u32[]{:S(2)}, u32[]{:S(2)}) async-start(bf16[32,128,128]{2,1,0:T(8,128)(2,1)} %get-tuple-element.39), calls=%async_computation.3 | async-start | bytes 2097152 | tf_op jit(solution)/shard_map/all_to_all | solution.py:468
  181.8 1.5 collective-permute-start.38
  183.2 3.4 %collective-permute-done.35 = bf16[16,128,128]{2,1,0:T(8,128)(2,1)} collective-permute-done((bf16[16,128,128]{2,1,0:T(8,128)(2,1)}, bf16[16,128,128]{2,1,0:T(8,128)(2,1)}, u32[]{:S(2)}, u32[]{:S(2)}) %collective-permute-start.35) | collective-permute-done | bytes 524320 | tf_op jit(solution)/shard_map/ppermute | solution.py:407
  189.0 2.7 %collective-permute-start.40 = (bf16[16,128,128]{2,1,0:T(8,128)(2,1)S(1)}, bf16[16,128,128]{2,1,0:T(8,128)(2,1)S(1)}, u32[]{:S(2)}, u32[]{:S(2)}) collective-permute-start(bf16[16,128,128]{2,1,0:T(8,128)(2,1)S(1)} %add_convert_fusion), channel_id=1, source_target_pairs={{0,96},{32,0},{64,32},{96,64},{1,97},{33,1},{65,33},{97,65},{2,98}... | collective-permute-start | bytes 1572872 | tf_op jit(solution)/shard_map/ppermute | solution.py:407
  191.8 5.0 %collective-permute-done.37.refs_2_ = bf16[16,128,128]{2,1,0:T(8,128)(2,1)S(1)} collective-permute-done((bf16[16,128,128]{2,1,0:T(8,128)(2,1)}, bf16[16,128,128]{2,1,0:T(8,128)(2,1)S(1)}, u32[]{:S(2)}, u32[]{:S(2)}) %collective-permute-start.37) | collective-permute-done | bytes 524320 | tf_op jit(solution)/shard_map/ppermute | solution.py:407
  197.7 11.2 %collective-permute-done.36.refs_1_ = bf16[16,128,128]{2,1,0:T(8,128)(2,1)S(1)} collective-permute-done((bf16[16,128,128]{2,1,0:T(8,128)(2,1)S(1)}, bf16[16,128,128]{2,1,0:T(8,128)(2,1)S(1)}, u32[]{:S(2)}, u32[]{:S(2)}) %collective-permute-start.36) | collective-permute-done | bytes 524320 | tf_op jit(solution)/shard_map/ppermute | solution.py:407
  208.9 1.6 join.1
  210.6 7.4 %all-to-all-start.4 = ((bf16[32,128,128]{2,1,0:T(8,128)(2,1)}), bf16[32,128,128]{2,1,0:T(8,128)(2,1)S(1)}, u32[]{:S(2)}, u32[]{:S(2)}) async-start(bf16[32,128,128]{2,1,0:T(8,128)(2,1)} %join.1), calls=%async_computation.4 | async-start | bytes 2097152 | tf_op jit(solution)/shard_map/all_to_all | solution.py:468
  218.6 2.8 %unpack.2 = f32[128,4096]{1,0:T(8,128)} custom-call(bf16[32,128,128]{2,1,0:T(8,128)(2,1)S(1)} %all-to-all-done.3.x), custom_call_target="tpu_custom_call" | custom-call | bytes 8388608 | tf_op jit(solution)/shard_map/unpack/pallas_call | solution.py:112
  221.4 13.5 %all-to-all-done.4.x = bf16[32,128,128]{2,1,0:T(8,128)(2,1)S(1)} async-done(((bf16[32,128,128]{2,1,0:T(8,128)(2,1)}), bf16[32,128,128]{2,1,0:T(8,128)(2,1)S(1)}, u32[]{:S(2)}, u32[]{:S(2)}) %all-to-all-start.4) | async-done | bytes 1048608 | tf_op jit(solution)/shard_map/all_to_all | solution.py:468
  234.9 2.8 %unpack.3 = f32[128,4096]{1,0:T(8,128)} custom-call(bf16[32,128,128]{2,1,0:T(8,128)(2,1)S(1)} %all-to-all-done.4.x), custom_call_target="tpu_custom_call" | custom-call | bytes 8388608 | tf_op jit(solution)/shard_map/unpack/pallas_call | solution.py:112
  (94 shorter events, 21.4 us)
Async XLA Ops:
  23.3 19.3 %collective-permute-start.1 = (bf16[32,64,128]{2,1,0:T(8,128)(2,1)S(1)}, bf16[32,64,128]{2,1,0:T(8,128)(2,1)S(1)}, u32[]{:S(2)}, u32[]{:S(2)}) collective-permute-start(bf16[32,64,128]{2,1,0:T(8,128)(2,1)S(1)} %all_to_all.25.refs_0_), channel_id=1, source_target_pairs={{0,32},{32,64},{64,96},{96,0},{1,33},{33,65},{65,97},{97,1},{2,34}... | collective-permute-start | bytes 1572872 | tf_op jit(solution)/shard_map/ppermute | solution.py:407
  24.9 17.7 %collective-permute-start = (bf16[32,64,128]{2,1,0:T(8,128)(2,1)S(1)}, bf16[32,64,128]{2,1,0:T(8,128)(2,1)S(1)}, u32[]{:S(2)}, u32[]{:S(2)}) collective-permute-start(bf16[32,64,128]{2,1,0:T(8,128)(2,1)S(1)} %all_to_all.25.refs_0_), channel_id=1, source_target_pairs={{0,96},{32,0},{64,32},{96,64},{1,97},{33,1},{65,33},{97,65},{2,98}... | collective-permute-start | bytes 1572872 | tf_op jit(solution)/shard_map/ppermute | solution.py:407
  27.0 15.5 %all-to-all-start = ((bf16[32,64,128]{2,1,0:T(8,128)(2,1)}), bf16[32,64,128]{2,1,0:T(8,128)(2,1)S(1)}, u32[]{:S(2)}, u32[]{:S(2)}) async-start(bf16[32,64,128]{2,1,0:T(8,128)(2,1)} %get-tuple-element.25), calls=%async_computation | async-start | bytes 1048576 | tf_op jit(solution)/shard_map/all_to_all | solution.py:468
  32.5 34.8 %copy-start.9 = (s32[1,32]{1,0:T(1,128)S(1)}, s32[1,32]{1,0:T(1,128)}, u32[]{:S(2)}) copy-start(s32[1,32]{1,0:T(1,128)} %param.8) | copy-start | bytes 388
  42.6 22.0 %all-to-all-start.2 = ((bf16[32,144,128]{2,1,0:T(8,128)(2,1)}), bf16[32,144,128]{2,1,0:T(8,128)(2,1)S(1)}, u32[]{:S(2)}, u32[]{:S(2)}) async-start(bf16[32,144,128]{2,1,0:T(8,128)(2,1)} %pack.2), calls=%async_computation.2 | async-start | bytes 2359296 | tf_op jit(solution)/shard_map/all_to_all | solution.py:468
  46.3 18.8 %collective-permute-start.3 = (bf16[32,64,128]{2,1,0:T(8,128)(2,1)S(1)}, bf16[32,64,128]{2,1,0:T(8,128)(2,1)}, u32[]{:S(2)}, u32[]{:S(2)}) collective-permute-start(bf16[32,64,128]{2,1,0:T(8,128)(2,1)S(1)} %all-to-all-done.refs_1_), channel_id=1, source_target_pairs={{0,32},{32,64},{64,96},{96,0},{1,33},{33,65},{65,97},{97,1},{2,34}... | collective-permute-start | bytes 1572872 | tf_op jit(solution)/shard_map/ppermute | solution.py:407
  46.4 19.0 %collective-permute-start.2 = (bf16[32,64,128]{2,1,0:T(8,128)(2,1)S(1)}, bf16[32,64,128]{2,1,0:T(8,128)(2,1)}, u32[]{:S(2)}, u32[]{:S(2)}) collective-permute-start(bf16[32,64,128]{2,1,0:T(8,128)(2,1)S(1)} %all-to-all-done.refs_1_), channel_id=1, source_target_pairs={{0,96},{32,0},{64,32},{96,64},{1,97},{33,1},{65,33},{97,65},{2,98}... | collective-permute-start | bytes 1572872 | tf_op jit(solution)/shard_map/ppermute | solution.py:407
  49.1 16.6 %collective-permute-start.7 = (bf16[32,64,128]{2,1,0:T(8,128)(2,1)S(1)}, bf16[32,64,128]{2,1,0:T(8,128)(2,1)}, u32[]{:S(2)}, u32[]{:S(2)}) collective-permute-start(bf16[32,64,128]{2,1,0:T(8,128)(2,1)S(1)} %all_to_all.25.refs_0_), channel_id=1, source_target_pairs={{0,1},{1,0},{2,3},{3,2},{4,5},{5,4},{6,7},{7,6},{8,9},{9,8},{10,11... | collective-permute-start | bytes 1572872 | tf_op jit(solution)/shard_map/ppermute | solution.py:420
  49.8 17.6 %collective-permute-start.8 = (bf16[32,64,128]{2,1,0:T(8,128)(2,1)S(1)}, bf16[32,64,128]{2,1,0:T(8,128)(2,1)}, u32[]{:S(2)}, u32[]{:S(2)}) collective-permute-start(bf16[32,64,128]{2,1,0:T(8,128)(2,1)S(1)} %all-to-all-done.refs_1_), channel_id=1, source_target_pairs={{0,1},{1,0},{2,3},{3,2},{4,5},{5,4},{6,7},{7,6},{8,9},{9,8},{10,11... | collective-permute-start | bytes 1572872 | tf_op jit(solution)/shard_map/ppermute | solution.py:420
  64.6 20.1 %collective-permute-start.6 = (bf16[32,144,128]{2,1,0:T(8,128)(2,1)S(1)}, bf16[32,144,128]{2,1,0:T(8,128)(2,1)}, u32[]{:S(2)}, u32[]{:S(2)}) collective-permute-start(bf16[32,144,128]{2,1,0:T(8,128)(2,1)S(1)} %all-to-all-done.2.q_own.refs_3_.q), channel_id=1, source_target_pairs={{0,1},{1,0},{2,3},{3,2},{4,5},{5,4},{6,7},{7,6},{8,9},{9,8},{10,11... | collective-permute-start | bytes 3538952 | tf_op jit(solution)/shard_map/ppermute | solution.py:420
  65.1 3.1 %collective-permute-start.13 = (bf16[32,64,128]{2,1,0:T(8,128)(2,1)S(1)}, bf16[32,64,128]{2,1,0:T(8,128)(2,1)S(1)}, u32[]{:S(2)}, u32[]{:S(2)}) collective-permute-start(bf16[32,64,128]{2,1,0:T(8,128)(2,1)S(1)} %collective-permute-done.1.refs_6_), channel_id=1, source_target_pairs={{0,1},{1,0},{2,3},{3,2},{4,5},{5,4},{6,7},{7,6},{8,9},{9,8},{10,11... | collective-permute-start | bytes 1572872 | tf_op jit(solution)/shard_map/ppermute | solution.py:420
  65.4 3.5 %collective-permute-start.9 = (bf16[32,64,128]{2,1,0:T(8,128)(2,1)S(1)}, bf16[32,64,128]{2,1,0:T(8,128)(2,1)S(1)}, u32[]{:S(2)}, u32[]{:S(2)}) collective-permute-start(bf16[32,64,128]{2,1,0:T(8,128)(2,1)S(1)} %collective-permute-done.refs_2_), channel_id=1, source_target_pairs={{0,1},{1,0},{2,3},{3,2},{4,5},{5,4},{6,7},{7,6},{8,9},{9,8},{10,11... | collective-permute-start | bytes 1572872 | tf_op jit(solution)/shard_map/ppermute | solution.py:420
  65.6 13.3 %collective-permute-start.4 = (bf16[32,64,128]{2,1,0:T(8,128)(2,1)S(1)}, bf16[32,64,128]{2,1,0:T(8,128)(2,1)S(1)}, u32[]{:S(2)}, u32[]{:S(2)}) collective-permute-start(bf16[32,64,128]{2,1,0:T(8,128)(2,1)S(1)} %collective-permute-done.refs_2_), channel_id=1, source_target_pairs={{0,96},{32,0},{64,32},{96,64},{1,97},{33,1},{65,33},{97,65},{2,98}... | collective-permute-start | bytes 1572872 | tf_op jit(solution)/shard_map/ppermute | solution.py:407
  67.4 14.4 %collective-permute-start.5 = (bf16[32,64,128]{2,1,0:T(8,128)(2,1)}, bf16[32,64,128]{2,1,0:T(8,128)(2,1)S(1)}, u32[]{:S(2)}, u32[]{:S(2)}) collective-permute-start(bf16[32,64,128]{2,1,0:T(8,128)(2,1)} %collective-permute-done.3.refs_7_), channel_id=1, source_target_pairs={{0,32},{32,64},{64,96},{96,0},{1,33},{33,65},{65,97},{97,1},{2,34}... | collective-permute-start | bytes 1572872 | tf_op jit(solution)/shard_map/ppermute | solution.py:407
  68.2 15.2 %collective-permute-start.14 = (bf16[32,64,128]{2,1,0:T(8,128)(2,1)}, bf16[32,64,128]{2,1,0:T(8,128)(2,1)S(1)}, u32[]{:S(2)}, u32[]{:S(2)}) collective-permute-start(bf16[32,64,128]{2,1,0:T(8,128)(2,1)} %collective-permute-done.3.refs_7_), channel_id=1, source_target_pairs={{0,1},{1,0},{2,3},{3,2},{4,5},{5,4},{6,7},{7,6},{8,9},{9,8},{10,11... | collective-permute-start | bytes 1572872 | tf_op jit(solution)/shard_map/ppermute | solution.py:420
  68.9 14.4 %collective-permute-start.10 = (bf16[32,64,128]{2,1,0:T(8,128)(2,1)}, bf16[32,64,128]{2,1,0:T(8,128)(2,1)S(1)}, u32[]{:S(2)}, u32[]{:S(2)}) collective-permute-start(bf16[32,64,128]{2,1,0:T(8,128)(2,1)} %collective-permute-done.2.refs_3_), channel_id=1, source_target_pairs={{0,1},{1,0},{2,3},{3,2},{4,5},{5,4},{6,7},{7,6},{8,9},{9,8},{10,11... | collective-permute-start | bytes 1572872 | tf_op jit(solution)/shard_map/ppermute | solution.py:420
  78.9 4.5 %collective-permute-start.11 = (bf16[32,64,128]{2,1,0:T(8,128)(2,1)S(1)}, bf16[32,64,128]{2,1,0:T(8,128)(2,1)S(1)}, u32[]{:S(2)}, u32[]{:S(2)}) collective-permute-start(bf16[32,64,128]{2,1,0:T(8,128)(2,1)S(1)} %collective-permute-done.4.refs_4_), channel_id=1, source_target_pairs={{0,1},{1,0},{2,3},{3,2},{4,5},{5,4},{6,7},{7,6},{8,9},{9,8},{10,11... | collective-permute-start | bytes 1572872 | tf_op jit(solution)/shard_map/ppermute | solution.py:420
  81.7 2.9 %collective-permute-start.12 = (bf16[32,64,128]{2,1,0:T(8,128)(2,1)S(1)}, bf16[32,64,128]{2,1,0:T(8,128)(2,1)S(1)}, u32[]{:S(2)}, u32[]{:S(2)}) collective-permute-start(bf16[32,64,128]{2,1,0:T(8,128)(2,1)S(1)} %collective-permute-done.5.refs_5_), channel_id=1, source_target_pairs={{0,1},{1,0},{2,3},{3,2},{4,5},{5,4},{6,7},{7,6},{8,9},{9,8},{10,11... | collective-permute-start | bytes 1572872 | tf_op jit(solution)/shard_map/ppermute | solution.py:420
  92.5 9.6 %collective-permute-start.15 = (f32[2,512,128]{2,1,0:T(8,128)S(1)}, f32[2,512,128]{2,1,0:T(8,128)S(1)}, u32[]{:S(2)}, u32[]{:S(2)}) collective-permute-start(f32[2,512,128]{2,1,0:T(8,128)S(1)} %get-tuple-element.33), channel_id=1, source_target_pairs={{0,8},{1,3},{2,10},{3,5},{4,12},{5,7},{6,14},{7,1},{8,16},{9,11},{... | collective-permute-start | bytes 1572872 | tf_op jit(solution)/shard_map/ppermute | solution.py:420
  92.6 9.7 %collective-permute-start.20 = (f32[2,512,128]{2,1,0:T(8,128)S(1)}, f32[2,512,128]{2,1,0:T(8,128)S(1)}, u32[]{:S(2)}, u32[]{:S(2)}) collective-permute-start(f32[2,512,128]{2,1,0:T(8,128)S(1)} %get-tuple-element.37), channel_id=1, source_target_pairs={{0,24},{1,7},{2,26},{3,1},{4,28},{5,3},{6,30},{7,5},{8,0},{9,15},{... | collective-permute-start | bytes 1572872 | tf_op jit(solution)/shard_map/ppermute | solution.py:420
  95.2 11.7 %collective-permute-start.17 = (f32[2,512,128]{2,1,0:T(8,128)S(1)}, f32[2,512,128]{2,1,0:T(8,128)S(1)}, u32[]{:S(2)}, u32[]{:S(2)}) collective-permute-start(f32[2,512,128]{2,1,0:T(8,128)S(1)} %get-tuple-element.34), channel_id=1, source_target_pairs={{0,24},{1,7},{2,26},{3,1},{4,28},{5,3},{6,30},{7,5},{8,0},{9,15},{... | collective-permute-start | bytes 1572872 | tf_op jit(solution)/shard_map/ppermute | solution.py:420
  95.2 12.4 %collective-permute-start.19 = (f32[2,512,128]{2,1,0:T(8,128)S(1)}, f32[2,512,128]{2,1,0:T(8,128)S(1)}, u32[]{:S(2)}, u32[]{:S(2)}) collective-permute-start(f32[2,512,128]{2,1,0:T(8,128)S(1)} %get-tuple-element.35), channel_id=1, source_target_pairs={{0,8},{1,3},{2,10},{3,5},{4,12},{5,7},{6,14},{7,1},{8,16},{9,11},{... | collective-permute-start | bytes 1572872 | tf_op jit(solution)/shard_map/ppermute | solution.py:420
  102.2 11.2 %collective-permute-start.16 = (f32[2,512,128]{2,1,0:T(8,128)S(1)}, f32[2,512,128]{2,1,0:T(8,128)S(1)}, u32[]{:S(2)}, u32[]{:S(2)}) collective-permute-start(f32[2,512,128]{2,1,0:T(8,128)S(1)} %add.99), channel_id=1, source_target_pairs={{0,8},{1,3},{2,10},{3,5},{4,12},{5,7},{6,14},{7,1},{8,16},{9,11},{... | collective-permute-start | bytes 1572872 | tf_op jit(solution)/shard_map/ppermute | solution.py:420
  102.3 11.0 %collective-permute-start.21 = (f32[2,512,128]{2,1,0:T(8,128)S(1)}, f32[2,512,128]{2,1,0:T(8,128)S(1)}, u32[]{:S(2)}, u32[]{:S(2)}) collective-permute-start(f32[2,512,128]{2,1,0:T(8,128)S(1)} %add.108), channel_id=1, source_target_pairs={{0,24},{1,7},{2,26},{3,1},{4,28},{5,3},{6,30},{7,5},{8,0},{9,15},{... | collective-permute-start | bytes 1572872 | tf_op jit(solution)/shard_map/ppermute | solution.py:420
  113.5 7.1 %collective-permute-start.22 = (f32[512,128]{1,0:T(8,128)S(1)}, f32[512,128]{1,0:T(8,128)S(1)}, u32[]{:S(2)}, u32[]{:S(2)}) collective-permute-start(f32[512,128]{1,0:T(8,128)S(1)} %get-tuple-element.47), channel_id=1, source_target_pairs={{0,4},{1,17},{2,6},{3,19},{4,0},{5,21},{6,2},{7,23},{8,12},{9,25},... | collective-permute-start | bytes 786440 | tf_op jit(solution)/shard_map/ppermute | solution.py:420
  114.3 7.8 %collective-permute-start.23 = (f32[512,128]{1,0:T(8,128)S(1)}, f32[512,128]{1,0:T(8,128)S(1)}, u32[]{:S(2)}, u32[]{:S(2)}) collective-permute-start(f32[512,128]{1,0:T(8,128)S(1)} %get-tuple-element.48), channel_id=1, source_target_pairs={{0,6},{1,25},{2,0},{3,27},{4,2},{5,29},{6,4},{7,31},{8,14},{9,1},{... | collective-permute-start | bytes 786440 | tf_op jit(solution)/shard_map/ppermute | solution.py:420
  115.0 8.4 %collective-permute-start.18 = (f32[512,128]{1,0:T(8,128)S(1)}, f32[512,128]{1,0:T(8,128)S(1)}, u32[]{:S(2)}, u32[]{:S(2)}) collective-permute-start(f32[512,128]{1,0:T(8,128)S(1)} %get-tuple-element.49), channel_id=1, source_target_pairs={{0,2},{1,9},{2,4},{3,11},{4,6},{5,13},{6,0},{7,15},{8,10},{9,17},{... | collective-permute-start | bytes 786440 | tf_op jit(solution)/shard_map/ppermute | solution.py:420
  123.5 4.2 %collective-permute-start.24 = (f32[512,128]{1,0:T(8,128)S(1)}, f32[512,128]{1,0:T(8,128)}, u32[]{:S(2)}, u32[]{:S(2)}) collective-permute-start(f32[512,128]{1,0:T(8,128)S(1)} %fusion.6.refs_0_), channel_id=1, source_target_pairs={{0,1},{1,0},{2,3},{3,2},{4,5},{5,4},{6,7},{7,6},{8,9},{9,8},{10,11... | collective-permute-start | bytes 786440 | tf_op jit(solution)/shard_map/ppermute | solution.py:420
  127.6 32.3 %copy-start.1 = (bf16[32,64,128]{2,1,0:T(8,128)(2,1)S(1)}, bf16[32,64,128]{2,1,0:T(8,128)(2,1)}, u32[]{:S(2)}) copy-start(bf16[32,64,128]{2,1,0:T(8,128)(2,1)} %copy-done) | copy-start | bytes 1572868
  127.6 32.3 %copy-start.3 = (bf16[32,64,128]{2,1,0:T(8,128)(2,1)S(1)}, bf16[32,64,128]{2,1,0:T(8,128)(2,1)}, u32[]{:S(2)}) copy-start(bf16[32,64,128]{2,1,0:T(8,128)(2,1)} %copy-done.2) | copy-start | bytes 1572868
  131.2 6.6 %collective-permute-start.27 = (bf16[528,128]{1,0:T(8,128)(2,1)S(1)}, bf16[528,128]{1,0:T(8,128)(2,1)S(1)}, u32[]{:S(2)}, u32[]{:S(2)}) collective-permute-start(bf16[528,128]{1,0:T(8,128)(2,1)S(1)} %softmax_weights.1), channel_id=1, source_target_pairs={{0,8},{1,3},{2,10},{3,5},{4,12},{5,7},{6,14},{7,1},{8,16},{9,11},{... | collective-permute-start | bytes 405512 | tf_op jit(solution)/shard_map/ppermute | solution.py:420
  131.3 6.5 %collective-permute-start.26 = (bf16[528,128]{1,0:T(8,128)(2,1)S(1)}, bf16[528,128]{1,0:T(8,128)(2,1)S(1)}, u32[]{:S(2)}, u32[]{:S(2)}) collective-permute-start(bf16[528,128]{1,0:T(8,128)(2,1)S(1)} %softmax_weights.1), channel_id=1, source_target_pairs={{0,16},{1,5},{2,18},{3,7},{4,20},{5,1},{6,22},{7,3},{8,24},{9,13},... | collective-permute-start | bytes 405512 | tf_op jit(solution)/shard_map/ppermute | solution.py:420
  133.5 5.1 %collective-permute-start.25 = (bf16[528,128]{1,0:T(8,128)(2,1)S(1)}, bf16[528,128]{1,0:T(8,128)(2,1)S(1)}, u32[]{:S(2)}, u32[]{:S(2)}) collective-permute-start(bf16[528,128]{1,0:T(8,128)(2,1)S(1)} %softmax_weights.1), channel_id=1, source_target_pairs={{0,24},{1,7},{2,26},{3,1},{4,28},{5,3},{6,30},{7,5},{8,0},{9,15},{... | collective-permute-start | bytes 405512 | tf_op jit(solution)/shard_map/ppermute | solution.py:420
  138.7 9.3 %collective-permute-start.29 = (bf16[4,528,128]{2,1,0:T(8,128)(2,1)S(1)}, bf16[4,528,128]{2,1,0:T(8,128)(2,1)S(1)}, u32[]{:S(2)}, u32[]{:S(2)}) collective-permute-start(bf16[4,528,128]{2,1,0:T(8,128)(2,1)S(1)} %pad_maximum_fusion.refs_0_), channel_id=1, source_target_pairs={{0,6},{1,25},{2,0},{3,27},{4,2},{5,29},{6,4},{7,31},{8,14},{9,1},{... | collective-permute-start | bytes 1622024 | tf_op jit(solution)/shard_map/ppermute | solution.py:420
  141.8 11.3 %collective-permute-start.28 = (bf16[4,528,128]{2,1,0:T(8,128)(2,1)S(1)}, bf16[4,528,128]{2,1,0:T(8,128)(2,1)S(1)}, u32[]{:S(2)}, u32[]{:S(2)}) collective-permute-start(bf16[4,528,128]{2,1,0:T(8,128)(2,1)S(1)} %pad_maximum_fusion.refs_0_), channel_id=1, source_target_pairs={{0,2},{1,9},{2,4},{3,11},{4,6},{5,13},{6,0},{7,15},{8,10},{9,17},{... | collective-permute-start | bytes 1622024 | tf_op jit(solution)/shard_map/ppermute | solution.py:420
  148.1 9.7 %collective-permute-start.30 = (bf16[4,528,128]{2,1,0:T(8,128)(2,1)S(1)}, bf16[4,528,128]{2,1,0:T(8,128)(2,1)S(1)}, u32[]{:S(2)}, u32[]{:S(2)}) collective-permute-start(bf16[4,528,128]{2,1,0:T(8,128)(2,1)S(1)} %collective-permute-done.29.refs_2_), channel_id=1, source_target_pairs={{0,6},{1,25},{2,0},{3,27},{4,2},{5,29},{6,4},{7,31},{8,14},{9,1},{... | collective-permute-start | bytes 1622024 | tf_op jit(solution)/shard_map/ppermute | solution.py:420
  151.5 9.9 %collective-permute-start.31 = (bf16[4,528,128]{2,1,0:T(8,128)(2,1)S(1)}, bf16[4,528,128]{2,1,0:T(8,128)(2,1)S(1)}, u32[]{:S(2)}, u32[]{:S(2)}) collective-permute-start(bf16[4,528,128]{2,1,0:T(8,128)(2,1)S(1)} %pad_maximum_fusion.refs_0_), channel_id=1, source_target_pairs={{0,1},{1,0},{2,3},{3,2},{4,5},{5,4},{6,7},{7,6},{8,9},{9,8},{10,11... | collective-permute-start | bytes 1622024 | tf_op jit(solution)/shard_map/ppermute | solution.py:420
  153.1 8.3 %collective-permute-start.33 = (bf16[4,528,128]{2,1,0:T(8,128)(2,1)S(1)}, bf16[4,528,128]{2,1,0:T(8,128)(2,1)S(1)}, u32[]{:S(2)}, u32[]{:S(2)}) collective-permute-start(bf16[4,528,128]{2,1,0:T(8,128)(2,1)S(1)} %collective-permute-done.29.refs_2_), channel_id=1, source_target_pairs={{0,1},{1,0},{2,3},{3,2},{4,5},{5,4},{6,7},{7,6},{8,9},{9,8},{10,11... | collective-permute-start | bytes 1622024 | tf_op jit(solution)/shard_map/ppermute | solution.py:420
  153.1 8.3 %collective-permute-start.32 = (bf16[4,528,128]{2,1,0:T(8,128)(2,1)S(1)}, bf16[4,528,128]{2,1,0:T(8,128)(2,1)S(1)}, u32[]{:S(2)}, u32[]{:S(2)}) collective-permute-start(bf16[4,528,128]{2,1,0:T(8,128)(2,1)S(1)} %collective-permute-done.28.refs_1_), channel_id=1, source_target_pairs={{0,1},{1,0},{2,3},{3,2},{4,5},{5,4},{6,7},{7,6},{8,9},{9,8},{10,11... | collective-permute-start | bytes 1622024 | tf_op jit(solution)/shard_map/ppermute | solution.py:420
  157.8 3.7 %collective-permute-start.34 = (bf16[4,528,128]{2,1,0:T(8,128)(2,1)S(1)}, bf16[4,528,128]{2,1,0:T(8,128)(2,1)S(1)}, u32[]{:S(2)}, u32[]{:S(2)}) collective-permute-start(bf16[4,528,128]{2,1,0:T(8,128)(2,1)S(1)} %collective-permute-done.30.refs_3_), channel_id=1, source_target_pairs={{0,1},{1,0},{2,3},{3,2},{4,5},{5,4},{6,7},{7,6},{8,9},{9,8},{10,11... | collective-permute-start | bytes 1622024 | tf_op jit(solution)/shard_map/ppermute | solution.py:420
  171.9 14.7 %collective-permute-start.35 = (bf16[16,128,128]{2,1,0:T(8,128)(2,1)}, bf16[16,128,128]{2,1,0:T(8,128)(2,1)}, u32[]{:S(2)}, u32[]{:S(2)}) collective-permute-start(bf16[16,128,128]{2,1,0:T(8,128)(2,1)} %get-tuple-element.42), channel_id=1, source_target_pairs={{0,32},{32,64},{64,96},{96,0},{1,33},{33,65},{65,97},{97,1},{2,34}... | collective-permute-start | bytes 1572872 | tf_op jit(solution)/shard_map/ppermute | solution.py:407
  171.9 15.9 %collective-permute-start.39 = (bf16[16,128,128]{2,1,0:T(8,128)(2,1)}, bf16[16,128,128]{2,1,0:T(8,128)(2,1)}, u32[]{:S(2)}, u32[]{:S(2)}) collective-permute-start(bf16[16,128,128]{2,1,0:T(8,128)(2,1)} %get-tuple-element.46), channel_id=1, source_target_pairs={{0,96},{32,0},{64,32},{96,64},{1,97},{33,1},{65,33},{97,65},{2,98}... | collective-permute-start | bytes 1572872 | tf_op jit(solution)/shard_map/ppermute | solution.py:407
  174.6 36.0 %all-to-all-start.3 = ((bf16[32,128,128]{2,1,0:T(8,128)(2,1)}), bf16[32,128,128]{2,1,0:T(8,128)(2,1)S(1)}, u32[]{:S(2)}, u32[]{:S(2)}) async-start(bf16[32,128,128]{2,1,0:T(8,128)(2,1)} %get-tuple-element.39), calls=%async_computation.3 | async-start | bytes 2097152 | tf_op jit(solution)/shard_map/all_to_all | solution.py:468
  181.7 15.1 %collective-permute-start.37 = (bf16[16,128,128]{2,1,0:T(8,128)(2,1)}, bf16[16,128,128]{2,1,0:T(8,128)(2,1)S(1)}, u32[]{:S(2)}, u32[]{:S(2)}) collective-permute-start(bf16[16,128,128]{2,1,0:T(8,128)(2,1)} %copy-done.7), channel_id=1, source_target_pairs={{0,96},{32,0},{64,32},{96,64},{1,97},{33,1},{65,33},{97,65},{2,98}... | collective-permute-start | bytes 1572872 | tf_op jit(solution)/shard_map/ppermute | solution.py:407
  181.8 15.9 %collective-permute-start.38 = (bf16[16,128,128]{2,1,0:T(8,128)(2,1)}, bf16[16,128,128]{2,1,0:T(8,128)(2,1)S(1)}, u32[]{:S(2)}, u32[]{:S(2)}) collective-permute-start(bf16[16,128,128]{2,1,0:T(8,128)(2,1)} %copy-done.6), channel_id=1, source_target_pairs={{0,32},{32,64},{64,96},{96,0},{1,33},{33,65},{65,97},{97,1},{2,34}... | collective-permute-start | bytes 1572872 | tf_op jit(solution)/shard_map/ppermute | solution.py:407
  187.8 21.2 %collective-permute-start.36 = (bf16[16,128,128]{2,1,0:T(8,128)(2,1)S(1)}, bf16[16,128,128]{2,1,0:T(8,128)(2,1)S(1)}, u32[]{:S(2)}, u32[]{:S(2)}) collective-permute-start(bf16[16,128,128]{2,1,0:T(8,128)(2,1)S(1)} %add_convert_fusion.1), channel_id=1, source_target_pairs={{0,32},{32,64},{64,96},{96,0},{1,33},{33,65},{65,97},{97,1},{2,34}... | collective-permute-start | bytes 1572872 | tf_op jit(solution)/shard_map/ppermute | solution.py:407
  189.0 19.9 %collective-permute-start.40 = (bf16[16,128,128]{2,1,0:T(8,128)(2,1)S(1)}, bf16[16,128,128]{2,1,0:T(8,128)(2,1)S(1)}, u32[]{:S(2)}, u32[]{:S(2)}) collective-permute-start(bf16[16,128,128]{2,1,0:T(8,128)(2,1)S(1)} %add_convert_fusion), channel_id=1, source_target_pairs={{0,96},{32,0},{64,32},{96,64},{1,97},{33,1},{65,33},{97,65},{2,98}... | collective-permute-start | bytes 1572872 | tf_op jit(solution)/shard_map/ppermute | solution.py:407
  210.6 24.3 %all-to-all-start.4 = ((bf16[32,128,128]{2,1,0:T(8,128)(2,1)}), bf16[32,128,128]{2,1,0:T(8,128)(2,1)S(1)}, u32[]{:S(2)}, u32[]{:S(2)}) async-start(bf16[32,128,128]{2,1,0:T(8,128)(2,1)} %join.1), calls=%async_computation.4 | async-start | bytes 2097152 | tf_op jit(solution)/shard_map/all_to_all | solution.py:468
  (7 other events, 90.1 us)

commit v5 on v4

--- a/solution.py
+++ b/solution.py
@@ -88,22 +88,15 @@
     )(*given)
 
 
-def unpack_kernel(x, out, xv, outv, sems):
-    number = x.shape[0] // PARTS
-    loads, stores = [], []
+def unpack_kernel(x, out, outv, sems):
+    copies = []
     for n in range(PARTS):
-        part = slice(n * number, (n + 1) * number)
-        loads.append(pltpu.make_async_copy(x.at[part], xv.at[part], sems.at[n]))
-        cols = slice(n * number * 128, (n + 1) * number * 128)
-        stores.append(pltpu.make_async_copy(outv.at[:, cols], out.at[:, cols], sems.at[PARTS + n]))
-    for copy in loads:
-        copy.start()
-    for n in range(PARTS):
-        loads[n].wait()
-        for m in range(n * number, (n + 1) * number):
-            outv[:, 128 * m : 128 * m + 128] = xv[m].astype(jnp.float32)
-        stores[n].start()
-    for copy in stores:
+        rows = slice(n * BLK // PARTS, (n + 1) * BLK // PARTS)
+        for m in range(x.shape[0]):
+            outv[rows, 128 * m : 128 * m + 128] = x[m, rows, :].astype(jnp.float32)
+        copies.append(pltpu.make_async_copy(outv.at[rows, :], out.at[rows, :], sems.at[n]))
+        copies[n].start()
+    for copy in copies:
         copy.wait()
 
 
@@ -111,13 +104,12 @@
     number = x.shape[0]
     return pl.pallas_call(
         unpack_kernel,
-        in_specs=[ANY],
+        in_specs=[VMEM],
         out_specs=ANY,
         out_shape=jax.ShapeDtypeStruct((BLK, number * 128), jnp.float32),
         scratch_shapes=[
-            pltpu.VMEM(x.shape, x.dtype),
             pltpu.VMEM((BLK, number * 128), jnp.float32),
-            pltpu.SemaphoreType.DMA((2 * PARTS,)),
+            pltpu.SemaphoreType.DMA((PARTS,)),
         ],
         **params(5, 8 * MIB),
         name="unpack",
@@ -280,79 +272,118 @@
     )(at, *terms, lists, q)
 
 
-def grad_kernel(ids, own, at, q, p, *refs):
-    parts, outs, gq, loss = refs[:8], refs[8:15], *refs[15:17]
-    wv, gq_sum, gp_sum = refs[17:]
-    core = at[0]
-
-    @pl.loop(0, gq_sum.shape[0])
+GATHERED = tuple((other, (0, 1, 2, 3)) for other in (0, 3, 1, 2))
+
+
+def weight_spots(at, n, parts):
+    side = jnp.where(at[0] == n, 0, 1)
+    spots = []
+    for m, (other, leads) in enumerate(GATHERED):
+        for e, lead in enumerate(leads):
+            spots.append((parts[len(GATHERED) * n + m], e, chip_at(at, side, lead, other)))
+    return side * PART, spots
+
+
+def for_pairs(spots, wv, use):
+    @pl.loop(0, PART // STEP)
+    def _(step):
+        for v in range(STEP // 2):
+            where = pl.ds(pl.multiple_of(8 * STEP * step + 16 * v, 16), 16)
+            for piece, e, chip in spots:
+                wv[v, chip] = piece[e, where, :]
+            two = wv[v].astype(jnp.float32)
+            for o in range(2):
+                tile = two[:, 8 * o : 8 * o + 8, :].reshape(BLK, 128).astype(jnp.bfloat16)
+                use(step * STEP + 2 * v + o, tile)
+
+
+def clear(total):
+    @pl.loop(0, total.shape[0] // 4)
     def _(n):
-        gq_sum[n] = jnp.zeros((BLK, 128), jnp.float32)
         for m in range(4):
-            gp_sum[4 * n + m] = jnp.zeros((BLK, 128), jnp.float32)
-
-    loss[...] = jnp.zeros(loss.shape, jnp.float32)
-    line = lax.broadcasted_iota(jnp.int32, (TAIL, 128), 0) // 3
-    mine = line == at[3] // 16
+            total[4 * n + m] = jnp.zeros((BLK, 128), jnp.float32)
+
+
+def grad_p_kernel(ids, own, at, q, *refs):
+    parts, outs, loss, wv, total = refs[:8], refs[8:15], *refs[15:]
+    clear(total)
+    mine = lax.broadcasted_iota(jnp.int32, (TAIL, 128), 0) // 3 == at[3] // 16
     for n in range(2):
-        side = jnp.where(core == n, 0, 1)
-        spots = []
-        for m in range(4):
-            for lead in range(4):
-                chip = chip_at(at, side, lead, (0, 3, 1, 2)[m])
-                spots.append((4 * n + m, lead, chip))
-                tail = parts[4 * n + m][lead, ROWS:, :].astype(jnp.float32)
-                loss[pl.ds(chip, 1), :] += jnp.sum(
-                    jnp.where(mine, tail, 0.0), axis=0, keepdims=True
-                )
-
-        @pl.loop(0, PART // STEP)
-        def _(step):
-            for v in range(STEP // 2):
-                where = pl.ds(pl.multiple_of(8 * STEP * step + 16 * v, 16), 16)
-                for m, lead, chip in spots:
-                    wv[v, chip] = parts[m][lead, where, :]
-                two = wv[v].astype(jnp.float32)
-                for o in range(2):
-                    t = side * PART + step * STEP + 2 * v + o
-                    here, there = own[t], ids[t]
-                    tile = two[:, 8 * o : 8 * o + 8, :].reshape(BLK, 128).astype(jnp.bfloat16)
-                    gq_sum[here] += jnp.dot(tile, p[there], preferred_element_type=jnp.float32)
-                    gp_sum[there] += lax.dot_general(
-                        tile,
-                        q[here, 0:BLK, :],
-                        (((0,), (0,)), ((), ())),
-                        preferred_element_type=jnp.float32,
-                    )
+        start, spots = weight_spots(at, n, parts)
+        for piece, e, chip in spots:
+            tail = jnp.where(mine, piece[e, ROWS:, :].astype(jnp.float32), 0.0)
+            line = jnp.sum(tail, axis=0, keepdims=True)
+            row = pl.ds(chip, 1)
+            loss[row, :] = line if n == 0 else loss[row, :] + line
+
+        def use(k, tile):
+            total[ids[start + k]] += lax.dot_general(
+                tile,
+                q[own[start + k], 0:BLK, :],
+                (((0,), (0,)), ((), ())),
+                preferred_element_type=jnp.float32,
+            )
+
+        for_pairs(spots, wv, use)
 
     @pl.loop(0, 16)
     def _(n):
         for m, (first, size) in enumerate(PIECES):
             for e in range(size // 16):
-                outs[m][16 * e + n] = gp_sum[first + 16 * e + n].astype(jnp.bfloat16)
-        for e in range(2):
-            gq[16 * e + n] = gq_sum[16 * e + n].astype(jnp.bfloat16)
+                outs[m][16 * e + n] = total[first + 16 * e + n].astype(jnp.bfloat16)
 
     loss[...] = pltpu.roll(loss[...], (128 - 8 * (at[3] % 16)) % 128, 1)
 
 
-def gradients(ids, own, at, q, p, parts):
-    nblk = q.shape[0]
-    shapes = [(size, BLK, 128) for _, size in PIECES] + [(nblk, BLK, 128)]
-    return pl.pallas_call(
-        grad_kernel,
-        in_specs=[SMEM] * 3 + [VMEM] * 10,
-        out_specs=[VMEM] * 9,
-        out_shape=[jax.ShapeDtypeStruct(s, jnp.bfloat16) for s in shapes]
-        + [jax.ShapeDtypeStruct((BLK // 8, 128), jnp.float32)],
+def grad_passages(ids, own, at, q, parts):
+    shapes = [jax.ShapeDtypeStruct((size, BLK, 128), jnp.bfloat16) for _, size in PIECES]
+    return pl.pallas_call(
+        grad_p_kernel,
+        in_specs=[SMEM] * 3 + [VMEM] * 9,
+        out_specs=[VMEM] * 8,
+        out_shape=shapes + [jax.ShapeDtypeStruct((BLK // 8, 128), jnp.float32)],
+        scratch_shapes=[
+            pltpu.VMEM((STEP // 2, BLK // 8, 16, 128), jnp.bfloat16),
+            pltpu.VMEM((PAIRS, BLK, 128), jnp.float32),
+        ],
+        **params(20, 20 * MIB),
+        name="grad_passages",
+    )(ids, own, at, q, *parts)
+
+
+def grad_q_kernel(ids, own, at, p, *refs):
+    parts, out, wv, total = refs[:8], *refs[8:]
+    clear(total)
+    for n in range(2):
+        start, spots = weight_spots(at, n, parts)
+
+        def use(k, tile):
+            total[own[start + k]] += jnp.dot(
+                tile, p[ids[start + k]], preferred_element_type=jnp.float32
+            )
+
+        for_pairs(spots, wv, use)
+
+    @pl.loop(0, total.shape[0] // 4)
+    def _(n):
+        for m in range(4):
+            out[4 * n + m] = total[4 * n + m].astype(jnp.bfloat16)
+
+
+def grad_queries(ids, own, at, p, parts):
+    nblk = p.shape[0] // 4
+    return pl.pallas_call(
+        grad_q_kernel,
+        in_specs=[SMEM] * 3 + [VMEM] * 9,
+        out_specs=VMEM,
+        out_shape=jax.ShapeDtypeStruct((nblk, BLK, 128), jnp.bfloat16),
         scratch_shapes=[
             pltpu.VMEM((STEP // 2, BLK // 8, 16, 128), jnp.bfloat16),
             pltpu.VMEM((nblk, BLK, 128), jnp.float32),
-            pltpu.VMEM((4 * nblk, BLK, 128), jnp.float32),
-        ],
-        **params(27, 32 * MIB),
-        name="gradients",
-    )(ids, own, at, q, p, *parts)
+        ],
+        **params(14, 20 * MIB),
+        name="grad_queries",
+    )(ids, own, at, p, *parts)
 
 
 def join_kernel(*refs):
@@ -496,10 +527,12 @@
 
     scores = scatter_scores(partial_scores(ids, own, at, q, pieces + others))
     weights = softmax_weights(at, (scores, flip(scores)), lists, q_own, width ** (-0.5))
-    *g, gq, lines = gradients(ids, own, at, q_own, place(pieces), gather_weights(weights))
+    parts = gather_weights(weights)
+    q_own, mine = lax.optimization_barrier((q_own, place(pieces)))
+    *g, lines = grad_passages(ids, own, at, q_own, parts)
 
     low, high = ring_terms("z", g[1:3], g[3:5], g[5:7])
-    q_rows = by_rows(exchange(gq))
+    q_rows = by_rows(exchange(grad_queries(ids, own, at, mine, parts)))
     p_rows = by_rows(exchange(join(g[0], low, high)))
     return lines[:, 0:8].reshape(BLK), q_rows, p_rows
 

time: 239 us -> 240 us (level)
  Pallas kernels: 32.5 us -> 35.7 us
    ppermute x12, waiting for transfers between devices: 32 us -> 28 us  [along(): return lambda v: lax.ppermute(v, 'grp', perm)]
    pallas_call x3 -> x4, Pallas kernels: 14.3 us -> 16.7 us  [the longest x1 7.85 us: grad_passages(): pl.pallas_call(grad_p_kernel, in_specs=[SMEM] * 3 + [VMEM] * 9, out_specs...]
  transfers between devices with their start and end apart: 45 -> 45, of which waited for: 24 -> 22; matrix products, arithmetic and copies ran while one was open for 2% -> 2% of each run, Pallas kernels for 3% -> 5%
where the time goes in v5:
time: 240 us; the launch traced here: 239 us
  waiting for transfers between devices  105 us (44%)
  starting transfers between devices  69.5 us (29%)
  Pallas kernels  35.7 us (15%)
  blocking collectives  20.2 us (8%)
  local copies, waits for them, and re-layouts  4.34 us (2%)
  other arithmetic  3.32 us (1%)
    ppermute x29, waiting for transfers between devices, along(): return lambda v: lax.ppermute(v, 'dev', perm)  38.5 us
    all_to_all x4, waiting for transfers between devices, exchange(): return lax.all_to_all(v, 'dev', 0, 0, tiled=True)  38.3 us
    ppermute x29, starting transfers between devices, along(): return lambda v: lax.ppermute(v, 'dev', perm)  32.1 us
    ppermute x12, waiting for transfers between devices, along(): return lambda v: lax.ppermute(v, 'grp', perm)  28 us
    all_to_all x4, starting transfers between devices, exchange(): return lax.all_to_all(v, 'dev', 0, 0, tiled=True)  21.4 us
    all_to_all x1, blocking collectives, exchange(): return lax.all_to_all(v, 'dev', 0, 0, tiled=True)  20.2 us
    ppermute x12, starting transfers between devices, along(): return lambda v: lax.ppermute(v, 'grp', perm)  16 us
    pallas_call x1, Pallas kernels, grad_passages(): pl.pallas_call(grad_p_kernel, in_specs=[SMEM] * 3 + [VMEM] * 9, out_specs...  7.85 us
  transfers between devices with their start and end apart: 45, of which 22 were waited for; matrix products, arithmetic and copies ran while one was open for 2% of the time, Pallas kernels for 5%

profile of v5, /device:TPU:1, one launch (start us, length us, event | category | flops | bytes accessed | tf_op | source)
XLA Modules:
  0.0 239.0 jit_solution(13410237327092299509)
XLA Ops:
  0.6 2.4 %pack.3 = (bf16[32,64,128]{2,1,0:T(8,128)(2,1)}, bf16[32,64,128]{2,1,0:T(8,128)(2,1)}) custom-call(f32[128,4096]{1,0:T(8,128)} %x.7), custom_call_target="tpu_custom_call" | custom-call | bytes 5242880 | tf_op jit(solution)/shard_map/pack/pallas_call | solution.py:75
  3.0 20.2 %all_to_all.25.refs_0_ = bf16[32,64,128]{2,1,0:T(8,128)(2,1)S(1)} all-to-all(bf16[32,64,128]{2,1,0:T(8,128)(2,1)} %get-tuple-element.27), channel_id=1, replica_groups=mesh['grp'=4,'dev'=32] {'dev'}, dimensions={0} | all-to-all | bytes 1048576 | tf_op jit(solution)/shard_map/all_to_all | solution.py:499
  23.3 3.8 %collective-permute-start = (bf16[32,64,128]{2,1,0:T(8,128)(2,1)S(1)}, bf16[32,64,128]{2,1,0:T(8,128)(2,1)S(1)}, u32[]{:S(2)}, u32[]{:S(2)}) collective-permute-start(bf16[32,64,128]{2,1,0:T(8,128)(2,1)S(1)} %all_to_all.25.refs_0_), channel_id=1, source_target_pairs={{0,96},{32,0},{64,32},{96,64},{1,97},{33,1},{65,33},{97,65},{2,98}... | collective-permute-start | bytes 1572872 | tf_op jit(solution)/shard_map/ppermute | solution.py:438
  27.0 3.9 %all-to-all-start = ((bf16[32,64,128]{2,1,0:T(8,128)(2,1)}), bf16[32,64,128]{2,1,0:T(8,128)(2,1)S(1)}, u32[]{:S(2)}, u32[]{:S(2)}) async-start(bf16[32,64,128]{2,1,0:T(8,128)(2,1)} %get-tuple-element.26), calls=%async_computation | async-start | bytes 1048576 | tf_op jit(solution)/shard_map/all_to_all | solution.py:499
  31.0 1.6 copy-done.4
  33.9 8.6 %all-to-all-done.refs_1_ = bf16[32,64,128]{2,1,0:T(8,128)(2,1)S(1)} async-done(((bf16[32,64,128]{2,1,0:T(8,128)(2,1)}), bf16[32,64,128]{2,1,0:T(8,128)(2,1)S(1)}, u32[]{:S(2)}, u32[]{:S(2)}) %all-to-all-start) | async-done | bytes 524320 | tf_op jit(solution)/shard_map/all_to_all | solution.py:499
  42.6 3.7 %all-to-all-start.2 = ((bf16[32,144,128]{2,1,0:T(8,128)(2,1)}), bf16[32,144,128]{2,1,0:T(8,128)(2,1)S(1)}, u32[]{:S(2)}, u32[]{:S(2)}) async-start(bf16[32,144,128]{2,1,0:T(8,128)(2,1)} %pack.2), calls=%async_computation.2 | async-start | bytes 2359296 | tf_op jit(solution)/shard_map/all_to_all | solution.py:499
  46.3 3.0 %collective-permute-start.2 = (bf16[32,64,128]{2,1,0:T(8,128)(2,1)S(1)}, bf16[32,64,128]{2,1,0:T(8,128)(2,1)}, u32[]{:S(2)}, u32[]{:S(2)}) collective-permute-start(bf16[32,64,128]{2,1,0:T(8,128)(2,1)S(1)} %all-to-all-done.refs_1_), channel_id=1, source_target_pairs={{0,96},{32,0},{64,32},{96,64},{1,97},{33,1},{65,33},{97,65},{2,98}... | collective-permute-start | bytes 1572872 | tf_op jit(solution)/shard_map/ppermute | solution.py:438
  49.8 14.8 %all-to-all-done.2.q_own.refs_3_.q = bf16[32,144,128]{2,1,0:T(8,128)(2,1)S(1)} async-done(((bf16[32,144,128]{2,1,0:T(8,128)(2,1)}), bf16[32,144,128]{2,1,0:T(8,128)(2,1)S(1)}, u32[]{:S(2)}, u32[]{:S(2)}) %all-to-all-start.2) | async-done | bytes 1179680 | tf_op jit(solution)/shard_map/all_to_all | solution.py:499
  65.7 2.9 %collective-permute-start.4 = (bf16[32,64,128]{2,1,0:T(8,128)(2,1)S(1)}, bf16[32,64,128]{2,1,0:T(8,128)(2,1)S(1)}, u32[]{:S(2)}, u32[]{:S(2)}) collective-permute-start(bf16[32,64,128]{2,1,0:T(8,128)(2,1)S(1)} %collective-permute-done.refs_2_), channel_id=1, source_target_pairs={{0,96},{32,0},{64,32},{96,64},{1,97},{33,1},{65,33},{97,65},{2,98}... | collective-permute-start | bytes 1572872 | tf_op jit(solution)/shard_map/ppermute | solution.py:438
  69.6 10.0 %collective-permute-done.4.refs_4_ = bf16[32,64,128]{2,1,0:T(8,128)(2,1)S(1)} collective-permute-done((bf16[32,64,128]{2,1,0:T(8,128)(2,1)S(1)}, bf16[32,64,128]{2,1,0:T(8,128)(2,1)S(1)}, u32[]{:S(2)}, u32[]{:S(2)}) %collective-permute-start.4) | collective-permute-done | bytes 524320 | tf_op jit(solution)/shard_map/ppermute | solution.py:438
  80.7 2.2 collective-permute-done.5.refs_5_
  83.0 1.4 collective-permute-start.12
  85.9 7.8 %partial_scores.1 = (f32[2,512,128]{2,1,0:T(8,128)S(1)}, f32[2,512,128]{2,1,0:T(8,128)S(1)}, f32[2,512,128]{2,1,0:T(8,128)S(1)}, f32[2,512,128]{2,1,0:T(8,128)S(...) custom-call(s32[128]{0:T(128)S(1)} %and_select_fusion.ids, ...), custom_call_target="tpu_custom_call" | custom-call | bytes 20971520 | tf_op jit(solution)/shard_map/partial_scores/pallas_call | solution.py:188
  93.8 2.7 %collective-permute-start.20 = (f32[2,512,128]{2,1,0:T(8,128)S(1)}, f32[2,512,128]{2,1,0:T(8,128)S(1)}, u32[]{:S(2)}, u32[]{:S(2)}) collective-permute-start(f32[2,512,128]{2,1,0:T(8,128)S(1)} %get-tuple-element.39), channel_id=1, source_target_pairs={{0,24},{1,7},{2,26},{3,1},{4,28},{5,3},{6,30},{7,5},{8,0},{9,15},{... | collective-permute-start | bytes 1572872 | tf_op jit(solution)/shard_map/ppermute | solution.py:451
  96.5 1.4 collective-permute-start.19
  97.9 5.4 %collective-permute-done.15 = f32[2,512,128]{2,1,0:T(8,128)S(1)} collective-permute-done((f32[2,512,128]{2,1,0:T(8,128)S(1)}, f32[2,512,128]{2,1,0:T(8,128)S(1)}, u32[]{:S(2)}, u32[]{:S(2)}) %collective-permute-start.15) | collective-permute-done | bytes 524320 | tf_op jit(solution)/shard_map/ppermute | solution.py:451
  103.5 2.7 %collective-permute-start.21 = (f32[2,512,128]{2,1,0:T(8,128)S(1)}, f32[2,512,128]{2,1,0:T(8,128)S(1)}, u32[]{:S(2)}, u32[]{:S(2)}) collective-permute-start(f32[2,512,128]{2,1,0:T(8,128)S(1)} %add.108), channel_id=1, source_target_pairs={{0,24},{1,7},{2,26},{3,1},{4,28},{5,3},{6,30},{7,5},{8,0},{9,15},{... | collective-permute-start | bytes 1572872 | tf_op jit(solution)/shard_map/ppermute | solution.py:451
  106.2 1.9 collective-permute-done.17
  108.9 5.6 %collective-permute-done.16 = f32[2,512,128]{2,1,0:T(8,128)S(1)} collective-permute-done((f32[2,512,128]{2,1,0:T(8,128)S(1)}, f32[2,512,128]{2,1,0:T(8,128)S(1)}, u32[]{:S(2)}, u32[]{:S(2)}) %collective-permute-start.16) | collective-permute-done | bytes 524320 | tf_op jit(solution)/shard_map/ppermute | solution.py:451
  114.8 2.3 collective-permute-start.22
  117.6 6.7 %collective-permute-done.18 = f32[512,128]{1,0:T(8,128)S(1)} collective-permute-done((f32[512,128]{1,0:T(8,128)S(1)}, f32[512,128]{1,0:T(8,128)S(1)}, u32[]{:S(2)}, u32[]{:S(2)}) %collective-permute-start.18) | collective-permute-done | bytes 262176 | tf_op jit(solution)/shard_map/ppermute | solution.py:451
  125.1 2.6 %collective-permute-start.24 = (f32[512,128]{1,0:T(8,128)S(1)}, f32[512,128]{1,0:T(8,128)}, u32[]{:S(2)}, u32[]{:S(2)}) collective-permute-start(f32[512,128]{1,0:T(8,128)S(1)} %fusion.6.refs_0_), channel_id=1, source_target_pairs={{0,1},{1,0},{2,3},{3,2},{4,5},{5,4},{6,7},{7,6},{8,9},{9,8},{10,11... | collective-permute-start | bytes 786440 | tf_op jit(solution)/shard_map/ppermute | solution.py:451
  129.6 3.5 %softmax_weights.1 = bf16[528,128]{1,0:T(8,128)(2,1)S(1)} custom-call(s32[5]{0:T(128)S(1)} %stack.53.at, f32[512,128]{1,0:T(8,128)S(1)} %fusion.6.refs_0_, f32[512,128]{1,0:T(8,128)} %collective-permute-done.24.refs_1_, s32[8,128]{1,0:T(8,128)S(1)} %stack.56.refs_2_, bf16[32,144,128]{2,1,0:T(8,128)(2,1)S(1)} %all-to-all-done.2.q_own.refs_3_.q), custom_call_target="tpu_custom_call" | custom-call | bytes 8388608 | tf_op jit(solution)/shard_map/softmax_weights/pallas_call | solution.py:259
  133.1 2.4 %collective-permute-start.25 = (bf16[528,128]{1,0:T(8,128)(2,1)S(1)}, bf16[528,128]{1,0:T(8,128)(2,1)S(1)}, u32[]{:S(2)}, u32[]{:S(2)}) collective-permute-start(bf16[528,128]{1,0:T(8,128)(2,1)S(1)} %softmax_weights.1), channel_id=1, source_target_pairs={{0,24},{1,7},{2,26},{3,1},{4,28},{5,3},{6,30},{7,5},{8,0},{9,15},{... | collective-permute-start | bytes 405512 | tf_op jit(solution)/shard_map/ppermute | solution.py:451
  136.2 2.7 %collective-permute-done.25 = bf16[528,128]{1,0:T(8,128)(2,1)S(1)} collective-permute-done((bf16[528,128]{1,0:T(8,128)(2,1)S(1)}, bf16[528,128]{1,0:T(8,128)(2,1)S(1)}, u32[]{:S(2)}, u32[]{:S(2)}) %collective-permute-start.25) | collective-permute-done | bytes 135200 | tf_op jit(solution)/shard_map/ppermute | solution.py:451
  138.9 2.3 collective-permute-done.26
  142.6 2.7 %collective-permute-start.29 = (bf16[4,528,128]{2,1,0:T(8,128)(2,1)S(1)}, bf16[4,528,128]{2,1,0:T(8,128)(2,1)S(1)}, u32[]{:S(2)}, u32[]{:S(2)}) collective-permute-start(bf16[4,528,128]{2,1,0:T(8,128)(2,1)S(1)} %pad_maximum_fusion.refs_0_), channel_id=1, source_target_pairs={{0,6},{1,25},{2,0},{3,27},{4,2},{5,29},{6,4},{7,31},{8,14},{9,1},{... | collective-permute-start | bytes 1622024 | tf_op jit(solution)/shard_map/ppermute | solution.py:451
  145.3 6.3 %collective-permute-done.29.refs_2_ = bf16[4,528,128]{2,1,0:T(8,128)(2,1)S(1)} collective-permute-done((bf16[4,528,128]{2,1,0:T(8,128)(2,1)S(1)}, bf16[4,528,128]{2,1,0:T(8,128)(2,1)S(1)}, u32[]{:S(2)}, u32[]{:S(2)}) %collective-permute-start.29) | collective-permute-done | bytes 540704 | tf_op jit(solution)/shard_map/ppermute | solution.py:451
  151.6 3.4 %collective-permute-start.30 = (bf16[4,528,128]{2,1,0:T(8,128)(2,1)S(1)}, bf16[4,528,128]{2,1,0:T(8,128)(2,1)S(1)}, u32[]{:S(2)}, u32[]{:S(2)}) collective-permute-start(bf16[4,528,128]{2,1,0:T(8,128)(2,1)S(1)} %collective-permute-done.29.refs_2_), channel_id=1, source_target_pairs={{0,6},{1,25},{2,0},{3,27},{4,2},{5,29},{6,4},{7,31},{8,14},{9,1},{... | collective-permute-start | bytes 1622024 | tf_op jit(solution)/shard_map/ppermute | solution.py:451
  155.0 2.4 %collective-permute-start.31 = (bf16[4,528,128]{2,1,0:T(8,128)(2,1)S(1)}, bf16[4,528,128]{2,1,0:T(8,128)(2,1)S(1)}, u32[]{:S(2)}, u32[]{:S(2)}) collective-permute-start(bf16[4,528,128]{2,1,0:T(8,128)(2,1)S(1)} %pad_maximum_fusion.refs_0_), channel_id=1, source_target_pairs={{0,1},{1,0},{2,3},{3,2},{4,5},{5,4},{6,7},{7,6},{8,9},{9,8},{10,11... | collective-permute-start | bytes 1622024 | tf_op jit(solution)/shard_map/ppermute | solution.py:451
  158.0 3.4 %collective-permute-done.30.refs_3_ = bf16[4,528,128]{2,1,0:T(8,128)(2,1)S(1)} collective-permute-done((bf16[4,528,128]{2,1,0:T(8,128)(2,1)S(1)}, bf16[4,528,128]{2,1,0:T(8,128)(2,1)S(1)}, u32[]{:S(2)}, u32[]{:S(2)}) %collective-permute-start.30) | collective-permute-done | bytes 540704 | tf_op jit(solution)/shard_map/ppermute | solution.py:451
  161.3 3.0 %collective-permute-start.34 = (bf16[4,528,128]{2,1,0:T(8,128)(2,1)S(1)}, bf16[4,528,128]{2,1,0:T(8,128)(2,1)S(1)}, u32[]{:S(2)}, u32[]{:S(2)}) collective-permute-start(bf16[4,528,128]{2,1,0:T(8,128)(2,1)S(1)} %collective-permute-done.30.refs_3_), channel_id=1, source_target_pairs={{0,1},{1,0},{2,3},{3,2},{4,5},{5,4},{6,7},{7,6},{8,9},{9,8},{10,11... | collective-permute-start | bytes 1622024 | tf_op jit(solution)/shard_map/ppermute | solution.py:451
  164.3 1.4 place.1.p
  165.9 7.8 %grad_passages.1 = (bf16[32,128,128]{2,1,0:T(8,128)(2,1)S(1)}, bf16[16,128,128]{2,1,0:T(8,128)(2,1)S(1)}, bf16[16,128,128]{2,1,0:T(8,128)(2,1)}, bf16[16,128,128...) custom-call(s32[128]{0:T(128)S(1)} %and_select_fusion.ids, ...), custom_call_target="tpu_custom_call" | custom-call | bytes 20971520 | tf_op jit(solution)/shard_map/grad_passages/pallas_call | solution.py:340
  175.2 1.7 collective-permute-start.37
  176.9 6.1 %grad_queries.1 = bf16[32,128,128]{2,1,0:T(8,128)(2,1)} custom-call(s32[128]{0:T(128)S(1)} %and_select_fusion.ids, s32[128]{0:T(128)S(1)} %convert_reduce_fusion.own, s32[5]{0:T(128)S(1)} %stack.53.at, bf16[128,128,128]{2,1,0:T(8,128)(2,1)S(1)} %place.1.p, bf16[4,528,128]{2,1,0:T(8,128)(2,1)S(1)} %pad_maximum_fusion.refs_0_, ...), custom_call_target="tpu_custom_call" | custom-call | bytes 20971520 | tf_op jit(solution)/shard_map/grad_queries/pallas_call | solution.py:375
  183.0 6.7 %all-to-all-start.3 = ((bf16[32,128,128]{2,1,0:T(8,128)(2,1)}), bf16[32,128,128]{2,1,0:T(8,128)(2,1)S(1)}, u32[]{:S(2)}, u32[]{:S(2)}) async-start(bf16[32,128,128]{2,1,0:T(8,128)(2,1)} %grad_queries.1), calls=%async_computation.3 | async-start | bytes 2097152 | tf_op jit(solution)/shard_map/all_to_all | solution.py:499
  190.9 3.0 %collective-permute-start.40 = (bf16[16,128,128]{2,1,0:T(8,128)(2,1)S(1)}, bf16[16,128,128]{2,1,0:T(8,128)(2,1)S(1)}, u32[]{:S(2)}, u32[]{:S(2)}) collective-permute-start(bf16[16,128,128]{2,1,0:T(8,128)(2,1)S(1)} %add_convert_fusion), channel_id=1, source_target_pairs={{0,96},{32,0},{64,32},{96,64},{1,97},{33,1},{65,33},{97,65},{2,98}... | collective-permute-start | bytes 1572872 | tf_op jit(solution)/shard_map/ppermute | solution.py:438
  195.2 3.2 %collective-permute-done.37.refs_2_ = bf16[16,128,128]{2,1,0:T(8,128)(2,1)} collective-permute-done((bf16[16,128,128]{2,1,0:T(8,128)(2,1)}, bf16[16,128,128]{2,1,0:T(8,128)(2,1)}, u32[]{:S(2)}, u32[]{:S(2)}) %collective-permute-start.37) | collective-permute-done | bytes 524320 | tf_op jit(solution)/shard_map/ppermute | solution.py:438
  198.4 1.4 collective-permute-done.38.refs_3_
  199.8 9.7 %collective-permute-done.40.refs_4_ = bf16[16,128,128]{2,1,0:T(8,128)(2,1)S(1)} collective-permute-done((bf16[16,128,128]{2,1,0:T(8,128)(2,1)S(1)}, bf16[16,128,128]{2,1,0:T(8,128)(2,1)S(1)}, u32[]{:S(2)}, u32[]{:S(2)}) %collective-permute-start.40) | collective-permute-done | bytes 524320 | tf_op jit(solution)/shard_map/ppermute | solution.py:438
  209.6 1.4 collective-permute-done.36.refs_1_
  211.0 2.5 %join.1 = bf16[32,128,128]{2,1,0:T(8,128)(2,1)} custom-call(bf16[32,128,128]{2,1,0:T(8,128)(2,1)S(1)} %get-tuple-element.42.refs_0_, bf16[16,128,128]{2,1,0:T(8,128)(2,1)S(1)} %collective-permute-done.36.refs_1_, bf16[16,128,128]{2,1,0:T(8,128)(2,1)} %collective-permute-done.37.refs_2_, bf16[16,128,128]{2,1,0:T(8,128)(2,1)} %collective-permute-done.38.refs_3_, ...), custom_call_target="tpu_custom_call" | custom-call | bytes 8388608 | tf_op jit(solution)/shard_map/join/pallas_call | solution.py:418
  213.5 7.1 %all-to-all-start.4 = ((bf16[32,128,128]{2,1,0:T(8,128)(2,1)}), bf16[32,128,128]{2,1,0:T(8,128)(2,1)S(1)}, u32[]{:S(2)}, u32[]{:S(2)}) async-start(bf16[32,128,128]{2,1,0:T(8,128)(2,1)} %join.1), calls=%async_computation.4 | async-start | bytes 2097152 | tf_op jit(solution)/shard_map/all_to_all | solution.py:499
  221.1 1.4 unpack.2
  222.5 14.9 %all-to-all-done.4.x = bf16[32,128,128]{2,1,0:T(8,128)(2,1)S(1)} async-done(((bf16[32,128,128]{2,1,0:T(8,128)(2,1)}), bf16[32,128,128]{2,1,0:T(8,128)(2,1)S(1)}, u32[]{:S(2)}, u32[]{:S(2)}) %all-to-all-start.4) | async-done | bytes 1048608 | tf_op jit(solution)/shard_map/all_to_all | solution.py:499
  237.5 1.4 unpack.3
  (91 shorter events, 18.2 us)
Async XLA Ops:
  23.3 19.3 %collective-permute-start = (bf16[32,64,128]{2,1,0:T(8,128)(2,1)S(1)}, bf16[32,64,128]{2,1,0:T(8,128)(2,1)S(1)}, u32[]{:S(2)}, u32[]{:S(2)}) collective-permute-start(bf16[32,64,128]{2,1,0:T(8,128)(2,1)S(1)} %all_to_all.25.refs_0_), channel_id=1, source_target_pairs={{0,96},{32,0},{64,32},{96,64},{1,97},{33,1},{65,33},{97,65},{2,98}... | collective-permute-start | bytes 1572872 | tf_op jit(solution)/shard_map/ppermute | solution.py:438
  27.0 15.5 %collective-permute-start.1 = (bf16[32,64,128]{2,1,0:T(8,128)(2,1)S(1)}, bf16[32,64,128]{2,1,0:T(8,128)(2,1)S(1)}, u32[]{:S(2)}, u32[]{:S(2)}) collective-permute-start(bf16[32,64,128]{2,1,0:T(8,128)(2,1)S(1)} %all_to_all.25.refs_0_), channel_id=1, source_target_pairs={{0,32},{32,64},{64,96},{96,0},{1,33},{33,65},{65,97},{97,1},{2,34}... | collective-permute-start | bytes 1572872 | tf_op jit(solution)/shard_map/ppermute | solution.py:438
  27.0 15.5 %all-to-all-start = ((bf16[32,64,128]{2,1,0:T(8,128)(2,1)}), bf16[32,64,128]{2,1,0:T(8,128)(2,1)S(1)}, u32[]{:S(2)}, u32[]{:S(2)}) async-start(bf16[32,64,128]{2,1,0:T(8,128)(2,1)} %get-tuple-element.26), calls=%async_computation | async-start | bytes 1048576 | tf_op jit(solution)/shard_map/all_to_all | solution.py:499
  32.5 36.0 %copy-start.7 = (s32[1,32]{1,0:T(1,128)S(1)}, s32[1,32]{1,0:T(1,128)}, u32[]{:S(2)}) copy-start(s32[1,32]{1,0:T(1,128)} %param.8) | copy-start | bytes 388
  42.6 22.1 %all-to-all-start.2 = ((bf16[32,144,128]{2,1,0:T(8,128)(2,1)}), bf16[32,144,128]{2,1,0:T(8,128)(2,1)S(1)}, u32[]{:S(2)}, u32[]{:S(2)}) async-start(bf16[32,144,128]{2,1,0:T(8,128)(2,1)} %pack.2), calls=%async_computation.2 | async-start | bytes 2359296 | tf_op jit(solution)/shard_map/all_to_all | solution.py:499
  46.3 18.9 %collective-permute-start.2 = (bf16[32,64,128]{2,1,0:T(8,128)(2,1)S(1)}, bf16[32,64,128]{2,1,0:T(8,128)(2,1)}, u32[]{:S(2)}, u32[]{:S(2)}) collective-permute-start(bf16[32,64,128]{2,1,0:T(8,128)(2,1)S(1)} %all-to-all-done.refs_1_), channel_id=1, source_target_pairs={{0,96},{32,0},{64,32},{96,64},{1,97},{33,1},{65,33},{97,65},{2,98}... | collective-permute-start | bytes 1572872 | tf_op jit(solution)/shard_map/ppermute | solution.py:438
  49.3 16.1 %collective-permute-start.3 = (bf16[32,64,128]{2,1,0:T(8,128)(2,1)S(1)}, bf16[32,64,128]{2,1,0:T(8,128)(2,1)}, u32[]{:S(2)}, u32[]{:S(2)}) collective-permute-start(bf16[32,64,128]{2,1,0:T(8,128)(2,1)S(1)} %all-to-all-done.refs_1_), channel_id=1, source_target_pairs={{0,32},{32,64},{64,96},{96,0},{1,33},{33,65},{65,97},{97,1},{2,34}... | collective-permute-start | bytes 1572872 | tf_op jit(solution)/shard_map/ppermute | solution.py:438
  49.3 16.4 %collective-permute-start.7 = (bf16[32,64,128]{2,1,0:T(8,128)(2,1)S(1)}, bf16[32,64,128]{2,1,0:T(8,128)(2,1)}, u32[]{:S(2)}, u32[]{:S(2)}) collective-permute-start(bf16[32,64,128]{2,1,0:T(8,128)(2,1)S(1)} %all_to_all.25.refs_0_), channel_id=1, source_target_pairs={{0,1},{1,0},{2,3},{3,2},{4,5},{5,4},{6,7},{7,6},{8,9},{9,8},{10,11... | collective-permute-start | bytes 1572872 | tf_op jit(solution)/shard_map/ppermute | solution.py:451
  49.8 18.8 %collective-permute-start.8 = (bf16[32,64,128]{2,1,0:T(8,128)(2,1)S(1)}, bf16[32,64,128]{2,1,0:T(8,128)(2,1)}, u32[]{:S(2)}, u32[]{:S(2)}) collective-permute-start(bf16[32,64,128]{2,1,0:T(8,128)(2,1)S(1)} %all-to-all-done.refs_1_), channel_id=1, source_target_pairs={{0,1},{1,0},{2,3},{3,2},{4,5},{5,4},{6,7},{7,6},{8,9},{9,8},{10,11... | collective-permute-start | bytes 1572872 | tf_op jit(solution)/shard_map/ppermute | solution.py:451
  64.6 21.3 %collective-permute-start.6 = (bf16[32,144,128]{2,1,0:T(8,128)(2,1)S(1)}, bf16[32,144,128]{2,1,0:T(8,128)(2,1)}, u32[]{:S(2)}, u32[]{:S(2)}) collective-permute-start(bf16[32,144,128]{2,1,0:T(8,128)(2,1)S(1)} %all-to-all-done.2.q_own.refs_3_.q), channel_id=1, source_target_pairs={{0,1},{1,0},{2,3},{3,2},{4,5},{5,4},{6,7},{7,6},{8,9},{9,8},{10,11... | collective-permute-start | bytes 3538952 | tf_op jit(solution)/shard_map/ppermute | solution.py:451
  65.2 3.7 %collective-permute-start.9 = (bf16[32,64,128]{2,1,0:T(8,128)(2,1)S(1)}, bf16[32,64,128]{2,1,0:T(8,128)(2,1)S(1)}, u32[]{:S(2)}, u32[]{:S(2)}) collective-permute-start(bf16[32,64,128]{2,1,0:T(8,128)(2,1)S(1)} %collective-permute-done.refs_2_), channel_id=1, source_target_pairs={{0,1},{1,0},{2,3},{3,2},{4,5},{5,4},{6,7},{7,6},{8,9},{9,8},{10,11... | collective-permute-start | bytes 1572872 | tf_op jit(solution)/shard_map/ppermute | solution.py:451
  65.4 4.1 %collective-permute-start.13 = (bf16[32,64,128]{2,1,0:T(8,128)(2,1)S(1)}, bf16[32,64,128]{2,1,0:T(8,128)(2,1)S(1)}, u32[]{:S(2)}, u32[]{:S(2)}) collective-permute-start(bf16[32,64,128]{2,1,0:T(8,128)(2,1)S(1)} %collective-permute-done.1.refs_6_), channel_id=1, source_target_pairs={{0,1},{1,0},{2,3},{3,2},{4,5},{5,4},{6,7},{7,6},{8,9},{9,8},{10,11... | collective-permute-start | bytes 1572872 | tf_op jit(solution)/shard_map/ppermute | solution.py:451
  65.7 13.9 %collective-permute-start.4 = (bf16[32,64,128]{2,1,0:T(8,128)(2,1)S(1)}, bf16[32,64,128]{2,1,0:T(8,128)(2,1)S(1)}, u32[]{:S(2)}, u32[]{:S(2)}) collective-permute-start(bf16[32,64,128]{2,1,0:T(8,128)(2,1)S(1)} %collective-permute-done.refs_2_), channel_id=1, source_target_pairs={{0,96},{32,0},{64,32},{96,64},{1,97},{33,1},{65,33},{97,65},{2,98}... | collective-permute-start | bytes 1572872 | tf_op jit(solution)/shard_map/ppermute | solution.py:438
  68.6 14.4 %collective-permute-start.5 = (bf16[32,64,128]{2,1,0:T(8,128)(2,1)}, bf16[32,64,128]{2,1,0:T(8,128)(2,1)S(1)}, u32[]{:S(2)}, u32[]{:S(2)}) collective-permute-start(bf16[32,64,128]{2,1,0:T(8,128)(2,1)} %collective-permute-done.3.refs_7_), channel_id=1, source_target_pairs={{0,32},{32,64},{64,96},{96,0},{1,33},{33,65},{65,97},{97,1},{2,34}... | collective-permute-start | bytes 1572872 | tf_op jit(solution)/shard_map/ppermute | solution.py:438
  68.9 15.6 %collective-permute-start.10 = (bf16[32,64,128]{2,1,0:T(8,128)(2,1)}, bf16[32,64,128]{2,1,0:T(8,128)(2,1)S(1)}, u32[]{:S(2)}, u32[]{:S(2)}) collective-permute-start(bf16[32,64,128]{2,1,0:T(8,128)(2,1)} %collective-permute-done.2.refs_3_), channel_id=1, source_target_pairs={{0,1},{1,0},{2,3},{3,2},{4,5},{5,4},{6,7},{7,6},{8,9},{9,8},{10,11... | collective-permute-start | bytes 1572872 | tf_op jit(solution)/shard_map/ppermute | solution.py:451
  69.5 15.0 %collective-permute-start.14 = (bf16[32,64,128]{2,1,0:T(8,128)(2,1)}, bf16[32,64,128]{2,1,0:T(8,128)(2,1)S(1)}, u32[]{:S(2)}, u32[]{:S(2)}) collective-permute-start(bf16[32,64,128]{2,1,0:T(8,128)(2,1)} %collective-permute-done.3.refs_7_), channel_id=1, source_target_pairs={{0,1},{1,0},{2,3},{3,2},{4,5},{5,4},{6,7},{7,6},{8,9},{9,8},{10,11... | collective-permute-start | bytes 1572872 | tf_op jit(solution)/shard_map/ppermute | solution.py:451
  79.6 4.9 %collective-permute-start.11 = (bf16[32,64,128]{2,1,0:T(8,128)(2,1)S(1)}, bf16[32,64,128]{2,1,0:T(8,128)(2,1)S(1)}, u32[]{:S(2)}, u32[]{:S(2)}) collective-permute-start(bf16[32,64,128]{2,1,0:T(8,128)(2,1)S(1)} %collective-permute-done.4.refs_4_), channel_id=1, source_target_pairs={{0,1},{1,0},{2,3},{3,2},{4,5},{5,4},{6,7},{7,6},{8,9},{9,8},{10,11... | collective-permute-start | bytes 1572872 | tf_op jit(solution)/shard_map/ppermute | solution.py:451
  83.0 2.9 %collective-permute-start.12 = (bf16[32,64,128]{2,1,0:T(8,128)(2,1)S(1)}, bf16[32,64,128]{2,1,0:T(8,128)(2,1)S(1)}, u32[]{:S(2)}, u32[]{:S(2)}) collective-permute-start(bf16[32,64,128]{2,1,0:T(8,128)(2,1)S(1)} %collective-permute-done.5.refs_5_), channel_id=1, source_target_pairs={{0,1},{1,0},{2,3},{3,2},{4,5},{5,4},{6,7},{7,6},{8,9},{9,8},{10,11... | collective-permute-start | bytes 1572872 | tf_op jit(solution)/shard_map/ppermute | solution.py:451
  93.7 9.6 %collective-permute-start.15 = (f32[2,512,128]{2,1,0:T(8,128)S(1)}, f32[2,512,128]{2,1,0:T(8,128)S(1)}, u32[]{:S(2)}, u32[]{:S(2)}) collective-permute-start(f32[2,512,128]{2,1,0:T(8,128)S(1)} %get-tuple-element.35), channel_id=1, source_target_pairs={{0,8},{1,3},{2,10},{3,5},{4,12},{5,7},{6,14},{7,1},{8,16},{9,11},{... | collective-permute-start | bytes 1572872 | tf_op jit(solution)/shard_map/ppermute | solution.py:451
  93.8 9.7 %collective-permute-start.20 = (f32[2,512,128]{2,1,0:T(8,128)S(1)}, f32[2,512,128]{2,1,0:T(8,128)S(1)}, u32[]{:S(2)}, u32[]{:S(2)}) collective-permute-start(f32[2,512,128]{2,1,0:T(8,128)S(1)} %get-tuple-element.39), channel_id=1, source_target_pairs={{0,24},{1,7},{2,26},{3,1},{4,28},{5,3},{6,30},{7,5},{8,0},{9,15},{... | collective-permute-start | bytes 1572872 | tf_op jit(solution)/shard_map/ppermute | solution.py:451
  96.4 11.7 %collective-permute-start.17 = (f32[2,512,128]{2,1,0:T(8,128)S(1)}, f32[2,512,128]{2,1,0:T(8,128)S(1)}, u32[]{:S(2)}, u32[]{:S(2)}) collective-permute-start(f32[2,512,128]{2,1,0:T(8,128)S(1)} %get-tuple-element.36), channel_id=1, source_target_pairs={{0,24},{1,7},{2,26},{3,1},{4,28},{5,3},{6,30},{7,5},{8,0},{9,15},{... | collective-permute-start | bytes 1572872 | tf_op jit(solution)/shard_map/ppermute | solution.py:451
  96.5 12.4 %collective-permute-start.19 = (f32[2,512,128]{2,1,0:T(8,128)S(1)}, f32[2,512,128]{2,1,0:T(8,128)S(1)}, u32[]{:S(2)}, u32[]{:S(2)}) collective-permute-start(f32[2,512,128]{2,1,0:T(8,128)S(1)} %get-tuple-element.37), channel_id=1, source_target_pairs={{0,8},{1,3},{2,10},{3,5},{4,12},{5,7},{6,14},{7,1},{8,16},{9,11},{... | collective-permute-start | bytes 1572872 | tf_op jit(solution)/shard_map/ppermute | solution.py:451
  103.4 11.2 %collective-permute-start.16 = (f32[2,512,128]{2,1,0:T(8,128)S(1)}, f32[2,512,128]{2,1,0:T(8,128)S(1)}, u32[]{:S(2)}, u32[]{:S(2)}) collective-permute-start(f32[2,512,128]{2,1,0:T(8,128)S(1)} %add.99), channel_id=1, source_target_pairs={{0,8},{1,3},{2,10},{3,5},{4,12},{5,7},{6,14},{7,1},{8,16},{9,11},{... | collective-permute-start | bytes 1572872 | tf_op jit(solution)/shard_map/ppermute | solution.py:451
  103.5 11.0 %collective-permute-start.21 = (f32[2,512,128]{2,1,0:T(8,128)S(1)}, f32[2,512,128]{2,1,0:T(8,128)S(1)}, u32[]{:S(2)}, u32[]{:S(2)}) collective-permute-start(f32[2,512,128]{2,1,0:T(8,128)S(1)} %add.108), channel_id=1, source_target_pairs={{0,24},{1,7},{2,26},{3,1},{4,28},{5,3},{6,30},{7,5},{8,0},{9,15},{... | collective-permute-start | bytes 1572872 | tf_op jit(solution)/shard_map/ppermute | solution.py:451
  114.7 9.6 %collective-permute-start.18 = (f32[512,128]{1,0:T(8,128)S(1)}, f32[512,128]{1,0:T(8,128)S(1)}, u32[]{:S(2)}, u32[]{:S(2)}) collective-permute-start(f32[512,128]{1,0:T(8,128)S(1)} %get-tuple-element.51), channel_id=1, source_target_pairs={{0,2},{1,9},{2,4},{3,11},{4,6},{5,13},{6,0},{7,15},{8,10},{9,17},{... | collective-permute-start | bytes 786440 | tf_op jit(solution)/shard_map/ppermute | solution.py:451
  114.8 9.5 %collective-permute-start.22 = (f32[512,128]{1,0:T(8,128)S(1)}, f32[512,128]{1,0:T(8,128)S(1)}, u32[]{:S(2)}, u32[]{:S(2)}) collective-permute-start(f32[512,128]{1,0:T(8,128)S(1)} %get-tuple-element.49), channel_id=1, source_target_pairs={{0,4},{1,17},{2,6},{3,19},{4,0},{5,21},{6,2},{7,23},{8,12},{9,25},... | collective-permute-start | bytes 786440 | tf_op jit(solution)/shard_map/ppermute | solution.py:451
  117.0 7.9 %collective-permute-start.23 = (f32[512,128]{1,0:T(8,128)S(1)}, f32[512,128]{1,0:T(8,128)S(1)}, u32[]{:S(2)}, u32[]{:S(2)}) collective-permute-start(f32[512,128]{1,0:T(8,128)S(1)} %get-tuple-element.50), channel_id=1, source_target_pairs={{0,6},{1,25},{2,0},{3,27},{4,2},{5,29},{6,4},{7,31},{8,14},{9,1},{... | collective-permute-start | bytes 786440 | tf_op jit(solution)/shard_map/ppermute | solution.py:451
  125.1 4.5 %collective-permute-start.24 = (f32[512,128]{1,0:T(8,128)S(1)}, f32[512,128]{1,0:T(8,128)}, u32[]{:S(2)}, u32[]{:S(2)}) collective-permute-start(f32[512,128]{1,0:T(8,128)S(1)} %fusion.6.refs_0_), channel_id=1, source_target_pairs={{0,1},{1,0},{2,3},{3,2},{4,5},{5,4},{6,7},{7,6},{8,9},{9,8},{10,11... | collective-permute-start | bytes 786440 | tf_op jit(solution)/shard_map/ppermute | solution.py:451
  129.5 34.8 %copy-start.1 = (bf16[32,64,128]{2,1,0:T(8,128)(2,1)S(1)}, bf16[32,64,128]{2,1,0:T(8,128)(2,1)}, u32[]{:S(2)}) copy-start(bf16[32,64,128]{2,1,0:T(8,128)(2,1)} %copy-done) | copy-start | bytes 1572868
  129.5 34.8 %copy-start.3 = (bf16[32,64,128]{2,1,0:T(8,128)(2,1)S(1)}, bf16[32,64,128]{2,1,0:T(8,128)(2,1)}, u32[]{:S(2)}) copy-start(bf16[32,64,128]{2,1,0:T(8,128)(2,1)} %copy-done.2) | copy-start | bytes 1572868
  133.1 5.8 %collective-permute-start.25 = (bf16[528,128]{1,0:T(8,128)(2,1)S(1)}, bf16[528,128]{1,0:T(8,128)(2,1)S(1)}, u32[]{:S(2)}, u32[]{:S(2)}) collective-permute-start(bf16[528,128]{1,0:T(8,128)(2,1)S(1)} %softmax_weights.1), channel_id=1, source_target_pairs={{0,24},{1,7},{2,26},{3,1},{4,28},{5,3},{6,30},{7,5},{8,0},{9,15},{... | collective-permute-start | bytes 405512 | tf_op jit(solution)/shard_map/ppermute | solution.py:451
  135.5 5.7 %collective-permute-start.26 = (bf16[528,128]{1,0:T(8,128)(2,1)S(1)}, bf16[528,128]{1,0:T(8,128)(2,1)S(1)}, u32[]{:S(2)}, u32[]{:S(2)}) collective-permute-start(bf16[528,128]{1,0:T(8,128)(2,1)S(1)} %softmax_weights.1), channel_id=1, source_target_pairs={{0,16},{1,5},{2,18},{3,7},{4,20},{5,1},{6,22},{7,3},{8,24},{9,13},... | collective-permute-start | bytes 405512 | tf_op jit(solution)/shard_map/ppermute | solution.py:451
  135.7 6.8 %collective-permute-start.27 = (bf16[528,128]{1,0:T(8,128)(2,1)S(1)}, bf16[528,128]{1,0:T(8,128)(2,1)S(1)}, u32[]{:S(2)}, u32[]{:S(2)}) collective-permute-start(bf16[528,128]{1,0:T(8,128)(2,1)S(1)} %softmax_weights.1), channel_id=1, source_target_pairs={{0,8},{1,3},{2,10},{3,5},{4,12},{5,7},{6,14},{7,1},{8,16},{9,11},{... | collective-permute-start | bytes 405512 | tf_op jit(solution)/shard_map/ppermute | solution.py:451
  142.6 9.0 %collective-permute-start.29 = (bf16[4,528,128]{2,1,0:T(8,128)(2,1)S(1)}, bf16[4,528,128]{2,1,0:T(8,128)(2,1)S(1)}, u32[]{:S(2)}, u32[]{:S(2)}) collective-permute-start(bf16[4,528,128]{2,1,0:T(8,128)(2,1)S(1)} %pad_maximum_fusion.refs_0_), channel_id=1, source_target_pairs={{0,6},{1,25},{2,0},{3,27},{4,2},{5,29},{6,4},{7,31},{8,14},{9,1},{... | collective-permute-start | bytes 1622024 | tf_op jit(solution)/shard_map/ppermute | solution.py:451
  145.3 12.1 %collective-permute-start.28 = (bf16[4,528,128]{2,1,0:T(8,128)(2,1)S(1)}, bf16[4,528,128]{2,1,0:T(8,128)(2,1)S(1)}, u32[]{:S(2)}, u32[]{:S(2)}) collective-permute-start(bf16[4,528,128]{2,1,0:T(8,128)(2,1)S(1)} %pad_maximum_fusion.refs_0_), channel_id=1, source_target_pairs={{0,2},{1,9},{2,4},{3,11},{4,6},{5,13},{6,0},{7,15},{8,10},{9,17},{... | collective-permute-start | bytes 1622024 | tf_op jit(solution)/shard_map/ppermute | solution.py:451
  151.6 9.7 %collective-permute-start.30 = (bf16[4,528,128]{2,1,0:T(8,128)(2,1)S(1)}, bf16[4,528,128]{2,1,0:T(8,128)(2,1)S(1)}, u32[]{:S(2)}, u32[]{:S(2)}) collective-permute-start(bf16[4,528,128]{2,1,0:T(8,128)(2,1)S(1)} %collective-permute-done.29.refs_2_), channel_id=1, source_target_pairs={{0,6},{1,25},{2,0},{3,27},{4,2},{5,29},{6,4},{7,31},{8,14},{9,1},{... | collective-permute-start | bytes 1622024 | tf_op jit(solution)/shard_map/ppermute | solution.py:451
  155.0 10.7 %collective-permute-start.31 = (bf16[4,528,128]{2,1,0:T(8,128)(2,1)S(1)}, bf16[4,528,128]{2,1,0:T(8,128)(2,1)S(1)}, u32[]{:S(2)}, u32[]{:S(2)}) collective-permute-start(bf16[4,528,128]{2,1,0:T(8,128)(2,1)S(1)} %pad_maximum_fusion.refs_0_), channel_id=1, source_target_pairs={{0,1},{1,0},{2,3},{3,2},{4,5},{5,4},{6,7},{7,6},{8,9},{9,8},{10,11... | collective-permute-start | bytes 1622024 | tf_op jit(solution)/shard_map/ppermute | solution.py:451
  157.4 8.3 %collective-permute-start.33 = (bf16[4,528,128]{2,1,0:T(8,128)(2,1)S(1)}, bf16[4,528,128]{2,1,0:T(8,128)(2,1)S(1)}, u32[]{:S(2)}, u32[]{:S(2)}) collective-permute-start(bf16[4,528,128]{2,1,0:T(8,128)(2,1)S(1)} %collective-permute-done.29.refs_2_), channel_id=1, source_target_pairs={{0,1},{1,0},{2,3},{3,2},{4,5},{5,4},{6,7},{7,6},{8,9},{9,8},{10,11... | collective-permute-start | bytes 1622024 | tf_op jit(solution)/shard_map/ppermute | solution.py:451
  157.5 8.3 %collective-permute-start.32 = (bf16[4,528,128]{2,1,0:T(8,128)(2,1)S(1)}, bf16[4,528,128]{2,1,0:T(8,128)(2,1)S(1)}, u32[]{:S(2)}, u32[]{:S(2)}) collective-permute-start(bf16[4,528,128]{2,1,0:T(8,128)(2,1)S(1)} %collective-permute-done.28.refs_1_), channel_id=1, source_target_pairs={{0,1},{1,0},{2,3},{3,2},{4,5},{5,4},{6,7},{7,6},{8,9},{9,8},{10,11... | collective-permute-start | bytes 1622024 | tf_op jit(solution)/shard_map/ppermute | solution.py:451
  161.3 4.6 %collective-permute-start.34 = (bf16[4,528,128]{2,1,0:T(8,128)(2,1)S(1)}, bf16[4,528,128]{2,1,0:T(8,128)(2,1)S(1)}, u32[]{:S(2)}, u32[]{:S(2)}) collective-permute-start(bf16[4,528,128]{2,1,0:T(8,128)(2,1)S(1)} %collective-permute-done.30.refs_3_), channel_id=1, source_target_pairs={{0,1},{1,0},{2,3},{3,2},{4,5},{5,4},{6,7},{7,6},{8,9},{9,8},{10,11... | collective-permute-start | bytes 1622024 | tf_op jit(solution)/shard_map/ppermute | solution.py:451
  173.7 16.0 %collective-permute-start.39 = (bf16[16,128,128]{2,1,0:T(8,128)(2,1)}, bf16[16,128,128]{2,1,0:T(8,128)(2,1)}, u32[]{:S(2)}, u32[]{:S(2)}) collective-permute-start(bf16[16,128,128]{2,1,0:T(8,128)(2,1)} %get-tuple-element.48), channel_id=1, source_target_pairs={{0,96},{32,0},{64,32},{96,64},{1,97},{33,1},{65,33},{97,65},{2,98}... | collective-permute-start | bytes 1572872 | tf_op jit(solution)/shard_map/ppermute | solution.py:438
  174.3 19.7 %collective-permute-start.35 = (bf16[16,128,128]{2,1,0:T(8,128)(2,1)}, bf16[16,128,128]{2,1,0:T(8,128)(2,1)}, u32[]{:S(2)}, u32[]{:S(2)}) collective-permute-start(bf16[16,128,128]{2,1,0:T(8,128)(2,1)} %get-tuple-element.44), channel_id=1, source_target_pairs={{0,32},{32,64},{64,96},{96,0},{1,33},{33,65},{65,97},{97,1},{2,34}... | collective-permute-start | bytes 1572872 | tf_op jit(solution)/shard_map/ppermute | solution.py:438
  175.2 23.2 %collective-permute-start.37 = (bf16[16,128,128]{2,1,0:T(8,128)(2,1)}, bf16[16,128,128]{2,1,0:T(8,128)(2,1)}, u32[]{:S(2)}, u32[]{:S(2)}) collective-permute-start(bf16[16,128,128]{2,1,0:T(8,128)(2,1)} %get-tuple-element.45), channel_id=1, source_target_pairs={{0,96},{32,0},{64,32},{96,64},{1,97},{33,1},{65,33},{97,65},{2,98}... | collective-permute-start | bytes 1572872 | tf_op jit(solution)/shard_map/ppermute | solution.py:438
  176.9 22.9 %collective-permute-start.38 = (bf16[16,128,128]{2,1,0:T(8,128)(2,1)}, bf16[16,128,128]{2,1,0:T(8,128)(2,1)}, u32[]{:S(2)}, u32[]{:S(2)}) collective-permute-start(bf16[16,128,128]{2,1,0:T(8,128)(2,1)} %get-tuple-element.46), channel_id=1, source_target_pairs={{0,32},{32,64},{64,96},{96,0},{1,33},{33,65},{65,97},{97,1},{2,34}... | collective-permute-start | bytes 1572872 | tf_op jit(solution)/shard_map/ppermute | solution.py:438
  183.0 30.5 %all-to-all-start.3 = ((bf16[32,128,128]{2,1,0:T(8,128)(2,1)}), bf16[32,128,128]{2,1,0:T(8,128)(2,1)S(1)}, u32[]{:S(2)}, u32[]{:S(2)}) async-start(bf16[32,128,128]{2,1,0:T(8,128)(2,1)} %grad_queries.1), calls=%async_computation.3 | async-start | bytes 2097152 | tf_op jit(solution)/shard_map/all_to_all | solution.py:499
  190.9 18.6 %collective-permute-start.40 = (bf16[16,128,128]{2,1,0:T(8,128)(2,1)S(1)}, bf16[16,128,128]{2,1,0:T(8,128)(2,1)S(1)}, u32[]{:S(2)}, u32[]{:S(2)}) collective-permute-start(bf16[16,128,128]{2,1,0:T(8,128)(2,1)S(1)} %add_convert_fusion), channel_id=1, source_target_pairs={{0,96},{32,0},{64,32},{96,64},{1,97},{33,1},{65,33},{97,65},{2,98}... | collective-permute-start | bytes 1572872 | tf_op jit(solution)/shard_map/ppermute | solution.py:438
  195.1 15.8 %collective-permute-start.36 = (bf16[16,128,128]{2,1,0:T(8,128)(2,1)S(1)}, bf16[16,128,128]{2,1,0:T(8,128)(2,1)S(1)}, u32[]{:S(2)}, u32[]{:S(2)}) collective-permute-start(bf16[16,128,128]{2,1,0:T(8,128)(2,1)S(1)} %add_convert_fusion.1), channel_id=1, source_target_pairs={{0,32},{32,64},{64,96},{96,0},{1,33},{33,65},{65,97},{97,1},{2,34}... | collective-permute-start | bytes 1572872 | tf_op jit(solution)/shard_map/ppermute | solution.py:438
  213.5 24.0 %all-to-all-start.4 = ((bf16[32,128,128]{2,1,0:T(8,128)(2,1)}), bf16[32,128,128]{2,1,0:T(8,128)(2,1)S(1)}, u32[]{:S(2)}, u32[]{:S(2)}) async-start(bf16[32,128,128]{2,1,0:T(8,128)(2,1)} %join.1), calls=%async_computation.4 | async-start | bytes 2097152 | tf_op jit(solution)/shard_map/all_to_all | solution.py:499
  (5 other events, 89.0 us)

commit v6 on v5

--- a/solution.py
+++ b/solution.py
@@ -34,58 +34,50 @@
         copy.wait()
 
 
-def pack_kernel(x, *refs):
-    *outs, xv, outv, marks, sems = refs
-    extra = outv.shape[1] - BLK
-    if extra:
-        run_copies([pltpu.make_async_copy(outs[0], marks, sems.at[0])])
-        outs = outs[1:]
-        tile = jnp.broadcast_to(marks[...].astype(jnp.float32), (extra, 128)).astype(jnp.bfloat16)
+def pack_kernel(x, *refs, rows):
+    *given, out, xv, outv, marks, sems = refs
+    tall = rows.stop - rows.start
     width = x.shape[1]
     number = outv.shape[0] // PARTS
-    tall = outv.shape[1] // len(outs)
     loads, stores = [], []
     for n in range(PARTS):
         cols = slice(n * width // PARTS, (n + 1) * width // PARTS)
-        loads.append(pltpu.make_async_copy(x.at[:, cols], xv.at[:, cols], sems.at[n]))
+        loads.append(pltpu.make_async_copy(x.at[rows, cols], xv.at[:, cols], sems.at[n]))
         part = slice(n * number, (n + 1) * number)
-        for m, out in enumerate(outs):
-            source = outv.at[part, m * tall : (m + 1) * tall, :]
-            sem = sems.at[PARTS * (1 + m) + n]
-            stores.append(pltpu.make_async_copy(source, out.at[part], sem))
+        stores.append(pltpu.make_async_copy(outv.at[part], out.at[part], sems.at[PARTS + n]))
     for copy in loads:
         copy.start()
+    if given:
+        run_copies([pltpu.make_async_copy(given[0], marks, sems.at[2 * PARTS])])
+        tile = jnp.broadcast_to(marks[...].astype(jnp.float32), (16, 128)).astype(jnp.bfloat16)
     for n in range(PARTS):
         loads[n].wait()
         for m in range(n * number, (n + 1) * number):
-            outv[m, 0:BLK, :] = xv[:, 128 * m : 128 * m + 128].astype(jnp.bfloat16)
-            if extra:
-                outv[m, BLK:, :] = tile
-        for copy in stores[n * len(outs) : (n + 1) * len(outs)]:
-            copy.start()
+            outv[m, 0:tall, :] = xv[:, 128 * m : 128 * m + 128].astype(jnp.bfloat16)
+            if given:
+                outv[m, tall:, :] = tile
+        stores[n].start()
     for copy in stores:
         copy.wait()
 
 
-def by_features(x, pos=None):
-    number = x.shape[1] // 128
-    tall = BLK + (0 if pos is None else 16)
-    shapes = [(number, HALF, 128)] * 2 if pos is None else [(number, tall, 128)]
-    given = (x,) if pos is None else (x, pos)
-    return pl.pallas_call(
-        pack_kernel,
-        in_specs=[ANY] * len(given),
-        out_specs=[ANY] * len(shapes),
-        out_shape=[jax.ShapeDtypeStruct(s, jnp.bfloat16) for s in shapes],
+def by_features(x, rows, *pos):
+    tall = rows.stop - rows.start
+    shape = (x.shape[1] // 128, tall + 16 * len(pos), 128)
+    return pl.pallas_call(
+        functools.partial(pack_kernel, rows=rows),
+        in_specs=[ANY] * (1 + len(pos)),
+        out_specs=ANY,
+        out_shape=jax.ShapeDtypeStruct(shape, jnp.bfloat16),
         scratch_shapes=[
-            pltpu.VMEM(x.shape, x.dtype),
-            pltpu.VMEM((number, tall, 128), jnp.bfloat16),
+            pltpu.VMEM((tall, x.shape[1]), x.dtype),
+            pltpu.VMEM(shape, jnp.bfloat16),
             pltpu.VMEM((1, BLK), jnp.int32),
-            pltpu.SemaphoreType.DMA((3 * PARTS,)),
+            pltpu.SemaphoreType.DMA((2 * PARTS + 1,)),
         ],
-        **params(56 if pos is None else 5, 5 * MIB),
+        **params(56 if rows.stop == HALF else 5, 4 * MIB),
         name="pack",
-    )(*given)
+    )(x, *pos)
 
 
 def unpack_kernel(x, out, outv, sems):
@@ -199,16 +191,7 @@
     )(ids, own, at, *q, *pieces)
 
 
-def softmax_kernel(at, *refs, scale):
-    terms, lists, q, out, xv, listv, markv, sems = refs[:2], *refs[2:]
-    loads = [
-        pltpu.make_async_copy(terms[n], xv.at[ROWS * n : ROWS * n + ROWS, :], sems.at[n])
-        for n in range(2)
-    ]
-    loads.append(pltpu.make_async_copy(lists, listv, sems.at[2]))
-    loads.append(pltpu.make_async_copy(q.at[:, BLK:, :], markv, sems.at[3]))
-    run_copies(loads)
-
+def softmax_kernel(at, x_own, x_sib, listv, q, out, *, scale):
     core = at[0]
     row = lax.broadcasted_iota(jnp.int32, (2 * ROWS, 1), 0)
     side = row // ROWS
@@ -218,7 +201,7 @@
     own = jnp.sum((listv[0:1, :] <= t).astype(jnp.int32), axis=1, keepdims=True)
     key = own * 8 + r
 
-    x = xv[...] * scale
+    x = jnp.concatenate([x_own[...], x_sib[...]], axis=0) * scale
     high = jnp.max(x, axis=1, keepdims=True)
     part = jnp.sum(jnp.exp(x - high), axis=1, keepdims=True)
     lines = jnp.where(lane == 0, high, jnp.where(lane == 1, part, key.astype(jnp.float32))).T
@@ -232,7 +215,7 @@
 
     block = lane == own
     first = t == jnp.sum(jnp.where(block, listv[1:2, :], 0), axis=1, keepdims=True)
-    marks = jnp.max(markv[...].astype(jnp.float32), axis=1)
+    marks = jnp.max(q[:, BLK:, :].astype(jnp.float32), axis=1)
     marks = jnp.concatenate([marks, jnp.zeros((128 - marks.shape[0], 128), jnp.float32)], axis=0)
     listed = jnp.dot(
         block.astype(jnp.bfloat16), marks.astype(jnp.bfloat16), preferred_element_type=jnp.float32
@@ -258,15 +241,9 @@
 def softmax_weights(at, terms, lists, q, scale):
     return pl.pallas_call(
         functools.partial(softmax_kernel, scale=scale),
-        in_specs=[SMEM] + [ANY] * 4,
+        in_specs=[SMEM] + [VMEM] * 4,
         out_specs=VMEM,
         out_shape=jax.ShapeDtypeStruct((ROWS + TAIL, 128), jnp.bfloat16),
-        scratch_shapes=[
-            pltpu.VMEM((2 * ROWS, 128), jnp.float32),
-            pltpu.VMEM(lists.shape, jnp.int32),
-            pltpu.VMEM((q.shape[0], TAIL, 128), jnp.bfloat16),
-            pltpu.SemaphoreType.DMA((4,)),
-        ],
         **params(16, 8 * MIB),
         name="softmax_weights",
     )(at, *terms, lists, q)
@@ -386,47 +363,35 @@
     )(ids, own, at, p, *parts)
 
 
-def join_kernel(*refs):
-    kept, terms, out, keptv, termv, outv, sems = refs[0], refs[1:5], refs[5], *refs[6:]
+def join_kernel(kept, *refs):
+    terms, out, outv, sems = refs[:4], *refs[4:]
     half = kept.shape[0] // 2
-    loads = [pltpu.make_async_copy(terms[n], termv.at[n], sems.at[n]) for n in range(4)]
-    stores = []
+    copies = []
     for h in range(2):
         part = slice(half * h, half * h + half)
-        loads.append(pltpu.make_async_copy(kept.at[part], keptv.at[part], sems.at[4 + h]))
-        stores.append(pltpu.make_async_copy(outv.at[part], out.at[part], sems.at[6 + h]))
-    for copy in loads:
-        copy.start()
-    for h in range(2):
-        for n in (4 + h, 2 * h, 2 * h + 1):
-            loads[n].wait()
-
-        @pl.loop(0, half)
+
+        @pl.loop(0, half // 4)
         def _(n):
-            value = keptv[half * h + n].astype(jnp.float32)
-            for m in (2 * h, 2 * h + 1):
-                value = value + termv[m, n].astype(jnp.float32)
-            outv[half * h + n] = value.astype(out.dtype)
-
-        stores[h].start()
-    for copy in stores:
+            for e in range(4):
+                value = kept[half * h + 4 * n + e].astype(jnp.float32)
+                for m in (2 * h, 2 * h + 1):
+                    value = value + terms[m][4 * n + e].astype(jnp.float32)
+                outv[half * h + 4 * n + e] = value.astype(outv.dtype)
+
+        copies.append(pltpu.make_async_copy(outv.at[part], out.at[part], sems.at[h]))
+        copies[h].start()
+    for copy in copies:
         copy.wait()
 
 
 def join(kept, low, high):
-    term = low[0].shape
     return pl.pallas_call(
         join_kernel,
-        in_specs=[ANY] * 5,
+        in_specs=[VMEM] * 5,
         out_specs=ANY,
         out_shape=jax.ShapeDtypeStruct(kept.shape, kept.dtype),
-        scratch_shapes=[
-            pltpu.VMEM(kept.shape, kept.dtype),
-            pltpu.VMEM((4,) + term, kept.dtype),
-            pltpu.VMEM(kept.shape, kept.dtype),
-            pltpu.SemaphoreType.DMA((8,)),
-        ],
-        **params(5, 8 * MIB),
+        scratch_shapes=[pltpu.VMEM(kept.shape, kept.dtype), pltpu.SemaphoreType.DMA((2,))],
+        **params(6, 8 * MIB),
         name="join",
     )(kept, *low, *high)
 
@@ -499,9 +464,10 @@
         return lax.all_to_all(v, "dev", 0, 0, tiled=True)
 
     up, down, flip = along("z", 1), along("z", -1), along("core", 1)
-    low, high = [exchange(v) for v in by_features(passages)]
+    halves = slice(0, HALF), slice(HALF, BLK)
+    low, high = [exchange(by_features(passages, rows)) for rows in halves]
     above0, below0 = down(low), up(low)
-    q_tiles = by_features(queries, positives.reshape(1, BLK))[0]
+    q_tiles = by_features(queries, slice(0, BLK), positives.reshape(1, BLK))
     q_tiles, late, *_ = lax.optimization_barrier((q_tiles, high, above0, below0))
     above1, below1 = down(late), up(late)
     last0, last1, *_ = lax.optimization_barrier((above0, below1, above1))

time: 240 us -> 240 us (level)
    pallas_call x3 -> x4, Pallas kernels: 6.28 us -> 7.09 us  [the longest x3 4.64 us: by_features(): pl.pallas_call(functools.partial(pack_kernel, rows=rows), in_specs=[ANY]...]
  transfers between devices with their start and end apart: 45 -> 45, of which waited for: 22 -> 22; matrix products, arithmetic and copies ran while one was open for 2% -> 2% of each run, Pallas kernels for 5% -> 6%
where the time goes in v6:
time: 240 us; the launch traced here: 239 us
  waiting for transfers between devices  105 us (44%)
  starting transfers between devices  69.6 us (29%)
  Pallas kernels  36 us (15%)
  blocking collectives  20.2 us (8%)
  local copies, waits for them, and re-layouts  4.34 us (2%)
  other arithmetic  3.32 us (1%)
    ppermute x29, waiting for transfers between devices, along(): return lambda v: lax.ppermute(v, 'dev', perm)  38.4 us
    all_to_all x4, waiting for transfers between devices, exchange(): return lax.all_to_all(v, 'dev', 0, 0, tiled=True)  38.3 us
    ppermute x29, starting transfers between devices, along(): return lambda v: lax.ppermute(v, 'dev', perm)  32.1 us
    ppermute x12, waiting for transfers between devices, along(): return lambda v: lax.ppermute(v, 'grp', perm)  28 us
    all_to_all x4, starting transfers between devices, exchange(): return lax.all_to_all(v, 'dev', 0, 0, tiled=True)  21.4 us
    all_to_all x1, blocking collectives, exchange(): return lax.all_to_all(v, 'dev', 0, 0, tiled=True)  20.2 us
    ppermute x12, starting transfers between devices, along(): return lambda v: lax.ppermute(v, 'grp', perm)  16 us
    pallas_call x1, Pallas kernels, grad_passages(): pl.pallas_call(grad_p_kernel, in_specs=[SMEM] * 3 + [VMEM] * 9, out_specs...  7.85 us
  transfers between devices with their start and end apart: 45, of which 22 were waited for; matrix products, arithmetic and copies ran while one was open for 2% of the time, Pallas kernels for 6%

profile of v6, /device:TPU:1, one launch (start us, length us, event | category | flops | bytes accessed | tf_op | source)
XLA Modules:
  0.0 239.4 jit_solution(14847389663292952232)
XLA Ops:
  0.6 2.2 pack.5
  2.9 20.2 %all_to_all.25.refs_0_ = bf16[32,64,128]{2,1,0:T(8,128)(2,1)S(1)} all-to-all(bf16[32,64,128]{2,1,0:T(8,128)(2,1)} %pack.5), channel_id=1, replica_groups=mesh['grp'=4,'dev'=32] {'dev'}, dimensions={0} | all-to-all | bytes 1048576 | tf_op jit(solution)/shard_map/all_to_all | solution.py:464
  23.1 3.8 %collective-permute-start = (bf16[32,64,128]{2,1,0:T(8,128)(2,1)S(1)}, bf16[32,64,128]{2,1,0:T(8,128)(2,1)S(1)}, u32[]{:S(2)}, u32[]{:S(2)}) collective-permute-start(bf16[32,64,128]{2,1,0:T(8,128)(2,1)S(1)} %all_to_all.25.refs_0_), channel_id=1, source_target_pairs={{0,96},{32,0},{64,32},{96,64},{1,97},{33,1},{65,33},{97,65},{2,98}... | collective-permute-start | bytes 1572872 | tf_op jit(solution)/shard_map/ppermute | solution.py:403
  28.0 3.9 %all-to-all-start = ((bf16[32,64,128]{2,1,0:T(8,128)(2,1)}), bf16[32,64,128]{2,1,0:T(8,128)(2,1)S(1)}, u32[]{:S(2)}, u32[]{:S(2)}) async-start(bf16[32,64,128]{2,1,0:T(8,128)(2,1)} %pack.4), calls=%async_computation | async-start | bytes 1048576 | tf_op jit(solution)/shard_map/all_to_all | solution.py:464
  31.9 1.6 copy-done.5
  34.8 8.7 %all-to-all-done.refs_1_ = bf16[32,64,128]{2,1,0:T(8,128)(2,1)S(1)} async-done(((bf16[32,64,128]{2,1,0:T(8,128)(2,1)}), bf16[32,64,128]{2,1,0:T(8,128)(2,1)S(1)}, u32[]{:S(2)}, u32[]{:S(2)}) %all-to-all-start) | async-done | bytes 524320 | tf_op jit(solution)/shard_map/all_to_all | solution.py:464
  43.5 3.7 %all-to-all-start.2 = ((bf16[32,144,128]{2,1,0:T(8,128)(2,1)}), bf16[32,144,128]{2,1,0:T(8,128)(2,1)S(1)}, u32[]{:S(2)}, u32[]{:S(2)}) async-start(bf16[32,144,128]{2,1,0:T(8,128)(2,1)} %pack.3), calls=%async_computation.2 | async-start | bytes 2359296 | tf_op jit(solution)/shard_map/all_to_all | solution.py:464
  47.3 3.0 %collective-permute-start.2 = (bf16[32,64,128]{2,1,0:T(8,128)(2,1)S(1)}, bf16[32,64,128]{2,1,0:T(8,128)(2,1)}, u32[]{:S(2)}, u32[]{:S(2)}) collective-permute-start(bf16[32,64,128]{2,1,0:T(8,128)(2,1)S(1)} %all-to-all-done.refs_1_), channel_id=1, source_target_pairs={{0,96},{32,0},{64,32},{96,64},{1,97},{33,1},{65,33},{97,65},{2,98}... | collective-permute-start | bytes 1572872 | tf_op jit(solution)/shard_map/ppermute | solution.py:403
  50.8 14.7 %all-to-all-done.2.q_own.q = bf16[32,144,128]{2,1,0:T(8,128)(2,1)S(1)} async-done(((bf16[32,144,128]{2,1,0:T(8,128)(2,1)}), bf16[32,144,128]{2,1,0:T(8,128)(2,1)S(1)}, u32[]{:S(2)}, u32[]{:S(2)}) %all-to-all-start.2) | async-done | bytes 1179680 | tf_op jit(solution)/shard_map/all_to_all | solution.py:464
  66.6 3.0 %collective-permute-start.4 = (bf16[32,64,128]{2,1,0:T(8,128)(2,1)S(1)}, bf16[32,64,128]{2,1,0:T(8,128)(2,1)S(1)}, u32[]{:S(2)}, u32[]{:S(2)}) collective-permute-start(bf16[32,64,128]{2,1,0:T(8,128)(2,1)S(1)} %collective-permute-done.refs_2_), channel_id=1, source_target_pairs={{0,96},{32,0},{64,32},{96,64},{1,97},{33,1},{65,33},{97,65},{2,98}... | collective-permute-start | bytes 1572872 | tf_op jit(solution)/shard_map/ppermute | solution.py:403
  70.6 10.0 %collective-permute-done.4.refs_4_ = bf16[32,64,128]{2,1,0:T(8,128)(2,1)S(1)} collective-permute-done((bf16[32,64,128]{2,1,0:T(8,128)(2,1)S(1)}, bf16[32,64,128]{2,1,0:T(8,128)(2,1)S(1)}, u32[]{:S(2)}, u32[]{:S(2)}) %collective-permute-start.4) | collective-permute-done | bytes 524320 | tf_op jit(solution)/shard_map/ppermute | solution.py:403
  81.7 2.2 collective-permute-done.5.refs_5_
  83.9 1.4 collective-permute-start.12
  86.8 7.8 %partial_scores.1 = (f32[2,512,128]{2,1,0:T(8,128)S(1)}, f32[2,512,128]{2,1,0:T(8,128)S(1)}, f32[2,512,128]{2,1,0:T(8,128)S(1)}, f32[2,512,128]{2,1,0:T(8,128)S(...) custom-call(s32[128]{0:T(128)S(1)} %and_select_fusion.ids, ...), custom_call_target="tpu_custom_call" | custom-call | bytes 20971520 | tf_op jit(solution)/shard_map/partial_scores/pallas_call | solution.py:180
  94.7 2.7 %collective-permute-start.20 = (f32[2,512,128]{2,1,0:T(8,128)S(1)}, f32[2,512,128]{2,1,0:T(8,128)S(1)}, u32[]{:S(2)}, u32[]{:S(2)}) collective-permute-start(f32[2,512,128]{2,1,0:T(8,128)S(1)} %get-tuple-element.35), channel_id=1, source_target_pairs={{0,24},{1,7},{2,26},{3,1},{4,28},{5,3},{6,30},{7,5},{8,0},{9,15},{... | collective-permute-start | bytes 1572872 | tf_op jit(solution)/shard_map/ppermute | solution.py:416
  97.4 1.4 collective-permute-start.19
  98.9 5.4 %collective-permute-done.15 = f32[2,512,128]{2,1,0:T(8,128)S(1)} collective-permute-done((f32[2,512,128]{2,1,0:T(8,128)S(1)}, f32[2,512,128]{2,1,0:T(8,128)S(1)}, u32[]{:S(2)}, u32[]{:S(2)}) %collective-permute-start.15) | collective-permute-done | bytes 524320 | tf_op jit(solution)/shard_map/ppermute | solution.py:416
  104.5 2.7 %collective-permute-start.21 = (f32[2,512,128]{2,1,0:T(8,128)S(1)}, f32[2,512,128]{2,1,0:T(8,128)S(1)}, u32[]{:S(2)}, u32[]{:S(2)}) collective-permute-start(f32[2,512,128]{2,1,0:T(8,128)S(1)} %add.108), channel_id=1, source_target_pairs={{0,24},{1,7},{2,26},{3,1},{4,28},{5,3},{6,30},{7,5},{8,0},{9,15},{... | collective-permute-start | bytes 1572872 | tf_op jit(solution)/shard_map/ppermute | solution.py:416
  107.2 1.9 collective-permute-done.17
  109.9 5.6 %collective-permute-done.16 = f32[2,512,128]{2,1,0:T(8,128)S(1)} collective-permute-done((f32[2,512,128]{2,1,0:T(8,128)S(1)}, f32[2,512,128]{2,1,0:T(8,128)S(1)}, u32[]{:S(2)}, u32[]{:S(2)}) %collective-permute-start.16) | collective-permute-done | bytes 524320 | tf_op jit(solution)/shard_map/ppermute | solution.py:416
  115.7 2.2 collective-permute-start.22
  118.5 6.7 %collective-permute-done.18 = f32[512,128]{1,0:T(8,128)S(1)} collective-permute-done((f32[512,128]{1,0:T(8,128)S(1)}, f32[512,128]{1,0:T(8,128)S(1)}, u32[]{:S(2)}, u32[]{:S(2)}) %collective-permute-start.18) | collective-permute-done | bytes 262176 | tf_op jit(solution)/shard_map/ppermute | solution.py:416
  126.0 2.6 %collective-permute-start.24 = (f32[512,128]{1,0:T(8,128)S(1)}, f32[512,128]{1,0:T(8,128)}, u32[]{:S(2)}, u32[]{:S(2)}) collective-permute-start(f32[512,128]{1,0:T(8,128)S(1)} %fusion.6.x_own), channel_id=1, source_target_pairs={{0,1},{1,0},{2,3},{3,2},{4,5},{5,4},{6,7},{7,6},{8,9},{9,8},{10,11... | collective-permute-start | bytes 786440 | tf_op jit(solution)/shard_map/ppermute | solution.py:416
  130.5 3.0 %softmax_weights.1 = bf16[528,128]{1,0:T(8,128)(2,1)S(1)} custom-call(s32[5]{0:T(128)S(1)} %stack.53.at, f32[512,128]{1,0:T(8,128)S(1)} %fusion.6.x_own, f32[512,128]{1,0:T(8,128)} %collective-permute-done.24.x_sib, s32[8,128]{1,0:T(8,128)S(1)} %stack.56.listv, bf16[32,144,128]{2,1,0:T(8,128)(2,1)S(1)} %all-to-all-done.2.q_own.q), custom_call_target="tpu_custom_call" | custom-call | bytes 8388608 | tf_op jit(solution)/shard_map/softmax_weights/pallas_call | solution.py:242
  133.6 2.4 %collective-permute-start.25 = (bf16[528,128]{1,0:T(8,128)(2,1)S(1)}, bf16[528,128]{1,0:T(8,128)(2,1)S(1)}, u32[]{:S(2)}, u32[]{:S(2)}) collective-permute-start(bf16[528,128]{1,0:T(8,128)(2,1)S(1)} %softmax_weights.1), channel_id=1, source_target_pairs={{0,24},{1,7},{2,26},{3,1},{4,28},{5,3},{6,30},{7,5},{8,0},{9,15},{... | collective-permute-start | bytes 405512 | tf_op jit(solution)/shard_map/ppermute | solution.py:416
  136.7 2.7 %collective-permute-done.25 = bf16[528,128]{1,0:T(8,128)(2,1)S(1)} collective-permute-done((bf16[528,128]{1,0:T(8,128)(2,1)S(1)}, bf16[528,128]{1,0:T(8,128)(2,1)S(1)}, u32[]{:S(2)}, u32[]{:S(2)}) %collective-permute-start.25) | collective-permute-done | bytes 135200 | tf_op jit(solution)/shard_map/ppermute | solution.py:416
  139.4 2.3 collective-permute-done.26
  143.0 2.7 %collective-permute-start.29 = (bf16[4,528,128]{2,1,0:T(8,128)(2,1)S(1)}, bf16[4,528,128]{2,1,0:T(8,128)(2,1)S(1)}, u32[]{:S(2)}, u32[]{:S(2)}) collective-permute-start(bf16[4,528,128]{2,1,0:T(8,128)(2,1)S(1)} %pad_maximum_fusion.refs_0_), channel_id=1, source_target_pairs={{0,6},{1,25},{2,0},{3,27},{4,2},{5,29},{6,4},{7,31},{8,14},{9,1},{... | collective-permute-start | bytes 1622024 | tf_op jit(solution)/shard_map/ppermute | solution.py:416
  145.8 6.3 %collective-permute-done.29.refs_2_ = bf16[4,528,128]{2,1,0:T(8,128)(2,1)S(1)} collective-permute-done((bf16[4,528,128]{2,1,0:T(8,128)(2,1)S(1)}, bf16[4,528,128]{2,1,0:T(8,128)(2,1)S(1)}, u32[]{:S(2)}, u32[]{:S(2)}) %collective-permute-start.29) | collective-permute-done | bytes 540704 | tf_op jit(solution)/shard_map/ppermute | solution.py:416
  152.1 3.4 %collective-permute-start.30 = (bf16[4,528,128]{2,1,0:T(8,128)(2,1)S(1)}, bf16[4,528,128]{2,1,0:T(8,128)(2,1)S(1)}, u32[]{:S(2)}, u32[]{:S(2)}) collective-permute-start(bf16[4,528,128]{2,1,0:T(8,128)(2,1)S(1)} %collective-permute-done.29.refs_2_), channel_id=1, source_target_pairs={{0,6},{1,25},{2,0},{3,27},{4,2},{5,29},{6,4},{7,31},{8,14},{9,1},{... | collective-permute-start | bytes 1622024 | tf_op jit(solution)/shard_map/ppermute | solution.py:416
  155.5 2.4 %collective-permute-start.31 = (bf16[4,528,128]{2,1,0:T(8,128)(2,1)S(1)}, bf16[4,528,128]{2,1,0:T(8,128)(2,1)S(1)}, u32[]{:S(2)}, u32[]{:S(2)}) collective-permute-start(bf16[4,528,128]{2,1,0:T(8,128)(2,1)S(1)} %pad_maximum_fusion.refs_0_), channel_id=1, source_target_pairs={{0,1},{1,0},{2,3},{3,2},{4,5},{5,4},{6,7},{7,6},{8,9},{9,8},{10,11... | collective-permute-start | bytes 1622024 | tf_op jit(solution)/shard_map/ppermute | solution.py:416
  158.4 3.4 %collective-permute-done.30.refs_3_ = bf16[4,528,128]{2,1,0:T(8,128)(2,1)S(1)} collective-permute-done((bf16[4,528,128]{2,1,0:T(8,128)(2,1)S(1)}, bf16[4,528,128]{2,1,0:T(8,128)(2,1)S(1)}, u32[]{:S(2)}, u32[]{:S(2)}) %collective-permute-start.30) | collective-permute-done | bytes 540704 | tf_op jit(solution)/shard_map/ppermute | solution.py:416
  161.8 3.0 %collective-permute-start.34 = (bf16[4,528,128]{2,1,0:T(8,128)(2,1)S(1)}, bf16[4,528,128]{2,1,0:T(8,128)(2,1)S(1)}, u32[]{:S(2)}, u32[]{:S(2)}) collective-permute-start(bf16[4,528,128]{2,1,0:T(8,128)(2,1)S(1)} %collective-permute-done.30.refs_3_), channel_id=1, source_target_pairs={{0,1},{1,0},{2,3},{3,2},{4,5},{5,4},{6,7},{7,6},{8,9},{9,8},{10,11... | collective-permute-start | bytes 1622024 | tf_op jit(solution)/shard_map/ppermute | solution.py:416
  164.8 1.4 place.1.p
  166.3 7.8 %grad_passages.1 = (bf16[32,128,128]{2,1,0:T(8,128)(2,1)S(1)}, bf16[16,128,128]{2,1,0:T(8,128)(2,1)S(1)}, bf16[16,128,128]{2,1,0:T(8,128)(2,1)}, bf16[16,128,128...) custom-call(s32[128]{0:T(128)S(1)} %and_select_fusion.ids, ...), custom_call_target="tpu_custom_call" | custom-call | bytes 20971520 | tf_op jit(solution)/shard_map/grad_passages/pallas_call | solution.py:317
  175.7 1.7 collective-permute-start.37
  177.4 6.1 %grad_queries.1 = bf16[32,128,128]{2,1,0:T(8,128)(2,1)} custom-call(s32[128]{0:T(128)S(1)} %and_select_fusion.ids, s32[128]{0:T(128)S(1)} %convert_reduce_fusion.own, s32[5]{0:T(128)S(1)} %stack.53.at, bf16[128,128,128]{2,1,0:T(8,128)(2,1)S(1)} %place.1.p, bf16[4,528,128]{2,1,0:T(8,128)(2,1)S(1)} %pad_maximum_fusion.refs_0_, ...), custom_call_target="tpu_custom_call" | custom-call | bytes 20971520 | tf_op jit(solution)/shard_map/grad_queries/pallas_call | solution.py:352
  183.5 6.7 %all-to-all-start.3 = ((bf16[32,128,128]{2,1,0:T(8,128)(2,1)}), bf16[32,128,128]{2,1,0:T(8,128)(2,1)S(1)}, u32[]{:S(2)}, u32[]{:S(2)}) async-start(bf16[32,128,128]{2,1,0:T(8,128)(2,1)} %grad_queries.1), calls=%async_computation.3 | async-start | bytes 2097152 | tf_op jit(solution)/shard_map/all_to_all | solution.py:464
  191.4 3.0 %collective-permute-start.40 = (bf16[16,128,128]{2,1,0:T(8,128)(2,1)S(1)}, bf16[16,128,128]{2,1,0:T(8,128)(2,1)S(1)}, u32[]{:S(2)}, u32[]{:S(2)}) collective-permute-start(bf16[16,128,128]{2,1,0:T(8,128)(2,1)S(1)} %add_convert_fusion), channel_id=1, source_target_pairs={{0,96},{32,0},{64,32},{96,64},{1,97},{33,1},{65,33},{97,65},{2,98}... | collective-permute-start | bytes 1572872 | tf_op jit(solution)/shard_map/ppermute | solution.py:403
  195.7 3.2 %collective-permute-done.37.refs_1_ = bf16[16,128,128]{2,1,0:T(8,128)(2,1)} collective-permute-done((bf16[16,128,128]{2,1,0:T(8,128)(2,1)}, bf16[16,128,128]{2,1,0:T(8,128)(2,1)}, u32[]{:S(2)}, u32[]{:S(2)}) %collective-permute-start.37) | collective-permute-done | bytes 524320 | tf_op jit(solution)/shard_map/ppermute | solution.py:403
  198.9 1.4 collective-permute-done.38.refs_2_
  200.3 9.7 %collective-permute-done.40.refs_3_ = bf16[16,128,128]{2,1,0:T(8,128)(2,1)S(1)} collective-permute-done((bf16[16,128,128]{2,1,0:T(8,128)(2,1)S(1)}, bf16[16,128,128]{2,1,0:T(8,128)(2,1)S(1)}, u32[]{:S(2)}, u32[]{:S(2)}) %collective-permute-start.40) | collective-permute-done | bytes 524320 | tf_op jit(solution)/shard_map/ppermute | solution.py:403
  210.0 1.4 collective-permute-done.36.refs_0_
  211.4 2.4 %join.1 = bf16[32,128,128]{2,1,0:T(8,128)(2,1)} custom-call(bf16[32,128,128]{2,1,0:T(8,128)(2,1)S(1)} %get-tuple-element.38.kept, bf16[16,128,128]{2,1,0:T(8,128)(2,1)S(1)} %collective-permute-done.36.refs_0_, bf16[16,128,128]{2,1,0:T(8,128)(2,1)} %collective-permute-done.37.refs_1_, bf16[16,128,128]{2,1,0:T(8,128)(2,1)} %collective-permute-done.38.refs_2_, ...), custom_call_target="tpu_custom_call" | custom-call | bytes 8388608 | tf_op jit(solution)/shard_map/join/pallas_call | solution.py:388
  213.9 7.0 %all-to-all-start.4 = ((bf16[32,128,128]{2,1,0:T(8,128)(2,1)}), bf16[32,128,128]{2,1,0:T(8,128)(2,1)S(1)}, u32[]{:S(2)}, u32[]{:S(2)}) async-start(bf16[32,128,128]{2,1,0:T(8,128)(2,1)} %join.1), calls=%async_computation.4 | async-start | bytes 2097152 | tf_op jit(solution)/shard_map/all_to_all | solution.py:464
  221.5 1.4 unpack.2
  222.9 14.9 %all-to-all-done.4.x = bf16[32,128,128]{2,1,0:T(8,128)(2,1)S(1)} async-done(((bf16[32,128,128]{2,1,0:T(8,128)(2,1)}), bf16[32,128,128]{2,1,0:T(8,128)(2,1)S(1)}, u32[]{:S(2)}, u32[]{:S(2)}) %all-to-all-start.4) | async-done | bytes 1048608 | tf_op jit(solution)/shard_map/all_to_all | solution.py:464
  237.8 1.4 unpack.3
  (94 shorter events, 19.2 us)
Async XLA Ops:
  23.1 20.4 %collective-permute-start = (bf16[32,64,128]{2,1,0:T(8,128)(2,1)S(1)}, bf16[32,64,128]{2,1,0:T(8,128)(2,1)S(1)}, u32[]{:S(2)}, u32[]{:S(2)}) collective-permute-start(bf16[32,64,128]{2,1,0:T(8,128)(2,1)S(1)} %all_to_all.25.refs_0_), channel_id=1, source_target_pairs={{0,96},{32,0},{64,32},{96,64},{1,97},{33,1},{65,33},{97,65},{2,98}... | collective-permute-start | bytes 1572872 | tf_op jit(solution)/shard_map/ppermute | solution.py:403
  26.8 16.7 %collective-permute-start.1 = (bf16[32,64,128]{2,1,0:T(8,128)(2,1)S(1)}, bf16[32,64,128]{2,1,0:T(8,128)(2,1)S(1)}, u32[]{:S(2)}, u32[]{:S(2)}) collective-permute-start(bf16[32,64,128]{2,1,0:T(8,128)(2,1)S(1)} %all_to_all.25.refs_0_), channel_id=1, source_target_pairs={{0,32},{32,64},{64,96},{96,0},{1,33},{33,65},{65,97},{97,1},{2,34}... | collective-permute-start | bytes 1572872 | tf_op jit(solution)/shard_map/ppermute | solution.py:403
  28.0 15.5 %all-to-all-start = ((bf16[32,64,128]{2,1,0:T(8,128)(2,1)}), bf16[32,64,128]{2,1,0:T(8,128)(2,1)S(1)}, u32[]{:S(2)}, u32[]{:S(2)}) async-start(bf16[32,64,128]{2,1,0:T(8,128)(2,1)} %pack.4), calls=%async_computation | async-start | bytes 1048576 | tf_op jit(solution)/shard_map/all_to_all | solution.py:464
  33.5 36.0 %copy-start.8 = (s32[1,32]{1,0:T(1,128)S(1)}, s32[1,32]{1,0:T(1,128)}, u32[]{:S(2)}) copy-start(s32[1,32]{1,0:T(1,128)} %param.8) | copy-start | bytes 388
  43.5 22.0 %all-to-all-start.2 = ((bf16[32,144,128]{2,1,0:T(8,128)(2,1)}), bf16[32,144,128]{2,1,0:T(8,128)(2,1)S(1)}, u32[]{:S(2)}, u32[]{:S(2)}) async-start(bf16[32,144,128]{2,1,0:T(8,128)(2,1)} %pack.3), calls=%async_computation.2 | async-start | bytes 2359296 | tf_op jit(solution)/shard_map/all_to_all | solution.py:464
  47.3 18.8 %collective-permute-start.2 = (bf16[32,64,128]{2,1,0:T(8,128)(2,1)S(1)}, bf16[32,64,128]{2,1,0:T(8,128)(2,1)}, u32[]{:S(2)}, u32[]{:S(2)}) collective-permute-start(bf16[32,64,128]{2,1,0:T(8,128)(2,1)S(1)} %all-to-all-done.refs_1_), channel_id=1, source_target_pairs={{0,96},{32,0},{64,32},{96,64},{1,97},{33,1},{65,33},{97,65},{2,98}... | collective-permute-start | bytes 1572872 | tf_op jit(solution)/shard_map/ppermute | solution.py:403
  50.3 16.0 %collective-permute-start.3 = (bf16[32,64,128]{2,1,0:T(8,128)(2,1)S(1)}, bf16[32,64,128]{2,1,0:T(8,128)(2,1)}, u32[]{:S(2)}, u32[]{:S(2)}) collective-permute-start(bf16[32,64,128]{2,1,0:T(8,128)(2,1)S(1)} %all-to-all-done.refs_1_), channel_id=1, source_target_pairs={{0,32},{32,64},{64,96},{96,0},{1,33},{33,65},{65,97},{97,1},{2,34}... | collective-permute-start | bytes 1572872 | tf_op jit(solution)/shard_map/ppermute | solution.py:403
  50.3 16.3 %collective-permute-start.7 = (bf16[32,64,128]{2,1,0:T(8,128)(2,1)S(1)}, bf16[32,64,128]{2,1,0:T(8,128)(2,1)}, u32[]{:S(2)}, u32[]{:S(2)}) collective-permute-start(bf16[32,64,128]{2,1,0:T(8,128)(2,1)S(1)} %all_to_all.25.refs_0_), channel_id=1, source_target_pairs={{0,1},{1,0},{2,3},{3,2},{4,5},{5,4},{6,7},{7,6},{8,9},{9,8},{10,11... | collective-permute-start | bytes 1572872 | tf_op jit(solution)/shard_map/ppermute | solution.py:416
  50.7 18.8 %collective-permute-start.8 = (bf16[32,64,128]{2,1,0:T(8,128)(2,1)S(1)}, bf16[32,64,128]{2,1,0:T(8,128)(2,1)}, u32[]{:S(2)}, u32[]{:S(2)}) collective-permute-start(bf16[32,64,128]{2,1,0:T(8,128)(2,1)S(1)} %all-to-all-done.refs_1_), channel_id=1, source_target_pairs={{0,1},{1,0},{2,3},{3,2},{4,5},{5,4},{6,7},{7,6},{8,9},{9,8},{10,11... | collective-permute-start | bytes 1572872 | tf_op jit(solution)/shard_map/ppermute | solution.py:416
  65.5 21.3 %collective-permute-start.6 = (bf16[32,144,128]{2,1,0:T(8,128)(2,1)S(1)}, bf16[32,144,128]{2,1,0:T(8,128)(2,1)}, u32[]{:S(2)}, u32[]{:S(2)}) collective-permute-start(bf16[32,144,128]{2,1,0:T(8,128)(2,1)S(1)} %all-to-all-done.2.q_own.q), channel_id=1, source_target_pairs={{0,1},{1,0},{2,3},{3,2},{4,5},{5,4},{6,7},{7,6},{8,9},{9,8},{10,11... | collective-permute-start | bytes 3538952 | tf_op jit(solution)/shard_map/ppermute | solution.py:416
  66.0 3.8 %collective-permute-start.9 = (bf16[32,64,128]{2,1,0:T(8,128)(2,1)S(1)}, bf16[32,64,128]{2,1,0:T(8,128)(2,1)S(1)}, u32[]{:S(2)}, u32[]{:S(2)}) collective-permute-start(bf16[32,64,128]{2,1,0:T(8,128)(2,1)S(1)} %collective-permute-done.refs_2_), channel_id=1, source_target_pairs={{0,1},{1,0},{2,3},{3,2},{4,5},{5,4},{6,7},{7,6},{8,9},{9,8},{10,11... | collective-permute-start | bytes 1572872 | tf_op jit(solution)/shard_map/ppermute | solution.py:416
  66.3 4.1 %collective-permute-start.13 = (bf16[32,64,128]{2,1,0:T(8,128)(2,1)S(1)}, bf16[32,64,128]{2,1,0:T(8,128)(2,1)S(1)}, u32[]{:S(2)}, u32[]{:S(2)}) collective-permute-start(bf16[32,64,128]{2,1,0:T(8,128)(2,1)S(1)} %collective-permute-done.1.refs_6_), channel_id=1, source_target_pairs={{0,1},{1,0},{2,3},{3,2},{4,5},{5,4},{6,7},{7,6},{8,9},{9,8},{10,11... | collective-permute-start | bytes 1572872 | tf_op jit(solution)/shard_map/ppermute | solution.py:416
  66.6 14.0 %collective-permute-start.4 = (bf16[32,64,128]{2,1,0:T(8,128)(2,1)S(1)}, bf16[32,64,128]{2,1,0:T(8,128)(2,1)S(1)}, u32[]{:S(2)}, u32[]{:S(2)}) collective-permute-start(bf16[32,64,128]{2,1,0:T(8,128)(2,1)S(1)} %collective-permute-done.refs_2_), channel_id=1, source_target_pairs={{0,96},{32,0},{64,32},{96,64},{1,97},{33,1},{65,33},{97,65},{2,98}... | collective-permute-start | bytes 1572872 | tf_op jit(solution)/shard_map/ppermute | solution.py:403
  69.5 14.4 %collective-permute-start.5 = (bf16[32,64,128]{2,1,0:T(8,128)(2,1)}, bf16[32,64,128]{2,1,0:T(8,128)(2,1)S(1)}, u32[]{:S(2)}, u32[]{:S(2)}) collective-permute-start(bf16[32,64,128]{2,1,0:T(8,128)(2,1)} %collective-permute-done.3.refs_7_), channel_id=1, source_target_pairs={{0,32},{32,64},{64,96},{96,0},{1,33},{33,65},{65,97},{97,1},{2,34}... | collective-permute-start | bytes 1572872 | tf_op jit(solution)/shard_map/ppermute | solution.py:403
  69.9 15.6 %collective-permute-start.10 = (bf16[32,64,128]{2,1,0:T(8,128)(2,1)}, bf16[32,64,128]{2,1,0:T(8,128)(2,1)S(1)}, u32[]{:S(2)}, u32[]{:S(2)}) collective-permute-start(bf16[32,64,128]{2,1,0:T(8,128)(2,1)} %collective-permute-done.2.refs_3_), channel_id=1, source_target_pairs={{0,1},{1,0},{2,3},{3,2},{4,5},{5,4},{6,7},{7,6},{8,9},{9,8},{10,11... | collective-permute-start | bytes 1572872 | tf_op jit(solution)/shard_map/ppermute | solution.py:416
  70.5 15.0 %collective-permute-start.14 = (bf16[32,64,128]{2,1,0:T(8,128)(2,1)}, bf16[32,64,128]{2,1,0:T(8,128)(2,1)S(1)}, u32[]{:S(2)}, u32[]{:S(2)}) collective-permute-start(bf16[32,64,128]{2,1,0:T(8,128)(2,1)} %collective-permute-done.3.refs_7_), channel_id=1, source_target_pairs={{0,1},{1,0},{2,3},{3,2},{4,5},{5,4},{6,7},{7,6},{8,9},{9,8},{10,11... | collective-permute-start | bytes 1572872 | tf_op jit(solution)/shard_map/ppermute | solution.py:416
  80.6 4.9 %collective-permute-start.11 = (bf16[32,64,128]{2,1,0:T(8,128)(2,1)S(1)}, bf16[32,64,128]{2,1,0:T(8,128)(2,1)S(1)}, u32[]{:S(2)}, u32[]{:S(2)}) collective-permute-start(bf16[32,64,128]{2,1,0:T(8,128)(2,1)S(1)} %collective-permute-done.4.refs_4_), channel_id=1, source_target_pairs={{0,1},{1,0},{2,3},{3,2},{4,5},{5,4},{6,7},{7,6},{8,9},{9,8},{10,11... | collective-permute-start | bytes 1572872 | tf_op jit(solution)/shard_map/ppermute | solution.py:416
  83.9 2.9 %collective-permute-start.12 = (bf16[32,64,128]{2,1,0:T(8,128)(2,1)S(1)}, bf16[32,64,128]{2,1,0:T(8,128)(2,1)S(1)}, u32[]{:S(2)}, u32[]{:S(2)}) collective-permute-start(bf16[32,64,128]{2,1,0:T(8,128)(2,1)S(1)} %collective-permute-done.5.refs_5_), channel_id=1, source_target_pairs={{0,1},{1,0},{2,3},{3,2},{4,5},{5,4},{6,7},{7,6},{8,9},{9,8},{10,11... | collective-permute-start | bytes 1572872 | tf_op jit(solution)/shard_map/ppermute | solution.py:416
  94.6 9.6 %collective-permute-start.15 = (f32[2,512,128]{2,1,0:T(8,128)S(1)}, f32[2,512,128]{2,1,0:T(8,128)S(1)}, u32[]{:S(2)}, u32[]{:S(2)}) collective-permute-start(f32[2,512,128]{2,1,0:T(8,128)S(1)} %get-tuple-element.31), channel_id=1, source_target_pairs={{0,8},{1,3},{2,10},{3,5},{4,12},{5,7},{6,14},{7,1},{8,16},{9,11},{... | collective-permute-start | bytes 1572872 | tf_op jit(solution)/shard_map/ppermute | solution.py:416
  94.7 9.7 %collective-permute-start.20 = (f32[2,512,128]{2,1,0:T(8,128)S(1)}, f32[2,512,128]{2,1,0:T(8,128)S(1)}, u32[]{:S(2)}, u32[]{:S(2)}) collective-permute-start(f32[2,512,128]{2,1,0:T(8,128)S(1)} %get-tuple-element.35), channel_id=1, source_target_pairs={{0,24},{1,7},{2,26},{3,1},{4,28},{5,3},{6,30},{7,5},{8,0},{9,15},{... | collective-permute-start | bytes 1572872 | tf_op jit(solution)/shard_map/ppermute | solution.py:416
  97.4 11.7 %collective-permute-start.17 = (f32[2,512,128]{2,1,0:T(8,128)S(1)}, f32[2,512,128]{2,1,0:T(8,128)S(1)}, u32[]{:S(2)}, u32[]{:S(2)}) collective-permute-start(f32[2,512,128]{2,1,0:T(8,128)S(1)} %get-tuple-element.32), channel_id=1, source_target_pairs={{0,24},{1,7},{2,26},{3,1},{4,28},{5,3},{6,30},{7,5},{8,0},{9,15},{... | collective-permute-start | bytes 1572872 | tf_op jit(solution)/shard_map/ppermute | solution.py:416
  97.4 12.4 %collective-permute-start.19 = (f32[2,512,128]{2,1,0:T(8,128)S(1)}, f32[2,512,128]{2,1,0:T(8,128)S(1)}, u32[]{:S(2)}, u32[]{:S(2)}) collective-permute-start(f32[2,512,128]{2,1,0:T(8,128)S(1)} %get-tuple-element.33), channel_id=1, source_target_pairs={{0,8},{1,3},{2,10},{3,5},{4,12},{5,7},{6,14},{7,1},{8,16},{9,11},{... | collective-permute-start | bytes 1572872 | tf_op jit(solution)/shard_map/ppermute | solution.py:416
  104.3 11.2 %collective-permute-start.16 = (f32[2,512,128]{2,1,0:T(8,128)S(1)}, f32[2,512,128]{2,1,0:T(8,128)S(1)}, u32[]{:S(2)}, u32[]{:S(2)}) collective-permute-start(f32[2,512,128]{2,1,0:T(8,128)S(1)} %add.99), channel_id=1, source_target_pairs={{0,8},{1,3},{2,10},{3,5},{4,12},{5,7},{6,14},{7,1},{8,16},{9,11},{... | collective-permute-start | bytes 1572872 | tf_op jit(solution)/shard_map/ppermute | solution.py:416
  104.5 11.0 %collective-permute-start.21 = (f32[2,512,128]{2,1,0:T(8,128)S(1)}, f32[2,512,128]{2,1,0:T(8,128)S(1)}, u32[]{:S(2)}, u32[]{:S(2)}) collective-permute-start(f32[2,512,128]{2,1,0:T(8,128)S(1)} %add.108), channel_id=1, source_target_pairs={{0,24},{1,7},{2,26},{3,1},{4,28},{5,3},{6,30},{7,5},{8,0},{9,15},{... | collective-permute-start | bytes 1572872 | tf_op jit(solution)/shard_map/ppermute | solution.py:416
  115.6 9.6 %collective-permute-start.18 = (f32[512,128]{1,0:T(8,128)S(1)}, f32[512,128]{1,0:T(8,128)S(1)}, u32[]{:S(2)}, u32[]{:S(2)}) collective-permute-start(f32[512,128]{1,0:T(8,128)S(1)} %get-tuple-element.47), channel_id=1, source_target_pairs={{0,2},{1,9},{2,4},{3,11},{4,6},{5,13},{6,0},{7,15},{8,10},{9,17},{... | collective-permute-start | bytes 786440 | tf_op jit(solution)/shard_map/ppermute | solution.py:416
  115.7 9.5 %collective-permute-start.22 = (f32[512,128]{1,0:T(8,128)S(1)}, f32[512,128]{1,0:T(8,128)S(1)}, u32[]{:S(2)}, u32[]{:S(2)}) collective-permute-start(f32[512,128]{1,0:T(8,128)S(1)} %get-tuple-element.45), channel_id=1, source_target_pairs={{0,4},{1,17},{2,6},{3,19},{4,0},{5,21},{6,2},{7,23},{8,12},{9,25},... | collective-permute-start | bytes 786440 | tf_op jit(solution)/shard_map/ppermute | solution.py:416
  118.0 7.9 %collective-permute-start.23 = (f32[512,128]{1,0:T(8,128)S(1)}, f32[512,128]{1,0:T(8,128)S(1)}, u32[]{:S(2)}, u32[]{:S(2)}) collective-permute-start(f32[512,128]{1,0:T(8,128)S(1)} %get-tuple-element.46), channel_id=1, source_target_pairs={{0,6},{1,25},{2,0},{3,27},{4,2},{5,29},{6,4},{7,31},{8,14},{9,1},{... | collective-permute-start | bytes 786440 | tf_op jit(solution)/shard_map/ppermute | solution.py:416
  126.0 4.5 %collective-permute-start.24 = (f32[512,128]{1,0:T(8,128)S(1)}, f32[512,128]{1,0:T(8,128)}, u32[]{:S(2)}, u32[]{:S(2)}) collective-permute-start(f32[512,128]{1,0:T(8,128)S(1)} %fusion.6.x_own), channel_id=1, source_target_pairs={{0,1},{1,0},{2,3},{3,2},{4,5},{5,4},{6,7},{7,6},{8,9},{9,8},{10,11... | collective-permute-start | bytes 786440 | tf_op jit(solution)/shard_map/ppermute | solution.py:416
  130.5 34.3 %copy-start.2 = (bf16[32,64,128]{2,1,0:T(8,128)(2,1)S(1)}, bf16[32,64,128]{2,1,0:T(8,128)(2,1)}, u32[]{:S(2)}) copy-start(bf16[32,64,128]{2,1,0:T(8,128)(2,1)} %copy-done.1) | copy-start | bytes 1572868
  130.5 34.3 %copy-start.4 = (bf16[32,64,128]{2,1,0:T(8,128)(2,1)S(1)}, bf16[32,64,128]{2,1,0:T(8,128)(2,1)}, u32[]{:S(2)}) copy-start(bf16[32,64,128]{2,1,0:T(8,128)(2,1)} %copy-done.3) | copy-start | bytes 1572868
  133.6 5.8 %collective-permute-start.25 = (bf16[528,128]{1,0:T(8,128)(2,1)S(1)}, bf16[528,128]{1,0:T(8,128)(2,1)S(1)}, u32[]{:S(2)}, u32[]{:S(2)}) collective-permute-start(bf16[528,128]{1,0:T(8,128)(2,1)S(1)} %softmax_weights.1), channel_id=1, source_target_pairs={{0,24},{1,7},{2,26},{3,1},{4,28},{5,3},{6,30},{7,5},{8,0},{9,15},{... | collective-permute-start | bytes 405512 | tf_op jit(solution)/shard_map/ppermute | solution.py:416
  136.0 5.7 %collective-permute-start.26 = (bf16[528,128]{1,0:T(8,128)(2,1)S(1)}, bf16[528,128]{1,0:T(8,128)(2,1)S(1)}, u32[]{:S(2)}, u32[]{:S(2)}) collective-permute-start(bf16[528,128]{1,0:T(8,128)(2,1)S(1)} %softmax_weights.1), channel_id=1, source_target_pairs={{0,16},{1,5},{2,18},{3,7},{4,20},{5,1},{6,22},{7,3},{8,24},{9,13},... | collective-permute-start | bytes 405512 | tf_op jit(solution)/shard_map/ppermute | solution.py:416
  136.2 6.8 %collective-permute-start.27 = (bf16[528,128]{1,0:T(8,128)(2,1)S(1)}, bf16[528,128]{1,0:T(8,128)(2,1)S(1)}, u32[]{:S(2)}, u32[]{:S(2)}) collective-permute-start(bf16[528,128]{1,0:T(8,128)(2,1)S(1)} %softmax_weights.1), channel_id=1, source_target_pairs={{0,8},{1,3},{2,10},{3,5},{4,12},{5,7},{6,14},{7,1},{8,16},{9,11},{... | collective-permute-start | bytes 405512 | tf_op jit(solution)/shard_map/ppermute | solution.py:416
  143.0 9.0 %collective-permute-start.29 = (bf16[4,528,128]{2,1,0:T(8,128)(2,1)S(1)}, bf16[4,528,128]{2,1,0:T(8,128)(2,1)S(1)}, u32[]{:S(2)}, u32[]{:S(2)}) collective-permute-start(bf16[4,528,128]{2,1,0:T(8,128)(2,1)S(1)} %pad_maximum_fusion.refs_0_), channel_id=1, source_target_pairs={{0,6},{1,25},{2,0},{3,27},{4,2},{5,29},{6,4},{7,31},{8,14},{9,1},{... | collective-permute-start | bytes 1622024 | tf_op jit(solution)/shard_map/ppermute | solution.py:416
  145.8 12.1 %collective-permute-start.28 = (bf16[4,528,128]{2,1,0:T(8,128)(2,1)S(1)}, bf16[4,528,128]{2,1,0:T(8,128)(2,1)S(1)}, u32[]{:S(2)}, u32[]{:S(2)}) collective-permute-start(bf16[4,528,128]{2,1,0:T(8,128)(2,1)S(1)} %pad_maximum_fusion.refs_0_), channel_id=1, source_target_pairs={{0,2},{1,9},{2,4},{3,11},{4,6},{5,13},{6,0},{7,15},{8,10},{9,17},{... | collective-permute-start | bytes 1622024 | tf_op jit(solution)/shard_map/ppermute | solution.py:416
  152.1 9.7 %collective-permute-start.30 = (bf16[4,528,128]{2,1,0:T(8,128)(2,1)S(1)}, bf16[4,528,128]{2,1,0:T(8,128)(2,1)S(1)}, u32[]{:S(2)}, u32[]{:S(2)}) collective-permute-start(bf16[4,528,128]{2,1,0:T(8,128)(2,1)S(1)} %collective-permute-done.29.refs_2_), channel_id=1, source_target_pairs={{0,6},{1,25},{2,0},{3,27},{4,2},{5,29},{6,4},{7,31},{8,14},{9,1},{... | collective-permute-start | bytes 1622024 | tf_op jit(solution)/shard_map/ppermute | solution.py:416
  155.5 10.8 %collective-permute-start.31 = (bf16[4,528,128]{2,1,0:T(8,128)(2,1)S(1)}, bf16[4,528,128]{2,1,0:T(8,128)(2,1)S(1)}, u32[]{:S(2)}, u32[]{:S(2)}) collective-permute-start(bf16[4,528,128]{2,1,0:T(8,128)(2,1)S(1)} %pad_maximum_fusion.refs_0_), channel_id=1, source_target_pairs={{0,1},{1,0},{2,3},{3,2},{4,5},{5,4},{6,7},{7,6},{8,9},{9,8},{10,11... | collective-permute-start | bytes 1622024 | tf_op jit(solution)/shard_map/ppermute | solution.py:416
  157.9 8.3 %collective-permute-start.33 = (bf16[4,528,128]{2,1,0:T(8,128)(2,1)S(1)}, bf16[4,528,128]{2,1,0:T(8,128)(2,1)S(1)}, u32[]{:S(2)}, u32[]{:S(2)}) collective-permute-start(bf16[4,528,128]{2,1,0:T(8,128)(2,1)S(1)} %collective-permute-done.29.refs_2_), channel_id=1, source_target_pairs={{0,1},{1,0},{2,3},{3,2},{4,5},{5,4},{6,7},{7,6},{8,9},{9,8},{10,11... | collective-permute-start | bytes 1622024 | tf_op jit(solution)/shard_map/ppermute | solution.py:416
  157.9 8.3 %collective-permute-start.32 = (bf16[4,528,128]{2,1,0:T(8,128)(2,1)S(1)}, bf16[4,528,128]{2,1,0:T(8,128)(2,1)S(1)}, u32[]{:S(2)}, u32[]{:S(2)}) collective-permute-start(bf16[4,528,128]{2,1,0:T(8,128)(2,1)S(1)} %collective-permute-done.28.refs_1_), channel_id=1, source_target_pairs={{0,1},{1,0},{2,3},{3,2},{4,5},{5,4},{6,7},{7,6},{8,9},{9,8},{10,11... | collective-permute-start | bytes 1622024 | tf_op jit(solution)/shard_map/ppermute | solution.py:416
  161.8 4.6 %collective-permute-start.34 = (bf16[4,528,128]{2,1,0:T(8,128)(2,1)S(1)}, bf16[4,528,128]{2,1,0:T(8,128)(2,1)S(1)}, u32[]{:S(2)}, u32[]{:S(2)}) collective-permute-start(bf16[4,528,128]{2,1,0:T(8,128)(2,1)S(1)} %collective-permute-done.30.refs_3_), channel_id=1, source_target_pairs={{0,1},{1,0},{2,3},{3,2},{4,5},{5,4},{6,7},{7,6},{8,9},{9,8},{10,11... | collective-permute-start | bytes 1622024 | tf_op jit(solution)/shard_map/ppermute | solution.py:416
  174.2 16.0 %collective-permute-start.39 = (bf16[16,128,128]{2,1,0:T(8,128)(2,1)}, bf16[16,128,128]{2,1,0:T(8,128)(2,1)}, u32[]{:S(2)}, u32[]{:S(2)}) collective-permute-start(bf16[16,128,128]{2,1,0:T(8,128)(2,1)} %get-tuple-element.44), channel_id=1, source_target_pairs={{0,96},{32,0},{64,32},{96,64},{1,97},{33,1},{65,33},{97,65},{2,98}... | collective-permute-start | bytes 1572872 | tf_op jit(solution)/shard_map/ppermute | solution.py:403
  174.7 19.7 %collective-permute-start.35 = (bf16[16,128,128]{2,1,0:T(8,128)(2,1)}, bf16[16,128,128]{2,1,0:T(8,128)(2,1)}, u32[]{:S(2)}, u32[]{:S(2)}) collective-permute-start(bf16[16,128,128]{2,1,0:T(8,128)(2,1)} %get-tuple-element.40), channel_id=1, source_target_pairs={{0,32},{32,64},{64,96},{96,0},{1,33},{33,65},{65,97},{97,1},{2,34}... | collective-permute-start | bytes 1572872 | tf_op jit(solution)/shard_map/ppermute | solution.py:403
  175.7 23.2 %collective-permute-start.37 = (bf16[16,128,128]{2,1,0:T(8,128)(2,1)}, bf16[16,128,128]{2,1,0:T(8,128)(2,1)}, u32[]{:S(2)}, u32[]{:S(2)}) collective-permute-start(bf16[16,128,128]{2,1,0:T(8,128)(2,1)} %get-tuple-element.41), channel_id=1, source_target_pairs={{0,96},{32,0},{64,32},{96,64},{1,97},{33,1},{65,33},{97,65},{2,98}... | collective-permute-start | bytes 1572872 | tf_op jit(solution)/shard_map/ppermute | solution.py:403
  177.4 22.9 %collective-permute-start.38 = (bf16[16,128,128]{2,1,0:T(8,128)(2,1)}, bf16[16,128,128]{2,1,0:T(8,128)(2,1)}, u32[]{:S(2)}, u32[]{:S(2)}) collective-permute-start(bf16[16,128,128]{2,1,0:T(8,128)(2,1)} %get-tuple-element.42), channel_id=1, source_target_pairs={{0,32},{32,64},{64,96},{96,0},{1,33},{33,65},{65,97},{97,1},{2,34}... | collective-permute-start | bytes 1572872 | tf_op jit(solution)/shard_map/ppermute | solution.py:403
  183.5 30.4 %all-to-all-start.3 = ((bf16[32,128,128]{2,1,0:T(8,128)(2,1)}), bf16[32,128,128]{2,1,0:T(8,128)(2,1)S(1)}, u32[]{:S(2)}, u32[]{:S(2)}) async-start(bf16[32,128,128]{2,1,0:T(8,128)(2,1)} %grad_queries.1), calls=%async_computation.3 | async-start | bytes 2097152 | tf_op jit(solution)/shard_map/all_to_all | solution.py:464
  191.4 18.6 %collective-permute-start.40 = (bf16[16,128,128]{2,1,0:T(8,128)(2,1)S(1)}, bf16[16,128,128]{2,1,0:T(8,128)(2,1)S(1)}, u32[]{:S(2)}, u32[]{:S(2)}) collective-permute-start(bf16[16,128,128]{2,1,0:T(8,128)(2,1)S(1)} %add_convert_fusion), channel_id=1, source_target_pairs={{0,96},{32,0},{64,32},{96,64},{1,97},{33,1},{65,33},{97,65},{2,98}... | collective-permute-start | bytes 1572872 | tf_op jit(solution)/shard_map/ppermute | solution.py:403
  195.6 15.8 %collective-permute-start.36 = (bf16[16,128,128]{2,1,0:T(8,128)(2,1)S(1)}, bf16[16,128,128]{2,1,0:T(8,128)(2,1)S(1)}, u32[]{:S(2)}, u32[]{:S(2)}) collective-permute-start(bf16[16,128,128]{2,1,0:T(8,128)(2,1)S(1)} %add_convert_fusion.1), channel_id=1, source_target_pairs={{0,32},{32,64},{64,96},{96,0},{1,33},{33,65},{65,97},{97,1},{2,34}... | collective-permute-start | bytes 1572872 | tf_op jit(solution)/shard_map/ppermute | solution.py:403
  213.9 24.0 %all-to-all-start.4 = ((bf16[32,128,128]{2,1,0:T(8,128)(2,1)}), bf16[32,128,128]{2,1,0:T(8,128)(2,1)S(1)}, u32[]{:S(2)}, u32[]{:S(2)}) async-start(bf16[32,128,128]{2,1,0:T(8,128)(2,1)} %join.1), calls=%async_computation.4 | async-start | bytes 2097152 | tf_op jit(solution)/shard_map/all_to_all | solution.py:464
  (6 other events, 93.7 us)

commit v7 on v6

--- a/solution.py
+++ b/solution.py
@@ -34,50 +34,58 @@
         copy.wait()
 
 
-def pack_kernel(x, *refs, rows):
-    *given, out, xv, outv, marks, sems = refs
-    tall = rows.stop - rows.start
+def pack_kernel(x, *refs):
+    *outs, xv, outv, marks, sems = refs
+    extra = outv.shape[1] - BLK
+    if extra:
+        run_copies([pltpu.make_async_copy(outs[0], marks, sems.at[0])])
+        outs = outs[1:]
+        tile = jnp.broadcast_to(marks[...].astype(jnp.float32), (extra, 128)).astype(jnp.bfloat16)
     width = x.shape[1]
     number = outv.shape[0] // PARTS
+    tall = outv.shape[1] // len(outs)
     loads, stores = [], []
     for n in range(PARTS):
         cols = slice(n * width // PARTS, (n + 1) * width // PARTS)
-        loads.append(pltpu.make_async_copy(x.at[rows, cols], xv.at[:, cols], sems.at[n]))
+        loads.append(pltpu.make_async_copy(x.at[:, cols], xv.at[:, cols], sems.at[n]))
         part = slice(n * number, (n + 1) * number)
-        stores.append(pltpu.make_async_copy(outv.at[part], out.at[part], sems.at[PARTS + n]))
+        for m, out in enumerate(outs):
+            source = outv.at[part, m * tall : (m + 1) * tall, :]
+            sem = sems.at[PARTS * (1 + m) + n]
+            stores.append(pltpu.make_async_copy(source, out.at[part], sem))
     for copy in loads:
         copy.start()
-    if given:
-        run_copies([pltpu.make_async_copy(given[0], marks, sems.at[2 * PARTS])])
-        tile = jnp.broadcast_to(marks[...].astype(jnp.float32), (16, 128)).astype(jnp.bfloat16)
     for n in range(PARTS):
         loads[n].wait()
         for m in range(n * number, (n + 1) * number):
-            outv[m, 0:tall, :] = xv[:, 128 * m : 128 * m + 128].astype(jnp.bfloat16)
-            if given:
-                outv[m, tall:, :] = tile
-        stores[n].start()
+            outv[m, 0:BLK, :] = xv[:, 128 * m : 128 * m + 128].astype(jnp.bfloat16)
+            if extra:
+                outv[m, BLK:, :] = tile
+        for copy in stores[n * len(outs) : (n + 1) * len(outs)]:
+            copy.start()
     for copy in stores:
         copy.wait()
 
 
-def by_features(x, rows, *pos):
-    tall = rows.stop - rows.start
-    shape = (x.shape[1] // 128, tall + 16 * len(pos), 128)
-    return pl.pallas_call(
-        functools.partial(pack_kernel, rows=rows),
-        in_specs=[ANY] * (1 + len(pos)),
-        out_specs=ANY,
-        out_shape=jax.ShapeDtypeStruct(shape, jnp.bfloat16),
+def by_features(x, pos=None):
+    number = x.shape[1] // 128
+    tall = BLK + (0 if pos is None else 16)
+    shapes = [(number, HALF, 128)] * 2 if pos is None else [(number, tall, 128)]
+    given = (x,) if pos is None else (x, pos)
+    return pl.pallas_call(
+        pack_kernel,
+        in_specs=[ANY] * len(given),
+        out_specs=[ANY] * len(shapes),
+        out_shape=[jax.ShapeDtypeStruct(s, jnp.bfloat16) for s in shapes],
         scratch_shapes=[
-            pltpu.VMEM((tall, x.shape[1]), x.dtype),
-            pltpu.VMEM(shape, jnp.bfloat16),
+            pltpu.VMEM(x.shape, x.dtype),
+            pltpu.VMEM((number, tall, 128), jnp.bfloat16),
             pltpu.VMEM((1, BLK), jnp.int32),
-            pltpu.SemaphoreType.DMA((2 * PARTS + 1,)),
+            pltpu.SemaphoreType.DMA((3 * PARTS,)),
         ],
-        **params(56 if rows.stop == HALF else 5, 4 * MIB),
+        **params(56 if pos is None else 5, 5 * MIB),
         name="pack",
-    )(x, *pos)
+    )(*given)
 
 
 def unpack_kernel(x, out, outv, sems):
@@ -437,12 +445,12 @@
 def scatter_scores(outs):
     halves = ring_terms("first", outs[0:2], outs[2:4], outs[4:6])
     sums = [outs[6][n] + halves[n // 2][0][n % 2] + halves[n // 2][1][n % 2] for n in range(4)]
-    got = [along("second", n)(sums[n]) for n in (1, 2, 3)]
+    got = [along("second", n)(sums[n]) for n in (2, 3, 1)]
     return sums[0] + got[0] + got[1] + got[2]
 
 
 def gather_weights(v):
-    got = {3: along("first", 1)(v), 1: along("first", -1)(v), 2: along("first", 2)(v)}
+    got = {2: along("first", 2)(v), 1: along("first", -1)(v), 3: along("first", 1)(v)}
     near = jnp.stack([v, got[1], got[2], got[3]])
     up, down, flip = along("second", 1), along("second", -1), along("core", 1)
     below, above = up(near), down(near)
@@ -464,12 +472,12 @@
         return lax.all_to_all(v, "dev", 0, 0, tiled=True)
 
     up, down, flip = along("z", 1), along("z", -1), along("core", 1)
-    halves = slice(0, HALF), slice(HALF, BLK)
-    low, high = [exchange(by_features(passages, rows)) for rows in halves]
+    low, high = [exchange(v) for v in by_features(passages)]
     above0, below0 = down(low), up(low)
-    q_tiles = by_features(queries, slice(0, BLK), positives.reshape(1, BLK))
-    q_tiles, late, *_ = lax.optimization_barrier((q_tiles, high, above0, below0))
+    q_tiles = by_features(queries, positives.reshape(1, BLK))[0]
+    late, *_ = lax.optimization_barrier((high, above0, below0))
     above1, below1 = down(late), up(late)
+    q_tiles, *_ = lax.optimization_barrier((q_tiles, above1, below1))
     last0, last1, *_ = lax.optimization_barrier((above0, below1, above1))
     far0, far1 = down(last0), up(last1)
     pieces = [low, high, above0, above1, far0, far1, below0, below1]

time: 240 us -> 257 us (1.071)
  blocking collectives: 20.2 us -> 35.7 us
  starting transfers between devices: 69.6 us -> 63 us
  waiting for transfers between devices: 105 us -> 111 us
  local copies, waits for them, and re-layouts: 4.34 us -> 7.14 us
    all_to_all x1 -> x2, blocking collectives: 20.2 us -> 35.7 us  [exchange(): return lax.all_to_all(v, 'dev', 0, 0, tiled=True)]
    ppermute x12, waiting for transfers between devices: 28 us -> 38.5 us  [along(): return lambda v: lax.ppermute(v, 'grp', perm)]
    all_to_all x4 -> x3, waiting for transfers between devices: 38.3 us -> 32.8 us  [exchange(): return lax.all_to_all(v, 'dev', 0, 0, tiled=True)]
    all_to_all x4 -> x3, starting transfers between devices: 21.4 us -> 18.4 us  [exchange(): return lax.all_to_all(v, 'dev', 0, 0, tiled=True)]
    unnamed x19 -> x35, local copies, waits for them, and re-layouts: 1.69 us -> 4.52 us
  transfers between devices with their start and end apart: 45 -> 44, of which waited for: 22 -> 26; matrix products, arithmetic and copies ran while one was open for 2% -> 2% of each run, Pallas kernels for 6% -> 5%
where the time goes in v7:
time: 257 us; the launch traced here: 256 us
  waiting for transfers between devices  111 us (43%)
  starting transfers between devices  63 us (25%)
  blocking collectives  35.7 us (14%)
  Pallas kernels  35.2 us (14%)
  local copies, waits for them, and re-layouts  7.14 us (3%)
  other arithmetic  3.3 us (1%)
    ppermute x29, waiting for transfers between devices, along(): return lambda v: lax.ppermute(v, 'dev', perm)  39.8 us
    ppermute x12, waiting for transfers between devices, along(): return lambda v: lax.ppermute(v, 'grp', perm)  38.5 us
    all_to_all x2, blocking collectives, exchange(): return lax.all_to_all(v, 'dev', 0, 0, tiled=True)  35.7 us
    all_to_all x3, waiting for transfers between devices, exchange(): return lax.all_to_all(v, 'dev', 0, 0, tiled=True)  32.8 us
    ppermute x29, starting transfers between devices, along(): return lambda v: lax.ppermute(v, 'dev', perm)  30.1 us
    all_to_all x3, starting transfers between devices, exchange(): return lax.all_to_all(v, 'dev', 0, 0, tiled=True)  18.4 us
    ppermute x12, starting transfers between devices, along(): return lambda v: lax.ppermute(v, 'grp', perm)  14.5 us
    pallas_call x1, Pallas kernels, grad_passages(): pl.pallas_call(grad_p_kernel, in_specs=[SMEM] * 3 + [VMEM] * 9, out_specs...  7.82 us
  transfers between devices with their start and end apart: 44, of which 26 were waited for; matrix products, arithmetic and copies ran while one was open for 2% of the time, Pallas kernels for 5%

profile of v7, /device:TPU:1, one launch (start us, length us, event | category | flops | bytes accessed | tf_op | source)
XLA Modules:
  0.0 256.5 jit_solution(9455533833125615468)
XLA Ops:
  0.7 2.5 pack.3
  3.2 20.2 %all_to_all.25.refs_0_ = bf16[32,64,128]{2,1,0:T(8,128)(2,1)S(1)} all-to-all(bf16[32,64,128]{2,1,0:T(8,128)(2,1)} %get-tuple-element.27), channel_id=1, replica_groups=mesh['grp'=4,'dev'=32] {'dev'}, dimensions={0} | all-to-all | bytes 1048576 | tf_op jit(solution)/shard_map/all_to_all | solution.py:472
  23.4 3.8 %collective-permute-start = (bf16[32,64,128]{2,1,0:T(8,128)(2,1)S(1)}, bf16[32,64,128]{2,1,0:T(8,128)(2,1)S(1)}, u32[]{:S(2)}, u32[]{:S(2)}) collective-permute-start(bf16[32,64,128]{2,1,0:T(8,128)(2,1)S(1)} %all_to_all.25.refs_0_), channel_id=1, source_target_pairs={{0,96},{32,0},{64,32},{96,64},{1,97},{33,1},{65,33},{97,65},{2,98}... | collective-permute-start | bytes 1572872 | tf_op jit(solution)/shard_map/ppermute | solution.py:411
  27.2 15.5 %all_to_all.26.refs_1_ = bf16[32,64,128]{2,1,0:T(8,128)(2,1)S(1)} all-to-all(bf16[32,64,128]{2,1,0:T(8,128)(2,1)} %get-tuple-element.26), channel_id=1, replica_groups=mesh['grp'=4,'dev'=32] {'dev'}, dimensions={0} | all-to-all | bytes 1048576 | tf_op jit(solution)/shard_map/all_to_all | solution.py:472
  42.7 3.0 %collective-permute-start.2 = (bf16[32,64,128]{2,1,0:T(8,128)(2,1)S(1)}, bf16[32,64,128]{2,1,0:T(8,128)(2,1)S(1)}, u32[]{:S(2)}, u32[]{:S(2)}) collective-permute-start(bf16[32,64,128]{2,1,0:T(8,128)(2,1)S(1)} %all_to_all.26.refs_1_), channel_id=1, source_target_pairs={{0,96},{32,0},{64,32},{96,64},{1,97},{33,1},{65,33},{97,65},{2,98}... | collective-permute-start | bytes 1572872 | tf_op jit(solution)/shard_map/ppermute | solution.py:411
  45.7 1.4 pack.2
  47.1 10.0 %collective-permute-done.2.refs_3_ = bf16[32,64,128]{2,1,0:T(8,128)(2,1)S(1)} collective-permute-done((bf16[32,64,128]{2,1,0:T(8,128)(2,1)S(1)}, bf16[32,64,128]{2,1,0:T(8,128)(2,1)S(1)}, u32[]{:S(2)}, u32[]{:S(2)}) %collective-permute-start.2) | collective-permute-done | bytes 524320 | tf_op jit(solution)/shard_map/ppermute | solution.py:411
  57.9 2.5 collective-permute-done.3.refs_7_
  60.5 4.4 %all-to-all-start.2 = ((bf16[32,144,128]{2,1,0:T(8,128)(2,1)}), bf16[32,144,128]{2,1,0:T(8,128)(2,1)S(1)}, u32[]{:S(2)}, u32[]{:S(2)}) async-start(bf16[32,144,128]{2,1,0:T(8,128)(2,1)} %pack.2), calls=%async_computation.2 | async-start | bytes 2359296 | tf_op jit(solution)/shard_map/all_to_all | solution.py:472
  65.5 17.9 %all-to-all-done.2.q_own.q = bf16[32,144,128]{2,1,0:T(8,128)(2,1)S(1)} async-done(((bf16[32,144,128]{2,1,0:T(8,128)(2,1)}), bf16[32,144,128]{2,1,0:T(8,128)(2,1)S(1)}, u32[]{:S(2)}, u32[]{:S(2)}) %all-to-all-start.2) | async-done | bytes 1179680 | tf_op jit(solution)/shard_map/all_to_all | solution.py:472
  88.0 9.7 %collective-permute-done.4.refs_4_ = bf16[32,64,128]{2,1,0:T(8,128)(2,1)S(1)} collective-permute-done((bf16[32,64,128]{2,1,0:T(8,128)(2,1)S(1)}, bf16[32,64,128]{2,1,0:T(8,128)(2,1)S(1)}, u32[]{:S(2)}, u32[]{:S(2)}) %collective-permute-start.4) | collective-permute-done | bytes 524320 | tf_op jit(solution)/shard_map/ppermute | solution.py:411
  99.5 1.4 collective-permute-start.12
  101.1 1.3 collective-permute-done.12.refs_13_
  103.5 7.6 %partial_scores.1 = (f32[2,512,128]{2,1,0:T(8,128)S(1)}, f32[2,512,128]{2,1,0:T(8,128)S(1)}, f32[2,512,128]{2,1,0:T(8,128)S(1)}, f32[2,512,128]{2,1,0:T(8,128)S(...) custom-call(s32[128]{0:T(128)S(1)} %and_select_fusion.ids, ...), custom_call_target="tpu_custom_call" | custom-call | bytes 20971520 | tf_op jit(solution)/shard_map/partial_scores/pallas_call | solution.py:188
  111.2 2.6 %collective-permute-start.19 = (f32[2,512,128]{2,1,0:T(8,128)S(1)}, f32[2,512,128]{2,1,0:T(8,128)S(1)}, u32[]{:S(2)}, u32[]{:S(2)}) collective-permute-start(f32[2,512,128]{2,1,0:T(8,128)S(1)} %get-tuple-element.39), channel_id=1, source_target_pairs={{0,24},{1,7},{2,26},{3,1},{4,28},{5,3},{6,30},{7,5},{8,0},{9,15},{... | collective-permute-start | bytes 1572872 | tf_op jit(solution)/shard_map/ppermute | solution.py:424
  113.9 1.4 collective-permute-start.18
  115.3 5.4 %collective-permute-done.15 = f32[2,512,128]{2,1,0:T(8,128)S(1)} collective-permute-done((f32[2,512,128]{2,1,0:T(8,128)S(1)}, f32[2,512,128]{2,1,0:T(8,128)S(1)}, u32[]{:S(2)}, u32[]{:S(2)}) %collective-permute-start.15) | collective-permute-done | bytes 524320 | tf_op jit(solution)/shard_map/ppermute | solution.py:424
  120.9 2.7 %collective-permute-start.20 = (f32[2,512,128]{2,1,0:T(8,128)S(1)}, f32[2,512,128]{2,1,0:T(8,128)S(1)}, u32[]{:S(2)}, u32[]{:S(2)}) collective-permute-start(f32[2,512,128]{2,1,0:T(8,128)S(1)} %add.104), channel_id=1, source_target_pairs={{0,24},{1,7},{2,26},{3,1},{4,28},{5,3},{6,30},{7,5},{8,0},{9,15},{... | collective-permute-start | bytes 1572872 | tf_op jit(solution)/shard_map/ppermute | solution.py:424
  123.7 1.9 collective-permute-done.17
  126.3 5.6 %collective-permute-done.16 = f32[2,512,128]{2,1,0:T(8,128)S(1)} collective-permute-done((f32[2,512,128]{2,1,0:T(8,128)S(1)}, f32[2,512,128]{2,1,0:T(8,128)S(1)}, u32[]{:S(2)}, u32[]{:S(2)}) %collective-permute-start.16) | collective-permute-done | bytes 524320 | tf_op jit(solution)/shard_map/ppermute | solution.py:424
  134.4 4.8 %collective-permute-done.21 = f32[512,128]{1,0:T(8,128)S(1)} collective-permute-done((f32[512,128]{1,0:T(8,128)S(1)}, f32[512,128]{1,0:T(8,128)S(1)}, u32[]{:S(2)}, u32[]{:S(2)}) %collective-permute-start.21) | collective-permute-done | bytes 262176 | tf_op jit(solution)/shard_map/ppermute | solution.py:424
  139.2 1.5 collective-permute-done.22
  142.1 2.3 collective-permute-start.24
  146.3 3.1 %softmax_weights.1 = bf16[528,128]{1,0:T(8,128)(2,1)S(1)} custom-call(s32[5]{0:T(128)S(1)} %stack.53.at, f32[512,128]{1,0:T(8,128)S(1)} %fusion.6.x_own, f32[512,128]{1,0:T(8,128)} %collective-permute-done.24.x_sib, s32[8,128]{1,0:T(8,128)S(1)} %stack.56.listv, bf16[32,144,128]{2,1,0:T(8,128)(2,1)S(1)} %all-to-all-done.2.q_own.q), custom_call_target="tpu_custom_call" | custom-call | bytes 8388608 | tf_op jit(solution)/shard_map/softmax_weights/pallas_call | solution.py:250
  151.7 1.9 collective-permute-done.25
  153.6 2.4 collective-permute-done.26
  156.0 1.6 collective-permute-done.27
  157.7 2.7 %collective-permute-start.29 = (bf16[4,528,128]{2,1,0:T(8,128)(2,1)S(1)}, bf16[4,528,128]{2,1,0:T(8,128)(2,1)S(1)}, u32[]{:S(2)}, u32[]{:S(2)}) collective-permute-start(bf16[4,528,128]{2,1,0:T(8,128)(2,1)S(1)} %pad_maximum_fusion.refs_0_), channel_id=1, source_target_pairs={{0,6},{1,25},{2,0},{3,27},{4,2},{5,29},{6,4},{7,31},{8,14},{9,1},{... | collective-permute-start | bytes 1622024 | tf_op jit(solution)/shard_map/ppermute | solution.py:424
  160.4 6.3 %collective-permute-done.29.refs_2_ = bf16[4,528,128]{2,1,0:T(8,128)(2,1)S(1)} collective-permute-done((bf16[4,528,128]{2,1,0:T(8,128)(2,1)S(1)}, bf16[4,528,128]{2,1,0:T(8,128)(2,1)S(1)}, u32[]{:S(2)}, u32[]{:S(2)}) %collective-permute-start.29) | collective-permute-done | bytes 540704 | tf_op jit(solution)/shard_map/ppermute | solution.py:424
  166.7 3.4 %collective-permute-start.30 = (bf16[4,528,128]{2,1,0:T(8,128)(2,1)S(1)}, bf16[4,528,128]{2,1,0:T(8,128)(2,1)S(1)}, u32[]{:S(2)}, u32[]{:S(2)}) collective-permute-start(bf16[4,528,128]{2,1,0:T(8,128)(2,1)S(1)} %collective-permute-done.29.refs_2_), channel_id=1, source_target_pairs={{0,6},{1,25},{2,0},{3,27},{4,2},{5,29},{6,4},{7,31},{8,14},{9,1},{... | collective-permute-start | bytes 1622024 | tf_op jit(solution)/shard_map/ppermute | solution.py:424
  170.1 2.3 collective-permute-start.31
  172.9 3.5 %collective-permute-done.30.refs_3_ = bf16[4,528,128]{2,1,0:T(8,128)(2,1)S(1)} collective-permute-done((bf16[4,528,128]{2,1,0:T(8,128)(2,1)S(1)}, bf16[4,528,128]{2,1,0:T(8,128)(2,1)S(1)}, u32[]{:S(2)}, u32[]{:S(2)}) %collective-permute-start.30) | collective-permute-done | bytes 540704 | tf_op jit(solution)/shard_map/ppermute | solution.py:424
  176.4 2.9 %collective-permute-start.34 = (bf16[4,528,128]{2,1,0:T(8,128)(2,1)S(1)}, bf16[4,528,128]{2,1,0:T(8,128)(2,1)S(1)}, u32[]{:S(2)}, u32[]{:S(2)}) collective-permute-start(bf16[4,528,128]{2,1,0:T(8,128)(2,1)S(1)} %collective-permute-done.30.refs_3_), channel_id=1, source_target_pairs={{0,1},{1,0},{2,3},{3,2},{4,5},{5,4},{6,7},{7,6},{8,9},{9,8},{10,11... | collective-permute-start | bytes 1622024 | tf_op jit(solution)/shard_map/ppermute | solution.py:424
  179.3 1.4 place.1.p
  180.9 7.8 %grad_passages.1 = (bf16[32,128,128]{2,1,0:T(8,128)(2,1)S(1)}, bf16[16,128,128]{2,1,0:T(8,128)(2,1)S(1)}, bf16[16,128,128]{2,1,0:T(8,128)(2,1)}, bf16[16,128,128...) custom-call(s32[128]{0:T(128)S(1)} %and_select_fusion.ids, ...), custom_call_target="tpu_custom_call" | custom-call | bytes 20971520 | tf_op jit(solution)/shard_map/grad_passages/pallas_call | solution.py:325
  192.7 1.7 collective-permute-start.37
  194.5 6.1 %grad_queries.1 = bf16[32,128,128]{2,1,0:T(8,128)(2,1)} custom-call(s32[128]{0:T(128)S(1)} %and_select_fusion.ids, s32[128]{0:T(128)S(1)} %convert_reduce_fusion.own, s32[5]{0:T(128)S(1)} %stack.53.at, bf16[128,128,128]{2,1,0:T(8,128)(2,1)S(1)} %place.1.p, bf16[4,528,128]{2,1,0:T(8,128)(2,1)S(1)} %pad_maximum_fusion.refs_0_, ...), custom_call_target="tpu_custom_call" | custom-call | bytes 20971520 | tf_op jit(solution)/shard_map/grad_queries/pallas_call | solution.py:360
  200.6 6.8 %all-to-all-start.3 = ((bf16[32,128,128]{2,1,0:T(8,128)(2,1)}), bf16[32,128,128]{2,1,0:T(8,128)(2,1)S(1)}, u32[]{:S(2)}, u32[]{:S(2)}) async-start(bf16[32,128,128]{2,1,0:T(8,128)(2,1)} %grad_queries.1), calls=%async_computation.3 | async-start | bytes 2097152 | tf_op jit(solution)/shard_map/all_to_all | solution.py:472
  208.7 3.0 %collective-permute-start.40 = (bf16[16,128,128]{2,1,0:T(8,128)(2,1)S(1)}, bf16[16,128,128]{2,1,0:T(8,128)(2,1)S(1)}, u32[]{:S(2)}, u32[]{:S(2)}) collective-permute-start(bf16[16,128,128]{2,1,0:T(8,128)(2,1)S(1)} %add_convert_fusion), channel_id=1, source_target_pairs={{0,96},{32,0},{64,32},{96,64},{1,97},{33,1},{65,33},{97,65},{2,98}... | collective-permute-start | bytes 1572872 | tf_op jit(solution)/shard_map/ppermute | solution.py:411
  213.0 2.9 %collective-permute-done.37.refs_1_ = bf16[16,128,128]{2,1,0:T(8,128)(2,1)} collective-permute-done((bf16[16,128,128]{2,1,0:T(8,128)(2,1)}, bf16[16,128,128]{2,1,0:T(8,128)(2,1)}, u32[]{:S(2)}, u32[]{:S(2)}) %collective-permute-start.37) | collective-permute-done | bytes 524320 | tf_op jit(solution)/shard_map/ppermute | solution.py:411
  215.9 1.4 collective-permute-done.38.refs_2_
  217.4 9.7 %collective-permute-done.40.refs_3_ = bf16[16,128,128]{2,1,0:T(8,128)(2,1)S(1)} collective-permute-done((bf16[16,128,128]{2,1,0:T(8,128)(2,1)S(1)}, bf16[16,128,128]{2,1,0:T(8,128)(2,1)S(1)}, u32[]{:S(2)}, u32[]{:S(2)}) %collective-permute-start.40) | collective-permute-done | bytes 524320 | tf_op jit(solution)/shard_map/ppermute | solution.py:411
  227.1 1.4 collective-permute-done.36.refs_0_
  228.5 2.4 join.1
  230.9 7.1 %all-to-all-start.4 = ((bf16[32,128,128]{2,1,0:T(8,128)(2,1)}), bf16[32,128,128]{2,1,0:T(8,128)(2,1)S(1)}, u32[]{:S(2)}, u32[]{:S(2)}) async-start(bf16[32,128,128]{2,1,0:T(8,128)(2,1)} %join.1), calls=%async_computation.4 | async-start | bytes 2097152 | tf_op jit(solution)/shard_map/all_to_all | solution.py:472
  238.6 1.4 unpack.2
  240.0 14.9 %all-to-all-done.4.x = bf16[32,128,128]{2,1,0:T(8,128)(2,1)S(1)} async-done(((bf16[32,128,128]{2,1,0:T(8,128)(2,1)}), bf16[32,128,128]{2,1,0:T(8,128)(2,1)S(1)}, u32[]{:S(2)}, u32[]{:S(2)}) %all-to-all-start.4) | async-done | bytes 1048608 | tf_op jit(solution)/shard_map/all_to_all | solution.py:472
  254.9 1.4 unpack.3
  (108 shorter events, 25.8 us)
Async XLA Ops:
  0.6 45.0 %copy-start.14 = (s32[128]{0:T(128)S(1)}, s32[128]{0:T(128)}, u32[]{:S(2)}) copy-start(s32[128]{0:T(128)} %param.9) | copy-start | bytes 1540
  0.6 45.0 %copy-start.7 = (f32[128,4096]{1,0:T(8,128)S(1)}, f32[128,4096]{1,0:T(8,128)}, u32[]{:S(2)}) copy-start(f32[128,4096]{1,0:T(8,128)} %x.6) | copy-start | bytes 6291460
  23.4 19.3 %collective-permute-start = (bf16[32,64,128]{2,1,0:T(8,128)(2,1)S(1)}, bf16[32,64,128]{2,1,0:T(8,128)(2,1)S(1)}, u32[]{:S(2)}, u32[]{:S(2)}) collective-permute-start(bf16[32,64,128]{2,1,0:T(8,128)(2,1)S(1)} %all_to_all.25.refs_0_), channel_id=1, source_target_pairs={{0,96},{32,0},{64,32},{96,64},{1,97},{33,1},{65,33},{97,65},{2,98}... | collective-permute-start | bytes 1572872 | tf_op jit(solution)/shard_map/ppermute | solution.py:411
  27.2 15.5 %collective-permute-start.1 = (bf16[32,64,128]{2,1,0:T(8,128)(2,1)S(1)}, bf16[32,64,128]{2,1,0:T(8,128)(2,1)S(1)}, u32[]{:S(2)}, u32[]{:S(2)}) collective-permute-start(bf16[32,64,128]{2,1,0:T(8,128)(2,1)S(1)} %all_to_all.25.refs_0_), channel_id=1, source_target_pairs={{0,32},{32,64},{64,96},{96,0},{1,33},{33,65},{65,97},{97,1},{2,34}... | collective-permute-start | bytes 1572872 | tf_op jit(solution)/shard_map/ppermute | solution.py:411
  42.7 14.4 %collective-permute-start.2 = (bf16[32,64,128]{2,1,0:T(8,128)(2,1)S(1)}, bf16[32,64,128]{2,1,0:T(8,128)(2,1)S(1)}, u32[]{:S(2)}, u32[]{:S(2)}) collective-permute-start(bf16[32,64,128]{2,1,0:T(8,128)(2,1)S(1)} %all_to_all.26.refs_1_), channel_id=1, source_target_pairs={{0,96},{32,0},{64,32},{96,64},{1,97},{33,1},{65,33},{97,65},{2,98}... | collective-permute-start | bytes 1572872 | tf_op jit(solution)/shard_map/ppermute | solution.py:411
  45.7 14.8 %collective-permute-start.3 = (bf16[32,64,128]{2,1,0:T(8,128)(2,1)S(1)}, bf16[32,64,128]{2,1,0:T(8,128)(2,1)}, u32[]{:S(2)}, u32[]{:S(2)}) collective-permute-start(bf16[32,64,128]{2,1,0:T(8,128)(2,1)S(1)} %all_to_all.26.refs_1_), channel_id=1, source_target_pairs={{0,32},{32,64},{64,96},{96,0},{1,33},{33,65},{65,97},{97,1},{2,34}... | collective-permute-start | bytes 1572872 | tf_op jit(solution)/shard_map/ppermute | solution.py:411
  45.7 38.0 %copy-start.15 = (s32[32,8]{0,1:T(8,128)S(1)}, s32[32,8]{0,1:T(8,128)}, u32[]{:S(2)}) copy-start(s32[32,8]{0,1:T(8,128)} %param.7) | copy-start | bytes 3076
  45.7 40.2 %copy-start.16 = (s32[1,32]{1,0:T(1,128)S(1)}, s32[1,32]{1,0:T(1,128)}, u32[]{:S(2)}) copy-start(s32[1,32]{1,0:T(1,128)} %param.8) | copy-start | bytes 388
  60.5 22.9 %all-to-all-start.2 = ((bf16[32,144,128]{2,1,0:T(8,128)(2,1)}), bf16[32,144,128]{2,1,0:T(8,128)(2,1)S(1)}, u32[]{:S(2)}, u32[]{:S(2)}) async-start(bf16[32,144,128]{2,1,0:T(8,128)(2,1)} %pack.2), calls=%async_computation.2 | async-start | bytes 2359296 | tf_op jit(solution)/shard_map/all_to_all | solution.py:472
  64.9 19.5 %collective-permute-start.7 = (bf16[32,64,128]{2,1,0:T(8,128)(2,1)S(1)}, bf16[32,64,128]{2,1,0:T(8,128)(2,1)}, u32[]{:S(2)}, u32[]{:S(2)}) collective-permute-start(bf16[32,64,128]{2,1,0:T(8,128)(2,1)S(1)} %all_to_all.25.refs_0_), channel_id=1, source_target_pairs={{0,1},{1,0},{2,3},{3,2},{4,5},{5,4},{6,7},{7,6},{8,9},{9,8},{10,11... | collective-permute-start | bytes 1572872 | tf_op jit(solution)/shard_map/ppermute | solution.py:424
  65.4 19.8 %collective-permute-start.8 = (bf16[32,64,128]{2,1,0:T(8,128)(2,1)S(1)}, bf16[32,64,128]{2,1,0:T(8,128)(2,1)}, u32[]{:S(2)}, u32[]{:S(2)}) collective-permute-start(bf16[32,64,128]{2,1,0:T(8,128)(2,1)S(1)} %all_to_all.26.refs_1_), channel_id=1, source_target_pairs={{0,1},{1,0},{2,3},{3,2},{4,5},{5,4},{6,7},{7,6},{8,9},{9,8},{10,11... | collective-permute-start | bytes 1572872 | tf_op jit(solution)/shard_map/ppermute | solution.py:424
  83.4 19.0 %collective-permute-start.6 = (bf16[32,144,128]{2,1,0:T(8,128)(2,1)S(1)}, bf16[32,144,128]{2,1,0:T(8,128)(2,1)}, u32[]{:S(2)}, u32[]{:S(2)}) collective-permute-start(bf16[32,144,128]{2,1,0:T(8,128)(2,1)S(1)} %all-to-all-done.2.q_own.q), channel_id=1, source_target_pairs={{0,1},{1,0},{2,3},{3,2},{4,5},{5,4},{6,7},{7,6},{8,9},{9,8},{10,11... | collective-permute-start | bytes 3538952 | tf_op jit(solution)/shard_map/ppermute | solution.py:424
  83.9 3.1 %collective-permute-start.9 = (bf16[32,64,128]{2,1,0:T(8,128)(2,1)S(1)}, bf16[32,64,128]{2,1,0:T(8,128)(2,1)S(1)}, u32[]{:S(2)}, u32[]{:S(2)}) collective-permute-start(bf16[32,64,128]{2,1,0:T(8,128)(2,1)S(1)} %collective-permute-done.refs_2_), channel_id=1, source_target_pairs={{0,1},{1,0},{2,3},{3,2},{4,5},{5,4},{6,7},{7,6},{8,9},{9,8},{10,11... | collective-permute-start | bytes 1572872 | tf_op jit(solution)/shard_map/ppermute | solution.py:424
  84.2 3.5 %collective-permute-start.13 = (bf16[32,64,128]{2,1,0:T(8,128)(2,1)S(1)}, bf16[32,64,128]{2,1,0:T(8,128)(2,1)S(1)}, u32[]{:S(2)}, u32[]{:S(2)}) collective-permute-start(bf16[32,64,128]{2,1,0:T(8,128)(2,1)S(1)} %collective-permute-done.1.refs_6_), channel_id=1, source_target_pairs={{0,1},{1,0},{2,3},{3,2},{4,5},{5,4},{6,7},{7,6},{8,9},{9,8},{10,11... | collective-permute-start | bytes 1572872 | tf_op jit(solution)/shard_map/ppermute | solution.py:424
  84.4 13.3 %collective-permute-start.4 = (bf16[32,64,128]{2,1,0:T(8,128)(2,1)S(1)}, bf16[32,64,128]{2,1,0:T(8,128)(2,1)S(1)}, u32[]{:S(2)}, u32[]{:S(2)}) collective-permute-start(bf16[32,64,128]{2,1,0:T(8,128)(2,1)S(1)} %collective-permute-done.refs_2_), channel_id=1, source_target_pairs={{0,96},{32,0},{64,32},{96,64},{1,97},{33,1},{65,33},{97,65},{2,98}... | collective-permute-start | bytes 1572872 | tf_op jit(solution)/shard_map/ppermute | solution.py:411
  85.1 14.4 %collective-permute-start.5 = (bf16[32,64,128]{2,1,0:T(8,128)(2,1)}, bf16[32,64,128]{2,1,0:T(8,128)(2,1)S(1)}, u32[]{:S(2)}, u32[]{:S(2)}) collective-permute-start(bf16[32,64,128]{2,1,0:T(8,128)(2,1)} %collective-permute-done.3.refs_7_), channel_id=1, source_target_pairs={{0,32},{32,64},{64,96},{96,0},{1,33},{33,65},{65,97},{97,1},{2,34}... | collective-permute-start | bytes 1572872 | tf_op jit(solution)/shard_map/ppermute | solution.py:411
  87.0 14.1 %collective-permute-start.10 = (bf16[32,64,128]{2,1,0:T(8,128)(2,1)}, bf16[32,64,128]{2,1,0:T(8,128)(2,1)S(1)}, u32[]{:S(2)}, u32[]{:S(2)}) collective-permute-start(bf16[32,64,128]{2,1,0:T(8,128)(2,1)} %copy-done), channel_id=1, source_target_pairs={{0,1},{1,0},{2,3},{3,2},{4,5},{5,4},{6,7},{7,6},{8,9},{9,8},{10,11... | collective-permute-start | bytes 1572872 | tf_op jit(solution)/shard_map/ppermute | solution.py:424
  87.7 13.4 %collective-permute-start.14 = (bf16[32,64,128]{2,1,0:T(8,128)(2,1)}, bf16[32,64,128]{2,1,0:T(8,128)(2,1)S(1)}, u32[]{:S(2)}, u32[]{:S(2)}) collective-permute-start(bf16[32,64,128]{2,1,0:T(8,128)(2,1)} %collective-permute-done.3.refs_7_), channel_id=1, source_target_pairs={{0,1},{1,0},{2,3},{3,2},{4,5},{5,4},{6,7},{7,6},{8,9},{9,8},{10,11... | collective-permute-start | bytes 1572872 | tf_op jit(solution)/shard_map/ppermute | solution.py:424
  97.7 3.4 %collective-permute-start.11 = (bf16[32,64,128]{2,1,0:T(8,128)(2,1)S(1)}, bf16[32,64,128]{2,1,0:T(8,128)(2,1)S(1)}, u32[]{:S(2)}, u32[]{:S(2)}) collective-permute-start(bf16[32,64,128]{2,1,0:T(8,128)(2,1)S(1)} %collective-permute-done.4.refs_4_), channel_id=1, source_target_pairs={{0,1},{1,0},{2,3},{3,2},{4,5},{5,4},{6,7},{7,6},{8,9},{9,8},{10,11... | collective-permute-start | bytes 1572872 | tf_op jit(solution)/shard_map/ppermute | solution.py:424
  99.5 2.9 %collective-permute-start.12 = (bf16[32,64,128]{2,1,0:T(8,128)(2,1)S(1)}, bf16[32,64,128]{2,1,0:T(8,128)(2,1)S(1)}, u32[]{:S(2)}, u32[]{:S(2)}) collective-permute-start(bf16[32,64,128]{2,1,0:T(8,128)(2,1)S(1)} %collective-permute-done.5.refs_5_), channel_id=1, source_target_pairs={{0,1},{1,0},{2,3},{3,2},{4,5},{5,4},{6,7},{7,6},{8,9},{9,8},{10,11... | collective-permute-start | bytes 1572872 | tf_op jit(solution)/shard_map/ppermute | solution.py:424
  111.1 9.6 %collective-permute-start.15 = (f32[2,512,128]{2,1,0:T(8,128)S(1)}, f32[2,512,128]{2,1,0:T(8,128)S(1)}, u32[]{:S(2)}, u32[]{:S(2)}) collective-permute-start(f32[2,512,128]{2,1,0:T(8,128)S(1)} %get-tuple-element.35), channel_id=1, source_target_pairs={{0,8},{1,3},{2,10},{3,5},{4,12},{5,7},{6,14},{7,1},{8,16},{9,11},{... | collective-permute-start | bytes 1572872 | tf_op jit(solution)/shard_map/ppermute | solution.py:424
  111.2 9.6 %collective-permute-start.19 = (f32[2,512,128]{2,1,0:T(8,128)S(1)}, f32[2,512,128]{2,1,0:T(8,128)S(1)}, u32[]{:S(2)}, u32[]{:S(2)}) collective-permute-start(f32[2,512,128]{2,1,0:T(8,128)S(1)} %get-tuple-element.39), channel_id=1, source_target_pairs={{0,24},{1,7},{2,26},{3,1},{4,28},{5,3},{6,30},{7,5},{8,0},{9,15},{... | collective-permute-start | bytes 1572872 | tf_op jit(solution)/shard_map/ppermute | solution.py:424
  113.9 11.7 %collective-permute-start.17 = (f32[2,512,128]{2,1,0:T(8,128)S(1)}, f32[2,512,128]{2,1,0:T(8,128)S(1)}, u32[]{:S(2)}, u32[]{:S(2)}) collective-permute-start(f32[2,512,128]{2,1,0:T(8,128)S(1)} %get-tuple-element.36), channel_id=1, source_target_pairs={{0,24},{1,7},{2,26},{3,1},{4,28},{5,3},{6,30},{7,5},{8,0},{9,15},{... | collective-permute-start | bytes 1572872 | tf_op jit(solution)/shard_map/ppermute | solution.py:424
  113.9 12.4 %collective-permute-start.18 = (f32[2,512,128]{2,1,0:T(8,128)S(1)}, f32[2,512,128]{2,1,0:T(8,128)S(1)}, u32[]{:S(2)}, u32[]{:S(2)}) collective-permute-start(f32[2,512,128]{2,1,0:T(8,128)S(1)} %get-tuple-element.37), channel_id=1, source_target_pairs={{0,8},{1,3},{2,10},{3,5},{4,12},{5,7},{6,14},{7,1},{8,16},{9,11},{... | collective-permute-start | bytes 1572872 | tf_op jit(solution)/shard_map/ppermute | solution.py:424
  120.8 11.2 %collective-permute-start.16 = (f32[2,512,128]{2,1,0:T(8,128)S(1)}, f32[2,512,128]{2,1,0:T(8,128)S(1)}, u32[]{:S(2)}, u32[]{:S(2)}) collective-permute-start(f32[2,512,128]{2,1,0:T(8,128)S(1)} %add.99), channel_id=1, source_target_pairs={{0,8},{1,3},{2,10},{3,5},{4,12},{5,7},{6,14},{7,1},{8,16},{9,11},{... | collective-permute-start | bytes 1572872 | tf_op jit(solution)/shard_map/ppermute | solution.py:424
  120.9 11.0 %collective-permute-start.20 = (f32[2,512,128]{2,1,0:T(8,128)S(1)}, f32[2,512,128]{2,1,0:T(8,128)S(1)}, u32[]{:S(2)}, u32[]{:S(2)}) collective-permute-start(f32[2,512,128]{2,1,0:T(8,128)S(1)} %add.104), channel_id=1, source_target_pairs={{0,24},{1,7},{2,26},{3,1},{4,28},{5,3},{6,30},{7,5},{8,0},{9,15},{... | collective-permute-start | bytes 1572872 | tf_op jit(solution)/shard_map/ppermute | solution.py:424
  132.1 7.1 %collective-permute-start.21 = (f32[512,128]{1,0:T(8,128)S(1)}, f32[512,128]{1,0:T(8,128)S(1)}, u32[]{:S(2)}, u32[]{:S(2)}) collective-permute-start(f32[512,128]{1,0:T(8,128)S(1)} %get-tuple-element.49), channel_id=1, source_target_pairs={{0,4},{1,17},{2,6},{3,19},{4,0},{5,21},{6,2},{7,23},{8,12},{9,25},... | collective-permute-start | bytes 786440 | tf_op jit(solution)/shard_map/ppermute | solution.py:424
  132.9 7.8 %collective-permute-start.22 = (f32[512,128]{1,0:T(8,128)S(1)}, f32[512,128]{1,0:T(8,128)S(1)}, u32[]{:S(2)}, u32[]{:S(2)}) collective-permute-start(f32[512,128]{1,0:T(8,128)S(1)} %get-tuple-element.50), channel_id=1, source_target_pairs={{0,6},{1,25},{2,0},{3,27},{4,2},{5,29},{6,4},{7,31},{8,14},{9,1},{... | collective-permute-start | bytes 786440 | tf_op jit(solution)/shard_map/ppermute | solution.py:424
  133.6 8.3 %collective-permute-start.23 = (f32[512,128]{1,0:T(8,128)S(1)}, f32[512,128]{1,0:T(8,128)S(1)}, u32[]{:S(2)}, u32[]{:S(2)}) collective-permute-start(f32[512,128]{1,0:T(8,128)S(1)} %get-tuple-element.51), channel_id=1, source_target_pairs={{0,2},{1,9},{2,4},{3,11},{4,6},{5,13},{6,0},{7,15},{8,10},{9,17},{... | collective-permute-start | bytes 786440 | tf_op jit(solution)/shard_map/ppermute | solution.py:424
  142.1 4.2 %collective-permute-start.24 = (f32[512,128]{1,0:T(8,128)S(1)}, f32[512,128]{1,0:T(8,128)}, u32[]{:S(2)}, u32[]{:S(2)}) collective-permute-start(f32[512,128]{1,0:T(8,128)S(1)} %fusion.6.x_own), channel_id=1, source_target_pairs={{0,1},{1,0},{2,3},{3,2},{4,5},{5,4},{6,7},{7,6},{8,9},{9,8},{10,11... | collective-permute-start | bytes 786440 | tf_op jit(solution)/shard_map/ppermute | solution.py:424
  149.3 4.2 %collective-permute-start.25 = (bf16[528,128]{1,0:T(8,128)(2,1)S(1)}, bf16[528,128]{1,0:T(8,128)(2,1)S(1)}, u32[]{:S(2)}, u32[]{:S(2)}) collective-permute-start(bf16[528,128]{1,0:T(8,128)(2,1)S(1)} %softmax_weights.1), channel_id=1, source_target_pairs={{0,24},{1,7},{2,26},{3,1},{4,28},{5,3},{6,30},{7,5},{8,0},{9,15},{... | collective-permute-start | bytes 405512 | tf_op jit(solution)/shard_map/ppermute | solution.py:424
  150.5 5.5 %collective-permute-start.26 = (bf16[528,128]{1,0:T(8,128)(2,1)S(1)}, bf16[528,128]{1,0:T(8,128)(2,1)S(1)}, u32[]{:S(2)}, u32[]{:S(2)}) collective-permute-start(bf16[528,128]{1,0:T(8,128)(2,1)S(1)} %softmax_weights.1), channel_id=1, source_target_pairs={{0,16},{1,5},{2,18},{3,7},{4,20},{5,1},{6,22},{7,3},{8,24},{9,13},... | collective-permute-start | bytes 405512 | tf_op jit(solution)/shard_map/ppermute | solution.py:424
  151.2 6.4 %collective-permute-start.27 = (bf16[528,128]{1,0:T(8,128)(2,1)S(1)}, bf16[528,128]{1,0:T(8,128)(2,1)S(1)}, u32[]{:S(2)}, u32[]{:S(2)}) collective-permute-start(bf16[528,128]{1,0:T(8,128)(2,1)S(1)} %softmax_weights.1), channel_id=1, source_target_pairs={{0,8},{1,3},{2,10},{3,5},{4,12},{5,7},{6,14},{7,1},{8,16},{9,11},{... | collective-permute-start | bytes 405512 | tf_op jit(solution)/shard_map/ppermute | solution.py:424
  157.7 9.0 %collective-permute-start.29 = (bf16[4,528,128]{2,1,0:T(8,128)(2,1)S(1)}, bf16[4,528,128]{2,1,0:T(8,128)(2,1)S(1)}, u32[]{:S(2)}, u32[]{:S(2)}) collective-permute-start(bf16[4,528,128]{2,1,0:T(8,128)(2,1)S(1)} %pad_maximum_fusion.refs_0_), channel_id=1, source_target_pairs={{0,6},{1,25},{2,0},{3,27},{4,2},{5,29},{6,4},{7,31},{8,14},{9,1},{... | collective-permute-start | bytes 1622024 | tf_op jit(solution)/shard_map/ppermute | solution.py:424
  160.4 12.0 %collective-permute-start.28 = (bf16[4,528,128]{2,1,0:T(8,128)(2,1)S(1)}, bf16[4,528,128]{2,1,0:T(8,128)(2,1)S(1)}, u32[]{:S(2)}, u32[]{:S(2)}) collective-permute-start(bf16[4,528,128]{2,1,0:T(8,128)(2,1)S(1)} %pad_maximum_fusion.refs_0_), channel_id=1, source_target_pairs={{0,2},{1,9},{2,4},{3,11},{4,6},{5,13},{6,0},{7,15},{8,10},{9,17},{... | collective-permute-start | bytes 1622024 | tf_op jit(solution)/shard_map/ppermute | solution.py:424
  166.7 9.7 %collective-permute-start.30 = (bf16[4,528,128]{2,1,0:T(8,128)(2,1)S(1)}, bf16[4,528,128]{2,1,0:T(8,128)(2,1)S(1)}, u32[]{:S(2)}, u32[]{:S(2)}) collective-permute-start(bf16[4,528,128]{2,1,0:T(8,128)(2,1)S(1)} %collective-permute-done.29.refs_2_), channel_id=1, source_target_pairs={{0,6},{1,25},{2,0},{3,27},{4,2},{5,29},{6,4},{7,31},{8,14},{9,1},{... | collective-permute-start | bytes 1622024 | tf_op jit(solution)/shard_map/ppermute | solution.py:424
  170.1 10.6 %collective-permute-start.31 = (bf16[4,528,128]{2,1,0:T(8,128)(2,1)S(1)}, bf16[4,528,128]{2,1,0:T(8,128)(2,1)S(1)}, u32[]{:S(2)}, u32[]{:S(2)}) collective-permute-start(bf16[4,528,128]{2,1,0:T(8,128)(2,1)S(1)} %pad_maximum_fusion.refs_0_), channel_id=1, source_target_pairs={{0,1},{1,0},{2,3},{3,2},{4,5},{5,4},{6,7},{7,6},{8,9},{9,8},{10,11... | collective-permute-start | bytes 1622024 | tf_op jit(solution)/shard_map/ppermute | solution.py:424
  172.4 8.3 %collective-permute-start.33 = (bf16[4,528,128]{2,1,0:T(8,128)(2,1)S(1)}, bf16[4,528,128]{2,1,0:T(8,128)(2,1)S(1)}, u32[]{:S(2)}, u32[]{:S(2)}) collective-permute-start(bf16[4,528,128]{2,1,0:T(8,128)(2,1)S(1)} %collective-permute-done.29.refs_2_), channel_id=1, source_target_pairs={{0,1},{1,0},{2,3},{3,2},{4,5},{5,4},{6,7},{7,6},{8,9},{9,8},{10,11... | collective-permute-start | bytes 1622024 | tf_op jit(solution)/shard_map/ppermute | solution.py:424
  172.4 8.3 %collective-permute-start.32 = (bf16[4,528,128]{2,1,0:T(8,128)(2,1)S(1)}, bf16[4,528,128]{2,1,0:T(8,128)(2,1)S(1)}, u32[]{:S(2)}, u32[]{:S(2)}) collective-permute-start(bf16[4,528,128]{2,1,0:T(8,128)(2,1)S(1)} %collective-permute-done.28.refs_1_), channel_id=1, source_target_pairs={{0,1},{1,0},{2,3},{3,2},{4,5},{5,4},{6,7},{7,6},{8,9},{9,8},{10,11... | collective-permute-start | bytes 1622024 | tf_op jit(solution)/shard_map/ppermute | solution.py:424
  176.4 4.4 %collective-permute-start.34 = (bf16[4,528,128]{2,1,0:T(8,128)(2,1)S(1)}, bf16[4,528,128]{2,1,0:T(8,128)(2,1)S(1)}, u32[]{:S(2)}, u32[]{:S(2)}) collective-permute-start(bf16[4,528,128]{2,1,0:T(8,128)(2,1)S(1)} %collective-permute-done.30.refs_3_), channel_id=1, source_target_pairs={{0,1},{1,0},{2,3},{3,2},{4,5},{5,4},{6,7},{7,6},{8,9},{9,8},{10,11... | collective-permute-start | bytes 1622024 | tf_op jit(solution)/shard_map/ppermute | solution.py:424
  191.3 16.2 %collective-permute-start.39 = (bf16[16,128,128]{2,1,0:T(8,128)(2,1)}, bf16[16,128,128]{2,1,0:T(8,128)(2,1)}, u32[]{:S(2)}, u32[]{:S(2)}) collective-permute-start(bf16[16,128,128]{2,1,0:T(8,128)(2,1)} %get-tuple-element.48), channel_id=1, source_target_pairs={{0,96},{32,0},{64,32},{96,64},{1,97},{33,1},{65,33},{97,65},{2,98}... | collective-permute-start | bytes 1572872 | tf_op jit(solution)/shard_map/ppermute | solution.py:411
  191.8 19.9 %collective-permute-start.35 = (bf16[16,128,128]{2,1,0:T(8,128)(2,1)}, bf16[16,128,128]{2,1,0:T(8,128)(2,1)}, u32[]{:S(2)}, u32[]{:S(2)}) collective-permute-start(bf16[16,128,128]{2,1,0:T(8,128)(2,1)} %get-tuple-element.44), channel_id=1, source_target_pairs={{0,32},{32,64},{64,96},{96,0},{1,33},{33,65},{65,97},{97,1},{2,34}... | collective-permute-start | bytes 1572872 | tf_op jit(solution)/shard_map/ppermute | solution.py:411
  192.7 23.2 %collective-permute-start.37 = (bf16[16,128,128]{2,1,0:T(8,128)(2,1)}, bf16[16,128,128]{2,1,0:T(8,128)(2,1)}, u32[]{:S(2)}, u32[]{:S(2)}) collective-permute-start(bf16[16,128,128]{2,1,0:T(8,128)(2,1)} %get-tuple-element.45), channel_id=1, source_target_pairs={{0,96},{32,0},{64,32},{96,64},{1,97},{33,1},{65,33},{97,65},{2,98}... | collective-permute-start | bytes 1572872 | tf_op jit(solution)/shard_map/ppermute | solution.py:411
  194.5 22.9 %collective-permute-start.38 = (bf16[16,128,128]{2,1,0:T(8,128)(2,1)}, bf16[16,128,128]{2,1,0:T(8,128)(2,1)}, u32[]{:S(2)}, u32[]{:S(2)}) collective-permute-start(bf16[16,128,128]{2,1,0:T(8,128)(2,1)} %get-tuple-element.46), channel_id=1, source_target_pairs={{0,32},{32,64},{64,96},{96,0},{1,33},{33,65},{65,97},{97,1},{2,34}... | collective-permute-start | bytes 1572872 | tf_op jit(solution)/shard_map/ppermute | solution.py:411
  200.6 30.4 %all-to-all-start.3 = ((bf16[32,128,128]{2,1,0:T(8,128)(2,1)}), bf16[32,128,128]{2,1,0:T(8,128)(2,1)S(1)}, u32[]{:S(2)}, u32[]{:S(2)}) async-start(bf16[32,128,128]{2,1,0:T(8,128)(2,1)} %grad_queries.1), calls=%async_computation.3 | async-start | bytes 2097152 | tf_op jit(solution)/shard_map/all_to_all | solution.py:472
  208.7 18.4 %collective-permute-start.40 = (bf16[16,128,128]{2,1,0:T(8,128)(2,1)S(1)}, bf16[16,128,128]{2,1,0:T(8,128)(2,1)S(1)}, u32[]{:S(2)}, u32[]{:S(2)}) collective-permute-start(bf16[16,128,128]{2,1,0:T(8,128)(2,1)S(1)} %add_convert_fusion), channel_id=1, source_target_pairs={{0,96},{32,0},{64,32},{96,64},{1,97},{33,1},{65,33},{97,65},{2,98}... | collective-permute-start | bytes 1572872 | tf_op jit(solution)/shard_map/ppermute | solution.py:411
  212.9 15.6 %collective-permute-start.36 = (bf16[16,128,128]{2,1,0:T(8,128)(2,1)S(1)}, bf16[16,128,128]{2,1,0:T(8,128)(2,1)S(1)}, u32[]{:S(2)}, u32[]{:S(2)}) collective-permute-start(bf16[16,128,128]{2,1,0:T(8,128)(2,1)S(1)} %add_convert_fusion.1), channel_id=1, source_target_pairs={{0,32},{32,64},{64,96},{96,0},{1,33},{33,65},{65,97},{97,1},{2,34}... | collective-permute-start | bytes 1572872 | tf_op jit(solution)/shard_map/ppermute | solution.py:411
  230.9 24.0 %all-to-all-start.4 = ((bf16[32,128,128]{2,1,0:T(8,128)(2,1)}), bf16[32,128,128]{2,1,0:T(8,128)(2,1)S(1)}, u32[]{:S(2)}, u32[]{:S(2)}) async-start(bf16[32,128,128]{2,1,0:T(8,128)(2,1)} %join.1), calls=%async_computation.4 | async-start | bytes 2097152 | tf_op jit(solution)/shard_map/all_to_all | solution.py:472
  (13 other events, 167.8 us)

commit v8 on v7

--- a/solution.py
+++ b/solution.py
@@ -475,9 +475,8 @@
     low, high = [exchange(v) for v in by_features(passages)]
     above0, below0 = down(low), up(low)
     q_tiles = by_features(queries, positives.reshape(1, BLK))[0]
-    late, *_ = lax.optimization_barrier((high, above0, below0))
+    q_tiles, late, *_ = lax.optimization_barrier((q_tiles, high, above0, below0))
     above1, below1 = down(late), up(late)
-    q_tiles, *_ = lax.optimization_barrier((q_tiles, above1, below1))
     last0, last1, *_ = lax.optimization_barrier((above0, below1, above1))
     far0, far1 = down(last0), up(last1)
     pieces = [low, high, above0, above1, far0, far1, below0, below1]

time: 257 us -> 237 us (0.922)
  blocking collectives: 35.7 us -> 20.2 us
  waiting for transfers between devices: 111 us -> 105 us
  starting transfers between devices: 63 us -> 67.6 us
  local copies, waits for them, and re-layouts: 7.14 us -> 4.34 us
    all_to_all x2 -> x1, blocking collectives: 35.7 us -> 20.2 us  [exchange(): return lax.all_to_all(v, 'dev', 0, 0, tiled=True)]
    ppermute x12, waiting for transfers between devices: 38.5 us -> 28 us  [along(): return lambda v: lax.ppermute(v, 'grp', perm)]
    all_to_all x3 -> x4, waiting for transfers between devices: 32.8 us -> 38.3 us  [exchange(): return lax.all_to_all(v, 'dev', 0, 0, tiled=True)]
    all_to_all x3 -> x4, starting transfers between devices: 18.4 us -> 21.4 us  [exchange(): return lax.all_to_all(v, 'dev', 0, 0, tiled=True)]
    unnamed x35 -> x17, local copies, waits for them, and re-layouts: 4.52 us -> 1.69 us
  transfers between devices with their start and end apart: 44 -> 45, of which waited for: 26 -> 23; matrix products, arithmetic and copies ran while one was open for 2% -> 2% of each run, Pallas kernels for 5% -> 5%
where the time goes in v8:
time: 237 us
  waiting for transfers between devices  105 us (44%)
  starting transfers between devices  67.6 us (29%)
  Pallas kernels  35.2 us (15%)
  blocking collectives  20.2 us (9%)
  local copies, waits for them, and re-layouts  4.34 us (2%)
  other arithmetic  3.32 us (1%)
    ppermute x29, waiting for transfers between devices, along(): return lambda v: lax.ppermute(v, 'dev', perm)  38.5 us
    all_to_all x4, waiting for transfers between devices, exchange(): return lax.all_to_all(v, 'dev', 0, 0, tiled=True)  38.3 us
    ppermute x29, starting transfers between devices, along(): return lambda v: lax.ppermute(v, 'dev', perm)  30.2 us
    ppermute x12, waiting for transfers between devices, along(): return lambda v: lax.ppermute(v, 'grp', perm)  28 us
    all_to_all x4, starting transfers between devices, exchange(): return lax.all_to_all(v, 'dev', 0, 0, tiled=True)  21.4 us
    all_to_all x1, blocking collectives, exchange(): return lax.all_to_all(v, 'dev', 0, 0, tiled=True)  20.2 us
    ppermute x12, starting transfers between devices, along(): return lambda v: lax.ppermute(v, 'grp', perm)  16 us
    pallas_call x1, Pallas kernels, grad_passages(): pl.pallas_call(grad_p_kernel, in_specs=[SMEM] * 3 + [VMEM] * 9, out_specs...  7.84 us
  transfers between devices with their start and end apart: 45, of which 23 were waited for; matrix products, arithmetic and copies ran while one was open for 2% of the time, Pallas kernels for 5%

profile of v8, /device:TPU:1, one launch (start us, length us, event | category | flops | bytes accessed | tf_op | source)
XLA Modules:
  0.0 236.6 jit_solution(13750746884011315153)
XLA Ops:
  0.6 2.4 %pack.3 = (bf16[32,64,128]{2,1,0:T(8,128)(2,1)}, bf16[32,64,128]{2,1,0:T(8,128)(2,1)}) custom-call(f32[128,4096]{1,0:T(8,128)} %x.7), custom_call_target="tpu_custom_call" | custom-call | bytes 5242880 | tf_op jit(solution)/shard_map/pack/pallas_call | solution.py:75
  3.0 20.2 %all_to_all.25.refs_0_ = bf16[32,64,128]{2,1,0:T(8,128)(2,1)S(1)} all-to-all(bf16[32,64,128]{2,1,0:T(8,128)(2,1)} %get-tuple-element.27), channel_id=1, replica_groups=mesh['grp'=4,'dev'=32] {'dev'}, dimensions={0} | all-to-all | bytes 1048576 | tf_op jit(solution)/shard_map/all_to_all | solution.py:472
  23.3 3.8 %collective-permute-start = (bf16[32,64,128]{2,1,0:T(8,128)(2,1)S(1)}, bf16[32,64,128]{2,1,0:T(8,128)(2,1)S(1)}, u32[]{:S(2)}, u32[]{:S(2)}) collective-permute-start(bf16[32,64,128]{2,1,0:T(8,128)(2,1)S(1)} %all_to_all.25.refs_0_), channel_id=1, source_target_pairs={{0,96},{32,0},{64,32},{96,64},{1,97},{33,1},{65,33},{97,65},{2,98}... | collective-permute-start | bytes 1572872 | tf_op jit(solution)/shard_map/ppermute | solution.py:411
  27.0 3.9 %all-to-all-start = ((bf16[32,64,128]{2,1,0:T(8,128)(2,1)}), bf16[32,64,128]{2,1,0:T(8,128)(2,1)S(1)}, u32[]{:S(2)}, u32[]{:S(2)}) async-start(bf16[32,64,128]{2,1,0:T(8,128)(2,1)} %get-tuple-element.26), calls=%async_computation | async-start | bytes 1048576 | tf_op jit(solution)/shard_map/all_to_all | solution.py:472
  31.0 1.6 copy-done.4
  33.9 8.6 %all-to-all-done.refs_1_ = bf16[32,64,128]{2,1,0:T(8,128)(2,1)S(1)} async-done(((bf16[32,64,128]{2,1,0:T(8,128)(2,1)}), bf16[32,64,128]{2,1,0:T(8,128)(2,1)S(1)}, u32[]{:S(2)}, u32[]{:S(2)}) %all-to-all-start) | async-done | bytes 524320 | tf_op jit(solution)/shard_map/all_to_all | solution.py:472
  42.6 3.7 %all-to-all-start.2 = ((bf16[32,144,128]{2,1,0:T(8,128)(2,1)}), bf16[32,144,128]{2,1,0:T(8,128)(2,1)S(1)}, u32[]{:S(2)}, u32[]{:S(2)}) async-start(bf16[32,144,128]{2,1,0:T(8,128)(2,1)} %pack.2), calls=%async_computation.2 | async-start | bytes 2359296 | tf_op jit(solution)/shard_map/all_to_all | solution.py:472
  46.3 3.0 %collective-permute-start.2 = (bf16[32,64,128]{2,1,0:T(8,128)(2,1)S(1)}, bf16[32,64,128]{2,1,0:T(8,128)(2,1)}, u32[]{:S(2)}, u32[]{:S(2)}) collective-permute-start(bf16[32,64,128]{2,1,0:T(8,128)(2,1)S(1)} %all-to-all-done.refs_1_), channel_id=1, source_target_pairs={{0,96},{32,0},{64,32},{96,64},{1,97},{33,1},{65,33},{97,65},{2,98}... | collective-permute-start | bytes 1572872 | tf_op jit(solution)/shard_map/ppermute | solution.py:411
  49.8 14.8 %all-to-all-done.2.q_own.q = bf16[32,144,128]{2,1,0:T(8,128)(2,1)S(1)} async-done(((bf16[32,144,128]{2,1,0:T(8,128)(2,1)}), bf16[32,144,128]{2,1,0:T(8,128)(2,1)S(1)}, u32[]{:S(2)}, u32[]{:S(2)}) %all-to-all-start.2) | async-done | bytes 1179680 | tf_op jit(solution)/shard_map/all_to_all | solution.py:472
  65.7 2.9 %collective-permute-start.4 = (bf16[32,64,128]{2,1,0:T(8,128)(2,1)S(1)}, bf16[32,64,128]{2,1,0:T(8,128)(2,1)S(1)}, u32[]{:S(2)}, u32[]{:S(2)}) collective-permute-start(bf16[32,64,128]{2,1,0:T(8,128)(2,1)S(1)} %collective-permute-done.refs_2_), channel_id=1, source_target_pairs={{0,96},{32,0},{64,32},{96,64},{1,97},{33,1},{65,33},{97,65},{2,98}... | collective-permute-start | bytes 1572872 | tf_op jit(solution)/shard_map/ppermute | solution.py:411
  69.6 10.0 %collective-permute-done.4.refs_4_ = bf16[32,64,128]{2,1,0:T(8,128)(2,1)S(1)} collective-permute-done((bf16[32,64,128]{2,1,0:T(8,128)(2,1)S(1)}, bf16[32,64,128]{2,1,0:T(8,128)(2,1)S(1)}, u32[]{:S(2)}, u32[]{:S(2)}) %collective-permute-start.4) | collective-permute-done | bytes 524320 | tf_op jit(solution)/shard_map/ppermute | solution.py:411
  80.7 2.2 collective-permute-done.5.refs_5_
  83.0 1.4 collective-permute-start.12
  85.9 7.8 %partial_scores.1 = (f32[2,512,128]{2,1,0:T(8,128)S(1)}, f32[2,512,128]{2,1,0:T(8,128)S(1)}, f32[2,512,128]{2,1,0:T(8,128)S(1)}, f32[2,512,128]{2,1,0:T(8,128)S(...) custom-call(s32[128]{0:T(128)S(1)} %and_select_fusion.ids, ...), custom_call_target="tpu_custom_call" | custom-call | bytes 20971520 | tf_op jit(solution)/shard_map/partial_scores/pallas_call | solution.py:188
  93.8 2.6 %collective-permute-start.19 = (f32[2,512,128]{2,1,0:T(8,128)S(1)}, f32[2,512,128]{2,1,0:T(8,128)S(1)}, u32[]{:S(2)}, u32[]{:S(2)}) collective-permute-start(f32[2,512,128]{2,1,0:T(8,128)S(1)} %get-tuple-element.39), channel_id=1, source_target_pairs={{0,24},{1,7},{2,26},{3,1},{4,28},{5,3},{6,30},{7,5},{8,0},{9,15},{... | collective-permute-start | bytes 1572872 | tf_op jit(solution)/shard_map/ppermute | solution.py:424
  96.5 1.4 collective-permute-start.18
  97.9 5.4 %collective-permute-done.15 = f32[2,512,128]{2,1,0:T(8,128)S(1)} collective-permute-done((f32[2,512,128]{2,1,0:T(8,128)S(1)}, f32[2,512,128]{2,1,0:T(8,128)S(1)}, u32[]{:S(2)}, u32[]{:S(2)}) %collective-permute-start.15) | collective-permute-done | bytes 524320 | tf_op jit(solution)/shard_map/ppermute | solution.py:424
  103.5 2.7 %collective-permute-start.20 = (f32[2,512,128]{2,1,0:T(8,128)S(1)}, f32[2,512,128]{2,1,0:T(8,128)S(1)}, u32[]{:S(2)}, u32[]{:S(2)}) collective-permute-start(f32[2,512,128]{2,1,0:T(8,128)S(1)} %add.104), channel_id=1, source_target_pairs={{0,24},{1,7},{2,26},{3,1},{4,28},{5,3},{6,30},{7,5},{8,0},{9,15},{... | collective-permute-start | bytes 1572872 | tf_op jit(solution)/shard_map/ppermute | solution.py:424
  106.2 1.9 collective-permute-done.17
  108.9 5.6 %collective-permute-done.16 = f32[2,512,128]{2,1,0:T(8,128)S(1)} collective-permute-done((f32[2,512,128]{2,1,0:T(8,128)S(1)}, f32[2,512,128]{2,1,0:T(8,128)S(1)}, u32[]{:S(2)}, u32[]{:S(2)}) %collective-permute-start.16) | collective-permute-done | bytes 524320 | tf_op jit(solution)/shard_map/ppermute | solution.py:424
  117.0 4.8 %collective-permute-done.21 = f32[512,128]{1,0:T(8,128)S(1)} collective-permute-done((f32[512,128]{1,0:T(8,128)S(1)}, f32[512,128]{1,0:T(8,128)S(1)}, u32[]{:S(2)}, u32[]{:S(2)}) %collective-permute-start.21) | collective-permute-done | bytes 262176 | tf_op jit(solution)/shard_map/ppermute | solution.py:424
  121.8 1.5 collective-permute-done.22
  124.7 2.3 collective-permute-start.24
  129.0 3.0 %softmax_weights.1 = bf16[528,128]{1,0:T(8,128)(2,1)S(1)} custom-call(s32[5]{0:T(128)S(1)} %stack.53.at, f32[512,128]{1,0:T(8,128)S(1)} %fusion.6.x_own, f32[512,128]{1,0:T(8,128)} %collective-permute-done.24.x_sib, s32[8,128]{1,0:T(8,128)S(1)} %stack.56.listv, bf16[32,144,128]{2,1,0:T(8,128)(2,1)S(1)} %all-to-all-done.2.q_own.q), custom_call_target="tpu_custom_call" | custom-call | bytes 8388608 | tf_op jit(solution)/shard_map/softmax_weights/pallas_call | solution.py:250
  134.3 1.9 collective-permute-done.25
  136.2 2.4 %collective-permute-done.26 = bf16[528,128]{1,0:T(8,128)(2,1)S(1)} collective-permute-done((bf16[528,128]{1,0:T(8,128)(2,1)S(1)}, bf16[528,128]{1,0:T(8,128)(2,1)S(1)}, u32[]{:S(2)}, u32[]{:S(2)}) %collective-permute-start.26) | collective-permute-done | bytes 135200 | tf_op jit(solution)/shard_map/ppermute | solution.py:424
  138.6 1.6 collective-permute-done.27
  140.3 2.7 %collective-permute-start.29 = (bf16[4,528,128]{2,1,0:T(8,128)(2,1)S(1)}, bf16[4,528,128]{2,1,0:T(8,128)(2,1)S(1)}, u32[]{:S(2)}, u32[]{:S(2)}) collective-permute-start(bf16[4,528,128]{2,1,0:T(8,128)(2,1)S(1)} %pad_maximum_fusion.refs_0_), channel_id=1, source_target_pairs={{0,6},{1,25},{2,0},{3,27},{4,2},{5,29},{6,4},{7,31},{8,14},{9,1},{... | collective-permute-start | bytes 1622024 | tf_op jit(solution)/shard_map/ppermute | solution.py:424
  143.1 6.3 %collective-permute-done.29.refs_2_ = bf16[4,528,128]{2,1,0:T(8,128)(2,1)S(1)} collective-permute-done((bf16[4,528,128]{2,1,0:T(8,128)(2,1)S(1)}, bf16[4,528,128]{2,1,0:T(8,128)(2,1)S(1)}, u32[]{:S(2)}, u32[]{:S(2)}) %collective-permute-start.29) | collective-permute-done | bytes 540704 | tf_op jit(solution)/shard_map/ppermute | solution.py:424
  149.4 3.4 %collective-permute-start.30 = (bf16[4,528,128]{2,1,0:T(8,128)(2,1)S(1)}, bf16[4,528,128]{2,1,0:T(8,128)(2,1)S(1)}, u32[]{:S(2)}, u32[]{:S(2)}) collective-permute-start(bf16[4,528,128]{2,1,0:T(8,128)(2,1)S(1)} %collective-permute-done.29.refs_2_), channel_id=1, source_target_pairs={{0,6},{1,25},{2,0},{3,27},{4,2},{5,29},{6,4},{7,31},{8,14},{9,1},{... | collective-permute-start | bytes 1622024 | tf_op jit(solution)/shard_map/ppermute | solution.py:424
  152.8 2.3 collective-permute-start.31
  155.6 3.5 %collective-permute-done.30.refs_3_ = bf16[4,528,128]{2,1,0:T(8,128)(2,1)S(1)} collective-permute-done((bf16[4,528,128]{2,1,0:T(8,128)(2,1)S(1)}, bf16[4,528,128]{2,1,0:T(8,128)(2,1)S(1)}, u32[]{:S(2)}, u32[]{:S(2)}) %collective-permute-start.30) | collective-permute-done | bytes 540704 | tf_op jit(solution)/shard_map/ppermute | solution.py:424
  159.1 2.9 %collective-permute-start.34 = (bf16[4,528,128]{2,1,0:T(8,128)(2,1)S(1)}, bf16[4,528,128]{2,1,0:T(8,128)(2,1)S(1)}, u32[]{:S(2)}, u32[]{:S(2)}) collective-permute-start(bf16[4,528,128]{2,1,0:T(8,128)(2,1)S(1)} %collective-permute-done.30.refs_3_), channel_id=1, source_target_pairs={{0,1},{1,0},{2,3},{3,2},{4,5},{5,4},{6,7},{7,6},{8,9},{9,8},{10,11... | collective-permute-start | bytes 1622024 | tf_op jit(solution)/shard_map/ppermute | solution.py:424
  162.0 1.4 place.1.p
  163.5 7.8 %grad_passages.1 = (bf16[32,128,128]{2,1,0:T(8,128)(2,1)S(1)}, bf16[16,128,128]{2,1,0:T(8,128)(2,1)S(1)}, bf16[16,128,128]{2,1,0:T(8,128)(2,1)}, bf16[16,128,128...) custom-call(s32[128]{0:T(128)S(1)} %and_select_fusion.ids, ...), custom_call_target="tpu_custom_call" | custom-call | bytes 20971520 | tf_op jit(solution)/shard_map/grad_passages/pallas_call | solution.py:325
  172.8 1.8 collective-permute-start.37
  174.6 6.1 %grad_queries.1 = bf16[32,128,128]{2,1,0:T(8,128)(2,1)} custom-call(s32[128]{0:T(128)S(1)} %and_select_fusion.ids, s32[128]{0:T(128)S(1)} %convert_reduce_fusion.own, s32[5]{0:T(128)S(1)} %stack.53.at, bf16[128,128,128]{2,1,0:T(8,128)(2,1)S(1)} %place.1.p, bf16[4,528,128]{2,1,0:T(8,128)(2,1)S(1)} %pad_maximum_fusion.refs_0_, ...), custom_call_target="tpu_custom_call" | custom-call | bytes 20971520 | tf_op jit(solution)/shard_map/grad_queries/pallas_call | solution.py:360
  180.7 6.7 %all-to-all-start.3 = ((bf16[32,128,128]{2,1,0:T(8,128)(2,1)}), bf16[32,128,128]{2,1,0:T(8,128)(2,1)S(1)}, u32[]{:S(2)}, u32[]{:S(2)}) async-start(bf16[32,128,128]{2,1,0:T(8,128)(2,1)} %grad_queries.1), calls=%async_computation.3 | async-start | bytes 2097152 | tf_op jit(solution)/shard_map/all_to_all | solution.py:472
  188.6 3.0 %collective-permute-start.40 = (bf16[16,128,128]{2,1,0:T(8,128)(2,1)S(1)}, bf16[16,128,128]{2,1,0:T(8,128)(2,1)S(1)}, u32[]{:S(2)}, u32[]{:S(2)}) collective-permute-start(bf16[16,128,128]{2,1,0:T(8,128)(2,1)S(1)} %add_convert_fusion), channel_id=1, source_target_pairs={{0,96},{32,0},{64,32},{96,64},{1,97},{33,1},{65,33},{97,65},{2,98}... | collective-permute-start | bytes 1572872 | tf_op jit(solution)/shard_map/ppermute | solution.py:411
  192.9 3.2 %collective-permute-done.37.refs_1_ = bf16[16,128,128]{2,1,0:T(8,128)(2,1)} collective-permute-done((bf16[16,128,128]{2,1,0:T(8,128)(2,1)}, bf16[16,128,128]{2,1,0:T(8,128)(2,1)}, u32[]{:S(2)}, u32[]{:S(2)}) %collective-permute-start.37) | collective-permute-done | bytes 524320 | tf_op jit(solution)/shard_map/ppermute | solution.py:411
  196.0 1.4 collective-permute-done.38.refs_2_
  197.5 9.7 %collective-permute-done.40.refs_3_ = bf16[16,128,128]{2,1,0:T(8,128)(2,1)S(1)} collective-permute-done((bf16[16,128,128]{2,1,0:T(8,128)(2,1)S(1)}, bf16[16,128,128]{2,1,0:T(8,128)(2,1)S(1)}, u32[]{:S(2)}, u32[]{:S(2)}) %collective-permute-start.40) | collective-permute-done | bytes 524320 | tf_op jit(solution)/shard_map/ppermute | solution.py:411
  207.2 1.4 collective-permute-done.36.refs_0_
  208.6 2.4 %join.1 = bf16[32,128,128]{2,1,0:T(8,128)(2,1)} custom-call(bf16[32,128,128]{2,1,0:T(8,128)(2,1)S(1)} %get-tuple-element.42.kept, bf16[16,128,128]{2,1,0:T(8,128)(2,1)S(1)} %collective-permute-done.36.refs_0_, bf16[16,128,128]{2,1,0:T(8,128)(2,1)} %collective-permute-done.37.refs_1_, bf16[16,128,128]{2,1,0:T(8,128)(2,1)} %collective-permute-done.38.refs_2_, ...), custom_call_target="tpu_custom_call" | custom-call | bytes 8388608 | tf_op jit(solution)/shard_map/join/pallas_call | solution.py:396
  211.1 7.0 %all-to-all-start.4 = ((bf16[32,128,128]{2,1,0:T(8,128)(2,1)}), bf16[32,128,128]{2,1,0:T(8,128)(2,1)S(1)}, u32[]{:S(2)}, u32[]{:S(2)}) async-start(bf16[32,128,128]{2,1,0:T(8,128)(2,1)} %join.1), calls=%async_computation.4 | async-start | bytes 2097152 | tf_op jit(solution)/shard_map/all_to_all | solution.py:472
  218.7 1.4 unpack.2
  220.1 14.9 %all-to-all-done.4.x = bf16[32,128,128]{2,1,0:T(8,128)(2,1)S(1)} async-done(((bf16[32,128,128]{2,1,0:T(8,128)(2,1)}), bf16[32,128,128]{2,1,0:T(8,128)(2,1)S(1)}, u32[]{:S(2)}, u32[]{:S(2)}) %all-to-all-start.4) | async-done | bytes 1048608 | tf_op jit(solution)/shard_map/all_to_all | solution.py:472
  235.1 1.4 unpack.3
  (91 shorter events, 20.8 us)
Async XLA Ops:
  23.3 19.3 %collective-permute-start = (bf16[32,64,128]{2,1,0:T(8,128)(2,1)S(1)}, bf16[32,64,128]{2,1,0:T(8,128)(2,1)S(1)}, u32[]{:S(2)}, u32[]{:S(2)}) collective-permute-start(bf16[32,64,128]{2,1,0:T(8,128)(2,1)S(1)} %all_to_all.25.refs_0_), channel_id=1, source_target_pairs={{0,96},{32,0},{64,32},{96,64},{1,97},{33,1},{65,33},{97,65},{2,98}... | collective-permute-start | bytes 1572872 | tf_op jit(solution)/shard_map/ppermute | solution.py:411
  27.0 15.5 %collective-permute-start.1 = (bf16[32,64,128]{2,1,0:T(8,128)(2,1)S(1)}, bf16[32,64,128]{2,1,0:T(8,128)(2,1)S(1)}, u32[]{:S(2)}, u32[]{:S(2)}) collective-permute-start(bf16[32,64,128]{2,1,0:T(8,128)(2,1)S(1)} %all_to_all.25.refs_0_), channel_id=1, source_target_pairs={{0,32},{32,64},{64,96},{96,0},{1,33},{33,65},{65,97},{97,1},{2,34}... | collective-permute-start | bytes 1572872 | tf_op jit(solution)/shard_map/ppermute | solution.py:411
  27.0 15.5 %all-to-all-start = ((bf16[32,64,128]{2,1,0:T(8,128)(2,1)}), bf16[32,64,128]{2,1,0:T(8,128)(2,1)S(1)}, u32[]{:S(2)}, u32[]{:S(2)}) async-start(bf16[32,64,128]{2,1,0:T(8,128)(2,1)} %get-tuple-element.26), calls=%async_computation | async-start | bytes 1048576 | tf_op jit(solution)/shard_map/all_to_all | solution.py:472
  32.5 36.0 %copy-start.7 = (s32[1,32]{1,0:T(1,128)S(1)}, s32[1,32]{1,0:T(1,128)}, u32[]{:S(2)}) copy-start(s32[1,32]{1,0:T(1,128)} %param.8) | copy-start | bytes 388
  42.6 22.1 %all-to-all-start.2 = ((bf16[32,144,128]{2,1,0:T(8,128)(2,1)}), bf16[32,144,128]{2,1,0:T(8,128)(2,1)S(1)}, u32[]{:S(2)}, u32[]{:S(2)}) async-start(bf16[32,144,128]{2,1,0:T(8,128)(2,1)} %pack.2), calls=%async_computation.2 | async-start | bytes 2359296 | tf_op jit(solution)/shard_map/all_to_all | solution.py:472
  46.3 18.9 %collective-permute-start.2 = (bf16[32,64,128]{2,1,0:T(8,128)(2,1)S(1)}, bf16[32,64,128]{2,1,0:T(8,128)(2,1)}, u32[]{:S(2)}, u32[]{:S(2)}) collective-permute-start(bf16[32,64,128]{2,1,0:T(8,128)(2,1)S(1)} %all-to-all-done.refs_1_), channel_id=1, source_target_pairs={{0,96},{32,0},{64,32},{96,64},{1,97},{33,1},{65,33},{97,65},{2,98}... | collective-permute-start | bytes 1572872 | tf_op jit(solution)/shard_map/ppermute | solution.py:411
  49.3 16.1 %collective-permute-start.3 = (bf16[32,64,128]{2,1,0:T(8,128)(2,1)S(1)}, bf16[32,64,128]{2,1,0:T(8,128)(2,1)}, u32[]{:S(2)}, u32[]{:S(2)}) collective-permute-start(bf16[32,64,128]{2,1,0:T(8,128)(2,1)S(1)} %all-to-all-done.refs_1_), channel_id=1, source_target_pairs={{0,32},{32,64},{64,96},{96,0},{1,33},{33,65},{65,97},{97,1},{2,34}... | collective-permute-start | bytes 1572872 | tf_op jit(solution)/shard_map/ppermute | solution.py:411
  49.3 16.4 %collective-permute-start.7 = (bf16[32,64,128]{2,1,0:T(8,128)(2,1)S(1)}, bf16[32,64,128]{2,1,0:T(8,128)(2,1)}, u32[]{:S(2)}, u32[]{:S(2)}) collective-permute-start(bf16[32,64,128]{2,1,0:T(8,128)(2,1)S(1)} %all_to_all.25.refs_0_), channel_id=1, source_target_pairs={{0,1},{1,0},{2,3},{3,2},{4,5},{5,4},{6,7},{7,6},{8,9},{9,8},{10,11... | collective-permute-start | bytes 1572872 | tf_op jit(solution)/shard_map/ppermute | solution.py:424
  49.8 18.8 %collective-permute-start.8 = (bf16[32,64,128]{2,1,0:T(8,128)(2,1)S(1)}, bf16[32,64,128]{2,1,0:T(8,128)(2,1)}, u32[]{:S(2)}, u32[]{:S(2)}) collective-permute-start(bf16[32,64,128]{2,1,0:T(8,128)(2,1)S(1)} %all-to-all-done.refs_1_), channel_id=1, source_target_pairs={{0,1},{1,0},{2,3},{3,2},{4,5},{5,4},{6,7},{7,6},{8,9},{9,8},{10,11... | collective-permute-start | bytes 1572872 | tf_op jit(solution)/shard_map/ppermute | solution.py:424
  64.6 21.3 %collective-permute-start.6 = (bf16[32,144,128]{2,1,0:T(8,128)(2,1)S(1)}, bf16[32,144,128]{2,1,0:T(8,128)(2,1)}, u32[]{:S(2)}, u32[]{:S(2)}) collective-permute-start(bf16[32,144,128]{2,1,0:T(8,128)(2,1)S(1)} %all-to-all-done.2.q_own.q), channel_id=1, source_target_pairs={{0,1},{1,0},{2,3},{3,2},{4,5},{5,4},{6,7},{7,6},{8,9},{9,8},{10,11... | collective-permute-start | bytes 3538952 | tf_op jit(solution)/shard_map/ppermute | solution.py:424
  65.2 3.7 %collective-permute-start.9 = (bf16[32,64,128]{2,1,0:T(8,128)(2,1)S(1)}, bf16[32,64,128]{2,1,0:T(8,128)(2,1)S(1)}, u32[]{:S(2)}, u32[]{:S(2)}) collective-permute-start(bf16[32,64,128]{2,1,0:T(8,128)(2,1)S(1)} %collective-permute-done.refs_2_), channel_id=1, source_target_pairs={{0,1},{1,0},{2,3},{3,2},{4,5},{5,4},{6,7},{7,6},{8,9},{9,8},{10,11... | collective-permute-start | bytes 1572872 | tf_op jit(solution)/shard_map/ppermute | solution.py:424
  65.4 4.1 %collective-permute-start.13 = (bf16[32,64,128]{2,1,0:T(8,128)(2,1)S(1)}, bf16[32,64,128]{2,1,0:T(8,128)(2,1)S(1)}, u32[]{:S(2)}, u32[]{:S(2)}) collective-permute-start(bf16[32,64,128]{2,1,0:T(8,128)(2,1)S(1)} %collective-permute-done.1.refs_6_), channel_id=1, source_target_pairs={{0,1},{1,0},{2,3},{3,2},{4,5},{5,4},{6,7},{7,6},{8,9},{9,8},{10,11... | collective-permute-start | bytes 1572872 | tf_op jit(solution)/shard_map/ppermute | solution.py:424
  65.7 13.9 %collective-permute-start.4 = (bf16[32,64,128]{2,1,0:T(8,128)(2,1)S(1)}, bf16[32,64,128]{2,1,0:T(8,128)(2,1)S(1)}, u32[]{:S(2)}, u32[]{:S(2)}) collective-permute-start(bf16[32,64,128]{2,1,0:T(8,128)(2,1)S(1)} %collective-permute-done.refs_2_), channel_id=1, source_target_pairs={{0,96},{32,0},{64,32},{96,64},{1,97},{33,1},{65,33},{97,65},{2,98}... | collective-permute-start | bytes 1572872 | tf_op jit(solution)/shard_map/ppermute | solution.py:411
  68.6 14.4 %collective-permute-start.5 = (bf16[32,64,128]{2,1,0:T(8,128)(2,1)}, bf16[32,64,128]{2,1,0:T(8,128)(2,1)S(1)}, u32[]{:S(2)}, u32[]{:S(2)}) collective-permute-start(bf16[32,64,128]{2,1,0:T(8,128)(2,1)} %collective-permute-done.3.refs_7_), channel_id=1, source_target_pairs={{0,32},{32,64},{64,96},{96,0},{1,33},{33,65},{65,97},{97,1},{2,34}... | collective-permute-start | bytes 1572872 | tf_op jit(solution)/shard_map/ppermute | solution.py:411
  68.9 15.6 %collective-permute-start.10 = (bf16[32,64,128]{2,1,0:T(8,128)(2,1)}, bf16[32,64,128]{2,1,0:T(8,128)(2,1)S(1)}, u32[]{:S(2)}, u32[]{:S(2)}) collective-permute-start(bf16[32,64,128]{2,1,0:T(8,128)(2,1)} %collective-permute-done.2.refs_3_), channel_id=1, source_target_pairs={{0,1},{1,0},{2,3},{3,2},{4,5},{5,4},{6,7},{7,6},{8,9},{9,8},{10,11... | collective-permute-start | bytes 1572872 | tf_op jit(solution)/shard_map/ppermute | solution.py:424
  69.5 15.0 %collective-permute-start.14 = (bf16[32,64,128]{2,1,0:T(8,128)(2,1)}, bf16[32,64,128]{2,1,0:T(8,128)(2,1)S(1)}, u32[]{:S(2)}, u32[]{:S(2)}) collective-permute-start(bf16[32,64,128]{2,1,0:T(8,128)(2,1)} %collective-permute-done.3.refs_7_), channel_id=1, source_target_pairs={{0,1},{1,0},{2,3},{3,2},{4,5},{5,4},{6,7},{7,6},{8,9},{9,8},{10,11... | collective-permute-start | bytes 1572872 | tf_op jit(solution)/shard_map/ppermute | solution.py:424
  79.6 4.9 %collective-permute-start.11 = (bf16[32,64,128]{2,1,0:T(8,128)(2,1)S(1)}, bf16[32,64,128]{2,1,0:T(8,128)(2,1)S(1)}, u32[]{:S(2)}, u32[]{:S(2)}) collective-permute-start(bf16[32,64,128]{2,1,0:T(8,128)(2,1)S(1)} %collective-permute-done.4.refs_4_), channel_id=1, source_target_pairs={{0,1},{1,0},{2,3},{3,2},{4,5},{5,4},{6,7},{7,6},{8,9},{9,8},{10,11... | collective-permute-start | bytes 1572872 | tf_op jit(solution)/shard_map/ppermute | solution.py:424
  83.0 2.9 %collective-permute-start.12 = (bf16[32,64,128]{2,1,0:T(8,128)(2,1)S(1)}, bf16[32,64,128]{2,1,0:T(8,128)(2,1)S(1)}, u32[]{:S(2)}, u32[]{:S(2)}) collective-permute-start(bf16[32,64,128]{2,1,0:T(8,128)(2,1)S(1)} %collective-permute-done.5.refs_5_), channel_id=1, source_target_pairs={{0,1},{1,0},{2,3},{3,2},{4,5},{5,4},{6,7},{7,6},{8,9},{9,8},{10,11... | collective-permute-start | bytes 1572872 | tf_op jit(solution)/shard_map/ppermute | solution.py:424
  93.7 9.6 %collective-permute-start.15 = (f32[2,512,128]{2,1,0:T(8,128)S(1)}, f32[2,512,128]{2,1,0:T(8,128)S(1)}, u32[]{:S(2)}, u32[]{:S(2)}) collective-permute-start(f32[2,512,128]{2,1,0:T(8,128)S(1)} %get-tuple-element.35), channel_id=1, source_target_pairs={{0,8},{1,3},{2,10},{3,5},{4,12},{5,7},{6,14},{7,1},{8,16},{9,11},{... | collective-permute-start | bytes 1572872 | tf_op jit(solution)/shard_map/ppermute | solution.py:424
  93.8 9.7 %collective-permute-start.19 = (f32[2,512,128]{2,1,0:T(8,128)S(1)}, f32[2,512,128]{2,1,0:T(8,128)S(1)}, u32[]{:S(2)}, u32[]{:S(2)}) collective-permute-start(f32[2,512,128]{2,1,0:T(8,128)S(1)} %get-tuple-element.39), channel_id=1, source_target_pairs={{0,24},{1,7},{2,26},{3,1},{4,28},{5,3},{6,30},{7,5},{8,0},{9,15},{... | collective-permute-start | bytes 1572872 | tf_op jit(solution)/shard_map/ppermute | solution.py:424
  96.4 11.7 %collective-permute-start.17 = (f32[2,512,128]{2,1,0:T(8,128)S(1)}, f32[2,512,128]{2,1,0:T(8,128)S(1)}, u32[]{:S(2)}, u32[]{:S(2)}) collective-permute-start(f32[2,512,128]{2,1,0:T(8,128)S(1)} %get-tuple-element.36), channel_id=1, source_target_pairs={{0,24},{1,7},{2,26},{3,1},{4,28},{5,3},{6,30},{7,5},{8,0},{9,15},{... | collective-permute-start | bytes 1572872 | tf_op jit(solution)/shard_map/ppermute | solution.py:424
  96.5 12.4 %collective-permute-start.18 = (f32[2,512,128]{2,1,0:T(8,128)S(1)}, f32[2,512,128]{2,1,0:T(8,128)S(1)}, u32[]{:S(2)}, u32[]{:S(2)}) collective-permute-start(f32[2,512,128]{2,1,0:T(8,128)S(1)} %get-tuple-element.37), channel_id=1, source_target_pairs={{0,8},{1,3},{2,10},{3,5},{4,12},{5,7},{6,14},{7,1},{8,16},{9,11},{... | collective-permute-start | bytes 1572872 | tf_op jit(solution)/shard_map/ppermute | solution.py:424
  103.4 11.2 %collective-permute-start.16 = (f32[2,512,128]{2,1,0:T(8,128)S(1)}, f32[2,512,128]{2,1,0:T(8,128)S(1)}, u32[]{:S(2)}, u32[]{:S(2)}) collective-permute-start(f32[2,512,128]{2,1,0:T(8,128)S(1)} %add.99), channel_id=1, source_target_pairs={{0,8},{1,3},{2,10},{3,5},{4,12},{5,7},{6,14},{7,1},{8,16},{9,11},{... | collective-permute-start | bytes 1572872 | tf_op jit(solution)/shard_map/ppermute | solution.py:424
  103.5 11.0 %collective-permute-start.20 = (f32[2,512,128]{2,1,0:T(8,128)S(1)}, f32[2,512,128]{2,1,0:T(8,128)S(1)}, u32[]{:S(2)}, u32[]{:S(2)}) collective-permute-start(f32[2,512,128]{2,1,0:T(8,128)S(1)} %add.104), channel_id=1, source_target_pairs={{0,24},{1,7},{2,26},{3,1},{4,28},{5,3},{6,30},{7,5},{8,0},{9,15},{... | collective-permute-start | bytes 1572872 | tf_op jit(solution)/shard_map/ppermute | solution.py:424
  114.7 7.1 %collective-permute-start.21 = (f32[512,128]{1,0:T(8,128)S(1)}, f32[512,128]{1,0:T(8,128)S(1)}, u32[]{:S(2)}, u32[]{:S(2)}) collective-permute-start(f32[512,128]{1,0:T(8,128)S(1)} %get-tuple-element.49), channel_id=1, source_target_pairs={{0,4},{1,17},{2,6},{3,19},{4,0},{5,21},{6,2},{7,23},{8,12},{9,25},... | collective-permute-start | bytes 786440 | tf_op jit(solution)/shard_map/ppermute | solution.py:424
  115.5 7.8 %collective-permute-start.22 = (f32[512,128]{1,0:T(8,128)S(1)}, f32[512,128]{1,0:T(8,128)S(1)}, u32[]{:S(2)}, u32[]{:S(2)}) collective-permute-start(f32[512,128]{1,0:T(8,128)S(1)} %get-tuple-element.50), channel_id=1, source_target_pairs={{0,6},{1,25},{2,0},{3,27},{4,2},{5,29},{6,4},{7,31},{8,14},{9,1},{... | collective-permute-start | bytes 786440 | tf_op jit(solution)/shard_map/ppermute | solution.py:424
  116.2 8.4 %collective-permute-start.23 = (f32[512,128]{1,0:T(8,128)S(1)}, f32[512,128]{1,0:T(8,128)S(1)}, u32[]{:S(2)}, u32[]{:S(2)}) collective-permute-start(f32[512,128]{1,0:T(8,128)S(1)} %get-tuple-element.51), channel_id=1, source_target_pairs={{0,2},{1,9},{2,4},{3,11},{4,6},{5,13},{6,0},{7,15},{8,10},{9,17},{... | collective-permute-start | bytes 786440 | tf_op jit(solution)/shard_map/ppermute | solution.py:424
  124.7 4.2 %collective-permute-start.24 = (f32[512,128]{1,0:T(8,128)S(1)}, f32[512,128]{1,0:T(8,128)}, u32[]{:S(2)}, u32[]{:S(2)}) collective-permute-start(f32[512,128]{1,0:T(8,128)S(1)} %fusion.6.x_own), channel_id=1, source_target_pairs={{0,1},{1,0},{2,3},{3,2},{4,5},{5,4},{6,7},{7,6},{8,9},{9,8},{10,11... | collective-permute-start | bytes 786440 | tf_op jit(solution)/shard_map/ppermute | solution.py:424
  128.9 33.0 %copy-start.1 = (bf16[32,64,128]{2,1,0:T(8,128)(2,1)S(1)}, bf16[32,64,128]{2,1,0:T(8,128)(2,1)}, u32[]{:S(2)}) copy-start(bf16[32,64,128]{2,1,0:T(8,128)(2,1)} %copy-done) | copy-start | bytes 1572868
  128.9 33.0 %copy-start.3 = (bf16[32,64,128]{2,1,0:T(8,128)(2,1)S(1)}, bf16[32,64,128]{2,1,0:T(8,128)(2,1)}, u32[]{:S(2)}) copy-start(bf16[32,64,128]{2,1,0:T(8,128)(2,1)} %copy-done.2) | copy-start | bytes 1572868
  132.0 4.2 %collective-permute-start.25 = (bf16[528,128]{1,0:T(8,128)(2,1)S(1)}, bf16[528,128]{1,0:T(8,128)(2,1)S(1)}, u32[]{:S(2)}, u32[]{:S(2)}) collective-permute-start(bf16[528,128]{1,0:T(8,128)(2,1)S(1)} %softmax_weights.1), channel_id=1, source_target_pairs={{0,24},{1,7},{2,26},{3,1},{4,28},{5,3},{6,30},{7,5},{8,0},{9,15},{... | collective-permute-start | bytes 405512 | tf_op jit(solution)/shard_map/ppermute | solution.py:424
  133.2 5.5 %collective-permute-start.26 = (bf16[528,128]{1,0:T(8,128)(2,1)S(1)}, bf16[528,128]{1,0:T(8,128)(2,1)S(1)}, u32[]{:S(2)}, u32[]{:S(2)}) collective-permute-start(bf16[528,128]{1,0:T(8,128)(2,1)S(1)} %softmax_weights.1), channel_id=1, source_target_pairs={{0,16},{1,5},{2,18},{3,7},{4,20},{5,1},{6,22},{7,3},{8,24},{9,13},... | collective-permute-start | bytes 405512 | tf_op jit(solution)/shard_map/ppermute | solution.py:424
  133.9 6.4 %collective-permute-start.27 = (bf16[528,128]{1,0:T(8,128)(2,1)S(1)}, bf16[528,128]{1,0:T(8,128)(2,1)S(1)}, u32[]{:S(2)}, u32[]{:S(2)}) collective-permute-start(bf16[528,128]{1,0:T(8,128)(2,1)S(1)} %softmax_weights.1), channel_id=1, source_target_pairs={{0,8},{1,3},{2,10},{3,5},{4,12},{5,7},{6,14},{7,1},{8,16},{9,11},{... | collective-permute-start | bytes 405512 | tf_op jit(solution)/shard_map/ppermute | solution.py:424
  140.3 9.0 %collective-permute-start.29 = (bf16[4,528,128]{2,1,0:T(8,128)(2,1)S(1)}, bf16[4,528,128]{2,1,0:T(8,128)(2,1)S(1)}, u32[]{:S(2)}, u32[]{:S(2)}) collective-permute-start(bf16[4,528,128]{2,1,0:T(8,128)(2,1)S(1)} %pad_maximum_fusion.refs_0_), channel_id=1, source_target_pairs={{0,6},{1,25},{2,0},{3,27},{4,2},{5,29},{6,4},{7,31},{8,14},{9,1},{... | collective-permute-start | bytes 1622024 | tf_op jit(solution)/shard_map/ppermute | solution.py:424
  143.1 12.0 %collective-permute-start.28 = (bf16[4,528,128]{2,1,0:T(8,128)(2,1)S(1)}, bf16[4,528,128]{2,1,0:T(8,128)(2,1)S(1)}, u32[]{:S(2)}, u32[]{:S(2)}) collective-permute-start(bf16[4,528,128]{2,1,0:T(8,128)(2,1)S(1)} %pad_maximum_fusion.refs_0_), channel_id=1, source_target_pairs={{0,2},{1,9},{2,4},{3,11},{4,6},{5,13},{6,0},{7,15},{8,10},{9,17},{... | collective-permute-start | bytes 1622024 | tf_op jit(solution)/shard_map/ppermute | solution.py:424
  149.4 9.7 %collective-permute-start.30 = (bf16[4,528,128]{2,1,0:T(8,128)(2,1)S(1)}, bf16[4,528,128]{2,1,0:T(8,128)(2,1)S(1)}, u32[]{:S(2)}, u32[]{:S(2)}) collective-permute-start(bf16[4,528,128]{2,1,0:T(8,128)(2,1)S(1)} %collective-permute-done.29.refs_2_), channel_id=1, source_target_pairs={{0,6},{1,25},{2,0},{3,27},{4,2},{5,29},{6,4},{7,31},{8,14},{9,1},{... | collective-permute-start | bytes 1622024 | tf_op jit(solution)/shard_map/ppermute | solution.py:424
  152.8 10.6 %collective-permute-start.31 = (bf16[4,528,128]{2,1,0:T(8,128)(2,1)S(1)}, bf16[4,528,128]{2,1,0:T(8,128)(2,1)S(1)}, u32[]{:S(2)}, u32[]{:S(2)}) collective-permute-start(bf16[4,528,128]{2,1,0:T(8,128)(2,1)S(1)} %pad_maximum_fusion.refs_0_), channel_id=1, source_target_pairs={{0,1},{1,0},{2,3},{3,2},{4,5},{5,4},{6,7},{7,6},{8,9},{9,8},{10,11... | collective-permute-start | bytes 1622024 | tf_op jit(solution)/shard_map/ppermute | solution.py:424
  155.1 8.3 %collective-permute-start.33 = (bf16[4,528,128]{2,1,0:T(8,128)(2,1)S(1)}, bf16[4,528,128]{2,1,0:T(8,128)(2,1)S(1)}, u32[]{:S(2)}, u32[]{:S(2)}) collective-permute-start(bf16[4,528,128]{2,1,0:T(8,128)(2,1)S(1)} %collective-permute-done.29.refs_2_), channel_id=1, source_target_pairs={{0,1},{1,0},{2,3},{3,2},{4,5},{5,4},{6,7},{7,6},{8,9},{9,8},{10,11... | collective-permute-start | bytes 1622024 | tf_op jit(solution)/shard_map/ppermute | solution.py:424
  155.1 8.3 %collective-permute-start.32 = (bf16[4,528,128]{2,1,0:T(8,128)(2,1)S(1)}, bf16[4,528,128]{2,1,0:T(8,128)(2,1)S(1)}, u32[]{:S(2)}, u32[]{:S(2)}) collective-permute-start(bf16[4,528,128]{2,1,0:T(8,128)(2,1)S(1)} %collective-permute-done.28.refs_1_), channel_id=1, source_target_pairs={{0,1},{1,0},{2,3},{3,2},{4,5},{5,4},{6,7},{7,6},{8,9},{9,8},{10,11... | collective-permute-start | bytes 1622024 | tf_op jit(solution)/shard_map/ppermute | solution.py:424
  159.1 4.4 %collective-permute-start.34 = (bf16[4,528,128]{2,1,0:T(8,128)(2,1)S(1)}, bf16[4,528,128]{2,1,0:T(8,128)(2,1)S(1)}, u32[]{:S(2)}, u32[]{:S(2)}) collective-permute-start(bf16[4,528,128]{2,1,0:T(8,128)(2,1)S(1)} %collective-permute-done.30.refs_3_), channel_id=1, source_target_pairs={{0,1},{1,0},{2,3},{3,2},{4,5},{5,4},{6,7},{7,6},{8,9},{9,8},{10,11... | collective-permute-start | bytes 1622024 | tf_op jit(solution)/shard_map/ppermute | solution.py:424
  171.4 16.0 %collective-permute-start.39 = (bf16[16,128,128]{2,1,0:T(8,128)(2,1)}, bf16[16,128,128]{2,1,0:T(8,128)(2,1)}, u32[]{:S(2)}, u32[]{:S(2)}) collective-permute-start(bf16[16,128,128]{2,1,0:T(8,128)(2,1)} %get-tuple-element.48), channel_id=1, source_target_pairs={{0,96},{32,0},{64,32},{96,64},{1,97},{33,1},{65,33},{97,65},{2,98}... | collective-permute-start | bytes 1572872 | tf_op jit(solution)/shard_map/ppermute | solution.py:411
  171.9 19.7 %collective-permute-start.35 = (bf16[16,128,128]{2,1,0:T(8,128)(2,1)}, bf16[16,128,128]{2,1,0:T(8,128)(2,1)}, u32[]{:S(2)}, u32[]{:S(2)}) collective-permute-start(bf16[16,128,128]{2,1,0:T(8,128)(2,1)} %get-tuple-element.44), channel_id=1, source_target_pairs={{0,32},{32,64},{64,96},{96,0},{1,33},{33,65},{65,97},{97,1},{2,34}... | collective-permute-start | bytes 1572872 | tf_op jit(solution)/shard_map/ppermute | solution.py:411
  172.8 23.2 %collective-permute-start.37 = (bf16[16,128,128]{2,1,0:T(8,128)(2,1)}, bf16[16,128,128]{2,1,0:T(8,128)(2,1)}, u32[]{:S(2)}, u32[]{:S(2)}) collective-permute-start(bf16[16,128,128]{2,1,0:T(8,128)(2,1)} %get-tuple-element.45), channel_id=1, source_target_pairs={{0,96},{32,0},{64,32},{96,64},{1,97},{33,1},{65,33},{97,65},{2,98}... | collective-permute-start | bytes 1572872 | tf_op jit(solution)/shard_map/ppermute | solution.py:411
  174.6 22.9 %collective-permute-start.38 = (bf16[16,128,128]{2,1,0:T(8,128)(2,1)}, bf16[16,128,128]{2,1,0:T(8,128)(2,1)}, u32[]{:S(2)}, u32[]{:S(2)}) collective-permute-start(bf16[16,128,128]{2,1,0:T(8,128)(2,1)} %get-tuple-element.46), channel_id=1, source_target_pairs={{0,32},{32,64},{64,96},{96,0},{1,33},{33,65},{65,97},{97,1},{2,34}... | collective-permute-start | bytes 1572872 | tf_op jit(solution)/shard_map/ppermute | solution.py:411
  180.7 30.4 %all-to-all-start.3 = ((bf16[32,128,128]{2,1,0:T(8,128)(2,1)}), bf16[32,128,128]{2,1,0:T(8,128)(2,1)S(1)}, u32[]{:S(2)}, u32[]{:S(2)}) async-start(bf16[32,128,128]{2,1,0:T(8,128)(2,1)} %grad_queries.1), calls=%async_computation.3 | async-start | bytes 2097152 | tf_op jit(solution)/shard_map/all_to_all | solution.py:472
  188.6 18.6 %collective-permute-start.40 = (bf16[16,128,128]{2,1,0:T(8,128)(2,1)S(1)}, bf16[16,128,128]{2,1,0:T(8,128)(2,1)S(1)}, u32[]{:S(2)}, u32[]{:S(2)}) collective-permute-start(bf16[16,128,128]{2,1,0:T(8,128)(2,1)S(1)} %add_convert_fusion), channel_id=1, source_target_pairs={{0,96},{32,0},{64,32},{96,64},{1,97},{33,1},{65,33},{97,65},{2,98}... | collective-permute-start | bytes 1572872 | tf_op jit(solution)/shard_map/ppermute | solution.py:411
  192.8 15.8 %collective-permute-start.36 = (bf16[16,128,128]{2,1,0:T(8,128)(2,1)S(1)}, bf16[16,128,128]{2,1,0:T(8,128)(2,1)S(1)}, u32[]{:S(2)}, u32[]{:S(2)}) collective-permute-start(bf16[16,128,128]{2,1,0:T(8,128)(2,1)S(1)} %add_convert_fusion.1), channel_id=1, source_target_pairs={{0,32},{32,64},{64,96},{96,0},{1,33},{33,65},{65,97},{97,1},{2,34}... | collective-permute-start | bytes 1572872 | tf_op jit(solution)/shard_map/ppermute | solution.py:411
  211.1 24.0 %all-to-all-start.4 = ((bf16[32,128,128]{2,1,0:T(8,128)(2,1)}), bf16[32,128,128]{2,1,0:T(8,128)(2,1)S(1)}, u32[]{:S(2)}, u32[]{:S(2)}) async-start(bf16[32,128,128]{2,1,0:T(8,128)(2,1)} %join.1), calls=%async_computation.4 | async-start | bytes 2097152 | tf_op jit(solution)/shard_map/all_to_all | solution.py:472
  (5 other events, 89.0 us)

commit v9 on v8

--- a/solution.py
+++ b/solution.py
@@ -473,10 +473,10 @@
 
     up, down, flip = along("z", 1), along("z", -1), along("core", 1)
     low, high = [exchange(v) for v in by_features(passages)]
-    above0, below0 = down(low), up(low)
+    below0, above0 = up(low), down(low)
     q_tiles = by_features(queries, positives.reshape(1, BLK))[0]
     q_tiles, late, *_ = lax.optimization_barrier((q_tiles, high, above0, below0))
-    above1, below1 = down(late), up(late)
+    below1, above1 = up(late), down(late)
     last0, last1, *_ = lax.optimization_barrier((above0, below1, above1))
     far0, far1 = down(last0), up(last1)
     pieces = [low, high, above0, above1, far0, far1, below0, below1]

time: 237 us -> 237 us (level)
  no operation moved by 1% of the time
where the time goes in v9:
time: 237 us
  waiting for transfers between devices  105 us (44%)
  starting transfers between devices  67.6 us (29%)
  Pallas kernels  35.2 us (15%)
  blocking collectives  20.2 us (9%)
  local copies, waits for them, and re-layouts  4.34 us (2%)
  other arithmetic  3.32 us (1%)
    ppermute x29, waiting for transfers between devices, along(): return lambda v: lax.ppermute(v, 'dev', perm)  38.5 us
    all_to_all x4, waiting for transfers between devices, exchange(): return lax.all_to_all(v, 'dev', 0, 0, tiled=True)  38.3 us
    ppermute x29, starting transfers between devices, along(): return lambda v: lax.ppermute(v, 'dev', perm)  30.2 us
    ppermute x12, waiting for transfers between devices, along(): return lambda v: lax.ppermute(v, 'grp', perm)  28 us
    all_to_all x4, starting transfers between devices, exchange(): return lax.all_to_all(v, 'dev', 0, 0, tiled=True)  21.4 us
    all_to_all x1, blocking collectives, exchange(): return lax.all_to_all(v, 'dev', 0, 0, tiled=True)  20.2 us
    ppermute x12, starting transfers between devices, along(): return lambda v: lax.ppermute(v, 'grp', perm)  16 us
    pallas_call x1, Pallas kernels, grad_passages(): pl.pallas_call(grad_p_kernel, in_specs=[SMEM] * 3 + [VMEM] * 9, out_specs...  7.84 us
  transfers between devices with their start and end apart: 45, of which 23 were waited for; matrix products, arithmetic and copies ran while one was open for 2% of the time, Pallas kernels for 5%

profile of v9, /device:TPU:1, one launch (start us, length us, event | category | flops | bytes accessed | tf_op | source)
XLA Modules:
  0.0 236.6 jit_solution(13750746884011315153)
XLA Ops:
  0.6 2.4 %pack.3 = (bf16[32,64,128]{2,1,0:T(8,128)(2,1)}, bf16[32,64,128]{2,1,0:T(8,128)(2,1)}) custom-call(f32[128,4096]{1,0:T(8,128)} %x.7), custom_call_target="tpu_custom_call" | custom-call | bytes 5242880 | tf_op jit(solution)/shard_map/pack/pallas_call | solution.py:75
  3.0 20.2 %all_to_all.25.refs_0_ = bf16[32,64,128]{2,1,0:T(8,128)(2,1)S(1)} all-to-all(bf16[32,64,128]{2,1,0:T(8,128)(2,1)} %get-tuple-element.27), channel_id=1, replica_groups=mesh['grp'=4,'dev'=32] {'dev'}, dimensions={0} | all-to-all | bytes 1048576 | tf_op jit(solution)/shard_map/all_to_all | solution.py:472
  23.3 3.8 %collective-permute-start = (bf16[32,64,128]{2,1,0:T(8,128)(2,1)S(1)}, bf16[32,64,128]{2,1,0:T(8,128)(2,1)S(1)}, u32[]{:S(2)}, u32[]{:S(2)}) collective-permute-start(bf16[32,64,128]{2,1,0:T(8,128)(2,1)S(1)} %all_to_all.25.refs_0_), channel_id=1, source_target_pairs={{0,96},{32,0},{64,32},{96,64},{1,97},{33,1},{65,33},{97,65},{2,98}... | collective-permute-start | bytes 1572872 | tf_op jit(solution)/shard_map/ppermute | solution.py:411
  27.0 3.9 %all-to-all-start = ((bf16[32,64,128]{2,1,0:T(8,128)(2,1)}), bf16[32,64,128]{2,1,0:T(8,128)(2,1)S(1)}, u32[]{:S(2)}, u32[]{:S(2)}) async-start(bf16[32,64,128]{2,1,0:T(8,128)(2,1)} %get-tuple-element.26), calls=%async_computation | async-start | bytes 1048576 | tf_op jit(solution)/shard_map/all_to_all | solution.py:472
  31.0 1.6 copy-done.4
  33.9 8.6 %all-to-all-done.refs_1_ = bf16[32,64,128]{2,1,0:T(8,128)(2,1)S(1)} async-done(((bf16[32,64,128]{2,1,0:T(8,128)(2,1)}), bf16[32,64,128]{2,1,0:T(8,128)(2,1)S(1)}, u32[]{:S(2)}, u32[]{:S(2)}) %all-to-all-start) | async-done | bytes 524320 | tf_op jit(solution)/shard_map/all_to_all | solution.py:472
  42.6 3.7 %all-to-all-start.2 = ((bf16[32,144,128]{2,1,0:T(8,128)(2,1)}), bf16[32,144,128]{2,1,0:T(8,128)(2,1)S(1)}, u32[]{:S(2)}, u32[]{:S(2)}) async-start(bf16[32,144,128]{2,1,0:T(8,128)(2,1)} %pack.2), calls=%async_computation.2 | async-start | bytes 2359296 | tf_op jit(solution)/shard_map/all_to_all | solution.py:472
  46.3 3.0 %collective-permute-start.2 = (bf16[32,64,128]{2,1,0:T(8,128)(2,1)S(1)}, bf16[32,64,128]{2,1,0:T(8,128)(2,1)}, u32[]{:S(2)}, u32[]{:S(2)}) collective-permute-start(bf16[32,64,128]{2,1,0:T(8,128)(2,1)S(1)} %all-to-all-done.refs_1_), channel_id=1, source_target_pairs={{0,96},{32,0},{64,32},{96,64},{1,97},{33,1},{65,33},{97,65},{2,98}... | collective-permute-start | bytes 1572872 | tf_op jit(solution)/shard_map/ppermute | solution.py:411
  49.8 14.8 %all-to-all-done.2.q_own.q = bf16[32,144,128]{2,1,0:T(8,128)(2,1)S(1)} async-done(((bf16[32,144,128]{2,1,0:T(8,128)(2,1)}), bf16[32,144,128]{2,1,0:T(8,128)(2,1)S(1)}, u32[]{:S(2)}, u32[]{:S(2)}) %all-to-all-start.2) | async-done | bytes 1179680 | tf_op jit(solution)/shard_map/all_to_all | solution.py:472
  65.7 2.9 %collective-permute-start.4 = (bf16[32,64,128]{2,1,0:T(8,128)(2,1)S(1)}, bf16[32,64,128]{2,1,0:T(8,128)(2,1)S(1)}, u32[]{:S(2)}, u32[]{:S(2)}) collective-permute-start(bf16[32,64,128]{2,1,0:T(8,128)(2,1)S(1)} %collective-permute-done.refs_2_), channel_id=1, source_target_pairs={{0,96},{32,0},{64,32},{96,64},{1,97},{33,1},{65,33},{97,65},{2,98}... | collective-permute-start | bytes 1572872 | tf_op jit(solution)/shard_map/ppermute | solution.py:411
  69.6 10.0 %collective-permute-done.4.refs_4_ = bf16[32,64,128]{2,1,0:T(8,128)(2,1)S(1)} collective-permute-done((bf16[32,64,128]{2,1,0:T(8,128)(2,1)S(1)}, bf16[32,64,128]{2,1,0:T(8,128)(2,1)S(1)}, u32[]{:S(2)}, u32[]{:S(2)}) %collective-permute-start.4) | collective-permute-done | bytes 524320 | tf_op jit(solution)/shard_map/ppermute | solution.py:411
  80.7 2.2 collective-permute-done.5.refs_5_
  83.0 1.4 collective-permute-start.12
  85.9 7.8 %partial_scores.1 = (f32[2,512,128]{2,1,0:T(8,128)S(1)}, f32[2,512,128]{2,1,0:T(8,128)S(1)}, f32[2,512,128]{2,1,0:T(8,128)S(1)}, f32[2,512,128]{2,1,0:T(8,128)S(...) custom-call(s32[128]{0:T(128)S(1)} %and_select_fusion.ids, ...), custom_call_target="tpu_custom_call" | custom-call | bytes 20971520 | tf_op jit(solution)/shard_map/partial_scores/pallas_call | solution.py:188
  93.8 2.7 %collective-permute-start.19 = (f32[2,512,128]{2,1,0:T(8,128)S(1)}, f32[2,512,128]{2,1,0:T(8,128)S(1)}, u32[]{:S(2)}, u32[]{:S(2)}) collective-permute-start(f32[2,512,128]{2,1,0:T(8,128)S(1)} %get-tuple-element.39), channel_id=1, source_target_pairs={{0,24},{1,7},{2,26},{3,1},{4,28},{5,3},{6,30},{7,5},{8,0},{9,15},{... | collective-permute-start | bytes 1572872 | tf_op jit(solution)/shard_map/ppermute | solution.py:424
  96.5 1.4 collective-permute-start.18
  97.9 5.4 %collective-permute-done.15 = f32[2,512,128]{2,1,0:T(8,128)S(1)} collective-permute-done((f32[2,512,128]{2,1,0:T(8,128)S(1)}, f32[2,512,128]{2,1,0:T(8,128)S(1)}, u32[]{:S(2)}, u32[]{:S(2)}) %collective-permute-start.15) | collective-permute-done | bytes 524320 | tf_op jit(solution)/shard_map/ppermute | solution.py:424
  103.5 2.7 %collective-permute-start.20 = (f32[2,512,128]{2,1,0:T(8,128)S(1)}, f32[2,512,128]{2,1,0:T(8,128)S(1)}, u32[]{:S(2)}, u32[]{:S(2)}) collective-permute-start(f32[2,512,128]{2,1,0:T(8,128)S(1)} %add.104), channel_id=1, source_target_pairs={{0,24},{1,7},{2,26},{3,1},{4,28},{5,3},{6,30},{7,5},{8,0},{9,15},{... | collective-permute-start | bytes 1572872 | tf_op jit(solution)/shard_map/ppermute | solution.py:424
  106.2 1.9 collective-permute-done.17
  108.9 5.6 %collective-permute-done.16 = f32[2,512,128]{2,1,0:T(8,128)S(1)} collective-permute-done((f32[2,512,128]{2,1,0:T(8,128)S(1)}, f32[2,512,128]{2,1,0:T(8,128)S(1)}, u32[]{:S(2)}, u32[]{:S(2)}) %collective-permute-start.16) | collective-permute-done | bytes 524320 | tf_op jit(solution)/shard_map/ppermute | solution.py:424
  117.0 4.8 %collective-permute-done.21 = f32[512,128]{1,0:T(8,128)S(1)} collective-permute-done((f32[512,128]{1,0:T(8,128)S(1)}, f32[512,128]{1,0:T(8,128)S(1)}, u32[]{:S(2)}, u32[]{:S(2)}) %collective-permute-start.21) | collective-permute-done | bytes 262176 | tf_op jit(solution)/shard_map/ppermute | solution.py:424
  121.8 1.5 collective-permute-done.22
  124.7 2.3 collective-permute-start.24
  129.0 3.0 %softmax_weights.1 = bf16[528,128]{1,0:T(8,128)(2,1)S(1)} custom-call(s32[5]{0:T(128)S(1)} %stack.53.at, f32[512,128]{1,0:T(8,128)S(1)} %fusion.6.x_own, f32[512,128]{1,0:T(8,128)} %collective-permute-done.24.x_sib, s32[8,128]{1,0:T(8,128)S(1)} %stack.56.listv, bf16[32,144,128]{2,1,0:T(8,128)(2,1)S(1)} %all-to-all-done.2.q_own.q), custom_call_target="tpu_custom_call" | custom-call | bytes 8388608 | tf_op jit(solution)/shard_map/softmax_weights/pallas_call | solution.py:250
  134.3 1.9 collective-permute-done.25
  136.2 2.4 %collective-permute-done.26 = bf16[528,128]{1,0:T(8,128)(2,1)S(1)} collective-permute-done((bf16[528,128]{1,0:T(8,128)(2,1)S(1)}, bf16[528,128]{1,0:T(8,128)(2,1)S(1)}, u32[]{:S(2)}, u32[]{:S(2)}) %collective-permute-start.26) | collective-permute-done | bytes 135200 | tf_op jit(solution)/shard_map/ppermute | solution.py:424
  138.6 1.6 collective-permute-done.27
  140.4 2.7 %collective-permute-start.29 = (bf16[4,528,128]{2,1,0:T(8,128)(2,1)S(1)}, bf16[4,528,128]{2,1,0:T(8,128)(2,1)S(1)}, u32[]{:S(2)}, u32[]{:S(2)}) collective-permute-start(bf16[4,528,128]{2,1,0:T(8,128)(2,1)S(1)} %pad_maximum_fusion.refs_0_), channel_id=1, source_target_pairs={{0,6},{1,25},{2,0},{3,27},{4,2},{5,29},{6,4},{7,31},{8,14},{9,1},{... | collective-permute-start | bytes 1622024 | tf_op jit(solution)/shard_map/ppermute | solution.py:424
  143.1 6.3 %collective-permute-done.29.refs_2_ = bf16[4,528,128]{2,1,0:T(8,128)(2,1)S(1)} collective-permute-done((bf16[4,528,128]{2,1,0:T(8,128)(2,1)S(1)}, bf16[4,528,128]{2,1,0:T(8,128)(2,1)S(1)}, u32[]{:S(2)}, u32[]{:S(2)}) %collective-permute-start.29) | collective-permute-done | bytes 540704 | tf_op jit(solution)/shard_map/ppermute | solution.py:424
  149.4 3.4 %collective-permute-start.30 = (bf16[4,528,128]{2,1,0:T(8,128)(2,1)S(1)}, bf16[4,528,128]{2,1,0:T(8,128)(2,1)S(1)}, u32[]{:S(2)}, u32[]{:S(2)}) collective-permute-start(bf16[4,528,128]{2,1,0:T(8,128)(2,1)S(1)} %collective-permute-done.29.refs_2_), channel_id=1, source_target_pairs={{0,6},{1,25},{2,0},{3,27},{4,2},{5,29},{6,4},{7,31},{8,14},{9,1},{... | collective-permute-start | bytes 1622024 | tf_op jit(solution)/shard_map/ppermute | solution.py:424
  152.8 2.3 collective-permute-start.31
  155.6 3.5 %collective-permute-done.30.refs_3_ = bf16[4,528,128]{2,1,0:T(8,128)(2,1)S(1)} collective-permute-done((bf16[4,528,128]{2,1,0:T(8,128)(2,1)S(1)}, bf16[4,528,128]{2,1,0:T(8,128)(2,1)S(1)}, u32[]{:S(2)}, u32[]{:S(2)}) %collective-permute-start.30) | collective-permute-done | bytes 540704 | tf_op jit(solution)/shard_map/ppermute | solution.py:424
  159.1 2.9 %collective-permute-start.34 = (bf16[4,528,128]{2,1,0:T(8,128)(2,1)S(1)}, bf16[4,528,128]{2,1,0:T(8,128)(2,1)S(1)}, u32[]{:S(2)}, u32[]{:S(2)}) collective-permute-start(bf16[4,528,128]{2,1,0:T(8,128)(2,1)S(1)} %collective-permute-done.30.refs_3_), channel_id=1, source_target_pairs={{0,1},{1,0},{2,3},{3,2},{4,5},{5,4},{6,7},{7,6},{8,9},{9,8},{10,11... | collective-permute-start | bytes 1622024 | tf_op jit(solution)/shard_map/ppermute | solution.py:424
  162.0 1.4 place.1.p
  163.5 7.8 %grad_passages.1 = (bf16[32,128,128]{2,1,0:T(8,128)(2,1)S(1)}, bf16[16,128,128]{2,1,0:T(8,128)(2,1)S(1)}, bf16[16,128,128]{2,1,0:T(8,128)(2,1)}, bf16[16,128,128...) custom-call(s32[128]{0:T(128)S(1)} %and_select_fusion.ids, ...), custom_call_target="tpu_custom_call" | custom-call | bytes 20971520 | tf_op jit(solution)/shard_map/grad_passages/pallas_call | solution.py:325
  172.8 1.8 collective-permute-start.37
  174.6 6.1 %grad_queries.1 = bf16[32,128,128]{2,1,0:T(8,128)(2,1)} custom-call(s32[128]{0:T(128)S(1)} %and_select_fusion.ids, s32[128]{0:T(128)S(1)} %convert_reduce_fusion.own, s32[5]{0:T(128)S(1)} %stack.53.at, bf16[128,128,128]{2,1,0:T(8,128)(2,1)S(1)} %place.1.p, bf16[4,528,128]{2,1,0:T(8,128)(2,1)S(1)} %pad_maximum_fusion.refs_0_, ...), custom_call_target="tpu_custom_call" | custom-call | bytes 20971520 | tf_op jit(solution)/shard_map/grad_queries/pallas_call | solution.py:360
  180.7 6.7 %all-to-all-start.3 = ((bf16[32,128,128]{2,1,0:T(8,128)(2,1)}), bf16[32,128,128]{2,1,0:T(8,128)(2,1)S(1)}, u32[]{:S(2)}, u32[]{:S(2)}) async-start(bf16[32,128,128]{2,1,0:T(8,128)(2,1)} %grad_queries.1), calls=%async_computation.3 | async-start | bytes 2097152 | tf_op jit(solution)/shard_map/all_to_all | solution.py:472
  188.6 3.0 %collective-permute-start.40 = (bf16[16,128,128]{2,1,0:T(8,128)(2,1)S(1)}, bf16[16,128,128]{2,1,0:T(8,128)(2,1)S(1)}, u32[]{:S(2)}, u32[]{:S(2)}) collective-permute-start(bf16[16,128,128]{2,1,0:T(8,128)(2,1)S(1)} %add_convert_fusion), channel_id=1, source_target_pairs={{0,96},{32,0},{64,32},{96,64},{1,97},{33,1},{65,33},{97,65},{2,98}... | collective-permute-start | bytes 1572872 | tf_op jit(solution)/shard_map/ppermute | solution.py:411
  192.9 3.2 %collective-permute-done.37.refs_1_ = bf16[16,128,128]{2,1,0:T(8,128)(2,1)} collective-permute-done((bf16[16,128,128]{2,1,0:T(8,128)(2,1)}, bf16[16,128,128]{2,1,0:T(8,128)(2,1)}, u32[]{:S(2)}, u32[]{:S(2)}) %collective-permute-start.37) | collective-permute-done | bytes 524320 | tf_op jit(solution)/shard_map/ppermute | solution.py:411
  196.1 1.4 collective-permute-done.38.refs_2_
  197.5 9.7 %collective-permute-done.40.refs_3_ = bf16[16,128,128]{2,1,0:T(8,128)(2,1)S(1)} collective-permute-done((bf16[16,128,128]{2,1,0:T(8,128)(2,1)S(1)}, bf16[16,128,128]{2,1,0:T(8,128)(2,1)S(1)}, u32[]{:S(2)}, u32[]{:S(2)}) %collective-permute-start.40) | collective-permute-done | bytes 524320 | tf_op jit(solution)/shard_map/ppermute | solution.py:411
  207.2 1.4 collective-permute-done.36.refs_0_
  208.6 2.4 %join.1 = bf16[32,128,128]{2,1,0:T(8,128)(2,1)} custom-call(bf16[32,128,128]{2,1,0:T(8,128)(2,1)S(1)} %get-tuple-element.42.kept, bf16[16,128,128]{2,1,0:T(8,128)(2,1)S(1)} %collective-permute-done.36.refs_0_, bf16[16,128,128]{2,1,0:T(8,128)(2,1)} %collective-permute-done.37.refs_1_, bf16[16,128,128]{2,1,0:T(8,128)(2,1)} %collective-permute-done.38.refs_2_, ...), custom_call_target="tpu_custom_call" | custom-call | bytes 8388608 | tf_op jit(solution)/shard_map/join/pallas_call | solution.py:396
  211.1 7.0 %all-to-all-start.4 = ((bf16[32,128,128]{2,1,0:T(8,128)(2,1)}), bf16[32,128,128]{2,1,0:T(8,128)(2,1)S(1)}, u32[]{:S(2)}, u32[]{:S(2)}) async-start(bf16[32,128,128]{2,1,0:T(8,128)(2,1)} %join.1), calls=%async_computation.4 | async-start | bytes 2097152 | tf_op jit(solution)/shard_map/all_to_all | solution.py:472
  218.7 1.4 unpack.2
  220.1 14.9 %all-to-all-done.4.x = bf16[32,128,128]{2,1,0:T(8,128)(2,1)S(1)} async-done(((bf16[32,128,128]{2,1,0:T(8,128)(2,1)}), bf16[32,128,128]{2,1,0:T(8,128)(2,1)S(1)}, u32[]{:S(2)}, u32[]{:S(2)}) %all-to-all-start.4) | async-done | bytes 1048608 | tf_op jit(solution)/shard_map/all_to_all | solution.py:472
  235.1 1.4 unpack.3
  (91 shorter events, 20.8 us)
Async XLA Ops:
  23.3 19.3 %collective-permute-start = (bf16[32,64,128]{2,1,0:T(8,128)(2,1)S(1)}, bf16[32,64,128]{2,1,0:T(8,128)(2,1)S(1)}, u32[]{:S(2)}, u32[]{:S(2)}) collective-permute-start(bf16[32,64,128]{2,1,0:T(8,128)(2,1)S(1)} %all_to_all.25.refs_0_), channel_id=1, source_target_pairs={{0,96},{32,0},{64,32},{96,64},{1,97},{33,1},{65,33},{97,65},{2,98}... | collective-permute-start | bytes 1572872 | tf_op jit(solution)/shard_map/ppermute | solution.py:411
  27.0 15.5 %collective-permute-start.1 = (bf16[32,64,128]{2,1,0:T(8,128)(2,1)S(1)}, bf16[32,64,128]{2,1,0:T(8,128)(2,1)S(1)}, u32[]{:S(2)}, u32[]{:S(2)}) collective-permute-start(bf16[32,64,128]{2,1,0:T(8,128)(2,1)S(1)} %all_to_all.25.refs_0_), channel_id=1, source_target_pairs={{0,32},{32,64},{64,96},{96,0},{1,33},{33,65},{65,97},{97,1},{2,34}... | collective-permute-start | bytes 1572872 | tf_op jit(solution)/shard_map/ppermute | solution.py:411
  27.0 15.5 %all-to-all-start = ((bf16[32,64,128]{2,1,0:T(8,128)(2,1)}), bf16[32,64,128]{2,1,0:T(8,128)(2,1)S(1)}, u32[]{:S(2)}, u32[]{:S(2)}) async-start(bf16[32,64,128]{2,1,0:T(8,128)(2,1)} %get-tuple-element.26), calls=%async_computation | async-start | bytes 1048576 | tf_op jit(solution)/shard_map/all_to_all | solution.py:472
  32.5 36.0 %copy-start.7 = (s32[1,32]{1,0:T(1,128)S(1)}, s32[1,32]{1,0:T(1,128)}, u32[]{:S(2)}) copy-start(s32[1,32]{1,0:T(1,128)} %param.8) | copy-start | bytes 388
  42.6 22.1 %all-to-all-start.2 = ((bf16[32,144,128]{2,1,0:T(8,128)(2,1)}), bf16[32,144,128]{2,1,0:T(8,128)(2,1)S(1)}, u32[]{:S(2)}, u32[]{:S(2)}) async-start(bf16[32,144,128]{2,1,0:T(8,128)(2,1)} %pack.2), calls=%async_computation.2 | async-start | bytes 2359296 | tf_op jit(solution)/shard_map/all_to_all | solution.py:472
  46.3 18.9 %collective-permute-start.2 = (bf16[32,64,128]{2,1,0:T(8,128)(2,1)S(1)}, bf16[32,64,128]{2,1,0:T(8,128)(2,1)}, u32[]{:S(2)}, u32[]{:S(2)}) collective-permute-start(bf16[32,64,128]{2,1,0:T(8,128)(2,1)S(1)} %all-to-all-done.refs_1_), channel_id=1, source_target_pairs={{0,96},{32,0},{64,32},{96,64},{1,97},{33,1},{65,33},{97,65},{2,98}... | collective-permute-start | bytes 1572872 | tf_op jit(solution)/shard_map/ppermute | solution.py:411
  49.3 16.1 %collective-permute-start.3 = (bf16[32,64,128]{2,1,0:T(8,128)(2,1)S(1)}, bf16[32,64,128]{2,1,0:T(8,128)(2,1)}, u32[]{:S(2)}, u32[]{:S(2)}) collective-permute-start(bf16[32,64,128]{2,1,0:T(8,128)(2,1)S(1)} %all-to-all-done.refs_1_), channel_id=1, source_target_pairs={{0,32},{32,64},{64,96},{96,0},{1,33},{33,65},{65,97},{97,1},{2,34}... | collective-permute-start | bytes 1572872 | tf_op jit(solution)/shard_map/ppermute | solution.py:411
  49.3 16.4 %collective-permute-start.7 = (bf16[32,64,128]{2,1,0:T(8,128)(2,1)S(1)}, bf16[32,64,128]{2,1,0:T(8,128)(2,1)}, u32[]{:S(2)}, u32[]{:S(2)}) collective-permute-start(bf16[32,64,128]{2,1,0:T(8,128)(2,1)S(1)} %all_to_all.25.refs_0_), channel_id=1, source_target_pairs={{0,1},{1,0},{2,3},{3,2},{4,5},{5,4},{6,7},{7,6},{8,9},{9,8},{10,11... | collective-permute-start | bytes 1572872 | tf_op jit(solution)/shard_map/ppermute | solution.py:424
  49.8 18.8 %collective-permute-start.8 = (bf16[32,64,128]{2,1,0:T(8,128)(2,1)S(1)}, bf16[32,64,128]{2,1,0:T(8,128)(2,1)}, u32[]{:S(2)}, u32[]{:S(2)}) collective-permute-start(bf16[32,64,128]{2,1,0:T(8,128)(2,1)S(1)} %all-to-all-done.refs_1_), channel_id=1, source_target_pairs={{0,1},{1,0},{2,3},{3,2},{4,5},{5,4},{6,7},{7,6},{8,9},{9,8},{10,11... | collective-permute-start | bytes 1572872 | tf_op jit(solution)/shard_map/ppermute | solution.py:424
  64.6 21.3 %collective-permute-start.6 = (bf16[32,144,128]{2,1,0:T(8,128)(2,1)S(1)}, bf16[32,144,128]{2,1,0:T(8,128)(2,1)}, u32[]{:S(2)}, u32[]{:S(2)}) collective-permute-start(bf16[32,144,128]{2,1,0:T(8,128)(2,1)S(1)} %all-to-all-done.2.q_own.q), channel_id=1, source_target_pairs={{0,1},{1,0},{2,3},{3,2},{4,5},{5,4},{6,7},{7,6},{8,9},{9,8},{10,11... | collective-permute-start | bytes 3538952 | tf_op jit(solution)/shard_map/ppermute | solution.py:424
  65.2 3.7 %collective-permute-start.9 = (bf16[32,64,128]{2,1,0:T(8,128)(2,1)S(1)}, bf16[32,64,128]{2,1,0:T(8,128)(2,1)S(1)}, u32[]{:S(2)}, u32[]{:S(2)}) collective-permute-start(bf16[32,64,128]{2,1,0:T(8,128)(2,1)S(1)} %collective-permute-done.refs_2_), channel_id=1, source_target_pairs={{0,1},{1,0},{2,3},{3,2},{4,5},{5,4},{6,7},{7,6},{8,9},{9,8},{10,11... | collective-permute-start | bytes 1572872 | tf_op jit(solution)/shard_map/ppermute | solution.py:424
  65.4 4.1 %collective-permute-start.13 = (bf16[32,64,128]{2,1,0:T(8,128)(2,1)S(1)}, bf16[32,64,128]{2,1,0:T(8,128)(2,1)S(1)}, u32[]{:S(2)}, u32[]{:S(2)}) collective-permute-start(bf16[32,64,128]{2,1,0:T(8,128)(2,1)S(1)} %collective-permute-done.1.refs_6_), channel_id=1, source_target_pairs={{0,1},{1,0},{2,3},{3,2},{4,5},{5,4},{6,7},{7,6},{8,9},{9,8},{10,11... | collective-permute-start | bytes 1572872 | tf_op jit(solution)/shard_map/ppermute | solution.py:424
  65.7 13.9 %collective-permute-start.4 = (bf16[32,64,128]{2,1,0:T(8,128)(2,1)S(1)}, bf16[32,64,128]{2,1,0:T(8,128)(2,1)S(1)}, u32[]{:S(2)}, u32[]{:S(2)}) collective-permute-start(bf16[32,64,128]{2,1,0:T(8,128)(2,1)S(1)} %collective-permute-done.refs_2_), channel_id=1, source_target_pairs={{0,96},{32,0},{64,32},{96,64},{1,97},{33,1},{65,33},{97,65},{2,98}... | collective-permute-start | bytes 1572872 | tf_op jit(solution)/shard_map/ppermute | solution.py:411
  68.6 14.4 %collective-permute-start.5 = (bf16[32,64,128]{2,1,0:T(8,128)(2,1)}, bf16[32,64,128]{2,1,0:T(8,128)(2,1)S(1)}, u32[]{:S(2)}, u32[]{:S(2)}) collective-permute-start(bf16[32,64,128]{2,1,0:T(8,128)(2,1)} %collective-permute-done.3.refs_7_), channel_id=1, source_target_pairs={{0,32},{32,64},{64,96},{96,0},{1,33},{33,65},{65,97},{97,1},{2,34}... | collective-permute-start | bytes 1572872 | tf_op jit(solution)/shard_map/ppermute | solution.py:411
  68.9 15.6 %collective-permute-start.10 = (bf16[32,64,128]{2,1,0:T(8,128)(2,1)}, bf16[32,64,128]{2,1,0:T(8,128)(2,1)S(1)}, u32[]{:S(2)}, u32[]{:S(2)}) collective-permute-start(bf16[32,64,128]{2,1,0:T(8,128)(2,1)} %collective-permute-done.2.refs_3_), channel_id=1, source_target_pairs={{0,1},{1,0},{2,3},{3,2},{4,5},{5,4},{6,7},{7,6},{8,9},{9,8},{10,11... | collective-permute-start | bytes 1572872 | tf_op jit(solution)/shard_map/ppermute | solution.py:424
  69.5 15.0 %collective-permute-start.14 = (bf16[32,64,128]{2,1,0:T(8,128)(2,1)}, bf16[32,64,128]{2,1,0:T(8,128)(2,1)S(1)}, u32[]{:S(2)}, u32[]{:S(2)}) collective-permute-start(bf16[32,64,128]{2,1,0:T(8,128)(2,1)} %collective-permute-done.3.refs_7_), channel_id=1, source_target_pairs={{0,1},{1,0},{2,3},{3,2},{4,5},{5,4},{6,7},{7,6},{8,9},{9,8},{10,11... | collective-permute-start | bytes 1572872 | tf_op jit(solution)/shard_map/ppermute | solution.py:424
  79.6 4.9 %collective-permute-start.11 = (bf16[32,64,128]{2,1,0:T(8,128)(2,1)S(1)}, bf16[32,64,128]{2,1,0:T(8,128)(2,1)S(1)}, u32[]{:S(2)}, u32[]{:S(2)}) collective-permute-start(bf16[32,64,128]{2,1,0:T(8,128)(2,1)S(1)} %collective-permute-done.4.refs_4_), channel_id=1, source_target_pairs={{0,1},{1,0},{2,3},{3,2},{4,5},{5,4},{6,7},{7,6},{8,9},{9,8},{10,11... | collective-permute-start | bytes 1572872 | tf_op jit(solution)/shard_map/ppermute | solution.py:424
  83.0 2.9 %collective-permute-start.12 = (bf16[32,64,128]{2,1,0:T(8,128)(2,1)S(1)}, bf16[32,64,128]{2,1,0:T(8,128)(2,1)S(1)}, u32[]{:S(2)}, u32[]{:S(2)}) collective-permute-start(bf16[32,64,128]{2,1,0:T(8,128)(2,1)S(1)} %collective-permute-done.5.refs_5_), channel_id=1, source_target_pairs={{0,1},{1,0},{2,3},{3,2},{4,5},{5,4},{6,7},{7,6},{8,9},{9,8},{10,11... | collective-permute-start | bytes 1572872 | tf_op jit(solution)/shard_map/ppermute | solution.py:424
  93.7 9.6 %collective-permute-start.15 = (f32[2,512,128]{2,1,0:T(8,128)S(1)}, f32[2,512,128]{2,1,0:T(8,128)S(1)}, u32[]{:S(2)}, u32[]{:S(2)}) collective-permute-start(f32[2,512,128]{2,1,0:T(8,128)S(1)} %get-tuple-element.35), channel_id=1, source_target_pairs={{0,8},{1,3},{2,10},{3,5},{4,12},{5,7},{6,14},{7,1},{8,16},{9,11},{... | collective-permute-start | bytes 1572872 | tf_op jit(solution)/shard_map/ppermute | solution.py:424
  93.8 9.7 %collective-permute-start.19 = (f32[2,512,128]{2,1,0:T(8,128)S(1)}, f32[2,512,128]{2,1,0:T(8,128)S(1)}, u32[]{:S(2)}, u32[]{:S(2)}) collective-permute-start(f32[2,512,128]{2,1,0:T(8,128)S(1)} %get-tuple-element.39), channel_id=1, source_target_pairs={{0,24},{1,7},{2,26},{3,1},{4,28},{5,3},{6,30},{7,5},{8,0},{9,15},{... | collective-permute-start | bytes 1572872 | tf_op jit(solution)/shard_map/ppermute | solution.py:424
  96.4 11.7 %collective-permute-start.17 = (f32[2,512,128]{2,1,0:T(8,128)S(1)}, f32[2,512,128]{2,1,0:T(8,128)S(1)}, u32[]{:S(2)}, u32[]{:S(2)}) collective-permute-start(f32[2,512,128]{2,1,0:T(8,128)S(1)} %get-tuple-element.36), channel_id=1, source_target_pairs={{0,24},{1,7},{2,26},{3,1},{4,28},{5,3},{6,30},{7,5},{8,0},{9,15},{... | collective-permute-start | bytes 1572872 | tf_op jit(solution)/shard_map/ppermute | solution.py:424
  96.5 12.4 %collective-permute-start.18 = (f32[2,512,128]{2,1,0:T(8,128)S(1)}, f32[2,512,128]{2,1,0:T(8,128)S(1)}, u32[]{:S(2)}, u32[]{:S(2)}) collective-permute-start(f32[2,512,128]{2,1,0:T(8,128)S(1)} %get-tuple-element.37), channel_id=1, source_target_pairs={{0,8},{1,3},{2,10},{3,5},{4,12},{5,7},{6,14},{7,1},{8,16},{9,11},{... | collective-permute-start | bytes 1572872 | tf_op jit(solution)/shard_map/ppermute | solution.py:424
  103.4 11.2 %collective-permute-start.16 = (f32[2,512,128]{2,1,0:T(8,128)S(1)}, f32[2,512,128]{2,1,0:T(8,128)S(1)}, u32[]{:S(2)}, u32[]{:S(2)}) collective-permute-start(f32[2,512,128]{2,1,0:T(8,128)S(1)} %add.99), channel_id=1, source_target_pairs={{0,8},{1,3},{2,10},{3,5},{4,12},{5,7},{6,14},{7,1},{8,16},{9,11},{... | collective-permute-start | bytes 1572872 | tf_op jit(solution)/shard_map/ppermute | solution.py:424
  103.5 11.0 %collective-permute-start.20 = (f32[2,512,128]{2,1,0:T(8,128)S(1)}, f32[2,512,128]{2,1,0:T(8,128)S(1)}, u32[]{:S(2)}, u32[]{:S(2)}) collective-permute-start(f32[2,512,128]{2,1,0:T(8,128)S(1)} %add.104), channel_id=1, source_target_pairs={{0,24},{1,7},{2,26},{3,1},{4,28},{5,3},{6,30},{7,5},{8,0},{9,15},{... | collective-permute-start | bytes 1572872 | tf_op jit(solution)/shard_map/ppermute | solution.py:424
  114.7 7.1 %collective-permute-start.21 = (f32[512,128]{1,0:T(8,128)S(1)}, f32[512,128]{1,0:T(8,128)S(1)}, u32[]{:S(2)}, u32[]{:S(2)}) collective-permute-start(f32[512,128]{1,0:T(8,128)S(1)} %get-tuple-element.49), channel_id=1, source_target_pairs={{0,4},{1,17},{2,6},{3,19},{4,0},{5,21},{6,2},{7,23},{8,12},{9,25},... | collective-permute-start | bytes 786440 | tf_op jit(solution)/shard_map/ppermute | solution.py:424
  115.5 7.8 %collective-permute-start.22 = (f32[512,128]{1,0:T(8,128)S(1)}, f32[512,128]{1,0:T(8,128)S(1)}, u32[]{:S(2)}, u32[]{:S(2)}) collective-permute-start(f32[512,128]{1,0:T(8,128)S(1)} %get-tuple-element.50), channel_id=1, source_target_pairs={{0,6},{1,25},{2,0},{3,27},{4,2},{5,29},{6,4},{7,31},{8,14},{9,1},{... | collective-permute-start | bytes 786440 | tf_op jit(solution)/shard_map/ppermute | solution.py:424
  116.2 8.4 %collective-permute-start.23 = (f32[512,128]{1,0:T(8,128)S(1)}, f32[512,128]{1,0:T(8,128)S(1)}, u32[]{:S(2)}, u32[]{:S(2)}) collective-permute-start(f32[512,128]{1,0:T(8,128)S(1)} %get-tuple-element.51), channel_id=1, source_target_pairs={{0,2},{1,9},{2,4},{3,11},{4,6},{5,13},{6,0},{7,15},{8,10},{9,17},{... | collective-permute-start | bytes 786440 | tf_op jit(solution)/shard_map/ppermute | solution.py:424
  124.7 4.2 %collective-permute-start.24 = (f32[512,128]{1,0:T(8,128)S(1)}, f32[512,128]{1,0:T(8,128)}, u32[]{:S(2)}, u32[]{:S(2)}) collective-permute-start(f32[512,128]{1,0:T(8,128)S(1)} %fusion.6.x_own), channel_id=1, source_target_pairs={{0,1},{1,0},{2,3},{3,2},{4,5},{5,4},{6,7},{7,6},{8,9},{9,8},{10,11... | collective-permute-start | bytes 786440 | tf_op jit(solution)/shard_map/ppermute | solution.py:424
  129.0 33.0 %copy-start.1 = (bf16[32,64,128]{2,1,0:T(8,128)(2,1)S(1)}, bf16[32,64,128]{2,1,0:T(8,128)(2,1)}, u32[]{:S(2)}) copy-start(bf16[32,64,128]{2,1,0:T(8,128)(2,1)} %copy-done) | copy-start | bytes 1572868
  129.0 33.0 %copy-start.3 = (bf16[32,64,128]{2,1,0:T(8,128)(2,1)S(1)}, bf16[32,64,128]{2,1,0:T(8,128)(2,1)}, u32[]{:S(2)}) copy-start(bf16[32,64,128]{2,1,0:T(8,128)(2,1)} %copy-done.2) | copy-start | bytes 1572868
  132.0 4.2 %collective-permute-start.25 = (bf16[528,128]{1,0:T(8,128)(2,1)S(1)}, bf16[528,128]{1,0:T(8,128)(2,1)S(1)}, u32[]{:S(2)}, u32[]{:S(2)}) collective-permute-start(bf16[528,128]{1,0:T(8,128)(2,1)S(1)} %softmax_weights.1), channel_id=1, source_target_pairs={{0,24},{1,7},{2,26},{3,1},{4,28},{5,3},{6,30},{7,5},{8,0},{9,15},{... | collective-permute-start | bytes 405512 | tf_op jit(solution)/shard_map/ppermute | solution.py:424
  133.2 5.5 %collective-permute-start.26 = (bf16[528,128]{1,0:T(8,128)(2,1)S(1)}, bf16[528,128]{1,0:T(8,128)(2,1)S(1)}, u32[]{:S(2)}, u32[]{:S(2)}) collective-permute-start(bf16[528,128]{1,0:T(8,128)(2,1)S(1)} %softmax_weights.1), channel_id=1, source_target_pairs={{0,16},{1,5},{2,18},{3,7},{4,20},{5,1},{6,22},{7,3},{8,24},{9,13},... | collective-permute-start | bytes 405512 | tf_op jit(solution)/shard_map/ppermute | solution.py:424
  133.9 6.4 %collective-permute-start.27 = (bf16[528,128]{1,0:T(8,128)(2,1)S(1)}, bf16[528,128]{1,0:T(8,128)(2,1)S(1)}, u32[]{:S(2)}, u32[]{:S(2)}) collective-permute-start(bf16[528,128]{1,0:T(8,128)(2,1)S(1)} %softmax_weights.1), channel_id=1, source_target_pairs={{0,8},{1,3},{2,10},{3,5},{4,12},{5,7},{6,14},{7,1},{8,16},{9,11},{... | collective-permute-start | bytes 405512 | tf_op jit(solution)/shard_map/ppermute | solution.py:424
  140.4 9.0 %collective-permute-start.29 = (bf16[4,528,128]{2,1,0:T(8,128)(2,1)S(1)}, bf16[4,528,128]{2,1,0:T(8,128)(2,1)S(1)}, u32[]{:S(2)}, u32[]{:S(2)}) collective-permute-start(bf16[4,528,128]{2,1,0:T(8,128)(2,1)S(1)} %pad_maximum_fusion.refs_0_), channel_id=1, source_target_pairs={{0,6},{1,25},{2,0},{3,27},{4,2},{5,29},{6,4},{7,31},{8,14},{9,1},{... | collective-permute-start | bytes 1622024 | tf_op jit(solution)/shard_map/ppermute | solution.py:424
  143.1 12.0 %collective-permute-start.28 = (bf16[4,528,128]{2,1,0:T(8,128)(2,1)S(1)}, bf16[4,528,128]{2,1,0:T(8,128)(2,1)S(1)}, u32[]{:S(2)}, u32[]{:S(2)}) collective-permute-start(bf16[4,528,128]{2,1,0:T(8,128)(2,1)S(1)} %pad_maximum_fusion.refs_0_), channel_id=1, source_target_pairs={{0,2},{1,9},{2,4},{3,11},{4,6},{5,13},{6,0},{7,15},{8,10},{9,17},{... | collective-permute-start | bytes 1622024 | tf_op jit(solution)/shard_map/ppermute | solution.py:424
  149.4 9.7 %collective-permute-start.30 = (bf16[4,528,128]{2,1,0:T(8,128)(2,1)S(1)}, bf16[4,528,128]{2,1,0:T(8,128)(2,1)S(1)}, u32[]{:S(2)}, u32[]{:S(2)}) collective-permute-start(bf16[4,528,128]{2,1,0:T(8,128)(2,1)S(1)} %collective-permute-done.29.refs_2_), channel_id=1, source_target_pairs={{0,6},{1,25},{2,0},{3,27},{4,2},{5,29},{6,4},{7,31},{8,14},{9,1},{... | collective-permute-start | bytes 1622024 | tf_op jit(solution)/shard_map/ppermute | solution.py:424
  152.8 10.6 %collective-permute-start.31 = (bf16[4,528,128]{2,1,0:T(8,128)(2,1)S(1)}, bf16[4,528,128]{2,1,0:T(8,128)(2,1)S(1)}, u32[]{:S(2)}, u32[]{:S(2)}) collective-permute-start(bf16[4,528,128]{2,1,0:T(8,128)(2,1)S(1)} %pad_maximum_fusion.refs_0_), channel_id=1, source_target_pairs={{0,1},{1,0},{2,3},{3,2},{4,5},{5,4},{6,7},{7,6},{8,9},{9,8},{10,11... | collective-permute-start | bytes 1622024 | tf_op jit(solution)/shard_map/ppermute | solution.py:424
  155.1 8.3 %collective-permute-start.33 = (bf16[4,528,128]{2,1,0:T(8,128)(2,1)S(1)}, bf16[4,528,128]{2,1,0:T(8,128)(2,1)S(1)}, u32[]{:S(2)}, u32[]{:S(2)}) collective-permute-start(bf16[4,528,128]{2,1,0:T(8,128)(2,1)S(1)} %collective-permute-done.29.refs_2_), channel_id=1, source_target_pairs={{0,1},{1,0},{2,3},{3,2},{4,5},{5,4},{6,7},{7,6},{8,9},{9,8},{10,11... | collective-permute-start | bytes 1622024 | tf_op jit(solution)/shard_map/ppermute | solution.py:424
  155.1 8.3 %collective-permute-start.32 = (bf16[4,528,128]{2,1,0:T(8,128)(2,1)S(1)}, bf16[4,528,128]{2,1,0:T(8,128)(2,1)S(1)}, u32[]{:S(2)}, u32[]{:S(2)}) collective-permute-start(bf16[4,528,128]{2,1,0:T(8,128)(2,1)S(1)} %collective-permute-done.28.refs_1_), channel_id=1, source_target_pairs={{0,1},{1,0},{2,3},{3,2},{4,5},{5,4},{6,7},{7,6},{8,9},{9,8},{10,11... | collective-permute-start | bytes 1622024 | tf_op jit(solution)/shard_map/ppermute | solution.py:424
  159.1 4.4 %collective-permute-start.34 = (bf16[4,528,128]{2,1,0:T(8,128)(2,1)S(1)}, bf16[4,528,128]{2,1,0:T(8,128)(2,1)S(1)}, u32[]{:S(2)}, u32[]{:S(2)}) collective-permute-start(bf16[4,528,128]{2,1,0:T(8,128)(2,1)S(1)} %collective-permute-done.30.refs_3_), channel_id=1, source_target_pairs={{0,1},{1,0},{2,3},{3,2},{4,5},{5,4},{6,7},{7,6},{8,9},{9,8},{10,11... | collective-permute-start | bytes 1622024 | tf_op jit(solution)/shard_map/ppermute | solution.py:424
  171.4 16.0 %collective-permute-start.39 = (bf16[16,128,128]{2,1,0:T(8,128)(2,1)}, bf16[16,128,128]{2,1,0:T(8,128)(2,1)}, u32[]{:S(2)}, u32[]{:S(2)}) collective-permute-start(bf16[16,128,128]{2,1,0:T(8,128)(2,1)} %get-tuple-element.48), channel_id=1, source_target_pairs={{0,96},{32,0},{64,32},{96,64},{1,97},{33,1},{65,33},{97,65},{2,98}... | collective-permute-start | bytes 1572872 | tf_op jit(solution)/shard_map/ppermute | solution.py:411
  171.9 19.7 %collective-permute-start.35 = (bf16[16,128,128]{2,1,0:T(8,128)(2,1)}, bf16[16,128,128]{2,1,0:T(8,128)(2,1)}, u32[]{:S(2)}, u32[]{:S(2)}) collective-permute-start(bf16[16,128,128]{2,1,0:T(8,128)(2,1)} %get-tuple-element.44), channel_id=1, source_target_pairs={{0,32},{32,64},{64,96},{96,0},{1,33},{33,65},{65,97},{97,1},{2,34}... | collective-permute-start | bytes 1572872 | tf_op jit(solution)/shard_map/ppermute | solution.py:411
  172.8 23.2 %collective-permute-start.37 = (bf16[16,128,128]{2,1,0:T(8,128)(2,1)}, bf16[16,128,128]{2,1,0:T(8,128)(2,1)}, u32[]{:S(2)}, u32[]{:S(2)}) collective-permute-start(bf16[16,128,128]{2,1,0:T(8,128)(2,1)} %get-tuple-element.45), channel_id=1, source_target_pairs={{0,96},{32,0},{64,32},{96,64},{1,97},{33,1},{65,33},{97,65},{2,98}... | collective-permute-start | bytes 1572872 | tf_op jit(solution)/shard_map/ppermute | solution.py:411
  174.6 22.9 %collective-permute-start.38 = (bf16[16,128,128]{2,1,0:T(8,128)(2,1)}, bf16[16,128,128]{2,1,0:T(8,128)(2,1)}, u32[]{:S(2)}, u32[]{:S(2)}) collective-permute-start(bf16[16,128,128]{2,1,0:T(8,128)(2,1)} %get-tuple-element.46), channel_id=1, source_target_pairs={{0,32},{32,64},{64,96},{96,0},{1,33},{33,65},{65,97},{97,1},{2,34}... | collective-permute-start | bytes 1572872 | tf_op jit(solution)/shard_map/ppermute | solution.py:411
  180.7 30.4 %all-to-all-start.3 = ((bf16[32,128,128]{2,1,0:T(8,128)(2,1)}), bf16[32,128,128]{2,1,0:T(8,128)(2,1)S(1)}, u32[]{:S(2)}, u32[]{:S(2)}) async-start(bf16[32,128,128]{2,1,0:T(8,128)(2,1)} %grad_queries.1), calls=%async_computation.3 | async-start | bytes 2097152 | tf_op jit(solution)/shard_map/all_to_all | solution.py:472
  188.6 18.6 %collective-permute-start.40 = (bf16[16,128,128]{2,1,0:T(8,128)(2,1)S(1)}, bf16[16,128,128]{2,1,0:T(8,128)(2,1)S(1)}, u32[]{:S(2)}, u32[]{:S(2)}) collective-permute-start(bf16[16,128,128]{2,1,0:T(8,128)(2,1)S(1)} %add_convert_fusion), channel_id=1, source_target_pairs={{0,96},{32,0},{64,32},{96,64},{1,97},{33,1},{65,33},{97,65},{2,98}... | collective-permute-start | bytes 1572872 | tf_op jit(solution)/shard_map/ppermute | solution.py:411
  192.8 15.8 %collective-permute-start.36 = (bf16[16,128,128]{2,1,0:T(8,128)(2,1)S(1)}, bf16[16,128,128]{2,1,0:T(8,128)(2,1)S(1)}, u32[]{:S(2)}, u32[]{:S(2)}) collective-permute-start(bf16[16,128,128]{2,1,0:T(8,128)(2,1)S(1)} %add_convert_fusion.1), channel_id=1, source_target_pairs={{0,32},{32,64},{64,96},{96,0},{1,33},{33,65},{65,97},{97,1},{2,34}... | collective-permute-start | bytes 1572872 | tf_op jit(solution)/shard_map/ppermute | solution.py:411
  211.1 24.0 %all-to-all-start.4 = ((bf16[32,128,128]{2,1,0:T(8,128)(2,1)}), bf16[32,128,128]{2,1,0:T(8,128)(2,1)S(1)}, u32[]{:S(2)}, u32[]{:S(2)}) async-start(bf16[32,128,128]{2,1,0:T(8,128)(2,1)} %join.1), calls=%async_computation.4 | async-start | bytes 2097152 | tf_op jit(solution)/shard_map/all_to_all | solution.py:472
  (5 other events, 89.0 us)
